TPU v7x, 32 devices: a whole 2x2x4 slice. The times are simulated.
32 devices in a mesh: dp: 4 (over x, core), seq: 8 (over z, y).
Axes of the slice: x: 2, y: 2, z: 4, core: 2. Of those that a mesh axis runs over, the one named last changes fastest.
Arguments:
- layer_input: bfloat16 [4, 1024, 4096], P('dp', 'seq'), may hold values from -6 to 6
- proj_weight: bfloat16 [4096, 256], replicated, may hold values from -0.0078125 to 0.0078125
- inputs: bfloat16 [4, 1024, 2048], P('dp', 'seq'), may hold values from -6 to 6
- step_size: float32 [4, 32, 1024], P('dp', None, 'seq'), may hold values from 0.02 to 0.2
- log_decay: float32 [4, 32, 1024], P('dp', None, 'seq'), may hold values from -0.8 to 0, as said below
- skip_gain: float32 [32], replicated, may hold values from 0.1 to 1.9
- grad_out: bfloat16 [4, 1024, 2048], P('dp', 'seq'), may hold values from -6 to 6
Outputs:
- grad_inputs: bfloat16 [4, 1024, 2048], P('dp', 'seq')
- grad_weight: float32 [4096, 256], P(('dp', 'seq'))
Inputs may be any that keep to these rules, and one draw needn't show every extreme that they name: `log_decay`: every entry is negative.
All inputs are finite; a program needn't handle non-finite values.
Results may differ from a plain program's by a relative error of at most 0.0069.
Values sent between devices are 32-bit elements; how exact they have to be, the bound alone decides.
No kernel may reach another device: no remote copies, remote signals or barrier semaphores. Data moves between devices by JAX's collectives and lax.ppermute only.
A program may use at most 192 MiB of HBM per device.

v0:
```python
import jax
import jax.numpy as jnp
from jax import lax
from jax.sharding import PartitionSpec as P

SHARD_CHANNELS = 32
HEAD_DIM = 64
STATE = 128
SPAN = 128


def prefix(value, axis, combine, identity, reverse):
    length, position = (lax.axis_size(axis), lax.axis_index(axis))
    everything = jax.tree.map(lambda part: lax.all_gather(part, axis), value)
    start = jax.tree.map(
        lambda part, zero: jnp.broadcast_to(jnp.asarray(zero, part.dtype), part.shape),
        value,
        identity,
    )

    def step(k, before):
        at = length - 1 - k if reverse else k
        reached = at > position if reverse else at < position
        new = combine(before, jax.tree.map(lambda part: part[at], everything))
        return jax.tree.map(lambda a, b: jnp.where(reached, a, b), new, before)

    return lax.fori_loop(0, length, step, start)


def span_inputs(proj, inputs, grad_out, step_size, log_decay):
    length = inputs.shape[0]
    spans = length // SPAN
    b_cols = proj[:, :STATE].reshape(spans, SPAN, STATE)
    c_cols = proj[:, STATE:].reshape(spans, SPAN, STATE)
    inputs_c = inputs.reshape(spans, SPAN, SHARD_CHANNELS, HEAD_DIM)
    grad_rows = grad_out.reshape(spans, SPAN, SHARD_CHANNELS, HEAD_DIM)
    step_rows = step_size.reshape(SHARD_CHANNELS, spans, SPAN).transpose(1, 0, 2)
    decay_sum = jnp.cumsum(
        log_decay.reshape(SHARD_CHANNELS, spans, SPAN).transpose(1, 0, 2), axis=2
    )
    span_total = decay_sum[:, :, -1]
    to_end = jnp.exp(span_total[:, :, None] - decay_sum)
    weighted = (
        inputs_c.astype(jnp.float32) * jnp.transpose(step_rows * to_end, (0, 2, 1))[..., None]
    ).astype(jnp.bfloat16)
    scaled = (
        grad_rows.astype(jnp.float32) * jnp.transpose(jnp.exp(decay_sum), (0, 2, 1))[..., None]
    ).astype(jnp.bfloat16)
    own_state = jnp.einsum("cqhp,cqn->chpn", weighted, b_cols, preferred_element_type=jnp.float32)
    own_grad = jnp.einsum("cqhp,cqn->chpn", scaled, c_cols, preferred_element_type=jnp.float32)
    return (
        b_cols,
        c_cols,
        inputs_c,
        grad_rows,
        step_rows,
        decay_sum,
        span_total,
        weighted,
        scaled,
        own_state,
        own_grad,
    )


def span_grads(
    b_cols,
    c_cols,
    inputs_c,
    grad_rows,
    step_rows,
    decay_sum,
    span_total,
    weighted,
    scaled,
    start,
    after,
    skip_gain,
):
    start_bf = start.astype(jnp.bfloat16)
    after_bf = after.astype(jnp.bfloat16)
    row_ids = lax.broadcasted_iota(jnp.int32, (SPAN, SPAN), 0)
    col_ids = lax.broadcasted_iota(jnp.int32, (SPAN, SPAN), 1)
    causal = row_ids >= col_ids
    log_gap = decay_sum[:, :, None] - decay_sum[:, None, :]
    decay_mat = jnp.exp(jnp.where(causal[None], log_gap, -jnp.inf))
    kernel = jnp.dot(c_cols, b_cols.T, preferred_element_type=jnp.float32)
    weights = (decay_mat * kernel[None]).astype(jnp.bfloat16)
    within = jnp.einsum("hsj,shp->jhp", weights, grad_rows, preferred_element_type=jnp.float32)
    carried = jnp.einsum("hpn,jn->jhp", after_bf, b_cols, preferred_element_type=jnp.float32)
    to_end = jnp.exp(span_total[:, None] - decay_sum)
    grad_x = step_rows.T[:, :, None] * (within + to_end.T[:, :, None] * carried) + skip_gain[
        None, :, None
    ] * grad_rows.astype(jnp.float32)
    intersection = jnp.einsum(
        "shp,jhp->hsj", grad_rows, inputs_c, preferred_element_type=jnp.float32
    )
    mixing = jnp.sum(decay_mat * step_rows[:, None, :] * intersection, axis=0).astype(jnp.bfloat16)
    grad_c = jnp.dot(mixing, b_cols, preferred_element_type=jnp.float32) + jnp.dot(
        scaled.reshape(SPAN, -1), start_bf.reshape(-1, STATE), preferred_element_type=jnp.float32
    )
    grad_b = jnp.dot(mixing.T, c_cols, preferred_element_type=jnp.float32) + jnp.dot(
        weighted.reshape(SPAN, -1), after_bf.reshape(-1, STATE), preferred_element_type=jnp.float32
    )
    grad_proj = jnp.concatenate([grad_b, grad_c], axis=1).astype(jnp.bfloat16)
    return (grad_x.astype(jnp.bfloat16).reshape(SPAN, -1), grad_proj)


def chain_step(earlier, later_part):
    return (earlier[0] * later_part[0], later_part[0][:, None, None] * earlier[1] + later_part[1])


def on_device(layer_input, proj_weight, inputs, step_size, log_decay, skip_gain, grad_out):
    tokens = layer_input[0]
    length = tokens.shape[0]
    proj = jnp.dot(tokens, proj_weight, preferred_element_type=jnp.float32).astype(jnp.bfloat16)
    pieces = span_inputs(proj, inputs[0], grad_out[0], step_size[0], log_decay[0])
    own_state, own_grad, span_total = (pieces[9], pieces[10], pieces[6])
    empty_state = jnp.zeros((SHARD_CHANNELS, HEAD_DIM, STATE), jnp.float32)
    unit_decay = jnp.ones((SHARD_CHANNELS,), jnp.float32)

    def advance(state_carry, piece):
        return (jnp.exp(piece[1])[:, None, None] * state_carry + piece[0], state_carry)

    last_state, local_starts = lax.scan(advance, empty_state, (own_state, span_total))
    last_grad, local_afters = lax.scan(advance, empty_state, (own_grad, span_total), reverse=True)
    device_decay = jnp.exp(jnp.sum(span_total, axis=0))
    _, state_entry = prefix(
        (device_decay, last_state), "seq", chain_step, (unit_decay, empty_state), False
    )
    _, grad_entry = prefix(
        (device_decay, last_grad), "seq", chain_step, (unit_decay, empty_state), True
    )
    running = jnp.cumsum(span_total, axis=0)
    before = running - span_total
    behind = jnp.sum(span_total, axis=0)[None] - running
    starts = local_starts + jnp.exp(before)[:, :, None, None] * state_entry[None]
    afters = local_afters + jnp.exp(behind)[:, :, None, None] * grad_entry[None]

    def finish(parts):
        return span_grads(*parts, skip_gain)

    grad_x, grad_proj = lax.map(finish, pieces[:9] + (starts, afters))
    grad_proj = grad_proj.reshape(length, 2 * STATE)
    scale_factor = 1.0 / (length * lax.axis_size("seq"))
    grad_weight = lax.psum_scatter(
        jnp.einsum("ld,ln->dn", tokens, grad_proj, preferred_element_type=jnp.float32)
        * scale_factor,
        ("dp", "seq"),
        scatter_dimension=0,
        tiled=True,
    )
    return (grad_x, grad_weight)


def solution(mesh):
    return jax.shard_map(
        on_device,
        mesh=mesh,
        in_specs=(
            P("dp", "seq", None),
            P(),
            P("dp", "seq", None),
            P("dp", None, "seq"),
            P("dp", None, "seq"),
            P(),
            P("dp", "seq", None),
        ),
        out_specs=(P("dp", "seq", None), P(("dp", "seq"), None)),
        check_vma=False,
    )
```

profile of v0, /device:TPU:0, one launch (start us, length us, event | category | flops | bytes accessed | tf_op | source)
XLA Modules:
  0.0 437.8 jit_solution(5426759698616698249)
XLA Ops:
  9.9 1.5 copy.33
  11.5 1.8 convolution_convert_fusion
  17.0 22.3 %all-gather = f32[8,32,1]{1,2,0:T(1,128)S(1)} all-gather(f32[1,32,1]{1,2,0:T(1,128)S(1)} %exp.70), channel_id=2, replica_groups=mesh['dp'=4,'seq'=8] {'seq'}, dimensions={0}, use_global_device_ids=true | all-gather | bytes 1152 | tf_op jit(solution)/shard_map/all_gather | solution.py:14
  39.3 2.1 multiply_reduce_fusion
  41.9 101.5 %all-gather.8.cloned.1.call-done = f32[256,64,128]{2,1,0:T(8,128)} async-done(((f32[32,64,128]{2,1,0:T(8,128)}), f32[256,64,128]{2,1,0:T(8,128)}) %all-gather.8.cloned.1.call-update) | async-done | bytes 8388624 | tf_op jit(solution)/shard_map/all_gather | solution.py:14
  143.4 21.6 %while.21 = (s32[]{:T(128)}, f32[32,64,128]{2,1,0:T(8,128)}, s32[]{:T(128)}, f32[8,32]{1,0:T(8,128)S(1)}, f32[8,32,64,128]{3,2,1,0:T(8,128)}, /*index=5*/s32[]{:T(128)}, s32[]{:T(128)}) while((s32[]{:T(128)}, f32[32,64,128]{2,1,0:T(8,128)}, s32[]{:T(128)}, f32[8,32]{1,0:T(8,128)S(1)}, f32[8,32,64,128]{3,2,1,0:T(8,128)}, ...), condition=%wide.region_5.6_spmd.clone, body=%wide.region_4.5_spmd.clone.sunk | while | flops 1048580 | bytes 3146217 | solution.py:27
  143.4 2.4 fusion.56
  145.8 2.7 fusion.56
  148.5 2.7 fusion.56
  151.2 3.0 fusion.56
  154.2 2.7 fusion.56
  156.9 2.7 fusion.56
  159.6 2.7 fusion.56
  162.3 2.7 fusion.56
  165.0 103.6 %all-gather.6.cloned.1.call-done = f32[256,64,128]{2,1,0:T(8,128)} async-done(((f32[32,64,128]{2,1,0:T(8,128)}), f32[256,64,128]{2,1,0:T(8,128)}) %all-gather.6.cloned.1.call-update) | async-done | bytes 8388624 | tf_op jit(solution)/shard_map/all_gather | solution.py:14
  268.7 12.1 %while.20 = (s32[]{:T(128)}, f32[32,64,128]{2,1,0:T(8,128)S(1)}, s32[]{:T(128)}, f32[8,32]{1,0:T(8,128)S(1)}, f32[8,32,64,128]{3,2,1,0:T(8,128)}, /*index=5*/s32[]{:T(128)}, s32[]{:T(128)}, s32[]{:T(128)}, s32[]{:T(128)}) while((s32[]{:T(128)}, f32[32,64,128]{2,1,0:T(8,128)S(1)}, s32[]{:T(128)}, f32[8,32]{1,0:T(8,128)S(1)}, ...), condition=%wide.region_2.3_spmd.clone, body=%wide.region_1.2_spmd.clone.sunk | while | flops 1048584 | bytes 3146279 | solution.py:27
  274.7 1.5 fusion.55
  276.2 1.5 fusion.55
  277.7 1.5 fusion.55
  280.7 2.0 fusion.10
  282.7 1.5 fusion.9
  284.3 2.6 fusion.2
  290.1 139.5 %reduce-scatter.2.cloned.1.call-done = f32[128,256]{0,1:T(8,128)} async-done(((f32[4096,256]{0,1:T(8,128)}), f32[128,256]{0,1:T(8,128)}) %reduce-scatter.2.cloned.1.call-update) | async-done | bytes 131088 | tf_op jit(solution)/shard_map/reduce_scatter | solution.py:146
  429.6 1.7 copy.36
  (63 shorter events, 17.5 us)
Async XLA Ops:
  7.2 4.3 copy-start
  7.2 4.2 copy-start.6
  7.2 136.2 %all-gather.8.cloned.1.call-start = ((), (), s32[]{:S(2)}) async-start(), calls=%async_computation.3 | async-start | bytes 9437184 | tf_op jit(solution)/shard_map/all_gather | solution.py:14
  9.9 3.4 copy-start.1
  11.4 2.9 copy-start.3
  14.3 1.4 copy-start.5
  15.6 253.1 %all-gather.6.cloned.1.call-start = ((), (), s32[]{:S(2)}) async-start(), calls=%async_computation.2 | async-start | bytes 9437184 | tf_op jit(solution)/shard_map/all_gather | solution.py:14
  16.9 412.7 %reduce-scatter.2.cloned.1.call-start = ((), (), s32[]{:S(2)}) async-start(), calls=%async_computation.1 | async-start | bytes 4325376 | tf_op jit(solution)/shard_map/reduce_scatter | solution.py:146
  280.7 3.5 copy-start.4
  286.9 1.0 copy-start.2
  286.9 1.0 copy-start.7
Sparse Core Ops, SparseCore 0:
  15.7 127.6 all-gather.7
  145.5 123.1 all-gather.5
  287.1 142.5 reduce-scatter.1
where the time goes:
time: 439 us; the launch traced here: 438 us
  waiting for transfers between devices  345 us (79%)
  other arithmetic  35.6 us (8%)
  blocking collectives  22.3 us (5%)
  matrix products  14.6 us (3%)
  between operations  13.9 us (3%)
  local copies, waits for them, and re-layouts  6.22 us (1%)
    all_gather x2, waiting for transfers between devices, prefix(): everything = jax.tree.map(lambda part: lax.all_gather(part, axis), value)  205 us
    reduce_scatter x1, waiting for transfers between devices, on_device(): lax.psum_scatter(jnp.einsum('ld,ln->dn', tokens, grad_proj, preferred_ele...  139 us
    select_n x16, other arithmetic, step(): return jax.tree.map(lambda a, b: jnp.where(reached, a, b), new, before)  33.3 us
    all_gather x1, blocking collectives, prefix(): everything = jax.tree.map(lambda part: lax.all_gather(part, axis), value)  22.3 us
  transfers between devices with their start and end apart: 3, of which 3 were waited for; matrix products, arithmetic and copies ran while one was open for 6% of the time, Pallas kernels for 0%

commit v1 on v0

v1 whole, which is shorter than its diff:
```python
import functools

import jax
import jax.numpy as jnp
from jax import lax
from jax.experimental import pallas as pl
from jax.experimental.pallas import tpu as pltpu
from jax.sharding import PartitionSpec as P

HEADS = 32
HEAD_DIM = 64
STATE = 128
SPAN = 128
CHUNKS = 2
F32 = jnp.float32
BF16 = jnp.bfloat16
VMEM_LIMIT = 40 * 1024 * 1024


def group_size(n_seq):
    q = 1
    while n_seq % (2 * q) == 0 and 4 * q * q <= n_seq:
        q *= 2
    return q


def nn(a, b):
    return lax.dot_general(a, b, (((1,), (0,)), ((), ())), preferred_element_type=F32)


def nt(a, b):
    return lax.dot_general(a, b, (((1,), (1,)), ((), ())), preferred_element_type=F32)


def tn(a, b):
    return lax.dot_general(a, b, (((0,), (0,)), ((), ())), preferred_element_type=F32)


def exact(a, b, dims):
    return lax.dot_general(
        a, b, (dims, ((), ())), preferred_element_type=F32, precision=lax.Precision.HIGHEST
    )


def call(body, outs, n_in, scratch=(), name=None, cost=None):
    specs = [pl.BlockSpec(memory_space=pltpu.SMEM)]
    specs += [pl.BlockSpec(memory_space=pltpu.VMEM)] * n_in
    return pl.pallas_call(
        body,
        out_shape=outs,
        in_specs=specs,
        out_specs=jax.tree.map(lambda _: pl.BlockSpec(memory_space=pltpu.VMEM), outs),
        scratch_shapes=scratch,
        compiler_params=pltpu.CompilerParams(vmem_limit_bytes=VMEM_LIMIT),
        cost_estimate=cost,
        name=name,
    )


def out(shape, dtype=F32):
    return jax.ShapeDtypeStruct(shape, dtype)


def iotas():
    rows = lax.broadcasted_iota(jnp.int32, (SPAN, SPAN), 0)
    cols = lax.broadcasted_iota(jnp.int32, (SPAN, SPAN), 1)
    return rows, cols


def columns(ref, start, width):
    return ref[:, pl.ds(pl.multiple_of(start, 128), width)]


def states_body(q, hc, chunk, *refs):
    n = q - 1
    it = iter(refs)
    ids, x_ref, g_ref = next(it), next(it), next(it)
    xg_in = [next(it) for _ in range(n)]
    bc_own = next(it)
    bc_in = [next(it) for _ in range(n)]
    ls_own = next(it)
    ls_in = [next(it) for _ in range(n)]
    xs, gs, ws, ss, f1s, ds, own_s, own_g, total_s, total_g, plane, bcs, cums, avs = it
    width = hc * HEAD_DIM
    y = ids[0]
    first = (y * CHUNKS + chunk) * width
    xs[y] = columns(x_ref, first, width)
    gs[y] = columns(g_ref, first, width)
    bcs[y] = bc_own[...].astype(BF16)
    cums[y] = ls_own[0]
    avs[y] = ls_own[1]
    for r in range(1, q):
        at = lax.rem(y - r + q, q)
        xs[at] = xg_in[r - 1][0].astype(BF16)
        gs[at] = xg_in[r - 1][1].astype(BF16)
        bcs[at] = bc_in[r - 1][...].astype(BF16)
        cums[at] = ls_in[r - 1][0]
        avs[at] = ls_in[r - 1][1]
    rows, cols = iotas()
    tri = (rows >= cols).astype(F32)
    eye = (rows == cols).astype(F32)
    head_of = lax.broadcasted_iota(jnp.int32, (hc, width), 1) // HEAD_DIM
    spread = (head_of == lax.broadcasted_iota(jnp.int32, (hc, width), 0)).astype(F32)
    last = ((1,), (1,))
    for b in range(q):
        decay = cums[b]
        cum_c = exact(tri, decay, last)
        a_c = cum_c - exact(eye, jnp.log(avs[b]), last)
        cums[b] = exact(decay, tri, last)
        cum_x = exact(cum_c, spread, ((1,), (0,)))
        a_x = exact(a_c, spread, ((1,), (0,)))
        avs[b] = exact(a_c, eye, ((0,), (0,)))
        total = cum_x[SPAN - 1 : SPAN, :]
        f1 = jnp.exp(total - a_x)
        f1s[b] = f1
        ds[b] = jnp.exp(total)
        weighted = (xs[b].astype(F32) * f1).astype(BF16)
        scaled = (gs[b].astype(F32) * jnp.exp(cum_x)).astype(BF16)
        ws[b] = weighted
        ss[b] = scaled
        own_s[b] = tn(bcs[b][:, :STATE], weighted)
        own_g[b] = tn(bcs[b][:, STATE:], scaled)
    forward, backward, through = own_s[0], own_g[q - 1], ds[0]
    for b in range(1, q):
        forward = ds[b] * forward + own_s[b]
        backward = ds[q - 1 - b] * backward + own_g[q - 1 - b]
        through = through * ds[b]
    total_s[...] = forward
    total_g[...] = backward
    plane[...] = through


def local_body(q, hc, ids, xs, gs, bcs, cums, avs, skip, gx, gp):
    rows, cols = iotas()
    causal = rows <= cols
    low = lax.broadcasted_iota(jnp.int32, (SPAN, 128), 1) < HEAD_DIM
    eye = (rows == cols).astype(F32)
    for b in range(q):
        b_cols, c_cols = bcs[b][:, :STATE], bcs[b][:, STATE:]
        kernel = nt(b_cols, c_cols)
        a_c = exact(eye, avs[b], ((1,), (1,)))
        mixing = jnp.zeros((SPAN, SPAN), F32)
        for pair in range(hc // 2):
            at = slice(pair * 128, pair * 128 + 128)
            x, g = xs[b][:, at], gs[b][:, at]
            parts = []
            for half in range(2):
                h = 2 * pair + half
                gap = cums[b][h : h + 1, :] - a_c[:, h : h + 1]
                decay = jnp.exp(jnp.where(causal, gap, -jnp.inf))
                picked = jnp.where(low if half == 0 else ~low, x, jnp.zeros_like(x))
                mixing += decay * nt(picked, g)
                parts.append(nn((decay * kernel).astype(BF16), g))
            gx[b, :, at] = jnp.where(low, parts[0], parts[1]) + skip[:, at] * g.astype(F32)
        mixed = mixing.astype(BF16)
        gp[b, :, :STATE] = nn(mixed, c_cols)
        gp[b, :, STATE:] = tn(mixed, b_cols)


def final_body(q, more, *refs):
    it = iter(refs)
    ids, start, after, own_s, own_g, ds, ws, ss, f1s, bcs, gx, gp = [next(it) for _ in range(12)]
    before = [next(it) for _ in range(q)] if more else None
    gx_out = [next(it) for _ in range(q)]
    gp_out = [next(it) for _ in range(q)]
    gx_all, gp_all = it
    y = ids[0]
    state = start[...]
    for b in range(q):
        gp_all[b, :, STATE:] = gp[b, :, STATE:] + nt(ss[b], state.astype(BF16))
        if b < q - 1:
            state = ds[b] * state + own_s[b]
    state = after[...]
    for b in range(q - 1, -1, -1):
        rounded = state.astype(BF16)
        gx_all[b] = gx[b] + f1s[b] * nn(bcs[b][:, :STATE], rounded)
        gp_all[b, :, :STATE] = gp[b, :, :STATE] + nt(ws[b], rounded)
        if b > 0:
            state = ds[b] * state + own_g[b]
    for r in range(q):
        at = lax.rem(y + r, q)
        gx_out[r][...] = gx_all[at]
        gp_out[r][...] = gp_all[at] if before is None else gp_all[at] + before[r][...]


def assemble_body(q, width, *refs):
    ids, result = refs[0], refs[-1]
    parts = refs[1:-1]
    y = ids[0]
    for r in range(q):
        group = lax.rem(y - r + q, q)
        for c in range(CHUNKS):
            at = pl.multiple_of((group * CHUNKS + c) * width, 128)
            result[:, pl.ds(at, width)] = parts[r * CHUNKS + c][...].astype(BF16)


def weight_body(n_dp, n_seq, rows, scale, *refs):
    it = iter(refs)
    ids, tokens = next(it), next(it)
    tokens_in = [next(it) for _ in range(n_dp - 1)]
    gp_own = next(it)
    gp_in = [next(it) for _ in range(n_dp - 1)]
    outs = [next(it) for _ in range(n_seq)]
    held, products = it
    width = n_seq * rows
    dp, seq = ids[2], ids[1]
    grads = [r[...].astype(BF16) for r in [gp_own] + gp_in]
    held[0] = columns(tokens, dp * width, width)
    for r in range(1, n_dp):
        held[r] = tokens_in[r - 1][...].astype(BF16)
    total = tn(held[0], grads[0])
    for r in range(1, n_dp):
        total += tn(held[r], grads[r])
    products[...] = (total * scale).reshape(n_seq, rows, 2 * STATE)
    for r in range(n_seq):
        outs[r][...] = products[lax.rem(seq + r, n_seq)]


def on_device(layer_input, proj_weight, inputs, step_size, log_decay, skip_gain, grad_out):
    n_seq, n_dp = lax.axis_size("seq"), lax.axis_size("dp")
    q = group_size(n_seq)
    planes = n_seq // q
    group_heads = HEADS // q
    hc = group_heads // CHUNKS
    width = hc * HEAD_DIM
    tokens, x, g = layer_input[0], inputs[0], grad_out[0]
    length, features = tokens.shape
    decay_step = jnp.stack([log_decay[0], step_size[0]])
    seq, dp = lax.axis_index("seq"), lax.axis_index("dp")
    y = lax.rem(seq, q)
    ids = jnp.stack([y, seq, dp]).astype(jnp.int32)

    def in_group(r):
        return [(z * q + i, z * q + (i + r) % q) for z in range(planes) for i in range(q)]

    def swap(value, r):
        return lax.ppermute(value, "seq", in_group(r))

    def heads_of(group, c):
        return lax.dynamic_slice_in_dim(decay_step, (group * CHUNKS + c) * hc, hc, axis=1)

    xg_in, ls_in = {}, {}
    for c in range(CHUNKS):
        for r in range(1, q):
            to = lax.rem(y + r, q)
            at = (to * CHUNKS + c) * width
            cut = [lax.dynamic_slice_in_dim(v, at, width, axis=1) for v in (x, g)]
            xg_in[c, r] = swap(jnp.stack(cut).astype(F32), r)
            ls_in[c, r] = swap(heads_of(to, c), r)
    proj = jnp.dot(tokens, proj_weight, preferred_element_type=F32)
    proj = lax.reduce_precision(proj, exponent_bits=8, mantissa_bits=7)
    bc_in = [swap(proj, r) for r in range(1, q)]
    columns_each = features // n_dp
    tokens_in = []
    for r in range(1, n_dp):
        to = lax.rem(dp + r, n_dp)
        piece = lax.dynamic_slice_in_dim(tokens, to * columns_each, columns_each, axis=1)
        pairs = [(i, (i + r) % n_dp) for i in range(n_dp)]
        tokens_in.append(lax.ppermute(piece.astype(F32), "dp", pairs))

    row_b, row_f = (q, SPAN, width), (q, SPAN, width)
    held = []
    for c in range(CHUNKS):
        outs = (
            out(row_b, BF16), out(row_b, BF16), out(row_b, BF16), out(row_b, BF16),
            out(row_f), out((q, 1, width)), out(row_f), out(row_f),
            out((STATE, width)), out((STATE, width)), out((1, width)),
            out((q, SPAN, 2 * STATE), BF16), out((q, hc, SPAN)), out((q, hc, SPAN)),
        )
        args = [x, g] + [xg_in[c, r] for r in range(1, q)] + [proj] + bc_in
        args += [heads_of(y, c)] + [ls_in[c, r] for r in range(1, q)]
        held.append(
            call(functools.partial(states_body, q, hc, c), outs, len(args), name="states")(ids, *args)
        )

    entries = []
    plane = seq // q
    for c in range(CHUNKS):
        total_s, total_g, through = held[c][8:11]
        sent, back = total_s, total_g
        start, after = jnp.zeros_like(total_s), jnp.zeros_like(total_g)
        for t in range(planes - 1):
            up = [(t * q + i, (t + 1) * q + i) for i in range(q)]
            top = planes - 1 - t
            down = [(top * q + i, (top - 1) * q + i) for i in range(q)]
            start += lax.ppermute(sent, "seq", up)
            after += lax.ppermute(back, "seq", down)
            if t < planes - 2:
                sent = total_s + through * start
                back = total_g + through * after
        entries.append((start, after))

    skip = jnp.repeat(skip_gain, HEAD_DIM)[None]
    before, gx_parts = [], {}
    for c in range(CHUNKS):
        xs, gs, ws, ss, f1s, ds, own_s, own_g, _, _, _, bcs, cums, avs = held[c]
        skip_c = lax.dynamic_slice_in_dim(skip, (y * CHUNKS + c) * width, width, axis=1)
        gx, gp = call(
            functools.partial(local_body, q, hc),
            (out(row_f), out((q, SPAN, 2 * STATE))), 6, name="local",
        )(ids, xs, gs, bcs, cums, avs, skip_c)
        start, after = entries[c]
        outs = (out((SPAN, width)),) * q + (out((SPAN, 2 * STATE)),) * q
        args = [start, after, own_s, own_g, ds, ws, ss, f1s, bcs, gx, gp] + before
        scratch = (pltpu.VMEM(row_f, F32), pltpu.VMEM((q, SPAN, 2 * STATE), F32))
        done = call(
            functools.partial(final_body, q, bool(before)), outs, len(args), scratch, name="final"
        )(ids, *args)
        for r in range(q):
            gx_parts[r, c] = done[r]
        before = list(done[q:])

    gp_own = before[0]
    for r in range(1, q):
        gp_own = gp_own + swap(before[r], r)
    gp_in = [
        lax.ppermute(gp_own, "dp", [(i, (i + r) % n_dp) for i in range(n_dp)]) for r in range(1, n_dp)
    ]
    rows = columns_each // n_seq
    scale = 1.0 / (length * n_seq)
    outs = (out((rows, 2 * STATE)),) * n_seq
    args = [tokens] + tokens_in + [gp_own] + gp_in
    scratch = (
        pltpu.VMEM((n_dp, length, columns_each), BF16),
        pltpu.VMEM((n_seq, rows, 2 * STATE), F32),
    )
    pieces = call(
        functools.partial(weight_body, n_dp, n_seq, rows, scale), outs, len(args), scratch, name="weight"
    )(ids, *args)
    grad_weight = pieces[0]
    for r in range(1, n_seq):
        pairs = [(i, (i + r) % n_seq) for i in range(n_seq)]
        grad_weight = grad_weight + lax.ppermute(pieces[r], "seq", pairs)

    parts = [gx_parts[0, c] for c in range(CHUNKS)]
    for r in range(1, q):
        parts += [swap(gx_parts[r, c], r) for c in range(CHUNKS)]
    grad_x = call(
        functools.partial(assemble_body, q, width),
        out((length, q * CHUNKS * width), BF16), len(parts), name="assemble",
    )(ids, *parts)
    return grad_x[None], grad_weight


def solution(mesh):
    return jax.shard_map(
        on_device,
        mesh=mesh,
        in_specs=(
            P("dp", "seq", None),
            P(),
            P("dp", "seq", None),
            P("dp", None, "seq"),
            P("dp", None, "seq"),
            P(),
            P("dp", "seq", None),
        ),
        out_specs=(P("dp", "seq", None), P(("dp", "seq"), None)),
        check_vma=False,
    )
```

time: 439 us -> 164 us (0.37)
  waiting for transfers between devices: 345 us -> 69.9 us
  starting transfers between devices: 0.12 us -> 42.1 us
  other arithmetic: 35.6 us -> 12.3 us
  blocking collectives: 22.3 us -> 0 us
  Pallas kernels: 0 us -> 16.5 us
  local copies, waits for them, and re-layouts: 6.22 us -> 20.8 us
  matrix products: 14.6 us -> 0.44 us
  between operations: 13.9 us -> 1.44 us
    all_gather x2 -> x0, waiting for transfers between devices: 205 us -> none  [prefix(): everything = jax.tree.map(lambda part: lax.all_gather(part, axis), value)]
    reduce_scatter x1 -> x0, waiting for transfers between devices: 139 us -> none  [on_device(): lax.psum_scatter(jnp.einsum('ld,ln->dn', tokens, grad_proj, preferred_ele...]
    ppermute x0 -> x33, waiting for transfers between devices: none -> 69.9 us  [the longest x8 27.6 us: swap(): return lax.ppermute(value, 'seq', in_group(r))]
    ppermute x0 -> x33, starting transfers between devices: none -> 42.1 us  [the longest x7 11.6 us: on_device(): grad_weight = grad_weight + lax.ppermute(pieces[r], 'seq', pairs)]
    select_n x16 -> x0, other arithmetic: 33.3 us -> none  [step(): return jax.tree.map(lambda a, b: jnp.where(reached, a, b), new, before)]
    all_gather x1 -> x0, blocking collectives: 22.3 us -> none  [prefix(): everything = jax.tree.map(lambda part: lax.all_gather(part, axis), value)]
    pallas_call x0 -> x8, Pallas kernels: none -> 16.5 us  [the longest x2 6.74 us: on_device(): call(functools.partial(states_body, q, hc, c), outs, len(args), name='sta...]
    dot_general x12 -> x1, matrix products: 14.6 us -> 0.44 us  [on_device(): proj = jnp.dot(tokens, proj_weight, preferred_element_type=F32)]
  transfers between devices with their start and end apart: 3 -> 33, of which waited for: 3 -> 10; matrix products, arithmetic and copies ran while one was open for 6% -> 8% of each run, Pallas kernels for 0% -> 10%
where the time goes in v1:
time: 164 us; the launch traced here: 163 us
  waiting for transfers between devices  69.9 us (43%)
  starting transfers between devices  42.1 us (26%)
  local copies, waits for them, and re-layouts  20.8 us (13%)
  Pallas kernels  16.5 us (10%)
  other arithmetic  12.3 us (8%)
    ppermute x8, waiting for transfers between devices, swap(): return lax.ppermute(value, 'seq', in_group(r))  27.6 us
    ppermute x6, waiting for transfers between devices, on_device(): after += lax.ppermute(back, 'seq', down)  18.1 us
    unnamed x121, local copies, waits for them, and re-layouts  18.1 us
    ppermute x7, waiting for transfers between devices, on_device(): grad_weight = grad_weight + lax.ppermute(pieces[r], 'seq', pairs)  16.8 us
    ppermute x7, starting transfers between devices, on_device(): grad_weight = grad_weight + lax.ppermute(pieces[r], 'seq', pairs)  11.6 us
    ppermute x8, starting transfers between devices, swap(): return lax.ppermute(value, 'seq', in_group(r))  10.4 us
    ppermute x6, starting transfers between devices, on_device(): start += lax.ppermute(sent, 'seq', up)  10 us
    pallas_call x2, Pallas kernels, on_device(): call(functools.partial(states_body, q, hc, c), outs, len(args), name='sta...  6.74 us
  transfers between devices with their start and end apart: 33, of which 10 were waited for; matrix products, arithmetic and copies ran while one was open for 8% of the time, Pallas kernels for 10%

profile of v1, /device:TPU:0, one launch (start us, length us, event | category | flops | bytes accessed | tf_op | source)
XLA Modules:
  0.0 163.5 jit_solution(2413526039272095343)
XLA Ops:
  2.8 3.0 %collective-permute-start = (f32[2,128,512]{2,1,0:T(8,128)}, f32[2,128,512]{2,1,0:T(8,128)}, u32[]{:S(2)}, u32[]{:S(2)}) collective-permute-start(f32[2,128,512]{2,1,0:T(8,128)} %maximum_convert_fusion), channel_id=1, source_target_pairs={{0,1},{1,0},{2,3},{3,2},{4,5},{5,4},{6,7},{7,6},{8,9},{9,8},{10,11... | collective-permute-start | bytes 1572872 | tf_op jit(solution)/shard_map/ppermute | solution.py:237
  7.2 2.0 %collective-permute-start.9 = (f32[2,128,512]{2,1,0:T(8,128)}, f32[2,128,512]{2,1,0:T(8,128)}, u32[]{:S(2)}, u32[]{:S(2)}) collective-permute-start(f32[2,128,512]{2,1,0:T(8,128)} %maximum_convert_fusion.1), channel_id=1, source_target_pairs={{0,1},{1,0},{2,3},{3,2},{4,5},{5,4},{6,7},{7,6},{8,9},{9,8},{10,11... | collective-permute-start | bytes 1572872 | tf_op jit(solution)/shard_map/ppermute | solution.py:237
  9.9 22.2 %collective-permute-done.2.refs_7_ = f32[2,8,128]{2,1,0:T(8,128)S(1)} collective-permute-done((f32[2,8,128]{2,1,0:T(8,128)S(1)}, f32[2,8,128]{2,1,0:T(8,128)S(1)}, u32[]{:S(2)}, u32[]{:S(2)}) %collective-permute-start.2) | collective-permute-done | bytes 8224 | tf_op jit(solution)/shard_map/ppermute | solution.py:237
  37.8 3.7 %states.2 = (bf16[2,128,512]{2,1,0:T(8,128)(2,1)S(1)}, bf16[2,128,512]{2,1,0:T(8,128)(2,1)S(1)}, bf16[2,128,512]{2,1,0:T(8,128)(2,1)S(1)}, bf16[2,128,512]{2,1,0...) custom-call(s32[3]{0:T(128)S(1)} %pad_add_fusion.refs_0_.ids, ...), custom_call_target="tpu_custom_call" | custom-call | tf_op jit(solution)/shard_map/states/pallas_call | solution.py:273
  50.6 4.4 %collective-permute-start.3 = (f32[128,512]{1,0:T(8,128)S(1)}, f32[128,512]{1,0:T(8,128)}, u32[]{:S(2)}, u32[]{:S(2)}) collective-permute-start(f32[128,512]{1,0:T(8,128)S(1)} %get-tuple-element.50), channel_id=1, source_target_pairs={{0,2},{1,3},{8,10},{9,11},{16,18},{17,19},{24,26},{25,27}} | collective-permute-start | bytes 786440 | tf_op jit(solution)/shard_map/ppermute | solution.py:286
  55.0 1.5 collective-permute-start.10
  58.9 1.5 collective-permute-start.20
  60.6 3.0 %states.3 = (bf16[2,128,512]{2,1,0:T(8,128)(2,1)S(1)}, bf16[2,128,512]{2,1,0:T(8,128)(2,1)S(1)}, bf16[2,128,512]{2,1,0:T(8,128)(2,1)S(1)}, bf16[2,128,512]{2,1,0...) custom-call(s32[3]{0:T(128)S(1)} %pad_add_fusion.refs_0_.ids, ...), custom_call_target="tpu_custom_call" | custom-call | tf_op jit(solution)/shard_map/states/pallas_call | solution.py:273
  67.7 4.4 %collective-permute-done.11 = f32[128,512]{1,0:T(8,128)S(1)} collective-permute-done((f32[128,512]{1,0:T(8,128)S(1)}, f32[128,512]{1,0:T(8,128)S(1)}, u32[]{:S(2)}, u32[]{:S(2)}) %collective-permute-start.11) | collective-permute-done | bytes 262176 | tf_op jit(solution)/shard_map/ppermute | solution.py:286
  74.4 2.1 %multiply_add_fusion.4 = (f32[128,512]{1,0:T(8,128)S(1)}, f32[128,512]{1,0:T(8,128)}, f32[128,512]{1,0:T(8,128)S(1)}, f32[128,512]{1,0:T(8,128)}) fusion(f32[128,512]{1,0:T(8,128)} %get-tuple-element.52, f32[512]{0:T(512)S(1)} %bitcast.27, f32[128,512]{1,0:T(8,128)} %collective-permute-done.6, f32[128,512]{1,0:T(8,128)S(1)} %collective-permute-done.7, ...), kind=kLoop, calls=%fused_computation.10 | loop fusion | flops 393216 | bytes 2623488 | tf_op jit(solution)/shard_map/add | solution.py:290
  76.6 1.5 collective-permute-start.5
  81.9 18.1 %collective-permute-done.8 = f32[128,512]{1,0:T(8,128)} collective-permute-done((f32[128,512]{1,0:T(8,128)S(1)}, f32[128,512]{1,0:T(8,128)}, u32[]{:S(2)}, u32[]{:S(2)}) %collective-permute-start.8) | collective-permute-done | bytes 262176 | tf_op jit(solution)/shard_map/ppermute | solution.py:287
  104.9 2.1 %local.2 = (f32[2,128,512]{2,1,0:T(8,128)S(1)}, f32[2,128,256]{2,1,0:T(8,128)S(1)}) custom-call(s32[3]{0:T(128)S(1)} %pad_add_fusion.refs_0_.ids, bf16[2,128,512]{2,1,0:T(8,128)(2,1)S(1)} %copy-done.34, bf16[2,128,512]{2,1,0:T(8,128)(2,1)S(1)} %copy-done.36, bf16[2,128,256]{2,1,0:T(8,128)(2,1)S(1)} %copy-done.16, f32[2,8,128]{2,1,0:T(8,128)S(1)} %copy-done.43, ...), custom_call_target="tpu_custom_call" | custom-call | tf_op jit(solution)/shard_map/local/pallas_call | solution.py:298
  108.9 2.1 %local.3 = (f32[2,128,512]{2,1,0:T(8,128)S(1)}, f32[2,128,256]{2,1,0:T(8,128)S(1)}) custom-call(s32[3]{0:T(128)S(1)} %pad_add_fusion.refs_0_.ids, bf16[2,128,512]{2,1,0:T(8,128)(2,1)S(1)} %copy-done.38, bf16[2,128,512]{2,1,0:T(8,128)(2,1)S(1)} %copy-done.40, bf16[2,128,256]{2,1,0:T(8,128)(2,1)S(1)} %copy-done.18, f32[2,8,128]{2,1,0:T(8,128)S(1)} %copy-done.47, ...), custom_call_target="tpu_custom_call" | custom-call | tf_op jit(solution)/shard_map/local/pallas_call | solution.py:298
  117.4 2.0 %collective-permute-start.22 = (f32[128,256]{1,0:T(8,128)S(1)}, f32[128,256]{1,0:T(8,128)S(1)}, u32[]{:S(2)}, u32[]{:S(2)}) collective-permute-start(f32[128,256]{1,0:T(8,128)S(1)} %get-tuple-element.89), channel_id=1, source_target_pairs={{0,1},{1,0},{2,3},{3,2},{4,5},{5,4},{6,7},{7,6},{8,9},{9,8},{10,11... | collective-permute-start | bytes 393224 | tf_op jit(solution)/shard_map/ppermute | solution.py:237
  119.5 4.2 %collective-permute-done.22 = f32[128,256]{1,0:T(8,128)S(1)} collective-permute-done((f32[128,256]{1,0:T(8,128)S(1)}, f32[128,256]{1,0:T(8,128)S(1)}, u32[]{:S(2)}, u32[]{:S(2)}) %collective-permute-start.22) | collective-permute-done | bytes 131104 | tf_op jit(solution)/shard_map/ppermute | solution.py:237
  126.2 1.7 %collective-permute-start.18 = (f32[128,512]{1,0:T(8,128)S(1)}, f32[128,512]{1,0:T(8,128)S(1)}, u32[]{:S(2)}, u32[]{:S(2)}) collective-permute-start(f32[128,512]{1,0:T(8,128)S(1)} %get-tuple-element.87), channel_id=1, source_target_pairs={{0,1},{1,0},{2,3},{3,2},{4,5},{5,4},{6,7},{7,6},{8,9},{9,8},{10,11... | collective-permute-start | bytes 786440 | tf_op jit(solution)/shard_map/ppermute | solution.py:237
  130.8 2.2 %weight.1 = (f32[128,256]{1,0:T(8,128)S(1)}, f32[128,256]{1,0:T(8,128)S(1)}, f32[128,256]{1,0:T(8,128)S(1)}, f32[128,256]{1,0:T(8,128)S(1)}, f32[128,256]{1,0:T(...) custom-call(s32[3]{0:T(128)S(1)} %pad_add_fusion.refs_0_.ids, ...), custom_call_target="tpu_custom_call" | custom-call | tf_op jit(solution)/shard_map/weight/pallas_call | solution.py:327
  133.0 1.6 %collective-permute-start.32 = (f32[128,256]{1,0:T(8,128)S(1)}, f32[128,256]{1,0:T(8,128)S(1)}, u32[]{:S(2)}, u32[]{:S(2)}) collective-permute-start(f32[128,256]{1,0:T(8,128)S(1)} %get-tuple-element.97), channel_id=1, source_target_pairs={{0,7},{1,0},{2,1},{3,2},{4,3},{5,4},{6,5},{7,6},{8,15},{9,8},{10,9... | collective-permute-start | bytes 393224 | tf_op jit(solution)/shard_map/ppermute | solution.py:333
  134.6 3.0 %collective-permute-start.31 = (f32[128,256]{1,0:T(8,128)S(1)}, f32[128,256]{1,0:T(8,128)S(1)}, u32[]{:S(2)}, u32[]{:S(2)}) collective-permute-start(f32[128,256]{1,0:T(8,128)S(1)} %get-tuple-element.96), channel_id=1, source_target_pairs={{0,6},{1,7},{2,0},{3,1},{4,2},{5,3},{6,4},{7,5},{8,14},{9,15},{10,... | collective-permute-start | bytes 393224 | tf_op jit(solution)/shard_map/ppermute | solution.py:333
  139.1 2.6 %collective-permute-start.28 = (f32[128,256]{1,0:T(8,128)S(1)}, f32[128,256]{1,0:T(8,128)S(1)}, u32[]{:S(2)}, u32[]{:S(2)}) collective-permute-start(f32[128,256]{1,0:T(8,128)S(1)} %get-tuple-element.93), channel_id=1, source_target_pairs={{0,3},{1,4},{2,5},{3,6},{4,7},{5,0},{6,1},{7,2},{8,11},{9,12},{10,... | collective-permute-start | bytes 393224 | tf_op jit(solution)/shard_map/ppermute | solution.py:333
  141.6 2.9 %collective-permute-start.27 = (f32[128,256]{1,0:T(8,128)S(1)}, f32[128,256]{1,0:T(8,128)S(1)}, u32[]{:S(2)}, u32[]{:S(2)}) collective-permute-start(f32[128,256]{1,0:T(8,128)S(1)} %get-tuple-element.92), channel_id=1, source_target_pairs={{0,2},{1,3},{2,4},{3,5},{4,6},{5,7},{6,0},{7,1},{8,10},{9,11},{10,... | collective-permute-start | bytes 393224 | tf_op jit(solution)/shard_map/ppermute | solution.py:333
  144.6 1.4 assemble.1
  146.0 16.1 %collective-permute-done.29 = f32[128,256]{1,0:T(8,128)S(1)} collective-permute-done((f32[128,256]{1,0:T(8,128)S(1)}, f32[128,256]{1,0:T(8,128)S(1)}, u32[]{:S(2)}, u32[]{:S(2)}) %collective-permute-start.29) | collective-permute-done | bytes 131104 | tf_op jit(solution)/shard_map/ppermute | solution.py:333
  (192 shorter events, 52.8 us)
Async XLA Ops:
  2.8 30.6 %collective-permute-start = (f32[2,128,512]{2,1,0:T(8,128)}, f32[2,128,512]{2,1,0:T(8,128)}, u32[]{:S(2)}, u32[]{:S(2)}) collective-permute-start(f32[2,128,512]{2,1,0:T(8,128)} %maximum_convert_fusion), channel_id=1, source_target_pairs={{0,1},{1,0},{2,3},{3,2},{4,5},{5,4},{6,7},{7,6},{8,9},{9,8},{10,11... | collective-permute-start | bytes 1572872 | tf_op jit(solution)/shard_map/ppermute | solution.py:237
  6.2 26.5 %collective-permute-start.1 = (f32[128,256]{1,0:T(8,128)S(1)}, f32[128,256]{1,0:T(8,128)S(1)}, u32[]{:S(2)}, u32[]{:S(2)}) collective-permute-start(f32[128,256]{1,0:T(8,128)S(1)} %convolution_reduce-precision_fusion.refs_4_), channel_id=1, source_target_pairs={{0,1},{1,0},{2,3},{3,2},{4,5},{5,4},{6,7},{7,6},{8,9},{9,8},{10,11... | collective-permute-start | bytes 393224 | tf_op jit(solution)/shard_map/ppermute | solution.py:237
  7.2 53.3 %collective-permute-start.9 = (f32[2,128,512]{2,1,0:T(8,128)}, f32[2,128,512]{2,1,0:T(8,128)}, u32[]{:S(2)}, u32[]{:S(2)}) collective-permute-start(f32[2,128,512]{2,1,0:T(8,128)} %maximum_convert_fusion.1), channel_id=1, source_target_pairs={{0,1},{1,0},{2,3},{3,2},{4,5},{5,4},{6,7},{7,6},{8,9},{9,8},{10,11... | collective-permute-start | bytes 1572872 | tf_op jit(solution)/shard_map/ppermute | solution.py:237
  9.9 22.3 %collective-permute-start.2 = (f32[2,8,128]{2,1,0:T(8,128)S(1)}, f32[2,8,128]{2,1,0:T(8,128)S(1)}, u32[]{:S(2)}, u32[]{:S(2)}) collective-permute-start(f32[2,8,128]{2,1,0:T(8,128)S(1)} %get-tuple-element.115), channel_id=1, source_target_pairs={{0,1},{1,0},{2,3},{3,2},{4,5},{5,4},{6,7},{7,6},{8,9},{9,8},{10,11... | collective-permute-start | bytes 24584 | tf_op jit(solution)/shard_map/ppermute | solution.py:237
  49.2 14.6 %collective-permute-start.6 = (f32[128,512]{1,0:T(8,128)}, f32[128,512]{1,0:T(8,128)}, u32[]{:S(2)}, u32[]{:S(2)}) collective-permute-start(f32[128,512]{1,0:T(8,128)} %get-tuple-element.52), channel_id=1, source_target_pairs={{6,4},{7,5},{14,12},{15,13},{22,20},{23,21},{30,28},{31,29}} | collective-permute-start | bytes 786440 | tf_op jit(solution)/shard_map/ppermute | solution.py:287
  50.6 13.9 %collective-permute-start.3 = (f32[128,512]{1,0:T(8,128)S(1)}, f32[128,512]{1,0:T(8,128)}, u32[]{:S(2)}, u32[]{:S(2)}) collective-permute-start(f32[128,512]{1,0:T(8,128)S(1)} %get-tuple-element.50), channel_id=1, source_target_pairs={{0,2},{1,3},{8,10},{9,11},{16,18},{17,19},{24,26},{25,27}} | collective-permute-start | bytes 786440 | tf_op jit(solution)/shard_map/ppermute | solution.py:286
  57.7 66.1 %collective-permute-start.19 = (f32[128,1024]{1,0:T(8,128)}, f32[128,1024]{1,0:T(8,128)}, u32[]{:S(2)}, u32[]{:S(2)}) collective-permute-start(f32[128,1024]{1,0:T(8,128)} %get-tuple-element.107), channel_id=1, source_target_pairs={{0,8},{8,16},{16,24},{24,0},{1,9},{9,17},{17,25},{25,1},{2,10},{10... | collective-permute-start | bytes 1572872 | tf_op jit(solution)/shard_map/ppermute | solution.py:259
  58.9 65.9 %collective-permute-start.20 = (f32[128,1024]{1,0:T(8,128)}, f32[128,1024]{1,0:T(8,128)}, u32[]{:S(2)}, u32[]{:S(2)}) collective-permute-start(f32[128,1024]{1,0:T(8,128)} %get-tuple-element.108), channel_id=1, source_target_pairs={{0,16},{8,24},{16,0},{24,8},{1,17},{9,25},{17,1},{25,9},{2,18},{10... | collective-permute-start | bytes 1572872 | tf_op jit(solution)/shard_map/ppermute | solution.py:259
  60.4 65.8 %collective-permute-start.21 = (f32[128,1024]{1,0:T(8,128)}, f32[128,1024]{1,0:T(8,128)}, u32[]{:S(2)}, u32[]{:S(2)}) collective-permute-start(f32[128,1024]{1,0:T(8,128)} %get-tuple-element.106), channel_id=1, source_target_pairs={{0,24},{8,0},{16,8},{24,16},{1,25},{9,1},{17,9},{25,17},{2,26},{10... | collective-permute-start | bytes 1572872 | tf_op jit(solution)/shard_map/ppermute | solution.py:259
  64.5 7.6 %collective-permute-start.11 = (f32[128,512]{1,0:T(8,128)S(1)}, f32[128,512]{1,0:T(8,128)S(1)}, u32[]{:S(2)}, u32[]{:S(2)}) collective-permute-start(f32[128,512]{1,0:T(8,128)S(1)} %get-tuple-element.67), channel_id=1, source_target_pairs={{0,2},{1,3},{8,10},{9,11},{16,18},{17,19},{24,26},{25,27}} | collective-permute-start | bytes 786440 | tf_op jit(solution)/shard_map/ppermute | solution.py:286
  78.1 21.8 %collective-permute-start.8 = (f32[128,512]{1,0:T(8,128)S(1)}, f32[128,512]{1,0:T(8,128)}, u32[]{:S(2)}, u32[]{:S(2)}) collective-permute-start(f32[128,512]{1,0:T(8,128)S(1)} %get-tuple-element.102), channel_id=1, source_target_pairs={{2,0},{3,1},{10,8},{11,9},{18,16},{19,17},{26,24},{27,25}} | collective-permute-start | bytes 786440 | tf_op jit(solution)/shard_map/ppermute | solution.py:287
  80.5 33.8 %collective-permute-start.13 = (f32[128,512]{1,0:T(8,128)}, f32[128,512]{1,0:T(8,128)}, u32[]{:S(2)}, u32[]{:S(2)}) collective-permute-start(f32[128,512]{1,0:T(8,128)} %get-tuple-element.119), channel_id=1, source_target_pairs={{4,6},{5,7},{12,14},{13,15},{20,22},{21,23},{28,30},{29,31}} | collective-permute-start | bytes 786440 | tf_op jit(solution)/shard_map/ppermute | solution.py:286
  100.0 15.3 %collective-permute-start.16 = (f32[128,512]{1,0:T(8,128)}, f32[128,512]{1,0:T(8,128)}, u32[]{:S(2)}, u32[]{:S(2)}) collective-permute-start(f32[128,512]{1,0:T(8,128)} %get-tuple-element.98), channel_id=1, source_target_pairs={{2,0},{3,1},{10,8},{11,9},{18,16},{19,17},{26,24},{27,25}} | collective-permute-start | bytes 786440 | tf_op jit(solution)/shard_map/ppermute | solution.py:287
  117.4 6.3 %collective-permute-start.22 = (f32[128,256]{1,0:T(8,128)S(1)}, f32[128,256]{1,0:T(8,128)S(1)}, u32[]{:S(2)}, u32[]{:S(2)}) collective-permute-start(f32[128,256]{1,0:T(8,128)S(1)} %get-tuple-element.89), channel_id=1, source_target_pairs={{0,1},{1,0},{2,3},{3,2},{4,5},{5,4},{6,7},{7,6},{8,9},{9,8},{10,11... | collective-permute-start | bytes 393224 | tf_op jit(solution)/shard_map/ppermute | solution.py:237
  119.3 19.7 %collective-permute-start.17 = (f32[128,512]{1,0:T(8,128)S(1)}, f32[128,512]{1,0:T(8,128)S(1)}, u32[]{:S(2)}, u32[]{:S(2)}) collective-permute-start(f32[128,512]{1,0:T(8,128)S(1)} %get-tuple-element.86), channel_id=1, source_target_pairs={{0,1},{1,0},{2,3},{3,2},{4,5},{5,4},{6,7},{7,6},{8,9},{9,8},{10,11... | collective-permute-start | bytes 786440 | tf_op jit(solution)/shard_map/ppermute | solution.py:237
  123.8 6.4 %collective-permute-start.24 = (f32[128,256]{1,0:T(8,128)S(1)}, f32[128,256]{1,0:T(8,128)S(1)}, u32[]{:S(2)}, u32[]{:S(2)}) collective-permute-start(f32[128,256]{1,0:T(8,128)S(1)} %add.161.refs_5_), channel_id=1, source_target_pairs={{0,16},{8,24},{16,0},{24,8},{1,17},{9,25},{17,1},{25,9},{2,18},{10... | collective-permute-start | bytes 393224 | tf_op jit(solution)/shard_map/ppermute | solution.py:317
  126.2 12.9 %collective-permute-start.18 = (f32[128,512]{1,0:T(8,128)S(1)}, f32[128,512]{1,0:T(8,128)S(1)}, u32[]{:S(2)}, u32[]{:S(2)}) collective-permute-start(f32[128,512]{1,0:T(8,128)S(1)} %get-tuple-element.87), channel_id=1, source_target_pairs={{0,1},{1,0},{2,3},{3,2},{4,5},{5,4},{6,7},{7,6},{8,9},{9,8},{10,11... | collective-permute-start | bytes 786440 | tf_op jit(solution)/shard_map/ppermute | solution.py:237
  133.0 8.6 %collective-permute-start.32 = (f32[128,256]{1,0:T(8,128)S(1)}, f32[128,256]{1,0:T(8,128)S(1)}, u32[]{:S(2)}, u32[]{:S(2)}) collective-permute-start(f32[128,256]{1,0:T(8,128)S(1)} %get-tuple-element.97), channel_id=1, source_target_pairs={{0,7},{1,0},{2,1},{3,2},{4,3},{5,4},{6,5},{7,6},{8,15},{9,8},{10,9... | collective-permute-start | bytes 393224 | tf_op jit(solution)/shard_map/ppermute | solution.py:333
  134.6 9.9 %collective-permute-start.31 = (f32[128,256]{1,0:T(8,128)S(1)}, f32[128,256]{1,0:T(8,128)S(1)}, u32[]{:S(2)}, u32[]{:S(2)}) collective-permute-start(f32[128,256]{1,0:T(8,128)S(1)} %get-tuple-element.96), channel_id=1, source_target_pairs={{0,6},{1,7},{2,0},{3,1},{4,2},{5,3},{6,4},{7,5},{8,14},{9,15},{10,... | collective-permute-start | bytes 393224 | tf_op jit(solution)/shard_map/ppermute | solution.py:333
  137.7 8.3 %collective-permute-start.30 = (f32[128,256]{1,0:T(8,128)S(1)}, f32[128,256]{1,0:T(8,128)S(1)}, u32[]{:S(2)}, u32[]{:S(2)}) collective-permute-start(f32[128,256]{1,0:T(8,128)S(1)} %get-tuple-element.95), channel_id=1, source_target_pairs={{0,5},{1,6},{2,7},{3,0},{4,1},{5,2},{6,3},{7,4},{8,13},{9,14},{10,... | collective-permute-start | bytes 393224 | tf_op jit(solution)/shard_map/ppermute | solution.py:333
  139.0 23.1 %collective-permute-start.29 = (f32[128,256]{1,0:T(8,128)S(1)}, f32[128,256]{1,0:T(8,128)S(1)}, u32[]{:S(2)}, u32[]{:S(2)}) collective-permute-start(f32[128,256]{1,0:T(8,128)S(1)} %get-tuple-element.94), channel_id=1, source_target_pairs={{0,4},{1,5},{2,6},{3,7},{4,0},{5,1},{6,2},{7,3},{8,12},{9,13},{10,... | collective-permute-start | bytes 393224 | tf_op jit(solution)/shard_map/ppermute | solution.py:333
  139.1 23.7 %collective-permute-start.28 = (f32[128,256]{1,0:T(8,128)S(1)}, f32[128,256]{1,0:T(8,128)S(1)}, u32[]{:S(2)}, u32[]{:S(2)}) collective-permute-start(f32[128,256]{1,0:T(8,128)S(1)} %get-tuple-element.93), channel_id=1, source_target_pairs={{0,3},{1,4},{2,5},{3,6},{4,7},{5,0},{6,1},{7,2},{8,11},{9,12},{10,... | collective-permute-start | bytes 393224 | tf_op jit(solution)/shard_map/ppermute | solution.py:333
  141.6 21.1 %collective-permute-start.27 = (f32[128,256]{1,0:T(8,128)S(1)}, f32[128,256]{1,0:T(8,128)S(1)}, u32[]{:S(2)}, u32[]{:S(2)}) collective-permute-start(f32[128,256]{1,0:T(8,128)S(1)} %get-tuple-element.92), channel_id=1, source_target_pairs={{0,2},{1,3},{2,4},{3,5},{4,6},{5,7},{6,0},{7,1},{8,10},{9,11},{10,... | collective-permute-start | bytes 393224 | tf_op jit(solution)/shard_map/ppermute | solution.py:333
  144.6 18.2 %collective-permute-start.26 = (f32[128,256]{1,0:T(8,128)S(1)}, f32[128,256]{1,0:T(8,128)S(1)}, u32[]{:S(2)}, u32[]{:S(2)}) collective-permute-start(f32[128,256]{1,0:T(8,128)S(1)} %get-tuple-element.91), channel_id=1, source_target_pairs={{0,1},{1,2},{2,3},{3,4},{4,5},{5,6},{6,7},{7,0},{8,9},{9,10},{10,1... | collective-permute-start | bytes 393224 | tf_op jit(solution)/shard_map/ppermute | solution.py:333
  (69 other events, 491.6 us)

commit v2 on v1

v2 whole, which is shorter than its diff:
```python
import functools

import jax
import jax.numpy as jnp
from jax import lax
from jax.experimental import pallas as pl
from jax.experimental.pallas import tpu as pltpu
from jax.sharding import PartitionSpec as P

HEADS = 32
HEAD_DIM = 64
STATE = 128
SPAN = 128
CHUNKS = 2
F32 = jnp.float32
BF16 = jnp.bfloat16
VMEM_LIMIT = 16 * 1024 * 1024


def group_size(n_seq):
    q = 1
    while n_seq % (2 * q) == 0 and 4 * q * q <= n_seq:
        q *= 2
    return q


def nn(a, b):
    return lax.dot_general(a, b, (((1,), (0,)), ((), ())), preferred_element_type=F32)


def nt(a, b):
    return lax.dot_general(a, b, (((1,), (1,)), ((), ())), preferred_element_type=F32)


def tn(a, b):
    return lax.dot_general(a, b, (((0,), (0,)), ((), ())), preferred_element_type=F32)


def exact(a, b, dims):
    return lax.dot_general(
        a, b, (dims, ((), ())), preferred_element_type=F32, precision=lax.Precision.HIGHEST
    )


def call(body, outs, n_in, scratch=(), name=None, cost=None, smem=1):
    specs = [pl.BlockSpec(memory_space=pltpu.SMEM)] * smem
    specs += [pl.BlockSpec(memory_space=pltpu.VMEM)] * n_in
    return pl.pallas_call(
        body,
        out_shape=outs,
        in_specs=specs,
        out_specs=jax.tree.map(lambda _: pl.BlockSpec(memory_space=pltpu.VMEM), outs),
        scratch_shapes=scratch,
        compiler_params=pltpu.CompilerParams(vmem_limit_bytes=VMEM_LIMIT),
        cost_estimate=cost,
        name=name,
    )


def out(shape, dtype=F32):
    return jax.ShapeDtypeStruct(shape, dtype)


def iotas():
    rows = lax.broadcasted_iota(jnp.int32, (SPAN, SPAN), 0)
    cols = lax.broadcasted_iota(jnp.int32, (SPAN, SPAN), 1)
    return rows, cols


def columns(ref, start, width):
    return ref[:, pl.ds(pl.multiple_of(start, 128), width)]


def pack_body(q, ids, *refs):
    x, g, packed = refs
    packed[0] = x[...].astype(F32)
    packed[1] = g[...].astype(F32)


def pack(ids, x, g, q, r, chunk, width):
    def place(i, ids):
        return 0, lax.rem(ids[0] + r, q) * CHUNKS + chunk

    block = pl.BlockSpec((SPAN, width), place)
    return pl.pallas_call(
        functools.partial(pack_body, q),
        out_shape=out((2, SPAN, width)),
        grid_spec=pltpu.PrefetchScalarGridSpec(
            num_scalar_prefetch=1,
            grid=(1,),
            in_specs=[block, block],
            out_specs=pl.BlockSpec((2, SPAN, width), lambda i, ids: (0, 0, 0)),
        ),
        compiler_params=pltpu.CompilerParams(vmem_limit_bytes=VMEM_LIMIT),
        name="pack",
    )(ids, x, g)


def project_body(q, ids, tokens, weight, decay, step, *bundles):
    proj = nn(tokens[...], weight[...]).astype(BF16).astype(F32)
    heads = HEADS // q
    for r in range(q):
        at = pl.multiple_of(lax.rem(ids[0] + r, q) * heads, heads)
        bundles[r][:SPAN, :] = proj
        bundles[r][SPAN:, :SPAN] = decay[pl.ds(at, heads), :]
        bundles[r][SPAN:, SPAN:] = step[pl.ds(at, heads), :]


def states_body(q, hc, chunk, *refs):
    n = q - 1
    it = iter(refs)
    ids, x_ref, g_ref = next(it), next(it), next(it)
    xg_in = [next(it) for _ in range(n)]
    bundles = [next(it) for _ in range(q)]
    xs, gs, ws, ss, f1s, ds, own_s, own_g, total_s, total_g, plane, bcs, cums, avs = it
    width = hc * HEAD_DIM
    y = ids[0]
    first = (y * CHUNKS + chunk) * width
    xs[y] = columns(x_ref, first, width)
    gs[y] = columns(g_ref, first, width)
    low = SPAN + chunk * hc
    for r in range(q):
        at = lax.rem(y - r + q, q)
        if r > 0:
            xs[at] = xg_in[r - 1][0].astype(BF16)
            gs[at] = xg_in[r - 1][1].astype(BF16)
        bcs[at] = bundles[r][:SPAN, :].astype(BF16)
        cums[at] = bundles[r][low : low + hc, :SPAN]
        avs[at] = bundles[r][low : low + hc, SPAN:]
    rows, cols = iotas()
    tri = (rows >= cols).astype(F32)
    eye = (rows == cols).astype(F32)
    head_of = lax.broadcasted_iota(jnp.int32, (hc, width), 1) // HEAD_DIM
    spread = (head_of == lax.broadcasted_iota(jnp.int32, (hc, width), 0)).astype(F32)
    last = ((1,), (1,))
    for b in range(q):
        decay = cums[b]
        cum_c = exact(tri, decay, last)
        a_c = cum_c - exact(eye, jnp.log(avs[b]), last)
        cums[b] = exact(decay, tri, last)
        cum_x = exact(cum_c, spread, ((1,), (0,)))
        a_x = exact(a_c, spread, ((1,), (0,)))
        avs[b] = exact(a_c, eye, ((0,), (0,)))
        total = cum_x[SPAN - 1 : SPAN, :]
        f1 = jnp.exp(total - a_x)
        f1s[b] = f1
        ds[b] = jnp.exp(total)
        weighted = (xs[b].astype(F32) * f1).astype(BF16)
        scaled = (gs[b].astype(F32) * jnp.exp(cum_x)).astype(BF16)
        ws[b] = weighted
        ss[b] = scaled
        own_s[b] = tn(bcs[b][:, :STATE], weighted)
        own_g[b] = tn(bcs[b][:, STATE:], scaled)
    forward, backward, through = own_s[0], own_g[q - 1], ds[0]
    for b in range(1, q):
        forward = ds[b] * forward + own_s[b]
        backward = ds[q - 1 - b] * backward + own_g[q - 1 - b]
        through = through * ds[b]
    total_s[...] = forward
    total_g[...] = backward
    plane[...] = through


def local_body(q, hc, chunk, ids, skip, xs, gs, bcs, cums, avs, gx, gp):
    rows, cols = iotas()
    causal = rows <= cols
    low = lax.broadcasted_iota(jnp.int32, (SPAN, 128), 1) < HEAD_DIM
    eye = (rows == cols).astype(F32)
    first = (ids[0] * CHUNKS + chunk) * hc
    for b in range(q):
        b_cols, c_cols = bcs[b][:, :STATE], bcs[b][:, STATE:]
        kernel = nt(b_cols, c_cols)
        a_c = exact(eye, avs[b], ((1,), (1,)))
        mixing = jnp.zeros((SPAN, SPAN), F32)
        for pair in range(hc // 2):
            at = slice(pair * 128, pair * 128 + 128)
            x, g = xs[b][:, at], gs[b][:, at]
            parts = []
            for half in range(2):
                h = 2 * pair + half
                gap = cums[b][h : h + 1, :] - a_c[:, h : h + 1]
                decay = jnp.exp(jnp.where(causal, gap, -jnp.inf))
                picked = jnp.where(low if half == 0 else ~low, x, jnp.zeros_like(x))
                mixing += decay * nt(picked, g)
                parts.append(nn((decay * kernel).astype(BF16), g))
            gains = jnp.where(low, skip[first + 2 * pair], skip[first + 2 * pair + 1])
            gx[b, :, at] = jnp.where(low, parts[0], parts[1]) + gains * g.astype(F32)
        mixed = mixing.astype(BF16)
        gp[b, :, :STATE] = nn(mixed, c_cols)
        gp[b, :, STATE:] = tn(mixed, b_cols)


def final_body(q, more, *refs):
    it = iter(refs)
    ids, start, after, own_s, own_g, ds, ws, ss, f1s, bcs, gx, gp = [next(it) for _ in range(12)]
    before = next(it) if more else None
    gx_out = [next(it) for _ in range(q)]
    gp_out, gx_all = it
    y = ids[0]
    state = start[...]
    for b in range(q):
        part = gp[b, :, STATE:] + nt(ss[b], state.astype(BF16))
        gp_out[b, :, STATE:] = part if before is None else part + before[b, :, STATE:]
        if b < q - 1:
            state = ds[b] * state + own_s[b]
    state = after[...]
    for b in range(q - 1, -1, -1):
        rounded = state.astype(BF16)
        gx_all[b] = gx[b] + f1s[b] * nn(bcs[b][:, :STATE], rounded)
        part = gp[b, :, :STATE] + nt(ws[b], rounded)
        gp_out[b, :, :STATE] = part if before is None else part + before[b, :, :STATE]
        if b > 0:
            state = ds[b] * state + own_g[b]
    for r in range(q):
        gx_out[r][...] = gx_all[lax.rem(y + r, q)]


def assemble_body(q, width, *refs):
    ids, result = refs[0], refs[-1]
    parts = refs[1:-1]
    y = ids[0]
    for r in range(q):
        group = lax.rem(y - r + q, q)
        for c in range(CHUNKS):
            at = pl.multiple_of((group * CHUNKS + c) * width, 128)
            result[:, pl.ds(at, width)] = parts[r * CHUNKS + c][...].astype(BF16)


def weight_body(n_dp, q, planes, rows, scale, *refs):
    it = iter(refs)
    ids = next(it)
    tokens = [next(it) for _ in range(n_dp)]
    swapped = [next(it) for _ in range(q - 1)]
    grads = [next(it) for _ in range(n_dp)]
    outs = [next(it) for _ in range(planes)]
    held, factors, products = it
    width = planes * rows
    y, z = ids[0], ids[1] // q
    for r in range(n_dp):
        held[y, r] = columns(tokens[r], y * width, width).astype(BF16)
        for b in range(q):
            factors[b, r] = grads[r][b].astype(BF16)
    for k in range(1, q):
        at = lax.rem(y - k + q, q)
        for r in range(n_dp):
            held[at, r] = swapped[k - 1][r].astype(BF16)
    total = tn(
        held[...].reshape(q * n_dp * SPAN, width), factors[...].reshape(q * n_dp * SPAN, 2 * STATE)
    )
    products[...] = (total * scale).reshape(planes, rows, 2 * STATE)
    for r in range(planes):
        outs[r][...] = products[lax.rem(z + r, planes)]


def behind(value, *others):
    return lax.optimization_barrier((value,) + others)[0]


def on_device(layer_input, proj_weight, inputs, step_size, log_decay, skip_gain, grad_out):
    n_seq, n_dp = lax.axis_size("seq"), lax.axis_size("dp")
    q = group_size(n_seq)
    planes = n_seq // q
    group_heads = HEADS // q
    hc = group_heads // CHUNKS
    width = hc * HEAD_DIM
    tokens, x, g = layer_input[0], inputs[0], grad_out[0]
    length, features = tokens.shape
    seq, dp = lax.axis_index("seq"), lax.axis_index("dp")
    y = lax.rem(seq, q)
    ids = jnp.stack([y, seq, dp]).astype(jnp.int32)

    def swap(value, r):
        pairs = [(z * q + i, z * q + (i + r) % q) for z in range(planes) for i in range(q)]
        return lax.ppermute(value, "seq", pairs)

    def across(value, r):
        return lax.ppermute(value, "dp", [(i, i ^ r) for i in range(n_dp)])

    xg_in = {}
    for r in range(1, q):
        xg_in[0, r] = swap(pack(ids, x, g, q, r, 0, width), r)
    bundle_out = (out((SPAN + group_heads, 2 * STATE)),) * q
    bundles = call(functools.partial(project_body, q), bundle_out, 4, name="project")(
        ids, tokens, proj_weight, log_decay[0], step_size[0]
    )
    bundles = [bundles[0]] + [swap(bundles[r], r) for r in range(1, q)]
    columns_each = features // n_dp
    rows = columns_each // n_seq
    part = planes * rows

    def quarter(owner):
        cut = lax.dynamic_slice_in_dim(tokens, owner * columns_each, columns_each, axis=1)
        order = [(z * q + i) * rows for i in range(q) for z in range(planes)]
        return jnp.concatenate([cut[:, at : at + rows] for at in order], axis=1)

    token_parts = [quarter(dp)]
    for r in range(1, n_dp):
        token_parts.append(across(quarter(dp ^ r).astype(F32), r))
    for c in range(1, CHUNKS):
        for r in range(1, q):
            packed = behind(pack(ids, x, g, q, r, c, width), xg_in[c - 1, r])
            xg_in[c, r] = swap(packed, r)
    swapped = []
    for r in range(1, q):
        at = lax.rem(y + r, q) * part
        cut = [lax.dynamic_slice_in_dim(v, at, part, axis=1).astype(F32) for v in token_parts]
        swapped.append(swap(behind(jnp.stack(cut), xg_in[CHUNKS - 1, r]), r))

    rows_of = (q, SPAN, width)
    held = []
    for c in range(CHUNKS):
        outs = (
            out(rows_of, BF16), out(rows_of, BF16), out(rows_of, BF16), out(rows_of, BF16),
            out(rows_of), out((q, 1, width)), out(rows_of), out(rows_of),
            out((STATE, width)), out((STATE, width)), out((1, width)),
            out((q, SPAN, 2 * STATE), BF16), out((q, hc, SPAN)), out((q, hc, SPAN)),
        )
        args = [x, g] + [xg_in[c, r] for r in range(1, q)] + bundles
        held.append(
            call(functools.partial(states_body, q, hc, c), outs, len(args), name="states")(ids, *args)
        )

    local = []
    for c in range(CHUNKS):
        xs, gs, _, _, _, _, _, _, _, _, _, bcs, cums, avs = held[c]
        local.append(
            call(
                functools.partial(local_body, q, hc, c),
                (out(rows_of), out((q, SPAN, 2 * STATE))), 5, smem=2, name="local",
            )(ids, skip_gain, xs, gs, bcs, cums, avs)
        )

    entries = []
    for c in range(CHUNKS):
        total_s, total_g, through = held[c][8:11]
        sent, back = total_s, total_g
        start, after = jnp.zeros_like(total_s), jnp.zeros_like(total_g)
        for t in range(planes - 1):
            up = [(t * q + i, (t + 1) * q + i) for i in range(q)]
            top = planes - 1 - t
            down = [(top * q + i, (top - 1) * q + i) for i in range(q)]
            got_s, got_g = lax.ppermute(sent, "seq", up), lax.ppermute(back, "seq", down)
            if t == planes - 2:
                got_s, got_g = behind(got_s, local[c]), behind(got_g, local[c])
            start += got_s
            after += got_g
            if t < planes - 2:
                sent = total_s + through * start
                back = total_g + through * after
        entries.append((start, after))

    before, gx_parts = [], {}
    for c in range(CHUNKS):
        _, _, ws, ss, f1s, ds, own_s, own_g, _, _, _, bcs, _, _ = held[c]
        gx, gp = local[c]
        start, after = entries[c]
        outs = (out((SPAN, width)),) * q + (out((q, SPAN, 2 * STATE)),)
        args = [start, after, own_s, own_g, ds, ws, ss, f1s, bcs, gx, gp] + before
        scratch = (pltpu.VMEM(rows_of, F32),)
        done = call(
            functools.partial(final_body, q, bool(before)), outs, len(args), scratch, name="final"
        )(ids, *args)
        for r in range(q):
            gx_parts[r, c] = done[r]
        before = [done[q]]

    gp = before[0]
    for r in range(1, q):
        gp = gp + swap(before[0], r)
    grads = {0: gp}
    bit = n_dp // 2
    while bit:
        for r in list(grads):
            grads[r ^ bit] = across(grads[r], bit)
        bit //= 2
    scale = 1.0 / (length * n_seq)
    outs = (out((rows, 2 * STATE)),) * planes
    args = token_parts + swapped + [grads[r] for r in range(n_dp)]
    scratch = (
        pltpu.VMEM((q, n_dp, SPAN, part), BF16),
        pltpu.VMEM((q, n_dp, SPAN, 2 * STATE), BF16),
        pltpu.VMEM((planes, rows, 2 * STATE), F32),
    )
    pieces = call(
        functools.partial(weight_body, n_dp, q, planes, rows, scale), outs, len(args), scratch, name="weight"
    )(ids, *args)
    grad_weight = pieces[0]
    for r in range(1, planes):
        pairs = [(z * q + i, (z + r) % planes * q + i) for z in range(planes) for i in range(q)]
        grad_weight = grad_weight + lax.ppermute(pieces[r], "seq", pairs)

    parts = [gx_parts[0, c] for c in range(CHUNKS)]
    for r in range(1, q):
        parts += [swap(gx_parts[r, c], r) for c in range(CHUNKS)]
    grad_x = call(
        functools.partial(assemble_body, q, width),
        out((length, q * CHUNKS * width), BF16), len(parts), name="assemble",
    )(ids, *parts)
    return grad_x[None], grad_weight


def solution(mesh):
    return jax.shard_map(
        on_device,
        mesh=mesh,
        in_specs=(
            P("dp", "seq", None),
            P(),
            P("dp", "seq", None),
            P("dp", None, "seq"),
            P("dp", None, "seq"),
            P(),
            P("dp", "seq", None),
        ),
        out_specs=(P("dp", "seq", None), P(("dp", "seq"), None)),
        check_vma=False,
    )
```

time: 164 us -> 124 us (0.76)
  local copies, waits for them, and re-layouts: 20.8 us -> 5.88 us
  waiting for transfers between devices: 69.9 us -> 55.2 us
  other arithmetic: 12.3 us -> 4.16 us
  starting transfers between devices: 42.1 us -> 38.1 us
  Pallas kernels: 16.5 us -> 18.7 us
    unnamed x121 -> x46, local copies, waits for them, and re-layouts: 18.1 us -> 5.64 us
    ppermute x7 -> x3, waiting for transfers between devices: 16.8 us -> 8.6 us  [on_device(): grad_weight = grad_weight + lax.ppermute(pieces[r], 'seq', pairs)]
    ppermute x26 -> x25, waiting for transfers between devices: 53.1 us -> 46.6 us  [the longest x6 17.8 us: across(): return lax.ppermute(value, 'dp', [(i, i ^ r) for i in range(n_dp)])]
    add x5, other arithmetic: 4.17 us -> 0.2 us  [the longest x2 0.09 us: on_device(): after += got_g]
    add x4, other arithmetic: 4.49 us -> 0.52 us  [on_device(): back = total_g + through * after]
    ppermute x26 -> x25, starting transfers between devices: 30.6 us -> 26.8 us  [the longest x7 10.3 us: swap(): return lax.ppermute(value, 'seq', pairs)]
    pallas_call x3 -> x6, Pallas kernels: 6.29 us -> 9.26 us  [the longest x2 4.16 us: on_device(): call(functools.partial(local_body, q, hc, c), (out(rows_of), out((q, SPAN...]
    dynamic_slice x3 -> x1, local copies, waits for them, and re-layouts: 1.91 us -> 0.09 us  [quarter(): lax.dynamic_slice_in_dim(tokens, owner * columns_each, columns_each, axis=1)]
  transfers between devices with their start and end apart: 33 -> 28, of which waited for: 10 -> 10; matrix products, arithmetic and copies ran while one was open for 8% -> 3% of each run, Pallas kernels for 10% -> 14%
where the time goes in v2:
time: 124 us; the launch traced here: 123 us
  waiting for transfers between devices  55.2 us (45%)
  starting transfers between devices  38.1 us (31%)
  Pallas kernels  18.7 us (15%)
  local copies, waits for them, and re-layouts  5.88 us (5%)
  other arithmetic  4.16 us (3%)
    ppermute x6, waiting for transfers between devices, across(): return lax.ppermute(value, 'dp', [(i, i ^ r) for i in range(n_dp)])  17.8 us
    ppermute x7, waiting for transfers between devices, swap(): return lax.ppermute(value, 'seq', pairs)  14.8 us
    ppermute x3, starting transfers between devices, on_device(): grad_weight = grad_weight + lax.ppermute(pieces[r], 'seq', pairs)  11.3 us
    ppermute x7, starting transfers between devices, swap(): return lax.ppermute(value, 'seq', pairs)  10.3 us
    ppermute x6, waiting for transfers between devices, on_device(): lax.ppermute(back, 'seq', down)  9.1 us
    ppermute x3, waiting for transfers between devices, on_device(): grad_weight = grad_weight + lax.ppermute(pieces[r], 'seq', pairs)  8.6 us
    ppermute x6, starting transfers between devices, on_device(): lax.ppermute(sent, 'seq', up)  7.62 us
    pallas_call x2, Pallas kernels, on_device(): call(functools.partial(states_body, q, hc, c), outs, len(args), name='sta...  6.02 us
  transfers between devices with their start and end apart: 28, of which 10 were waited for; matrix products, arithmetic and copies ran while one was open for 3% of the time, Pallas kernels for 14%

profile of v2, /device:TPU:0, one launch (start us, length us, event | category | flops | bytes accessed | tf_op | source)
XLA Modules:
  0.0 123.2 jit_solution(10124849984385783563)
XLA Ops:
  4.2 3.0 %collective-permute-start = (f32[2,128,512]{2,1,0:T(8,128)}, f32[2,128,512]{2,1,0:T(8,128)}, u32[]{:S(2)}, u32[]{:S(2)}) collective-permute-start(f32[2,128,512]{2,1,0:T(8,128)} %pack.2), channel_id=1, source_target_pairs={{0,1},{1,0},{2,3},{3,2},{4,5},{5,4},{6,7},{7,6},{8,9},{9,8},{10,11... | collective-permute-start | bytes 1572872 | tf_op jit(solution)/shard_map/ppermute | solution.py:274
  7.1 1.6 %copy-done.5 = bf16[4096,256]{1,0:T(8,128)(2,1)S(1)} copy-done((bf16[4096,256]{1,0:T(8,128)(2,1)S(1)}, bf16[4096,256]{1,0:T(8,128)(2,1)}, u32[]{:S(2)}) %copy-start.5) | copy-done | bytes 2097176
  13.5 2.0 %collective-permute-start.18 = (f32[128,1024]{1,0:T(8,128)}, f32[128,1024]{1,0:T(8,128)S(1)}, u32[]{:S(2)}, u32[]{:S(2)}) collective-permute-start(f32[128,1024]{1,0:T(8,128)} %convert_element_type.11), channel_id=1, source_target_pairs={{0,16},{8,24},{16,0},{24,8},{1,17},{9,25},{17,1},{25,9},{2,18},{10... | collective-permute-start | bytes 1572872 | tf_op jit(solution)/shard_map/ppermute | solution.py:277
  16.8 1.4 %pack.3 = f32[2,128,512]{2,1,0:T(8,128)} custom-call(s32[3]{0:T(128)S(1)} %pad_add_fusion.ids.refs_0_, bf16[128,2048]{1,0:T(8,128)(2,1)S(1)} %bitcast.29, bf16[128,2048]{1,0:T(8,128)(2,1)S(1)} %bitcast.33), custom_call_target="tpu_custom_call" | custom-call | tf_op jit(solution)/shard_map/pack/pallas_call | solution.py:85
  18.2 2.0 %collective-permute-done.refs_3_ = f32[2,128,512]{2,1,0:T(8,128)} collective-permute-done((f32[2,128,512]{2,1,0:T(8,128)}, f32[2,128,512]{2,1,0:T(8,128)}, u32[]{:S(2)}, u32[]{:S(2)}) %collective-permute-start) | collective-permute-done | bytes 524320 | tf_op jit(solution)/shard_map/ppermute | solution.py:274
  20.2 2.1 %collective-permute-start.8 = (f32[2,128,512]{2,1,0:T(8,128)}, f32[2,128,512]{2,1,0:T(8,128)}, u32[]{:S(2)}, u32[]{:S(2)}) collective-permute-start(f32[2,128,512]{2,1,0:T(8,128)} %pack.3), channel_id=1, source_target_pairs={{0,1},{1,0},{2,3},{3,2},{4,5},{5,4},{6,7},{7,6},{8,9},{9,8},{10,11... | collective-permute-start | bytes 1572872 | tf_op jit(solution)/shard_map/ppermute | solution.py:274
  23.3 3.0 %states.2 = (bf16[2,128,512]{2,1,0:T(8,128)(2,1)S(1)}, bf16[2,128,512]{2,1,0:T(8,128)(2,1)S(1)}, bf16[2,128,512]{2,1,0:T(8,128)(2,1)S(1)}, bf16[2,128,512]{2,1,0...) custom-call(s32[3]{0:T(128)S(1)} %pad_add_fusion.ids.refs_0_, ...), custom_call_target="tpu_custom_call" | custom-call | tf_op jit(solution)/shard_map/states/pallas_call | solution.py:320
  27.0 12.3 %collective-permute-done.19.refs_4_ = f32[128,1024]{1,0:T(8,128)S(1)} collective-permute-done((f32[128,1024]{1,0:T(8,128)}, f32[128,1024]{1,0:T(8,128)S(1)}, u32[]{:S(2)}, u32[]{:S(2)}) %collective-permute-start.19) | collective-permute-done | bytes 524320 | tf_op jit(solution)/shard_map/ppermute | solution.py:277
  39.2 3.6 %collective-permute-start.2 = (f32[128,512]{1,0:T(8,128)S(1)}, f32[128,512]{1,0:T(8,128)S(1)}, u32[]{:S(2)}, u32[]{:S(2)}) collective-permute-start(f32[128,512]{1,0:T(8,128)S(1)} %get-tuple-element.54), channel_id=1, source_target_pairs={{0,2},{1,3},{8,10},{9,11},{16,18},{17,19},{24,26},{25,27}} | collective-permute-start | bytes 786440 | tf_op jit(solution)/shard_map/ppermute | solution.py:342
  43.0 3.0 %states.3 = (bf16[2,128,512]{2,1,0:T(8,128)(2,1)S(1)}, bf16[2,128,512]{2,1,0:T(8,128)(2,1)S(1)}, bf16[2,128,512]{2,1,0:T(8,128)(2,1)S(1)}, bf16[2,128,512]{2,1,0...) custom-call(s32[3]{0:T(128)S(1)} %pad_add_fusion.ids.refs_0_, ...), custom_call_target="tpu_custom_call" | custom-call | tf_op jit(solution)/shard_map/states/pallas_call | solution.py:320
  50.6 3.7 %collective-permute-done.9 = f32[128,512]{1,0:T(8,128)S(1)} collective-permute-done((f32[128,512]{1,0:T(8,128)S(1)}, f32[128,512]{1,0:T(8,128)S(1)}, u32[]{:S(2)}, u32[]{:S(2)}) %collective-permute-start.9) | collective-permute-done | bytes 262176 | tf_op jit(solution)/shard_map/ppermute | solution.py:342
  60.3 1.6 %collective-permute-start.20 = (f32[4,128,512]{2,1,0:T(8,128)S(1)}, f32[4,128,512]{2,1,0:T(8,128)S(1)}, u32[]{:S(2)}, u32[]{:S(2)}) collective-permute-start(f32[4,128,512]{2,1,0:T(8,128)S(1)} %pad_maximum_fusion), channel_id=1, source_target_pairs={{0,1},{1,0},{2,3},{3,2},{4,5},{5,4},{6,7},{7,6},{8,9},{9,8},{10,11... | collective-permute-start | bytes 3145736 | tf_op jit(solution)/shard_map/ppermute | solution.py:274
  61.9 2.1 %local.2 = (f32[2,128,512]{2,1,0:T(8,128)S(1)}, f32[2,128,256]{2,1,0:T(8,128)S(1)}) custom-call(s32[3]{0:T(128)S(1)} %pad_add_fusion.ids.refs_0_, f32[32]{0:T(128)S(1)} %copy-done.8, bf16[2,128,512]{2,1,0:T(8,128)(2,1)S(1)} %get-tuple-element.56.xs, bf16[2,128,512]{2,1,0:T(8,128)(2,1)S(1)} %get-tuple-element.57.gs, ...), custom_call_target="tpu_custom_call" | custom-call | tf_op jit(solution)/shard_map/local/pallas_call | solution.py:327
  64.0 2.1 %local.3 = (f32[2,128,512]{2,1,0:T(8,128)S(1)}, f32[2,128,256]{2,1,0:T(8,128)S(1)}) custom-call(s32[3]{0:T(128)S(1)} %pad_add_fusion.ids.refs_0_, f32[32]{0:T(128)S(1)} %copy-done.8, bf16[2,128,512]{2,1,0:T(8,128)(2,1)S(1)} %get-tuple-element.76.xs, bf16[2,128,512]{2,1,0:T(8,128)(2,1)S(1)} %get-tuple-element.77.gs, ...), custom_call_target="tpu_custom_call" | custom-call | tf_op jit(solution)/shard_map/local/pallas_call | solution.py:327
  66.0 6.5 %collective-permute-done.7 = f32[128,512]{1,0:T(8,128)S(1)} collective-permute-done((f32[128,512]{1,0:T(8,128)S(1)}, f32[128,512]{1,0:T(8,128)S(1)}, u32[]{:S(2)}, u32[]{:S(2)}) %collective-permute-start.7) | collective-permute-done | bytes 262176 | tf_op jit(solution)/shard_map/ppermute | solution.py:342
  73.6 2.6 %collective-permute-done.14 = f32[128,512]{1,0:T(8,128)S(1)} collective-permute-done((f32[128,512]{1,0:T(8,128)S(1)}, f32[128,512]{1,0:T(8,128)S(1)}, u32[]{:S(2)}, u32[]{:S(2)}) %collective-permute-start.14) | collective-permute-done | bytes 262176 | tf_op jit(solution)/shard_map/ppermute | solution.py:342
  77.3 1.6 %collective-permute-start.21 = (f32[2,128,256]{2,1,0:T(8,128)S(1)}, f32[2,128,256]{2,1,0:T(8,128)S(1)}, u32[]{:S(2)}, u32[]{:S(2)}) collective-permute-start(f32[2,128,256]{2,1,0:T(8,128)S(1)} %get-tuple-element.97), channel_id=1, source_target_pairs={{0,1},{1,0},{2,3},{3,2},{4,5},{5,4},{6,7},{7,6},{8,9},{9,8},{10,11... | collective-permute-start | bytes 786440 | tf_op jit(solution)/shard_map/ppermute | solution.py:274
  78.9 11.8 %collective-permute-done.21 = f32[2,128,256]{2,1,0:T(8,128)S(1)} collective-permute-done((f32[2,128,256]{2,1,0:T(8,128)S(1)}, f32[2,128,256]{2,1,0:T(8,128)S(1)}, u32[]{:S(2)}, u32[]{:S(2)}) %collective-permute-start.21) | collective-permute-done | bytes 262176 | tf_op jit(solution)/shard_map/ppermute | solution.py:274
  90.8 1.6 %collective-permute-start.23 = (f32[2,128,256]{2,1,0:T(8,128)S(1)}, f32[2,128,256]{2,1,0:T(8,128)S(1)}, u32[]{:S(2)}, u32[]{:S(2)}) collective-permute-start(f32[2,128,256]{2,1,0:T(8,128)S(1)} %add.103.refs_6_), channel_id=1, source_target_pairs={{0,16},{8,24},{16,0},{24,8},{1,17},{9,25},{17,1},{25,9},{2,18},{10... | collective-permute-start | bytes 786440 | tf_op jit(solution)/shard_map/ppermute | solution.py:277
  92.4 5.5 %collective-permute-done.23.refs_8_ = f32[2,128,256]{2,1,0:T(8,128)S(1)} collective-permute-done((f32[2,128,256]{2,1,0:T(8,128)S(1)}, f32[2,128,256]{2,1,0:T(8,128)S(1)}, u32[]{:S(2)}, u32[]{:S(2)}) %collective-permute-start.23) | collective-permute-done | bytes 262176 | tf_op jit(solution)/shard_map/ppermute | solution.py:277
  97.9 1.5 %collective-permute-start.15 = (f32[128,512]{1,0:T(8,128)S(1)}, f32[128,512]{1,0:T(8,128)S(1)}, u32[]{:S(2)}, u32[]{:S(2)}) collective-permute-start(f32[128,512]{1,0:T(8,128)S(1)} %get-tuple-element.94), channel_id=1, source_target_pairs={{0,1},{1,0},{2,3},{3,2},{4,5},{5,4},{6,7},{7,6},{8,9},{9,8},{10,11... | collective-permute-start | bytes 786440 | tf_op jit(solution)/shard_map/ppermute | solution.py:274
  101.3 9.3 %collective-permute-start.26 = (f32[128,256]{1,0:T(8,128)S(1)}, f32[128,256]{1,0:T(8,128)S(1)}, u32[]{:S(2)}, u32[]{:S(2)}) collective-permute-start(f32[128,256]{1,0:T(8,128)S(1)} %get-tuple-element.100), channel_id=1, source_target_pairs={{0,4},{1,5},{2,6},{3,7},{4,0},{5,1},{6,2},{7,3},{8,12},{9,13},{10,... | collective-permute-start | bytes 393224 | tf_op jit(solution)/shard_map/ppermute | solution.py:390
  110.6 1.9 %collective-permute-start.25 = (f32[128,256]{1,0:T(8,128)S(1)}, f32[128,256]{1,0:T(8,128)S(1)}, u32[]{:S(2)}, u32[]{:S(2)}) collective-permute-start(f32[128,256]{1,0:T(8,128)S(1)} %get-tuple-element.99), channel_id=1, source_target_pairs={{0,2},{1,3},{2,4},{3,5},{4,6},{5,7},{6,0},{7,1},{8,10},{9,11},{10,... | collective-permute-start | bytes 393224 | tf_op jit(solution)/shard_map/ppermute | solution.py:390
  113.9 8.6 %collective-permute-done.26 = f32[128,256]{1,0:T(8,128)S(1)} collective-permute-done((f32[128,256]{1,0:T(8,128)S(1)}, f32[128,256]{1,0:T(8,128)S(1)}, u32[]{:S(2)}, u32[]{:S(2)}) %collective-permute-start.26) | collective-permute-done | bytes 131104 | tf_op jit(solution)/shard_map/ppermute | solution.py:390
  (113 shorter events, 27.7 us)
Async XLA Ops:
  4.2 16.0 %collective-permute-start = (f32[2,128,512]{2,1,0:T(8,128)}, f32[2,128,512]{2,1,0:T(8,128)}, u32[]{:S(2)}, u32[]{:S(2)}) collective-permute-start(f32[2,128,512]{2,1,0:T(8,128)} %pack.2), channel_id=1, source_target_pairs={{0,1},{1,0},{2,3},{3,2},{4,5},{5,4},{6,7},{7,6},{8,9},{9,8},{10,11... | collective-permute-start | bytes 1572872 | tf_op jit(solution)/shard_map/ppermute | solution.py:274
  11.2 12.1 %collective-permute-start.1 = (f32[144,256]{1,0:T(8,128)S(1)}, f32[144,256]{1,0:T(8,128)S(1)}, u32[]{:S(2)}, u32[]{:S(2)}) collective-permute-start(f32[144,256]{1,0:T(8,128)S(1)} %get-tuple-element.53), channel_id=1, source_target_pairs={{0,1},{1,0},{2,3},{3,2},{4,5},{5,4},{6,7},{7,6},{8,9},{9,8},{10,11... | collective-permute-start | bytes 442376 | tf_op jit(solution)/shard_map/ppermute | solution.py:274
  12.4 30.5 %collective-permute-start.17 = (f32[128,1024]{1,0:T(8,128)}, f32[128,1024]{1,0:T(8,128)S(1)}, u32[]{:S(2)}, u32[]{:S(2)}) collective-permute-start(f32[128,1024]{1,0:T(8,128)} %convert_element_type.10), channel_id=1, source_target_pairs={{0,8},{8,0},{16,24},{24,16},{1,9},{9,1},{17,25},{25,17},{2,10},{10... | collective-permute-start | bytes 1572872 | tf_op jit(solution)/shard_map/ppermute | solution.py:277
  13.5 29.4 %collective-permute-start.18 = (f32[128,1024]{1,0:T(8,128)}, f32[128,1024]{1,0:T(8,128)S(1)}, u32[]{:S(2)}, u32[]{:S(2)}) collective-permute-start(f32[128,1024]{1,0:T(8,128)} %convert_element_type.11), channel_id=1, source_target_pairs={{0,16},{8,24},{16,0},{24,8},{1,17},{9,25},{17,1},{25,9},{2,18},{10... | collective-permute-start | bytes 1572872 | tf_op jit(solution)/shard_map/ppermute | solution.py:277
  16.5 22.8 %collective-permute-start.19 = (f32[128,1024]{1,0:T(8,128)}, f32[128,1024]{1,0:T(8,128)S(1)}, u32[]{:S(2)}, u32[]{:S(2)}) collective-permute-start(f32[128,1024]{1,0:T(8,128)} %convert_element_type.12), channel_id=1, source_target_pairs={{0,24},{8,16},{16,8},{24,0},{1,25},{9,17},{17,9},{25,1},{2,26},{10... | collective-permute-start | bytes 1572872 | tf_op jit(solution)/shard_map/ppermute | solution.py:277
  20.2 22.8 %collective-permute-start.8 = (f32[2,128,512]{2,1,0:T(8,128)}, f32[2,128,512]{2,1,0:T(8,128)}, u32[]{:S(2)}, u32[]{:S(2)}) collective-permute-start(f32[2,128,512]{2,1,0:T(8,128)} %pack.3), channel_id=1, source_target_pairs={{0,1},{1,0},{2,3},{3,2},{4,5},{5,4},{6,7},{7,6},{8,9},{9,8},{10,11... | collective-permute-start | bytes 1572872 | tf_op jit(solution)/shard_map/ppermute | solution.py:274
  26.3 21.7 %collective-permute-start.5 = (f32[128,512]{1,0:T(8,128)S(1)}, f32[128,512]{1,0:T(8,128)S(1)}, u32[]{:S(2)}, u32[]{:S(2)}) collective-permute-start(f32[128,512]{1,0:T(8,128)S(1)} %get-tuple-element.64), channel_id=1, source_target_pairs={{6,4},{7,5},{14,12},{15,13},{22,20},{23,21},{30,28},{31,29}} | collective-permute-start | bytes 786440 | tf_op jit(solution)/shard_map/ppermute | solution.py:342
  39.2 9.9 %collective-permute-start.2 = (f32[128,512]{1,0:T(8,128)S(1)}, f32[128,512]{1,0:T(8,128)S(1)}, u32[]{:S(2)}, u32[]{:S(2)}) collective-permute-start(f32[128,512]{1,0:T(8,128)S(1)} %get-tuple-element.54), channel_id=1, source_target_pairs={{0,2},{1,3},{8,10},{9,11},{16,18},{17,19},{24,26},{25,27}} | collective-permute-start | bytes 786440 | tf_op jit(solution)/shard_map/ppermute | solution.py:342
  46.7 7.7 %collective-permute-start.9 = (f32[128,512]{1,0:T(8,128)S(1)}, f32[128,512]{1,0:T(8,128)S(1)}, u32[]{:S(2)}, u32[]{:S(2)}) collective-permute-start(f32[128,512]{1,0:T(8,128)S(1)} %get-tuple-element.74), channel_id=1, source_target_pairs={{0,2},{1,3},{8,10},{9,11},{16,18},{17,19},{24,26},{25,27}} | collective-permute-start | bytes 786440 | tf_op jit(solution)/shard_map/ppermute | solution.py:342
  49.2 6.6 %collective-permute-start.6 = (f32[128,512]{1,0:T(8,128)S(1)}, f32[128,512]{1,0:T(8,128)S(1)}, u32[]{:S(2)}, u32[]{:S(2)}) collective-permute-start(f32[128,512]{1,0:T(8,128)S(1)} %get-tuple-element.120), channel_id=1, source_target_pairs={{4,2},{5,3},{12,10},{13,11},{20,18},{21,19},{28,26},{29,27}} | collective-permute-start | bytes 786440 | tf_op jit(solution)/shard_map/ppermute | solution.py:342
  49.9 5.9 %collective-permute-start.3 = (f32[128,512]{1,0:T(8,128)S(1)}, f32[128,512]{1,0:T(8,128)S(1)}, u32[]{:S(2)}, u32[]{:S(2)}) collective-permute-start(f32[128,512]{1,0:T(8,128)S(1)} %get-tuple-element.121), channel_id=1, source_target_pairs={{2,4},{3,5},{10,12},{11,13},{18,20},{19,21},{26,28},{27,29}} | collective-permute-start | bytes 786440 | tf_op jit(solution)/shard_map/ppermute | solution.py:342
  56.0 10.0 %collective-permute-start.4 = (f32[128,512]{1,0:T(8,128)S(1)}, f32[128,512]{1,0:T(8,128)S(1)}, u32[]{:S(2)}, u32[]{:S(2)}) collective-permute-start(f32[128,512]{1,0:T(8,128)S(1)} %get-tuple-element.118), channel_id=1, source_target_pairs={{4,6},{5,7},{12,14},{13,15},{20,22},{21,23},{28,30},{29,31}} | collective-permute-start | bytes 786440 | tf_op jit(solution)/shard_map/ppermute | solution.py:342
  56.7 15.8 %collective-permute-start.7 = (f32[128,512]{1,0:T(8,128)S(1)}, f32[128,512]{1,0:T(8,128)S(1)}, u32[]{:S(2)}, u32[]{:S(2)}) collective-permute-start(f32[128,512]{1,0:T(8,128)S(1)} %get-tuple-element.106), channel_id=1, source_target_pairs={{2,0},{3,1},{10,8},{11,9},{18,16},{19,17},{26,24},{27,25}} | collective-permute-start | bytes 786440 | tf_op jit(solution)/shard_map/ppermute | solution.py:342
  58.2 15.4 %collective-permute-start.11 = (f32[128,512]{1,0:T(8,128)S(1)}, f32[128,512]{1,0:T(8,128)S(1)}, u32[]{:S(2)}, u32[]{:S(2)}) collective-permute-start(f32[128,512]{1,0:T(8,128)S(1)} %get-tuple-element.114), channel_id=1, source_target_pairs={{4,6},{5,7},{12,14},{13,15},{20,22},{21,23},{28,30},{29,31}} | collective-permute-start | bytes 786440 | tf_op jit(solution)/shard_map/ppermute | solution.py:342
  58.9 17.3 %collective-permute-start.14 = (f32[128,512]{1,0:T(8,128)S(1)}, f32[128,512]{1,0:T(8,128)S(1)}, u32[]{:S(2)}, u32[]{:S(2)}) collective-permute-start(f32[128,512]{1,0:T(8,128)S(1)} %get-tuple-element.102), channel_id=1, source_target_pairs={{2,0},{3,1},{10,8},{11,9},{18,16},{19,17},{26,24},{27,25}} | collective-permute-start | bytes 786440 | tf_op jit(solution)/shard_map/ppermute | solution.py:342
  60.3 39.6 %collective-permute-start.20 = (f32[4,128,512]{2,1,0:T(8,128)S(1)}, f32[4,128,512]{2,1,0:T(8,128)S(1)}, u32[]{:S(2)}, u32[]{:S(2)}) collective-permute-start(f32[4,128,512]{2,1,0:T(8,128)S(1)} %pad_maximum_fusion), channel_id=1, source_target_pairs={{0,1},{1,0},{2,3},{3,2},{4,5},{5,4},{6,7},{7,6},{8,9},{9,8},{10,11... | collective-permute-start | bytes 3145736 | tf_op jit(solution)/shard_map/ppermute | solution.py:274
  77.3 13.4 %collective-permute-start.21 = (f32[2,128,256]{2,1,0:T(8,128)S(1)}, f32[2,128,256]{2,1,0:T(8,128)S(1)}, u32[]{:S(2)}, u32[]{:S(2)}) collective-permute-start(f32[2,128,256]{2,1,0:T(8,128)S(1)} %get-tuple-element.97), channel_id=1, source_target_pairs={{0,1},{1,0},{2,3},{3,2},{4,5},{5,4},{6,7},{7,6},{8,9},{9,8},{10,11... | collective-permute-start | bytes 786440 | tf_op jit(solution)/shard_map/ppermute | solution.py:274
  90.8 7.1 %collective-permute-start.23 = (f32[2,128,256]{2,1,0:T(8,128)S(1)}, f32[2,128,256]{2,1,0:T(8,128)S(1)}, u32[]{:S(2)}, u32[]{:S(2)}) collective-permute-start(f32[2,128,256]{2,1,0:T(8,128)S(1)} %add.103.refs_6_), channel_id=1, source_target_pairs={{0,16},{8,24},{16,0},{24,8},{1,17},{9,25},{17,1},{25,9},{2,18},{10... | collective-permute-start | bytes 786440 | tf_op jit(solution)/shard_map/ppermute | solution.py:277
  92.3 7.6 %collective-permute-start.22 = (f32[2,128,256]{2,1,0:T(8,128)S(1)}, f32[2,128,256]{2,1,0:T(8,128)S(1)}, u32[]{:S(2)}, u32[]{:S(2)}) collective-permute-start(f32[2,128,256]{2,1,0:T(8,128)S(1)} %add.103.refs_6_), channel_id=1, source_target_pairs={{0,8},{8,0},{16,24},{24,16},{1,9},{9,1},{17,25},{25,17},{2,10},{10... | collective-permute-start | bytes 786440 | tf_op jit(solution)/shard_map/ppermute | solution.py:277
  97.9 14.6 %collective-permute-start.15 = (f32[128,512]{1,0:T(8,128)S(1)}, f32[128,512]{1,0:T(8,128)S(1)}, u32[]{:S(2)}, u32[]{:S(2)}) collective-permute-start(f32[128,512]{1,0:T(8,128)S(1)} %get-tuple-element.94), channel_id=1, source_target_pairs={{0,1},{1,0},{2,3},{3,2},{4,5},{5,4},{6,7},{7,6},{8,9},{9,8},{10,11... | collective-permute-start | bytes 786440 | tf_op jit(solution)/shard_map/ppermute | solution.py:274
  99.4 13.1 %collective-permute-start.16 = (f32[128,512]{1,0:T(8,128)S(1)}, f32[128,512]{1,0:T(8,128)S(1)}, u32[]{:S(2)}, u32[]{:S(2)}) collective-permute-start(f32[128,512]{1,0:T(8,128)S(1)} %get-tuple-element.95), channel_id=1, source_target_pairs={{0,1},{1,0},{2,3},{3,2},{4,5},{5,4},{6,7},{7,6},{8,9},{9,8},{10,11... | collective-permute-start | bytes 786440 | tf_op jit(solution)/shard_map/ppermute | solution.py:274
  101.3 12.7 %collective-permute-start.27 = (f32[128,256]{1,0:T(8,128)S(1)}, f32[128,256]{1,0:T(8,128)S(1)}, u32[]{:S(2)}, u32[]{:S(2)}) collective-permute-start(f32[128,256]{1,0:T(8,128)S(1)} %get-tuple-element.101), channel_id=1, source_target_pairs={{0,6},{1,7},{2,0},{3,1},{4,2},{5,3},{6,4},{7,5},{8,14},{9,15},{10,... | collective-permute-start | bytes 393224 | tf_op jit(solution)/shard_map/ppermute | solution.py:390
  101.3 21.2 %collective-permute-start.26 = (f32[128,256]{1,0:T(8,128)S(1)}, f32[128,256]{1,0:T(8,128)S(1)}, u32[]{:S(2)}, u32[]{:S(2)}) collective-permute-start(f32[128,256]{1,0:T(8,128)S(1)} %get-tuple-element.100), channel_id=1, source_target_pairs={{0,4},{1,5},{2,6},{3,7},{4,0},{5,1},{6,2},{7,3},{8,12},{9,13},{10,... | collective-permute-start | bytes 393224 | tf_op jit(solution)/shard_map/ppermute | solution.py:390
  110.6 11.9 %collective-permute-start.25 = (f32[128,256]{1,0:T(8,128)S(1)}, f32[128,256]{1,0:T(8,128)S(1)}, u32[]{:S(2)}, u32[]{:S(2)}) collective-permute-start(f32[128,256]{1,0:T(8,128)S(1)} %get-tuple-element.99), channel_id=1, source_target_pairs={{0,2},{1,3},{2,4},{3,5},{4,6},{5,7},{6,0},{7,1},{8,10},{9,11},{10,... | collective-permute-start | bytes 393224 | tf_op jit(solution)/shard_map/ppermute | solution.py:390
  (13 other events, 38.3 us)

commit v3 on v2

v3 whole, which is shorter than its diff:
```python
import functools

import jax
import jax.numpy as jnp
from jax import lax
from jax.experimental import pallas as pl
from jax.experimental.pallas import tpu as pltpu
from jax.sharding import PartitionSpec as P

HEADS = 32
HEAD_DIM = 64
STATE = 128
SPAN = 128
PARTS = 3
F32 = jnp.float32
BF16 = jnp.bfloat16
VMEM_LIMIT = 16 * 1024 * 1024


def group_size(n_seq):
    q = 1
    while n_seq % (2 * q) == 0 and 4 * q * q <= n_seq:
        q *= 2
    return q


def nn(a, b):
    return lax.dot_general(a, b, (((1,), (0,)), ((), ())), preferred_element_type=F32)


def nt(a, b):
    return lax.dot_general(a, b, (((1,), (1,)), ((), ())), preferred_element_type=F32)


def tn(a, b):
    return lax.dot_general(a, b, (((0,), (0,)), ((), ())), preferred_element_type=F32)


def terms(a):
    high = a.astype(BF16)
    rest = a - high.astype(F32)
    mid = rest.astype(BF16)
    return high, mid, (rest - mid.astype(F32)).astype(BF16)


def head_chunks(heads):
    pairs, found, first = heads // 2, [], 0
    for c in range(PARTS):
        count = 2 * ((pairs + PARTS - 1 - c) // PARTS)
        found.append((first, count))
        first += count
    return found


def call(body, outs, n_in, scratch=(), name=None, smem=0, hbm=0):
    specs = [pl.BlockSpec(memory_space=pltpu.SMEM)] * smem
    specs += [pl.BlockSpec(memory_space=pltpu.HBM)] * hbm
    specs += [pl.BlockSpec(memory_space=pltpu.VMEM)] * n_in
    return pl.pallas_call(
        body,
        out_shape=outs,
        in_specs=specs,
        out_specs=jax.tree.map(lambda _: pl.BlockSpec(memory_space=pltpu.VMEM), outs),
        scratch_shapes=scratch,
        compiler_params=pltpu.CompilerParams(vmem_limit_bytes=VMEM_LIMIT),
        name=name,
    )


def in_group(q):
    return lax.rem(lax.axis_index("seq"), q)


def out(shape, dtype=F32):
    return jax.ShapeDtypeStruct(shape, dtype)


def iotas():
    rows = lax.broadcasted_iota(jnp.int32, (SPAN, SPAN), 0)
    cols = lax.broadcasted_iota(jnp.int32, (SPAN, SPAN), 1)
    return rows, cols


def columns(ref, start, width):
    return ref[:, pl.ds(pl.multiple_of(start, 128), width)]


def pack_body(q, group, first, width, x, g, own, *refs):
    packed, (stage, sems) = refs[: q - 1], refs[q - 1 :]
    y = in_group(q)
    copies = {}
    for r in list(range(1, q)) + [0]:
        at = pl.multiple_of(lax.rem(y + r, q) * group + first, 128)
        for k, source in enumerate((x, g)):
            target = stage.at[r - 1, k] if r else own.at[k]
            copy = pltpu.make_async_copy(source.at[:, pl.ds(at, width)], target, sems.at[r, k])
            copy.start()
            copies[r, k] = copy
    for r in range(1, q):
        for k in range(2):
            copies[r, k].wait()
            packed[r - 1][k] = stage[r - 1, k].astype(F32)
    for k in range(2):
        copies[0, k].wait()


def project_body(q, tokens, weight, decay, step, *bundles):
    proj = nn(tokens[...], weight[...]).astype(BF16).astype(F32)
    heads = HEADS // q
    y = in_group(q)
    for r in range(q):
        at = pl.multiple_of(lax.rem(y + r, q) * heads, heads)
        bundles[r][:SPAN, :] = proj
        bundles[r][SPAN:, :SPAN] = decay[pl.ds(at, heads), :]
        bundles[r][SPAN:, SPAN:] = step[pl.ds(at, heads), :]


def decays_body(q, heads, *refs):
    bundles = refs[:q]
    bcs, cums, a_cols, f1s, f2s, ds, steps = refs[q:]
    width = heads * HEAD_DIM
    y = in_group(q)
    for r in range(q):
        at = lax.rem(y - r + q, q)
        bcs[at] = bundles[r][:SPAN, :].astype(BF16)
        cums[at] = bundles[r][SPAN:, :SPAN]
        steps[at] = bundles[r][SPAN:, SPAN:]
    rows, cols = iotas()
    tri = jnp.where(rows <= cols, 1.0, 0.0).astype(BF16)
    head_of = lax.broadcasted_iota(jnp.int32, (heads, width), 1) // HEAD_DIM
    spread = head_of == lax.broadcasted_iota(jnp.int32, (heads, width), 0)
    spread = jnp.where(spread, 1.0, 0.0).astype(BF16)
    for b in range(q):
        cum = sum(nn(term, tri) for term in terms(cums[b]))
        a = cum - jnp.log(steps[b])
        cums[b] = cum
        cum_c, a_c = cum.T, a.T
        a_cols[b] = a_c
        cum_x = sum(nn(term, spread) for term in terms(cum_c))
        a_x = sum(nn(term, spread) for term in terms(a_c))
        total = cum_x[SPAN - 1 : SPAN, :]
        f1s[b] = jnp.exp(total - a_x)
        f2s[b] = jnp.exp(cum_x)
        ds[b] = jnp.exp(total)


def states_body(q, at, *refs):
    it = iter(refs)
    own = next(it)
    xg_in = [next(it) for _ in range(q - 1)]
    bcs, f1s, f2s, ds, xs, gs, ws, ss, own_s, own_g, total_s, total_g, plane = it
    y = in_group(q)
    xs[y] = own[0]
    gs[y] = own[1]
    for r in range(1, q):
        block = lax.rem(y - r + q, q)
        xs[block] = xg_in[r - 1][0].astype(BF16)
        gs[block] = xg_in[r - 1][1].astype(BF16)
    for b in range(q):
        ws[b] = (xs[b].astype(F32) * f1s[b, :, at]).astype(BF16)
        ss[b] = (gs[b].astype(F32) * f2s[b, :, at]).astype(BF16)
        own_s[b] = tn(bcs[b, :, :STATE], ws[b])
        own_g[b] = tn(bcs[b, :, STATE:], ss[b])
    forward, backward, through = own_s[0], own_g[q - 1], ds[0, :, at]
    for b in range(1, q):
        forward = ds[b, :, at] * forward + own_s[b]
        backward = ds[q - 1 - b, :, at] * backward + own_g[q - 1 - b]
        through = through * ds[b, :, at]
    total_s[...] = forward
    total_g[...] = backward
    plane[...] = through


def local_body(q, first, hc, skip, xs, gs, bcs, cums, a_cols, gx, gp):
    rows, cols = iotas()
    causal = rows <= cols
    low = lax.broadcasted_iota(jnp.int32, (SPAN, 128), 1) < HEAD_DIM
    skip_at = in_group(q) * (HEADS // q) + first
    for b in range(q):
        b_cols, c_cols = bcs[b, :, :STATE], bcs[b, :, STATE:]
        kernel = nt(b_cols, c_cols)
        mixing = jnp.zeros((SPAN, SPAN), F32)
        for pair in range(hc // 2):
            at = slice(pair * 128, pair * 128 + 128)
            x, g = xs[b, :, at], gs[b, :, at]
            parts = []
            for half in range(2):
                h = first + 2 * pair + half
                gap = cums[b, h : h + 1, :] - a_cols[b, :, h : h + 1]
                decay = jnp.exp(jnp.where(causal, gap, -jnp.inf))
                picked = jnp.where(low if half == 0 else ~low, x, jnp.zeros_like(x))
                mixing += decay * nt(picked, g)
                parts.append(nn((decay * kernel).astype(BF16), g))
            gains = jnp.where(low, skip[skip_at + 2 * pair], skip[skip_at + 2 * pair + 1])
            gx[b, :, at] = jnp.where(low, parts[0], parts[1]) + gains * g.astype(F32)
        mixed = mixing.astype(BF16)
        gp[b, :, :STATE] = nn(mixed, c_cols)
        gp[b, :, STATE:] = tn(mixed, b_cols)


def final_body(q, at, more, *refs):
    it = iter(refs)
    start, after, own_s, own_g, ds, ws, ss, f1s, bcs, gx, gp = [next(it) for _ in range(11)]
    before = next(it) if more else None
    gx_out = [next(it) for _ in range(q)]
    gp_out, gx_all = it
    y = in_group(q)
    state = start[...]
    for b in range(q):
        part = gp[b, :, STATE:] + nt(ss[b], state.astype(BF16))
        gp_out[b, :, STATE:] = part if before is None else part + before[b, :, STATE:]
        if b < q - 1:
            state = ds[b, :, at] * state + own_s[b]
    state = after[...]
    for b in range(q - 1, -1, -1):
        rounded = state.astype(BF16)
        gx_all[b] = gx[b] + f1s[b, :, at] * nn(bcs[b, :, :STATE], rounded)
        part = gp[b, :, :STATE] + nt(ws[b], rounded)
        gp_out[b, :, :STATE] = part if before is None else part + before[b, :, :STATE]
        if b > 0:
            state = ds[b, :, at] * state + own_g[b]
    for r in range(q):
        gx_out[r][...] = gx_all[lax.rem(y + r, q)]


def assemble_body(q, group, spans, *refs):
    parts, result = refs[:-1], refs[-1]
    y = in_group(q)
    for r in range(q):
        base = lax.rem(y - r + q, q) * group
        for c, (first, width) in enumerate(spans):
            at = pl.multiple_of(base + first, 128)
            result[:, pl.ds(at, width)] = parts[r * len(spans) + c][...].astype(BF16)


def weight_body(n_dp, q, planes, rows, scale, *refs):
    it = iter(refs)
    tokens = [next(it) for _ in range(n_dp)]
    swapped = [next(it) for _ in range(q - 1)]
    grads = [next(it) for _ in range(n_dp)]
    outs = [next(it) for _ in range(planes)]
    held, factors, products = it
    width = planes * rows
    seq = lax.axis_index("seq")
    y, z = lax.rem(seq, q), lax.div(seq, q)
    for r in range(n_dp):
        held[y, r] = columns(tokens[r], y * width, width).astype(BF16)
        for b in range(q):
            factors[b, r] = grads[r][b].astype(BF16)
    for k in range(1, q):
        at = lax.rem(y - k + q, q)
        for r in range(n_dp):
            held[at, r] = swapped[k - 1][r].astype(BF16)
    total = tn(
        held[...].reshape(q * n_dp * SPAN, width), factors[...].reshape(q * n_dp * SPAN, 2 * STATE)
    )
    products[...] = (total * scale).reshape(planes, rows, 2 * STATE)
    for r in range(planes):
        outs[r][...] = products[lax.rem(z + r, planes)]


def behind(value, *others):
    return lax.optimization_barrier((value,) + others)[0]


def on_device(layer_input, proj_weight, inputs, step_size, log_decay, skip_gain, grad_out):
    n_seq, n_dp = lax.axis_size("seq"), lax.axis_size("dp")
    q = group_size(n_seq)
    planes = n_seq // q
    heads = HEADS // q
    group = heads * HEAD_DIM
    chunks = head_chunks(heads)
    spans = [(first * HEAD_DIM, count * HEAD_DIM) for first, count in chunks]
    tokens, x, g = layer_input[0], inputs[0], grad_out[0]
    length, features = tokens.shape
    y, dp = in_group(q), lax.axis_index("dp")

    def swap(value, r):
        pairs = [(z * q + i, z * q + (i + r) % q) for z in range(planes) for i in range(q)]
        return lax.ppermute(value, "seq", pairs)

    def across(value, r):
        return lax.ppermute(value, "dp", [(i, i ^ r) for i in range(n_dp)])

    def pack(first, width):
        scratch = (pltpu.VMEM((q - 1, 2, SPAN, width), BF16), pltpu.SemaphoreType.DMA((q, 2)))
        outs = (out((2, SPAN, width), BF16),) + (out((2, SPAN, width)),) * (q - 1)
        body = functools.partial(pack_body, q, group, first, width)
        return call(body, outs, 0, scratch, name="pack", hbm=2)(x, g)

    packed = pack(*spans[0])
    own, xg_in = [packed[0]], [[swap(packed[r], r) for r in range(1, q)]]
    bundle_out = (out((SPAN + heads, 2 * STATE)),) * q
    bundles = call(functools.partial(project_body, q), bundle_out, 4, name="project")(
        tokens, proj_weight, log_decay[0], step_size[0]
    )
    bundles = [bundles[0]] + [swap(bundles[r], r) for r in range(1, q)]
    columns_each = features // n_dp
    rows = columns_each // n_seq
    part = planes * rows

    def quarter(owner):
        cut = lax.dynamic_slice_in_dim(tokens, owner * columns_each, columns_each, axis=1)
        order = [(z * q + i) * rows for i in range(q) for z in range(planes)]
        return jnp.concatenate([cut[:, at : at + rows] for at in order], axis=1)

    token_parts = [quarter(dp)] + [None] * (n_dp - 1)
    for r in range(n_dp - 1, 0, -1):
        token_parts[r] = across(quarter(dp ^ r).astype(F32), r)
    for c in range(1, PARTS):
        packed = pack(*spans[c])
        own.append(packed[0])
        got = [behind(packed[r], *xg_in[c - 1]) for r in range(1, q)]
        xg_in.append([swap(got[r - 1], r) for r in range(1, q)])

    rows_of = (q, SPAN, group)
    bcs, cums, a_cols, f1s, f2s, ds = call(
        functools.partial(decays_body, q, heads),
        (
            out((q, SPAN, 2 * STATE), BF16), out((q, heads, SPAN)), out((q, SPAN, heads)),
            out(rows_of), out(rows_of), out((q, 1, group)),
        ),
        q, (pltpu.VMEM((q, heads, SPAN), F32),), name="decays",
    )(*bundles)
    held = []
    for c, (first, width) in enumerate(spans):
        at = slice(first, first + width)
        wide, state = (q, SPAN, width), out((STATE, width))
        outs = (out(wide, BF16),) * 4 + (out(wide),) * 2 + (state, state, out((1, width)))
        args = [own[c]] + xg_in[c] + [bcs, f1s, f2s, ds]
        held.append(call(functools.partial(states_body, q, at), outs, len(args), name="states")(*args))

    swapped = []
    for r in range(1, q):
        at = lax.rem(y + r, q) * part
        ready = behind(tuple(token_parts), held[-1][6])
        cut = [lax.dynamic_slice_in_dim(v, at, part, axis=1).astype(F32) for v in ready]
        swapped.append(swap(jnp.stack(cut), r))

    local = []
    for c, (first, count) in enumerate(chunks):
        wide = (q, SPAN, count * HEAD_DIM)
        local.append(
            call(
                functools.partial(local_body, q, first, count),
                (out(wide), out((q, SPAN, 2 * STATE))), 5, smem=1, name="local",
            )(skip_gain, held[c][0], held[c][1], bcs, cums, a_cols)
        )

    sent = [(h[6], h[7]) for h in held]
    entries = [(jnp.zeros_like(h[6]), jnp.zeros_like(h[7])) for h in held]
    for t in range(planes - 1):
        up = [(t * q + i, (t + 1) * q + i) for i in range(q)]
        top = planes - 1 - t
        down = [(top * q + i, (top - 1) * q + i) for i in range(q)]
        for c in range(PARTS):
            got_s = lax.ppermute(sent[c][0], "seq", up)
            got_g = lax.ppermute(sent[c][1], "seq", down)
            if t == planes - 2:
                got_s, got_g = behind((got_s, got_g), local[c])
            start, after = entries[c][0] + got_s, entries[c][1] + got_g
            entries[c] = start, after
            total_s, total_g, through = held[c][6:9]
            sent[c] = total_s + through * start, total_g + through * after

    before, gx_parts = [], {}
    for c, (first, width) in enumerate(spans):
        _, _, ws, ss, own_s, own_g, _, _, _ = held[c]
        gx, gp = local[c]
        start, after = entries[c]
        at = slice(first, first + width)
        outs = (out((SPAN, width)),) * q + (out((q, SPAN, 2 * STATE)),)
        args = [start, after, own_s, own_g, ds, ws, ss, f1s, bcs, gx, gp] + before
        scratch = (pltpu.VMEM((q, SPAN, width), F32),)
        body = functools.partial(final_body, q, at, bool(before))
        done = call(body, outs, len(args), scratch, name="final")(*args)
        for r in range(q):
            gx_parts[r, c] = done[r]
        before = [done[q]]

    gp = before[0]
    for r in range(1, q):
        gp = gp + swap(before[0], r)
    grads = {0: gp}
    bit = n_dp // 2
    while bit:
        for r in list(grads):
            grads[r ^ bit] = across(grads[r], bit)
        bit //= 2
    scale = 1.0 / (length * n_seq)
    outs = (out((rows, 2 * STATE)),) * planes
    args = token_parts + swapped + [grads[r] for r in range(n_dp)]
    scratch = (
        pltpu.VMEM((q, n_dp, SPAN, part), BF16),
        pltpu.VMEM((q, n_dp, SPAN, 2 * STATE), BF16),
        pltpu.VMEM((planes, rows, 2 * STATE), F32),
    )
    body = functools.partial(weight_body, n_dp, q, planes, rows, scale)
    pieces = call(body, outs, len(args), scratch, name="weight")(*args)
    grad_weight = pieces[0]
    for r in range(1, planes):
        pairs = [(z * q + i, (z + r) % planes * q + i) for z in range(planes) for i in range(q)]
        grad_weight = grad_weight + lax.ppermute(pieces[r], "seq", pairs)

    parts = [gx_parts[0, c] for c in range(PARTS)]
    for r in range(1, q):
        parts += [swap(gx_parts[r, c], r) for c in range(PARTS)]
    grad_x = call(
        functools.partial(assemble_body, q, group, spans),
        out((length, q * group), BF16), len(parts), name="assemble",
    )(*parts)
    return grad_x[None], grad_weight


def solution(mesh):
    return jax.shard_map(
        on_device,
        mesh=mesh,
        in_specs=(
            P("dp", "seq", None),
            P(),
            P("dp", "seq", None),
            P("dp", None, "seq"),
            P("dp", None, "seq"),
            P(),
            P("dp", "seq", None),
        ),
        out_specs=(P("dp", "seq", None), P(("dp", "seq"), None)),
        check_vma=False,
    )
```

time: 124 us -> 151 us (1.22)
  local copies, waits for them, and re-layouts: 5.88 us -> 32.8 us
  waiting for transfers between devices: 55.2 us -> 37.3 us
  starting transfers between devices: 38.1 us -> 50.2 us
  other arithmetic: 4.16 us -> 10.4 us
    unnamed x46 -> x132, local copies, waits for them, and re-layouts: 5.64 us -> 30.3 us
    ppermute x12 -> x18, starting transfers between devices: 12.9 us -> 27.5 us  [the longest x9 18.9 us: on_device(): got_s = lax.ppermute(sent[c][0], 'seq', up)]
    ppermute x6, waiting for transfers between devices: 17.8 us -> 4.92 us  [across(): return lax.ppermute(value, 'dp', [(i, i ^ r) for i in range(n_dp)])]
    add x8 -> x12, other arithmetic: 0.69 us -> 6.08 us  [the longest x6 5.95 us: on_device(): sent[c] = (total_s + through * start, total_g + through * after)]
    ppermute x3, starting transfers between devices: 11.3 us -> 6.6 us  [on_device(): grad_weight = grad_weight + lax.ppermute(pieces[r], 'seq', pairs)]
    ppermute x12 -> x18, waiting for transfers between devices: 14 us -> 9.48 us  [the longest x9 8.06 us: on_device(): got_g = lax.ppermute(sent[c][1], 'seq', down)]
    ppermute x7 -> x9, starting transfers between devices: 10.3 us -> 12.6 us  [swap(): return lax.ppermute(value, 'seq', pairs)]
    pallas_call x10 -> x15, Pallas kernels: 17.7 us -> 17.1 us  [the longest x3 5.35 us: on_device(): call(functools.partial(states_body, q, at), outs, len(args), name='states')]
  transfers between devices with their start and end apart: 28 -> 36, of which waited for: 10 -> 10; matrix products, arithmetic and copies ran while one was open for 3% -> 12% of each run, Pallas kernels for 14% -> 11%
where the time goes in v3:
time: 151 us; the launch traced here: 150 us
  starting transfers between devices  50.2 us (33%)
  waiting for transfers between devices  37.3 us (25%)
  local copies, waits for them, and re-layouts  32.8 us (22%)
  Pallas kernels  17.6 us (12%)
  other arithmetic  10.4 us (7%)
  between operations  1.55 us (1%)
    unnamed x132, local copies, waits for them, and re-layouts  30.3 us
    ppermute x9, starting transfers between devices, on_device(): got_s = lax.ppermute(sent[c][0], 'seq', up)  18.9 us
    ppermute x9, waiting for transfers between devices, swap(): return lax.ppermute(value, 'seq', pairs)  15.2 us
    ppermute x9, starting transfers between devices, swap(): return lax.ppermute(value, 'seq', pairs)  12.6 us
    ppermute x9, starting transfers between devices, on_device(): got_g = lax.ppermute(sent[c][1], 'seq', down)  8.67 us
    ppermute x9, waiting for transfers between devices, on_device(): got_g = lax.ppermute(sent[c][1], 'seq', down)  8.06 us
    ppermute x3, waiting for transfers between devices, on_device(): grad_weight = grad_weight + lax.ppermute(pieces[r], 'seq', pairs)  7.7 us
    ppermute x3, starting transfers between devices, on_device(): grad_weight = grad_weight + lax.ppermute(pieces[r], 'seq', pairs)  6.6 us
  transfers between devices with their start and end apart: 36, of which 10 were waited for; matrix products, arithmetic and copies ran while one was open for 12% of the time, Pallas kernels for 11%

profile of v3, /device:TPU:0, one launch (start us, length us, event | category | flops | bytes accessed | tf_op | source)
XLA Modules:
  0.0 149.9 jit_solution(12013421985564801380)
XLA Ops:
  4.3 3.0 %collective-permute-start = (f32[2,128,384]{2,1,0:T(8,128)}, f32[2,128,384]{2,1,0:T(8,128)}, u32[]{:S(2)}, u32[]{:S(2)}) collective-permute-start(f32[2,128,384]{2,1,0:T(8,128)} %get-tuple-element.75), channel_id=1, source_target_pairs={{0,1},{1,0},{2,3},{3,2},{4,5},{5,4},{6,7},{7,6},{8,9},{9,8},{10,11... | collective-permute-start | bytes 1179656 | tf_op jit(solution)/shard_map/ppermute | solution.py:280
  8.5 1.6 %copy-done.6 = bf16[4096,256]{1,0:T(8,128)(2,1)S(1)} copy-done((bf16[4096,256]{1,0:T(8,128)(2,1)S(1)}, bf16[4096,256]{1,0:T(8,128)(2,1)}, u32[]{:S(2)}) %copy-start.6) | copy-done | bytes 2097176
  14.8 2.0 %collective-permute-start.26 = (f32[128,1024]{1,0:T(8,128)}, f32[128,1024]{1,0:T(8,128)S(1)}, u32[]{:S(2)}, u32[]{:S(2)}) collective-permute-start(f32[128,1024]{1,0:T(8,128)} %convert_element_type.11), channel_id=1, source_target_pairs={{0,16},{8,24},{16,0},{24,8},{1,17},{9,25},{17,1},{25,9},{2,18},{10... | collective-permute-start | bytes 1572872 | tf_op jit(solution)/shard_map/ppermute | solution.py:283
  29.5 2.1 %states.3 = (bf16[2,128,384]{2,1,0:T(8,128)(2,1)S(1)}, bf16[2,128,384]{2,1,0:T(8,128)(2,1)S(1)}, bf16[2,128,384]{2,1,0:T(8,128)(2,1)S(1)}, bf16[2,128,384]{2,1,0...) custom-call(bf16[2,128,384]{2,1,0:T(8,128)(2,1)S(1)} %copy-done.34, ...), custom_call_target="tpu_custom_call" | custom-call | tf_op jit(solution)/shard_map/states/pallas_call | solution.py:331
  37.1 4.2 %collective-permute-start.2 = (f32[128,384]{1,0:T(8,128)}, f32[128,384]{1,0:T(8,128)}, u32[]{:S(2)}, u32[]{:S(2)}) collective-permute-start(f32[128,384]{1,0:T(8,128)} %get-tuple-element.82), channel_id=1, source_target_pairs={{0,2},{1,3},{8,10},{9,11},{16,18},{17,19},{24,26},{25,27}} | collective-permute-start | bytes 589832 | tf_op jit(solution)/shard_map/ppermute | solution.py:357
  48.1 4.5 %collective-permute-done.8.refs_1_ = f32[2,128,384]{2,1,0:T(8,128)} collective-permute-done((f32[2,128,384]{2,1,0:T(8,128)}, f32[2,128,384]{2,1,0:T(8,128)}, u32[]{:S(2)}, u32[]{:S(2)}) %collective-permute-start.8) | collective-permute-done | bytes 393248 | tf_op jit(solution)/shard_map/ppermute | solution.py:280
  53.5 2.0 %states.4 = (bf16[2,128,384]{2,1,0:T(8,128)(2,1)S(1)}, bf16[2,128,384]{2,1,0:T(8,128)(2,1)S(1)}, bf16[2,128,384]{2,1,0:T(8,128)(2,1)S(1)}, bf16[2,128,384]{2,1,0...) custom-call(bf16[2,128,384]{2,1,0:T(8,128)(2,1)S(1)} %copy-done.36, ...), custom_call_target="tpu_custom_call" | custom-call | tf_op jit(solution)/shard_map/states/pallas_call | solution.py:331
  62.4 5.1 %collective-permute-start.9 = (f32[128,384]{1,0:T(8,128)}, f32[128,384]{1,0:T(8,128)}, u32[]{:S(2)}, u32[]{:S(2)}) collective-permute-start(f32[128,384]{1,0:T(8,128)} %get-tuple-element.101), channel_id=1, source_target_pairs={{0,2},{1,3},{8,10},{9,11},{16,18},{17,19},{24,26},{25,27}} | collective-permute-start | bytes 589832 | tf_op jit(solution)/shard_map/ppermute | solution.py:357
  68.2 1.5 %collective-permute-start.15 = (f32[2,128,256]{2,1,0:T(8,128)}, f32[2,128,256]{2,1,0:T(8,128)}, u32[]{:S(2)}, u32[]{:S(2)}) collective-permute-start(f32[2,128,256]{2,1,0:T(8,128)} %get-tuple-element.118), channel_id=1, source_target_pairs={{0,1},{1,0},{2,3},{3,2},{4,5},{5,4},{6,7},{7,6},{8,9},{9,8},{10,11... | collective-permute-start | bytes 786440 | tf_op jit(solution)/shard_map/ppermute | solution.py:280
  69.8 2.2 %multiply_add_fusion.4 = (f32[128,384]{1,0:T(8,128)}, f32[128,384]{1,0:T(8,128)}, f32[128,384]{1,0:T(8,128)}, f32[128,384]{1,0:T(8,128)}) fusion(f32[128,384]{1,0:T(8,128)} %get-tuple-element.84, f32[384]{0:T(512)S(1)} %reduce, f32[128,384]{1,0:T(8,128)} %collective-permute-done.5, f32[128,384]{1,0:T(8,128)S(1)} %collective-permute-done.6, ...), kind=kLoop, calls=%fused_computation.12 | loop fusion | flops 294912 | bytes 1967616 | tf_op jit(solution)/shard_map/add | solution.py:364
  74.1 3.1 %collective-permute-done.15.refs_1_ = f32[2,128,256]{2,1,0:T(8,128)} collective-permute-done((f32[2,128,256]{2,1,0:T(8,128)}, f32[2,128,256]{2,1,0:T(8,128)}, u32[]{:S(2)}, u32[]{:S(2)}) %collective-permute-start.15) | collective-permute-done | bytes 262176 | tf_op jit(solution)/shard_map/ppermute | solution.py:280
  81.9 5.2 %collective-permute-start.16 = (f32[128,256]{1,0:T(8,128)S(1)}, f32[128,256]{1,0:T(8,128)S(1)}, u32[]{:S(2)}, u32[]{:S(2)}) collective-permute-start(f32[128,256]{1,0:T(8,128)S(1)} %get-tuple-element.119), channel_id=1, source_target_pairs={{0,2},{1,3},{8,10},{9,11},{16,18},{17,19},{24,26},{25,27}} | collective-permute-start | bytes 393224 | tf_op jit(solution)/shard_map/ppermute | solution.py:357
  90.1 1.6 %collective-permute-start.28 = (f32[4,128,512]{2,1,0:T(8,128)S(1)}, f32[4,128,512]{2,1,0:T(8,128)S(1)}, u32[]{:S(2)}, u32[]{:S(2)}) collective-permute-start(f32[4,128,512]{2,1,0:T(8,128)S(1)} %pad_maximum_fusion), channel_id=1, source_target_pairs={{0,1},{1,0},{2,3},{3,2},{4,5},{5,4},{6,7},{7,6},{8,9},{9,8},{10,11... | collective-permute-start | bytes 3145736 | tf_op jit(solution)/shard_map/ppermute | solution.py:280
  98.8 1.6 %local.3 = (f32[2,128,384]{2,1,0:T(8,128)S(1)}, f32[2,128,256]{2,1,0:T(8,128)S(1)}) custom-call(f32[32]{0:T(128)S(1)} %copy-done.45, bf16[2,128,384]{2,1,0:T(8,128)(2,1)S(1)} %copy-done.22, bf16[2,128,384]{2,1,0:T(8,128)(2,1)S(1)} %copy-done.24, bf16[2,128,256]{2,1,0:T(8,128)(2,1)S(1)} %get-tuple-element.78.refs_2_.bcs.refs_8_, ...), custom_call_target="tpu_custom_call" | custom-call | tf_op jit(solution)/shard_map/local/pallas_call | solution.py:344
  100.4 1.6 %local.4 = (f32[2,128,384]{2,1,0:T(8,128)S(1)}, f32[2,128,256]{2,1,0:T(8,128)S(1)}) custom-call(f32[32]{0:T(128)S(1)} %copy-done.45, bf16[2,128,384]{2,1,0:T(8,128)(2,1)S(1)} %copy-done.26, bf16[2,128,384]{2,1,0:T(8,128)(2,1)S(1)} %copy-done.28, bf16[2,128,256]{2,1,0:T(8,128)(2,1)S(1)} %get-tuple-element.78.refs_2_.bcs.refs_8_, ...), custom_call_target="tpu_custom_call" | custom-call | tf_op jit(solution)/shard_map/local/pallas_call | solution.py:344
  104.0 7.2 %collective-permute-done.14 = f32[128,384]{1,0:T(8,128)S(1)} collective-permute-done((f32[128,384]{1,0:T(8,128)S(1)}, f32[128,384]{1,0:T(8,128)S(1)}, u32[]{:S(2)}, u32[]{:S(2)}) %collective-permute-start.14) | collective-permute-done | bytes 196640 | tf_op jit(solution)/shard_map/ppermute | solution.py:358
  114.4 5.4 %collective-permute-done.29 = f32[2,128,256]{2,1,0:T(8,128)S(1)} collective-permute-done((f32[2,128,256]{2,1,0:T(8,128)S(1)}, f32[2,128,256]{2,1,0:T(8,128)S(1)}, u32[]{:S(2)}, u32[]{:S(2)}) %collective-permute-start.29) | collective-permute-done | bytes 262176 | tf_op jit(solution)/shard_map/ppermute | solution.py:280
  119.9 1.5 %collective-permute-start.31 = (f32[2,128,256]{2,1,0:T(8,128)S(1)}, f32[2,128,256]{2,1,0:T(8,128)S(1)}, u32[]{:S(2)}, u32[]{:S(2)}) collective-permute-start(f32[2,128,256]{2,1,0:T(8,128)S(1)} %add.135.refs_5_), channel_id=1, source_target_pairs={{0,16},{8,24},{16,0},{24,8},{1,17},{9,25},{17,1},{25,9},{2,18},{10... | collective-permute-start | bytes 786440 | tf_op jit(solution)/shard_map/ppermute | solution.py:283
  121.4 4.9 %collective-permute-done.31.refs_7_ = f32[2,128,256]{2,1,0:T(8,128)S(1)} collective-permute-done((f32[2,128,256]{2,1,0:T(8,128)S(1)}, f32[2,128,256]{2,1,0:T(8,128)S(1)}, u32[]{:S(2)}, u32[]{:S(2)}) %collective-permute-start.31) | collective-permute-done | bytes 262176 | tf_op jit(solution)/shard_map/ppermute | solution.py:283
  129.9 1.9 %weight.3 = (f32[128,256]{1,0:T(8,128)S(1)}, f32[128,256]{1,0:T(8,128)S(1)}, f32[128,256]{1,0:T(8,128)S(1)}, f32[128,256]{1,0:T(8,128)S(1)}) custom-call(bf16[128,1024]{1,0:T(8,128)(2,1)} %constant_dynamic-update-slice_fusion.refs_0_, f32[128,1024]{1,0:T(8,128)S(1)} %collective-permute-done.25.refs_1_, f32[128,1024]{1,0:T(8,128)S(1)} %collective-permute-done.26.refs_2_, ...), custom_call_target="tpu_custom_call" | custom-call | tf_op jit(solution)/shard_map/weight/pallas_call | solution.py:399
  131.8 3.3 %collective-permute-start.35 = (f32[128,256]{1,0:T(8,128)S(1)}, f32[128,256]{1,0:T(8,128)S(1)}, u32[]{:S(2)}, u32[]{:S(2)}) collective-permute-start(f32[128,256]{1,0:T(8,128)S(1)} %get-tuple-element.145), channel_id=1, source_target_pairs={{0,6},{1,7},{2,0},{3,1},{4,2},{5,3},{6,4},{7,5},{8,14},{9,15},{10,... | collective-permute-start | bytes 393224 | tf_op jit(solution)/shard_map/ppermute | solution.py:403
  135.1 2.6 %collective-permute-start.34 = (f32[128,256]{1,0:T(8,128)S(1)}, f32[128,256]{1,0:T(8,128)S(1)}, u32[]{:S(2)}, u32[]{:S(2)}) collective-permute-start(f32[128,256]{1,0:T(8,128)S(1)} %get-tuple-element.144), channel_id=1, source_target_pairs={{0,4},{1,5},{2,6},{3,7},{4,0},{5,1},{6,2},{7,3},{8,12},{9,13},{10,... | collective-permute-start | bytes 393224 | tf_op jit(solution)/shard_map/ppermute | solution.py:403
  138.4 2.2 %collective-permute-done.24.refs_5_ = f32[128,256]{1,0:T(8,128)S(1)} collective-permute-done((f32[128,256]{1,0:T(8,128)S(1)}, f32[128,256]{1,0:T(8,128)S(1)}, u32[]{:S(2)}, u32[]{:S(2)}) %collective-permute-start.24) | collective-permute-done | bytes 131104 | tf_op jit(solution)/shard_map/ppermute | solution.py:280
  141.5 7.7 %collective-permute-done.34 = f32[128,256]{1,0:T(8,128)S(1)} collective-permute-done((f32[128,256]{1,0:T(8,128)S(1)}, f32[128,256]{1,0:T(8,128)S(1)}, u32[]{:S(2)}, u32[]{:S(2)}) %collective-permute-start.34) | collective-permute-done | bytes 131104 | tf_op jit(solution)/shard_map/ppermute | solution.py:403
  (224 shorter events, 70.4 us)
Async XLA Ops:
  4.3 24.3 %collective-permute-start = (f32[2,128,384]{2,1,0:T(8,128)}, f32[2,128,384]{2,1,0:T(8,128)}, u32[]{:S(2)}, u32[]{:S(2)}) collective-permute-start(f32[2,128,384]{2,1,0:T(8,128)} %get-tuple-element.75), channel_id=1, source_target_pairs={{0,1},{1,0},{2,3},{3,2},{4,5},{5,4},{6,7},{7,6},{8,9},{9,8},{10,11... | collective-permute-start | bytes 1179656 | tf_op jit(solution)/shard_map/ppermute | solution.py:280
  12.6 12.0 %collective-permute-start.1 = (f32[144,256]{1,0:T(8,128)S(1)}, f32[144,256]{1,0:T(8,128)S(1)}, u32[]{:S(2)}, u32[]{:S(2)}) collective-permute-start(f32[144,256]{1,0:T(8,128)S(1)} %get-tuple-element.77), channel_id=1, source_target_pairs={{0,1},{1,0},{2,3},{3,2},{4,5},{5,4},{6,7},{7,6},{8,9},{9,8},{10,11... | collective-permute-start | bytes 442376 | tf_op jit(solution)/shard_map/ppermute | solution.py:280
  13.8 66.8 %collective-permute-start.25 = (f32[128,1024]{1,0:T(8,128)}, f32[128,1024]{1,0:T(8,128)S(1)}, u32[]{:S(2)}, u32[]{:S(2)}) collective-permute-start(f32[128,1024]{1,0:T(8,128)} %convert_element_type.10), channel_id=1, source_target_pairs={{0,8},{8,0},{16,24},{24,16},{1,9},{9,1},{17,25},{25,17},{2,10},{10... | collective-permute-start | bytes 1572872 | tf_op jit(solution)/shard_map/ppermute | solution.py:283
  14.8 66.4 %collective-permute-start.26 = (f32[128,1024]{1,0:T(8,128)}, f32[128,1024]{1,0:T(8,128)S(1)}, u32[]{:S(2)}, u32[]{:S(2)}) collective-permute-start(f32[128,1024]{1,0:T(8,128)} %convert_element_type.11), channel_id=1, source_target_pairs={{0,16},{8,24},{16,0},{24,8},{1,17},{9,25},{17,1},{25,9},{2,18},{10... | collective-permute-start | bytes 1572872 | tf_op jit(solution)/shard_map/ppermute | solution.py:283
  41.3 11.3 %collective-permute-start.8 = (f32[2,128,384]{2,1,0:T(8,128)}, f32[2,128,384]{2,1,0:T(8,128)}, u32[]{:S(2)}, u32[]{:S(2)}) collective-permute-start(f32[2,128,384]{2,1,0:T(8,128)} %copy-done.46), channel_id=1, source_target_pairs={{0,1},{1,0},{2,3},{3,2},{4,5},{5,4},{6,7},{7,6},{8,9},{9,8},{10,11... | collective-permute-start | bytes 1179656 | tf_op jit(solution)/shard_map/ppermute | solution.py:280
  46.7 15.7 %collective-permute-start.6 = (f32[128,384]{1,0:T(8,128)S(1)}, f32[128,384]{1,0:T(8,128)S(1)}, u32[]{:S(2)}, u32[]{:S(2)}) collective-permute-start(f32[128,384]{1,0:T(8,128)S(1)} %get-tuple-element.168), channel_id=1, source_target_pairs={{4,2},{5,3},{12,10},{13,11},{20,18},{21,19},{28,26},{29,27}} | collective-permute-start | bytes 589832 | tf_op jit(solution)/shard_map/ppermute | solution.py:358
  47.4 15.0 %collective-permute-start.3 = (f32[128,384]{1,0:T(8,128)S(1)}, f32[128,384]{1,0:T(8,128)S(1)}, u32[]{:S(2)}, u32[]{:S(2)}) collective-permute-start(f32[128,384]{1,0:T(8,128)S(1)} %get-tuple-element.169), channel_id=1, source_target_pairs={{2,4},{3,5},{10,12},{11,13},{18,20},{19,21},{26,28},{27,29}} | collective-permute-start | bytes 589832 | tf_op jit(solution)/shard_map/ppermute | solution.py:357
  62.4 19.5 %collective-permute-start.27 = (f32[128,1024]{1,0:T(8,128)}, f32[128,1024]{1,0:T(8,128)}, u32[]{:S(2)}, u32[]{:S(2)}) collective-permute-start(f32[128,1024]{1,0:T(8,128)} %convert_element_type.12), channel_id=1, source_target_pairs={{0,24},{8,16},{16,8},{24,0},{1,25},{9,17},{17,9},{25,1},{2,26},{10... | collective-permute-start | bytes 1572872 | tf_op jit(solution)/shard_map/ppermute | solution.py:283
  62.4 9.7 %collective-permute-start.9 = (f32[128,384]{1,0:T(8,128)}, f32[128,384]{1,0:T(8,128)}, u32[]{:S(2)}, u32[]{:S(2)}) collective-permute-start(f32[128,384]{1,0:T(8,128)} %get-tuple-element.101), channel_id=1, source_target_pairs={{0,2},{1,3},{8,10},{9,11},{16,18},{17,19},{24,26},{25,27}} | collective-permute-start | bytes 589832 | tf_op jit(solution)/shard_map/ppermute | solution.py:357
  68.2 8.9 %collective-permute-start.15 = (f32[2,128,256]{2,1,0:T(8,128)}, f32[2,128,256]{2,1,0:T(8,128)}, u32[]{:S(2)}, u32[]{:S(2)}) collective-permute-start(f32[2,128,256]{2,1,0:T(8,128)} %get-tuple-element.118), channel_id=1, source_target_pairs={{0,1},{1,0},{2,3},{3,2},{4,5},{5,4},{6,7},{7,6},{8,9},{9,8},{10,11... | collective-permute-start | bytes 786440 | tf_op jit(solution)/shard_map/ppermute | solution.py:280
  72.1 24.7 %collective-permute-start.4 = (f32[128,384]{1,0:T(8,128)}, f32[128,384]{1,0:T(8,128)S(1)}, u32[]{:S(2)}, u32[]{:S(2)}) collective-permute-start(f32[128,384]{1,0:T(8,128)} %get-tuple-element.166), channel_id=1, source_target_pairs={{4,6},{5,7},{12,14},{13,15},{20,22},{21,23},{28,30},{29,31}} | collective-permute-start | bytes 589832 | tf_op jit(solution)/shard_map/ppermute | solution.py:357
  77.1 20.4 %collective-permute-start.7 = (f32[128,384]{1,0:T(8,128)}, f32[128,384]{1,0:T(8,128)S(1)}, u32[]{:S(2)}, u32[]{:S(2)}) collective-permute-start(f32[128,384]{1,0:T(8,128)} %get-tuple-element.154), channel_id=1, source_target_pairs={{2,0},{3,1},{10,8},{11,9},{18,16},{19,17},{26,24},{27,25}} | collective-permute-start | bytes 589832 | tf_op jit(solution)/shard_map/ppermute | solution.py:358
  80.5 11.2 %collective-permute-start.13 = (f32[128,384]{1,0:T(8,128)S(1)}, f32[128,384]{1,0:T(8,128)S(1)}, u32[]{:S(2)}, u32[]{:S(2)}) collective-permute-start(f32[128,384]{1,0:T(8,128)S(1)} %get-tuple-element.164), channel_id=1, source_target_pairs={{4,2},{5,3},{12,10},{13,11},{20,18},{21,19},{28,26},{29,27}} | collective-permute-start | bytes 589832 | tf_op jit(solution)/shard_map/ppermute | solution.py:358
  90.1 39.8 %collective-permute-start.28 = (f32[4,128,512]{2,1,0:T(8,128)S(1)}, f32[4,128,512]{2,1,0:T(8,128)S(1)}, u32[]{:S(2)}, u32[]{:S(2)}) collective-permute-start(f32[4,128,512]{2,1,0:T(8,128)S(1)} %pad_maximum_fusion), channel_id=1, source_target_pairs={{0,1},{1,0},{2,3},{3,2},{4,5},{5,4},{6,7},{7,6},{8,9},{9,8},{10,11... | collective-permute-start | bytes 3145736 | tf_op jit(solution)/shard_map/ppermute | solution.py:280
  94.6 9.4 %collective-permute-start.11 = (f32[128,384]{1,0:T(8,128)S(1)}, f32[128,384]{1,0:T(8,128)S(1)}, u32[]{:S(2)}, u32[]{:S(2)}) collective-permute-start(f32[128,384]{1,0:T(8,128)S(1)} %get-tuple-element.162), channel_id=1, source_target_pairs={{4,6},{5,7},{12,14},{13,15},{20,22},{21,23},{28,30},{29,31}} | collective-permute-start | bytes 589832 | tf_op jit(solution)/shard_map/ppermute | solution.py:357
  95.4 15.7 %collective-permute-start.14 = (f32[128,384]{1,0:T(8,128)S(1)}, f32[128,384]{1,0:T(8,128)S(1)}, u32[]{:S(2)}, u32[]{:S(2)}) collective-permute-start(f32[128,384]{1,0:T(8,128)S(1)} %get-tuple-element.150), channel_id=1, source_target_pairs={{2,0},{3,1},{10,8},{11,9},{18,16},{19,17},{26,24},{27,25}} | collective-permute-start | bytes 589832 | tf_op jit(solution)/shard_map/ppermute | solution.py:358
  96.8 14.9 %collective-permute-start.18 = (f32[128,256]{1,0:T(8,128)S(1)}, f32[128,256]{1,0:T(8,128)S(1)}, u32[]{:S(2)}, u32[]{:S(2)}) collective-permute-start(f32[128,256]{1,0:T(8,128)S(1)} %get-tuple-element.170), channel_id=1, source_target_pairs={{4,6},{5,7},{12,14},{13,15},{20,22},{21,23},{28,30},{29,31}} | collective-permute-start | bytes 393224 | tf_op jit(solution)/shard_map/ppermute | solution.py:357
  97.5 15.1 %collective-permute-start.21 = (f32[128,256]{1,0:T(8,128)S(1)}, f32[128,256]{1,0:T(8,128)S(1)}, u32[]{:S(2)}, u32[]{:S(2)}) collective-permute-start(f32[128,256]{1,0:T(8,128)S(1)} %get-tuple-element.146), channel_id=1, source_target_pairs={{2,0},{3,1},{10,8},{11,9},{18,16},{19,17},{26,24},{27,25}} | collective-permute-start | bytes 393224 | tf_op jit(solution)/shard_map/ppermute | solution.py:358
  126.3 11.4 %collective-permute-start.22 = (f32[128,384]{1,0:T(8,128)S(1)}, f32[128,384]{1,0:T(8,128)S(1)}, u32[]{:S(2)}, u32[]{:S(2)}) collective-permute-start(f32[128,384]{1,0:T(8,128)S(1)} %get-tuple-element.134), channel_id=1, source_target_pairs={{0,1},{1,0},{2,3},{3,2},{4,5},{5,4},{6,7},{7,6},{8,9},{9,8},{10,11... | collective-permute-start | bytes 589832 | tf_op jit(solution)/shard_map/ppermute | solution.py:280
  127.8 12.8 %collective-permute-start.23 = (f32[128,384]{1,0:T(8,128)S(1)}, f32[128,384]{1,0:T(8,128)S(1)}, u32[]{:S(2)}, u32[]{:S(2)}) collective-permute-start(f32[128,384]{1,0:T(8,128)S(1)} %get-tuple-element.135), channel_id=1, source_target_pairs={{0,1},{1,0},{2,3},{3,2},{4,5},{5,4},{6,7},{7,6},{8,9},{9,8},{10,11... | collective-permute-start | bytes 589832 | tf_op jit(solution)/shard_map/ppermute | solution.py:280
  128.3 12.3 %collective-permute-start.24 = (f32[128,256]{1,0:T(8,128)S(1)}, f32[128,256]{1,0:T(8,128)S(1)}, u32[]{:S(2)}, u32[]{:S(2)}) collective-permute-start(f32[128,256]{1,0:T(8,128)S(1)} %get-tuple-element.136), channel_id=1, source_target_pairs={{0,1},{1,0},{2,3},{3,2},{4,5},{5,4},{6,7},{7,6},{8,9},{9,8},{10,11... | collective-permute-start | bytes 393224 | tf_op jit(solution)/shard_map/ppermute | solution.py:280
  131.8 9.7 %collective-permute-start.35 = (f32[128,256]{1,0:T(8,128)S(1)}, f32[128,256]{1,0:T(8,128)S(1)}, u32[]{:S(2)}, u32[]{:S(2)}) collective-permute-start(f32[128,256]{1,0:T(8,128)S(1)} %get-tuple-element.145), channel_id=1, source_target_pairs={{0,6},{1,7},{2,0},{3,1},{4,2},{5,3},{6,4},{7,5},{8,14},{9,15},{10,... | collective-permute-start | bytes 393224 | tf_op jit(solution)/shard_map/ppermute | solution.py:403
  135.1 14.1 %collective-permute-start.34 = (f32[128,256]{1,0:T(8,128)S(1)}, f32[128,256]{1,0:T(8,128)S(1)}, u32[]{:S(2)}, u32[]{:S(2)}) collective-permute-start(f32[128,256]{1,0:T(8,128)S(1)} %get-tuple-element.144), channel_id=1, source_target_pairs={{0,4},{1,5},{2,6},{3,7},{4,0},{5,1},{6,2},{7,3},{8,12},{9,13},{10,... | collective-permute-start | bytes 393224 | tf_op jit(solution)/shard_map/ppermute | solution.py:403
  137.8 11.5 %collective-permute-start.33 = (f32[128,256]{1,0:T(8,128)S(1)}, f32[128,256]{1,0:T(8,128)S(1)}, u32[]{:S(2)}, u32[]{:S(2)}) collective-permute-start(f32[128,256]{1,0:T(8,128)S(1)} %get-tuple-element.143), channel_id=1, source_target_pairs={{0,2},{1,3},{2,4},{3,5},{4,6},{5,7},{6,0},{7,1},{8,10},{9,11},{10,... | collective-permute-start | bytes 393224 | tf_op jit(solution)/shard_map/ppermute | solution.py:403
  (64 other events, 268.8 us)

commit v4 on v3

--- a/solution.py
+++ b/solution.py
@@ -52,19 +52,38 @@
     return found
 
 
-def call(body, outs, n_in, scratch=(), name=None, smem=0, hbm=0):
-    specs = [pl.BlockSpec(memory_space=pltpu.SMEM)] * smem
-    specs += [pl.BlockSpec(memory_space=pltpu.HBM)] * hbm
-    specs += [pl.BlockSpec(memory_space=pltpu.VMEM)] * n_in
-    return pl.pallas_call(
-        body,
-        out_shape=outs,
-        in_specs=specs,
-        out_specs=jax.tree.map(lambda _: pl.BlockSpec(memory_space=pltpu.VMEM), outs),
-        scratch_shapes=scratch,
-        compiler_params=pltpu.CompilerParams(vmem_limit_bytes=VMEM_LIMIT),
-        name=name,
-    )
+def whole(shape):
+    return pl.BlockSpec(shape, lambda i, rank=len(shape): (0,) * rank)
+
+
+def call(body, outs, scratch=(), name=None, smem=0, hbm=0):
+    def run(*args):
+        args = list(args)
+        for k in range(smem, len(args)):
+            if isinstance(args[k], list):
+                args[k] = args[k][0]
+            else:
+                args[k] = pltpu.with_memory_space_constraint(args[k], pltpu.HBM)
+        specs = [pl.BlockSpec(memory_space=pltpu.SMEM)] * smem
+        specs += [pl.BlockSpec(memory_space=pltpu.HBM)] * hbm
+        specs += [whole(a.shape) for a in args[smem + hbm :]]
+        shapes = [o[0] if isinstance(o, list) else pltpu.HBM(o.shape, o.dtype) for o in outs]
+        return pl.pallas_call(
+            body,
+            out_shape=tuple(shapes),
+            grid=(1,),
+            in_specs=specs,
+            out_specs=tuple(whole(o.shape) for o in shapes),
+            scratch_shapes=scratch,
+            compiler_params=pltpu.CompilerParams(vmem_limit_bytes=VMEM_LIMIT),
+            name=name,
+        )(*args)
+
+    return run
+
+
+def loose(values):
+    return [[value] for value in values]
 
 
 def in_group(q):
@@ -102,6 +121,25 @@
             packed[r - 1][k] = stage[r - 1, k].astype(F32)
     for k in range(2):
         copies[0, k].wait()
+
+
+def deal_body(rows, q, planes, tokens, *outs):
+    n_dp = len(outs)
+    each = q * planes * rows
+    dp = lax.axis_index("dp")
+    for r in range(n_dp - 1, -1, -1):
+        cut = columns(tokens, lax.bitwise_xor(dp, r) * each, each).astype(F32)
+        for k in range(q * planes):
+            at = (k % planes * q + k // planes) * rows
+            outs[r][:, k * rows : (k + 1) * rows] = cut[:, at : at + rows]
+
+
+def hand_body(q, part, *refs):
+    tokens, outs = refs[: 1 - q], refs[1 - q :]
+    y = in_group(q)
+    for r in range(1, q):
+        for k, ref in enumerate(tokens):
+            outs[r - 1][k] = columns(ref, lax.rem(y + r, q) * part, part)
 
 
 def project_body(q, tokens, weight, decay, step, *bundles):
@@ -284,14 +322,14 @@
 
     def pack(first, width):
         scratch = (pltpu.VMEM((q - 1, 2, SPAN, width), BF16), pltpu.SemaphoreType.DMA((q, 2)))
-        outs = (out((2, SPAN, width), BF16),) + (out((2, SPAN, width)),) * (q - 1)
+        outs = [out((2, SPAN, width), BF16)] + loose([out((2, SPAN, width))] * (q - 1))
         body = functools.partial(pack_body, q, group, first, width)
-        return call(body, outs, 0, scratch, name="pack", hbm=2)(x, g)
+        return call(body, outs, scratch, name="pack", hbm=2)(x, g)
 
     packed = pack(*spans[0])
     own, xg_in = [packed[0]], [[swap(packed[r], r) for r in range(1, q)]]
-    bundle_out = (out((SPAN + heads, 2 * STATE)),) * q
-    bundles = call(functools.partial(project_body, q), bundle_out, 4, name="project")(
+    bundle_out = loose([out((SPAN + heads, 2 * STATE))] * q)
+    bundles = call(functools.partial(project_body, q), bundle_out, name="project")(
         tokens, proj_weight, log_decay[0], step_size[0]
     )
     bundles = [bundles[0]] + [swap(bundles[r], r) for r in range(1, q)]
@@ -299,18 +337,16 @@
     rows = columns_each // n_seq
     part = planes * rows
 
-    def quarter(owner):
-        cut = lax.dynamic_slice_in_dim(tokens, owner * columns_each, columns_each, axis=1)
-        order = [(z * q + i) * rows for i in range(q) for z in range(planes)]
-        return jnp.concatenate([cut[:, at : at + rows] for at in order], axis=1)
-
-    token_parts = [quarter(dp)] + [None] * (n_dp - 1)
+    shapes = [out((length, columns_each))] + loose([out((length, columns_each))] * (n_dp - 1))
+    token_parts = list(call(functools.partial(deal_body, rows, q, planes), shapes, name="deal")(tokens))
+    dealt = tuple(token_parts[1:])
     for r in range(n_dp - 1, 0, -1):
-        token_parts[r] = across(quarter(dp ^ r).astype(F32), r)
+        token_parts[r] = across(token_parts[r], r)
     for c in range(1, PARTS):
         packed = pack(*spans[c])
         own.append(packed[0])
-        got = [behind(packed[r], *xg_in[c - 1]) for r in range(1, q)]
+        ahead = dealt if c == 1 else xg_in[c - 2]
+        got = [behind(packed[r], *ahead) for r in range(1, q)]
         xg_in.append([swap(got[r - 1], r) for r in range(1, q)])
 
     rows_of = (q, SPAN, group)
@@ -320,22 +356,21 @@
             out((q, SPAN, 2 * STATE), BF16), out((q, heads, SPAN)), out((q, SPAN, heads)),
             out(rows_of), out(rows_of), out((q, 1, group)),
         ),
-        q, (pltpu.VMEM((q, heads, SPAN), F32),), name="decays",
-    )(*bundles)
+        (pltpu.VMEM((q, heads, SPAN), F32),), name="decays",
+    )(*loose(bundles))
     held = []
     for c, (first, width) in enumerate(spans):
         at = slice(first, first + width)
         wide, state = (q, SPAN, width), out((STATE, width))
-        outs = (out(wide, BF16),) * 4 + (out(wide),) * 2 + (state, state, out((1, width)))
-        args = [own[c]] + xg_in[c] + [bcs, f1s, f2s, ds]
-        held.append(call(functools.partial(states_body, q, at), outs, len(args), name="states")(*args))
-
-    swapped = []
-    for r in range(1, q):
-        at = lax.rem(y + r, q) * part
-        ready = behind(tuple(token_parts), held[-1][6])
-        cut = [lax.dynamic_slice_in_dim(v, at, part, axis=1).astype(F32) for v in ready]
-        swapped.append(swap(jnp.stack(cut), r))
+        outs = [out(wide, BF16)] * 4 + [out(wide)] * 2 + loose([state, state, out((1, width))])
+        args = [own[c]] + loose(xg_in[c]) + [bcs, f1s, f2s, ds]
+        held.append(call(functools.partial(states_body, q, at), outs, name="states")(*args))
+
+    ready = behind(tuple(token_parts), held[-1][6])
+    handed = call(
+        functools.partial(hand_body, q, part), loose([out((n_dp, length, part))] * (q - 1)), name="hand"
+    )(ready[0], *loose(ready[1:]))
+    swapped = [swap(handed[r - 1], r) for r in range(1, q)]
 
     local = []
     for c, (first, count) in enumerate(chunks):
@@ -343,7 +378,7 @@
         local.append(
             call(
                 functools.partial(local_body, q, first, count),
-                (out(wide), out((q, SPAN, 2 * STATE))), 5, smem=1, name="local",
+                (out(wide), out((q, SPAN, 2 * STATE))), smem=1, name="local",
             )(skip_gain, held[c][0], held[c][1], bcs, cums, a_cols)
         )
 
@@ -369,11 +404,11 @@
         gx, gp = local[c]
         start, after = entries[c]
         at = slice(first, first + width)
-        outs = (out((SPAN, width)),) * q + (out((q, SPAN, 2 * STATE)),)
-        args = [start, after, own_s, own_g, ds, ws, ss, f1s, bcs, gx, gp] + before
+        outs = [out((SPAN, width))] + loose([out((SPAN, width))] * (q - 1) + [out((q, SPAN, 2 * STATE))])
+        args = [[start], [after], own_s, own_g, ds, ws, ss, f1s, bcs, gx, gp] + loose(before)
         scratch = (pltpu.VMEM((q, SPAN, width), F32),)
         body = functools.partial(final_body, q, at, bool(before))
-        done = call(body, outs, len(args), scratch, name="final")(*args)
+        done = call(body, outs, scratch, name="final")(*args)
         for r in range(q):
             gx_parts[r, c] = done[r]
         before = [done[q]]
@@ -388,15 +423,15 @@
             grads[r ^ bit] = across(grads[r], bit)
         bit //= 2
     scale = 1.0 / (length * n_seq)
-    outs = (out((rows, 2 * STATE)),) * planes
-    args = token_parts + swapped + [grads[r] for r in range(n_dp)]
+    outs = loose([out((rows, 2 * STATE))] * planes)
+    args = token_parts[:1] + loose(token_parts[1:] + swapped + [grads[r] for r in range(n_dp)])
     scratch = (
         pltpu.VMEM((q, n_dp, SPAN, part), BF16),
         pltpu.VMEM((q, n_dp, SPAN, 2 * STATE), BF16),
         pltpu.VMEM((planes, rows, 2 * STATE), F32),
     )
     body = functools.partial(weight_body, n_dp, q, planes, rows, scale)
-    pieces = call(body, outs, len(args), scratch, name="weight")(*args)
+    pieces = call(body, outs, scratch, name="weight")(*args)
     grad_weight = pieces[0]
     for r in range(1, planes):
         pairs = [(z * q + i, (z + r) % planes * q + i) for z in range(planes) for i in range(q)]
@@ -404,10 +439,9 @@
 
     parts = [gx_parts[0, c] for c in range(PARTS)]
     for r in range(1, q):
-        parts += [swap(gx_parts[r, c], r) for c in range(PARTS)]
-    grad_x = call(
-        functools.partial(assemble_body, q, group, spans),
-        out((length, q * group), BF16), len(parts), name="assemble",
+        parts += loose([swap(gx_parts[r, c], r) for c in range(PARTS)])
+    (grad_x,) = call(
+        functools.partial(assemble_body, q, group, spans), [[out((length, q * group), BF16)]], name="assemble"
     )(*parts)
     return grad_x[None], grad_weight
 

time: 151 us -> 142 us (0.940)
  local copies, waits for them, and re-layouts: 32.8 us -> 0.01 us
  Pallas kernels: 17.6 us -> 43.2 us
  other arithmetic: 10.4 us -> 5.04 us
  waiting for transfers between devices: 37.3 us -> 42.1 us
    unnamed x132 -> x6, local copies, waits for them, and re-layouts: 30.3 us -> 0.01 us
    pallas_call x16 -> x18, Pallas kernels: 17.6 us -> 43.2 us  [run(): pl.pallas_call(body, out_shape=tuple(shapes), grid=(1,), in_specs=specs,...]
    ppermute x6, waiting for transfers between devices: 4.92 us -> 12.3 us  [across(): return lax.ppermute(value, 'dp', [(i, i ^ r) for i in range(n_dp)])]
    ppermute x9, waiting for transfers between devices: 8.06 us -> 1.11 us  [on_device(): got_g = lax.ppermute(sent[c][1], 'seq', down)]
    ppermute x3, starting transfers between devices: 6.6 us -> 10.2 us  [on_device(): grad_weight = grad_weight + lax.ppermute(pieces[r], 'seq', pairs)]
    ppermute x9, starting transfers between devices: 18.9 us -> 15.3 us  [on_device(): got_s = lax.ppermute(sent[c][0], 'seq', up)]
    convert_element_type x3 -> x0, other arithmetic: 2.54 us -> none  [on_device(): token_parts[r] = across(quarter(dp ^ r).astype(F32), r)]
    ppermute x9, waiting for transfers between devices: 15.2 us -> 17.4 us  [swap(): return lax.ppermute(value, 'seq', pairs)]
  transfers between devices with their start and end apart: 36 -> 36, of which waited for: 10 -> 8; matrix products, arithmetic and copies ran while one was open for 12% -> 3% of each run, Pallas kernels for 11% -> 29%
where the time goes in v4:
time: 142 us; the launch traced here: 141 us
  starting transfers between devices  49.9 us (35%)
  Pallas kernels  43.2 us (30%)
  waiting for transfers between devices  42.1 us (30%)
  other arithmetic  5.04 us (4%)
    pallas_call x18, Pallas kernels, run(): pl.pallas_call(body, out_shape=tuple(shapes), grid=(1,), in_specs=specs,...  43.2 us
    ppermute x9, waiting for transfers between devices, swap(): return lax.ppermute(value, 'seq', pairs)  17.4 us
    ppermute x9, starting transfers between devices, on_device(): got_s = lax.ppermute(sent[c][0], 'seq', up)  15.3 us
    ppermute x6, waiting for transfers between devices, across(): return lax.ppermute(value, 'dp', [(i, i ^ r) for i in range(n_dp)])  12.3 us
    ppermute x9, starting transfers between devices, swap(): return lax.ppermute(value, 'seq', pairs)  12.3 us
    ppermute x3, starting transfers between devices, on_device(): grad_weight = grad_weight + lax.ppermute(pieces[r], 'seq', pairs)  10.2 us
    ppermute x9, starting transfers between devices, on_device(): got_g = lax.ppermute(sent[c][1], 'seq', down)  8.66 us
    ppermute x3, waiting for transfers between devices, on_device(): grad_weight = grad_weight + lax.ppermute(pieces[r], 'seq', pairs)  7.77 us
  transfers between devices with their start and end apart: 36, of which 8 were waited for; matrix products, arithmetic and copies ran while one was open for 3% of the time, Pallas kernels for 29%

profile of v4, /device:TPU:0, one launch (start us, length us, event | category | flops | bytes accessed | tf_op | source)
XLA Modules:
  0.0 141.3 jit_solution(15839433467931373283)
XLA Ops:
  2.4 3.0 %collective-permute-start = (f32[2,128,384]{2,1,0:T(8,128)S(1)}, f32[2,128,384]{2,1,0:T(8,128)S(1)}, u32[]{:S(2)}, u32[]{:S(2)}) collective-permute-start(f32[2,128,384]{2,1,0:T(8,128)S(1)} %get-tuple-element.79), channel_id=1, source_target_pairs={{0,1},{1,0},{2,3},{3,2},{4,5},{5,4},{6,7},{7,6},{8,9},{9,8},{10,11... | collective-permute-start | bytes 1179656 | tf_op jit(solution)/shard_map/ppermute | solution.py:318
  7.2 2.4 %deal.1 = (f32[128,1024]{1,0:T(8,128)}, f32[128,1024]{1,0:T(8,128)}, f32[128,1024]{1,0:T(8,128)}, f32[128,1024]{1,0:T(8,128)S(1)}) custom-call(bf16[128,4096]{1,0:T(8,128)(2,1)} %bitcast.15), custom_call_target="tpu_custom_call" | custom-call | tf_op jit(solution)/shard_map/deal/pallas_call | solution.py:71
  9.7 2.3 %project.1 = (f32[144,256]{1,0:T(8,128)S(1)}, f32[144,256]{1,0:T(8,128)S(1)}) custom-call(bf16[128,4096]{1,0:T(8,128)(2,1)} %bitcast.16, bf16[4096,256]{1,0:T(8,128)(2,1)} %weight.2, f32[32,128]{1,0:T(8,128)} %bitcast.18, f32[32,128]{1,0:T(8,128)} %bitcast.19), custom_call_target="tpu_custom_call" | custom-call | tf_op jit(solution)/shard_map/project/pallas_call | solution.py:71
  12.0 2.1 %collective-permute-start.1 = (f32[144,256]{1,0:T(8,128)S(1)}, f32[144,256]{1,0:T(8,128)S(1)}, u32[]{:S(2)}, u32[]{:S(2)}) collective-permute-start(f32[144,256]{1,0:T(8,128)S(1)} %get-tuple-element.81), channel_id=1, source_target_pairs={{0,1},{1,0},{2,3},{3,2},{4,5},{5,4},{6,7},{7,6},{8,9},{9,8},{10,11... | collective-permute-start | bytes 442376 | tf_op jit(solution)/shard_map/ppermute | solution.py:318
  14.0 12.1 %collective-permute-done.1.refs_1_ = f32[144,256]{1,0:T(8,128)S(1)} collective-permute-done((f32[144,256]{1,0:T(8,128)S(1)}, f32[144,256]{1,0:T(8,128)S(1)}, u32[]{:S(2)}, u32[]{:S(2)}) %collective-permute-start.1) | collective-permute-done | bytes 147488 | tf_op jit(solution)/shard_map/ppermute | solution.py:318
  26.1 2.8 %decays.1 = (bf16[2,128,256]{2,1,0:T(8,128)(2,1)}, f32[2,16,128]{2,1,0:T(8,128)}, f32[2,128,16]{2,1,0:T(8,128)}, f32[2,128,1024]{2,1,0:T(8,128)}, f32[2,128,1024]{2,1,0:T(8,128)}, /*index=5*/f32[2,1,1024]{2,1,0:T(1,128)}) custom-call(f32[144,256]{1,0:T(8,128)S(1)} %get-tuple-element.80.refs_0_, f32[144,256]{1,0:T(8,128)S(1)} %collective-permute-done.1.refs_1_), custom_call_target="tpu_custom_call" | custom-call | tf_op jit(solution)/shard_map/decays/pallas_call | solution.py:71
  28.9 3.0 %states.3 = (bf16[2,128,384]{2,1,0:T(8,128)(2,1)}, bf16[2,128,384]{2,1,0:T(8,128)(2,1)}, bf16[2,128,384]{2,1,0:T(8,128)(2,1)}, bf16[2,128,384]{2,1,0:T(8,128)(2,...) custom-call(bf16[2,128,384]{2,1,0:T(8,128)(2,1)} %get-tuple-element., ...), custom_call_target="tpu_custom_call" | custom-call | tf_op jit(solution)/shard_map/states/pallas_call | solution.py:71
  32.6 4.4 %collective-permute-start.2 = (f32[128,384]{1,0:T(8,128)S(1)}, f32[128,384]{1,0:T(8,128)}, u32[]{:S(2)}, u32[]{:S(2)}) collective-permute-start(f32[128,384]{1,0:T(8,128)S(1)} %get-tuple-element.86), channel_id=1, source_target_pairs={{0,2},{1,3},{8,10},{9,11},{16,18},{17,19},{24,26},{25,27}} | collective-permute-start | bytes 589832 | tf_op jit(solution)/shard_map/ppermute | solution.py:392
  37.0 3.0 %states.4 = (bf16[2,128,384]{2,1,0:T(8,128)(2,1)}, bf16[2,128,384]{2,1,0:T(8,128)(2,1)}, bf16[2,128,384]{2,1,0:T(8,128)(2,1)}, bf16[2,128,384]{2,1,0:T(8,128)(2,...) custom-call(bf16[2,128,384]{2,1,0:T(8,128)(2,1)} %get-tuple-element., ...), custom_call_target="tpu_custom_call" | custom-call | tf_op jit(solution)/shard_map/states/pallas_call | solution.py:71
  48.8 3.5 %collective-permute-done.9 = f32[128,384]{1,0:T(8,128)S(1)} collective-permute-done((f32[128,384]{1,0:T(8,128)S(1)}, f32[128,384]{1,0:T(8,128)S(1)}, u32[]{:S(2)}, u32[]{:S(2)}) %collective-permute-start.9) | collective-permute-done | bytes 196640 | tf_op jit(solution)/shard_map/ppermute | solution.py:392
  55.0 2.7 %states.5 = (bf16[2,128,256]{2,1,0:T(8,128)(2,1)}, bf16[2,128,256]{2,1,0:T(8,128)(2,1)}, bf16[2,128,256]{2,1,0:T(8,128)(2,1)}, bf16[2,128,256]{2,1,0:T(8,128)(2,...) custom-call(bf16[2,128,256]{2,1,0:T(8,128)(2,1)} %get-tuple-element., ...), custom_call_target="tpu_custom_call" | custom-call | tf_op jit(solution)/shard_map/states/pallas_call | solution.py:71
  59.2 7.4 %collective-permute-done.27.refs_3_ = f32[128,1024]{1,0:T(8,128)S(1)} collective-permute-done((f32[128,1024]{1,0:T(8,128)S(1)}, f32[128,1024]{1,0:T(8,128)S(1)}, u32[]{:S(2)}, u32[]{:S(2)}) %collective-permute-start.27) | collective-permute-done | bytes 524320 | tf_op jit(solution)/shard_map/ppermute | solution.py:321
  66.7 5.6 %collective-permute-start.16 = (f32[128,256]{1,0:T(8,128)S(1)}, f32[128,256]{1,0:T(8,128)S(1)}, u32[]{:S(2)}, u32[]{:S(2)}) collective-permute-start(f32[128,256]{1,0:T(8,128)S(1)} %get-tuple-element.126), channel_id=1, source_target_pairs={{0,2},{1,3},{8,10},{9,11},{16,18},{17,19},{24,26},{25,27}} | collective-permute-start | bytes 393224 | tf_op jit(solution)/shard_map/ppermute | solution.py:392
  85.3 2.9 %local.3 = (f32[2,128,384]{2,1,0:T(8,128)}, f32[2,128,256]{2,1,0:T(8,128)}) custom-call(f32[32]{0:T(128)S(1)} %copy-done, bf16[2,128,384]{2,1,0:T(8,128)(2,1)} %get-tuple-element.89.xs, bf16[2,128,384]{2,1,0:T(8,128)(2,1)} %get-tuple-element.90.gs, bf16[2,128,256]{2,1,0:T(8,128)(2,1)} %get-tuple-element.82.refs_2_.bcs.refs_8_, ...), custom_call_target="tpu_custom_call" | custom-call | tf_op jit(solution)/shard_map/local/pallas_call | solution.py:71
  88.2 2.9 %local.4 = (f32[2,128,384]{2,1,0:T(8,128)}, f32[2,128,256]{2,1,0:T(8,128)}) custom-call(f32[32]{0:T(128)S(1)} %copy-done, bf16[2,128,384]{2,1,0:T(8,128)(2,1)} %get-tuple-element.111.xs, bf16[2,128,384]{2,1,0:T(8,128)(2,1)} %get-tuple-element.112.gs, bf16[2,128,256]{2,1,0:T(8,128)(2,1)} %get-tuple-element.82.refs_2_.bcs.refs_8_, ...), custom_call_target="tpu_custom_call" | custom-call | tf_op jit(solution)/shard_map/local/pallas_call | solution.py:71
  91.1 2.7 %local.5 = (f32[2,128,256]{2,1,0:T(8,128)}, f32[2,128,256]{2,1,0:T(8,128)}) custom-call(f32[32]{0:T(128)S(1)} %copy-done, bf16[2,128,256]{2,1,0:T(8,128)(2,1)} %get-tuple-element.129.xs, bf16[2,128,256]{2,1,0:T(8,128)(2,1)} %get-tuple-element.130.gs, bf16[2,128,256]{2,1,0:T(8,128)(2,1)} %get-tuple-element.82.refs_2_.bcs.refs_8_, ...), custom_call_target="tpu_custom_call" | custom-call | tf_op jit(solution)/shard_map/local/pallas_call | solution.py:71
  93.9 2.9 %final.3 = (f32[128,384]{1,0:T(8,128)}, f32[128,384]{1,0:T(8,128)S(1)}, f32[2,128,256]{2,1,0:T(8,128)S(1)}) custom-call(f32[128,384]{1,0:T(8,128)S(1)} %add.90.refs_0_, f32[128,384]{1,0:T(8,128)S(1)} %add.91.refs_1_, f32[2,128,384]{2,1,0:T(8,128)} %get-tuple-element.97.refs_2_, f32[2,128,384]{2,1,0:T(8,128)} %get-tuple-element.98.refs_3_, ...), custom_call_target="tpu_custom_call" | custom-call | tf_op jit(solution)/shard_map/final/pallas_call | solution.py:71
  96.9 2.9 %final.4 = (f32[128,384]{1,0:T(8,128)}, f32[128,384]{1,0:T(8,128)S(1)}, f32[2,128,256]{2,1,0:T(8,128)S(1)}) custom-call(f32[128,384]{1,0:T(8,128)S(1)} %add.98.refs_0_, f32[128,384]{1,0:T(8,128)S(1)} %add.99.refs_1_, f32[2,128,384]{2,1,0:T(8,128)} %get-tuple-element.117.refs_2_, f32[2,128,384]{2,1,0:T(8,128)} %get-tuple-element.118.refs_3_, ...), custom_call_target="tpu_custom_call" | custom-call | tf_op jit(solution)/shard_map/final/pallas_call | solution.py:71
  99.8 2.6 %final.5 = (f32[128,256]{1,0:T(8,128)}, f32[128,256]{1,0:T(8,128)S(1)}, f32[2,128,256]{2,1,0:T(8,128)S(1)}) custom-call(f32[128,256]{1,0:T(8,128)S(1)} %add.106.refs_0_, f32[128,256]{1,0:T(8,128)S(1)} %add.107.refs_1_, f32[2,128,256]{2,1,0:T(8,128)} %get-tuple-element.135.refs_2_, f32[2,128,256]{2,1,0:T(8,128)} %get-tuple-element.136.refs_3_, ...), custom_call_target="tpu_custom_call" | custom-call | tf_op jit(solution)/shard_map/final/pallas_call | solution.py:71
  104.0 4.9 %collective-permute-done.29 = f32[2,128,256]{2,1,0:T(8,128)S(1)} collective-permute-done((f32[2,128,256]{2,1,0:T(8,128)S(1)}, f32[2,128,256]{2,1,0:T(8,128)S(1)}, u32[]{:S(2)}, u32[]{:S(2)}) %collective-permute-start.29) | collective-permute-done | bytes 262176 | tf_op jit(solution)/shard_map/ppermute | solution.py:318
  110.4 4.9 %collective-permute-done.31.refs_7_ = f32[2,128,256]{2,1,0:T(8,128)S(1)} collective-permute-done((f32[2,128,256]{2,1,0:T(8,128)S(1)}, f32[2,128,256]{2,1,0:T(8,128)S(1)}, u32[]{:S(2)}, u32[]{:S(2)}) %collective-permute-start.31) | collective-permute-done | bytes 262176 | tf_op jit(solution)/shard_map/ppermute | solution.py:321
  121.8 7.3 %collective-permute-start.34 = (f32[128,256]{1,0:T(8,128)S(1)}, f32[128,256]{1,0:T(8,128)S(1)}, u32[]{:S(2)}, u32[]{:S(2)}) collective-permute-start(f32[128,256]{1,0:T(8,128)S(1)} %get-tuple-element.152), channel_id=1, source_target_pairs={{0,4},{1,5},{2,6},{3,7},{4,0},{5,1},{6,2},{7,3},{8,12},{9,13},{10,... | collective-permute-start | bytes 393224 | tf_op jit(solution)/shard_map/ppermute | solution.py:438
  130.9 2.0 %assemble.1 = bf16[128,2048]{1,0:T(8,128)(2,1)} custom-call(f32[128,384]{1,0:T(8,128)} %get-tuple-element.101.refs_0_, f32[128,384]{1,0:T(8,128)} %get-tuple-element.122.refs_1_, f32[128,256]{1,0:T(8,128)} %get-tuple-element.140.refs_2_, f32[128,384]{1,0:T(8,128)S(1)} %collective-permute-done.22.refs_3_, f32[128,384]{1,0:T(8,128)S(1)} %collective-permute-done.23.refs_4_, ...), custom_call_target="tpu_custom_call" | custom-call | tf_op jit(solution)/shard_map/assemble/pallas_call | solution.py:71
  132.9 7.8 %collective-permute-done.34 = f32[128,256]{1,0:T(8,128)S(1)} collective-permute-done((f32[128,256]{1,0:T(8,128)S(1)}, f32[128,256]{1,0:T(8,128)S(1)}, u32[]{:S(2)}, u32[]{:S(2)}) %collective-permute-start.34) | collective-permute-done | bytes 131104 | tf_op jit(solution)/shard_map/ppermute | solution.py:438
  (88 shorter events, 42.3 us)
Async XLA Ops:
  2.4 26.5 %collective-permute-start = (f32[2,128,384]{2,1,0:T(8,128)S(1)}, f32[2,128,384]{2,1,0:T(8,128)S(1)}, u32[]{:S(2)}, u32[]{:S(2)}) collective-permute-start(f32[2,128,384]{2,1,0:T(8,128)S(1)} %get-tuple-element.79), channel_id=1, source_target_pairs={{0,1},{1,0},{2,3},{3,2},{4,5},{5,4},{6,7},{7,6},{8,9},{9,8},{10,11... | collective-permute-start | bytes 1179656 | tf_op jit(solution)/shard_map/ppermute | solution.py:318
  9.6 27.3 %collective-permute-start.8 = (f32[2,128,384]{2,1,0:T(8,128)S(1)}, f32[2,128,384]{2,1,0:T(8,128)S(1)}, u32[]{:S(2)}, u32[]{:S(2)}) collective-permute-start(f32[2,128,384]{2,1,0:T(8,128)S(1)} %get-tuple-element.107), channel_id=1, source_target_pairs={{0,1},{1,0},{2,3},{3,2},{4,5},{5,4},{6,7},{7,6},{8,9},{9,8},{10,11... | collective-permute-start | bytes 1179656 | tf_op jit(solution)/shard_map/ppermute | solution.py:318
  12.0 14.2 %collective-permute-start.1 = (f32[144,256]{1,0:T(8,128)S(1)}, f32[144,256]{1,0:T(8,128)S(1)}, u32[]{:S(2)}, u32[]{:S(2)}) collective-permute-start(f32[144,256]{1,0:T(8,128)S(1)} %get-tuple-element.81), channel_id=1, source_target_pairs={{0,1},{1,0},{2,3},{3,2},{4,5},{5,4},{6,7},{7,6},{8,9},{9,8},{10,11... | collective-permute-start | bytes 442376 | tf_op jit(solution)/shard_map/ppermute | solution.py:318
  31.9 10.9 %collective-permute-start.5 = (f32[128,384]{1,0:T(8,128)S(1)}, f32[128,384]{1,0:T(8,128)S(1)}, u32[]{:S(2)}, u32[]{:S(2)}) collective-permute-start(f32[128,384]{1,0:T(8,128)S(1)} %get-tuple-element.88), channel_id=1, source_target_pairs={{6,4},{7,5},{14,12},{15,13},{22,20},{23,21},{30,28},{31,29}} | collective-permute-start | bytes 589832 | tf_op jit(solution)/shard_map/ppermute | solution.py:393
  32.6 12.2 %collective-permute-start.2 = (f32[128,384]{1,0:T(8,128)S(1)}, f32[128,384]{1,0:T(8,128)}, u32[]{:S(2)}, u32[]{:S(2)}) collective-permute-start(f32[128,384]{1,0:T(8,128)S(1)} %get-tuple-element.86), channel_id=1, source_target_pairs={{0,2},{1,3},{8,10},{9,11},{16,18},{17,19},{24,26},{25,27}} | collective-permute-start | bytes 589832 | tf_op jit(solution)/shard_map/ppermute | solution.py:392
  41.3 16.4 %collective-permute-start.25 = (f32[128,1024]{1,0:T(8,128)}, f32[128,1024]{1,0:T(8,128)S(1)}, u32[]{:S(2)}, u32[]{:S(2)}) collective-permute-start(f32[128,1024]{1,0:T(8,128)} %get-tuple-element.104), channel_id=1, source_target_pairs={{0,8},{8,0},{16,24},{24,16},{1,9},{9,1},{17,25},{25,17},{2,10},{10... | collective-permute-start | bytes 1572872 | tf_op jit(solution)/shard_map/ppermute | solution.py:321
  41.3 17.3 %collective-permute-start.26 = (f32[128,1024]{1,0:T(8,128)}, f32[128,1024]{1,0:T(8,128)S(1)}, u32[]{:S(2)}, u32[]{:S(2)}) collective-permute-start(f32[128,1024]{1,0:T(8,128)} %get-tuple-element.105), channel_id=1, source_target_pairs={{0,16},{8,24},{16,0},{24,8},{1,17},{9,25},{17,1},{25,9},{2,18},{10... | collective-permute-start | bytes 1572872 | tf_op jit(solution)/shard_map/ppermute | solution.py:321
  42.8 23.9 %collective-permute-start.27 = (f32[128,1024]{1,0:T(8,128)S(1)}, f32[128,1024]{1,0:T(8,128)S(1)}, u32[]{:S(2)}, u32[]{:S(2)}) collective-permute-start(f32[128,1024]{1,0:T(8,128)S(1)} %get-tuple-element.106), channel_id=1, source_target_pairs={{0,24},{8,16},{16,8},{24,0},{1,25},{9,17},{17,9},{25,1},{2,26},{10... | collective-permute-start | bytes 1572872 | tf_op jit(solution)/shard_map/ppermute | solution.py:321
  52.3 21.1 %collective-permute-start.6 = (f32[128,384]{1,0:T(8,128)S(1)}, f32[128,384]{1,0:T(8,128)S(1)}, u32[]{:S(2)}, u32[]{:S(2)}) collective-permute-start(f32[128,384]{1,0:T(8,128)S(1)} %get-tuple-element.172), channel_id=1, source_target_pairs={{4,2},{5,3},{12,10},{13,11},{20,18},{21,19},{28,26},{29,27}} | collective-permute-start | bytes 589832 | tf_op jit(solution)/shard_map/ppermute | solution.py:393
  53.4 20.8 %collective-permute-start.3 = (f32[128,384]{1,0:T(8,128)S(1)}, f32[128,384]{1,0:T(8,128)S(1)}, u32[]{:S(2)}, u32[]{:S(2)}) collective-permute-start(f32[128,384]{1,0:T(8,128)S(1)} %get-tuple-element.173), channel_id=1, source_target_pairs={{2,4},{3,5},{10,12},{11,13},{18,20},{19,21},{26,28},{27,29}} | collective-permute-start | bytes 589832 | tf_op jit(solution)/shard_map/ppermute | solution.py:392
  57.7 20.1 %collective-permute-start.13 = (f32[128,384]{1,0:T(8,128)S(1)}, f32[128,384]{1,0:T(8,128)S(1)}, u32[]{:S(2)}, u32[]{:S(2)}) collective-permute-start(f32[128,384]{1,0:T(8,128)S(1)} %get-tuple-element.168), channel_id=1, source_target_pairs={{4,2},{5,3},{12,10},{13,11},{20,18},{21,19},{28,26},{29,27}} | collective-permute-start | bytes 589832 | tf_op jit(solution)/shard_map/ppermute | solution.py:393
  58.6 19.9 %collective-permute-start.10 = (f32[128,384]{1,0:T(8,128)S(1)}, f32[128,384]{1,0:T(8,128)S(1)}, u32[]{:S(2)}, u32[]{:S(2)}) collective-permute-start(f32[128,384]{1,0:T(8,128)S(1)} %get-tuple-element.169), channel_id=1, source_target_pairs={{2,4},{3,5},{10,12},{11,13},{18,20},{19,21},{26,28},{27,29}} | collective-permute-start | bytes 589832 | tf_op jit(solution)/shard_map/ppermute | solution.py:392
  66.7 9.8 %collective-permute-start.16 = (f32[128,256]{1,0:T(8,128)S(1)}, f32[128,256]{1,0:T(8,128)S(1)}, u32[]{:S(2)}, u32[]{:S(2)}) collective-permute-start(f32[128,256]{1,0:T(8,128)S(1)} %get-tuple-element.126), channel_id=1, source_target_pairs={{0,2},{1,3},{8,10},{9,11},{16,18},{17,19},{24,26},{25,27}} | collective-permute-start | bytes 393224 | tf_op jit(solution)/shard_map/ppermute | solution.py:392
  74.1 44.7 %collective-permute-start.28 = (f32[4,128,512]{2,1,0:T(8,128)S(1)}, f32[4,128,512]{2,1,0:T(8,128)S(1)}, u32[]{:S(2)}, u32[]{:S(2)}) collective-permute-start(f32[4,128,512]{2,1,0:T(8,128)S(1)} %hand.1), channel_id=1, source_target_pairs={{0,1},{1,0},{2,3},{3,2},{4,5},{5,4},{6,7},{7,6},{8,9},{9,8},{10,11... | collective-permute-start | bytes 3145736 | tf_op jit(solution)/shard_map/ppermute | solution.py:318
  80.2 13.6 %collective-permute-start.11 = (f32[128,384]{1,0:T(8,128)S(1)}, f32[128,384]{1,0:T(8,128)S(1)}, u32[]{:S(2)}, u32[]{:S(2)}) collective-permute-start(f32[128,384]{1,0:T(8,128)S(1)} %get-tuple-element.166), channel_id=1, source_target_pairs={{4,6},{5,7},{12,14},{13,15},{20,22},{21,23},{28,30},{29,31}} | collective-permute-start | bytes 589832 | tf_op jit(solution)/shard_map/ppermute | solution.py:392
  80.9 12.9 %collective-permute-start.14 = (f32[128,384]{1,0:T(8,128)S(1)}, f32[128,384]{1,0:T(8,128)S(1)}, u32[]{:S(2)}, u32[]{:S(2)}) collective-permute-start(f32[128,384]{1,0:T(8,128)S(1)} %get-tuple-element.158), channel_id=1, source_target_pairs={{2,0},{3,1},{10,8},{11,9},{18,16},{19,17},{26,24},{27,25}} | collective-permute-start | bytes 589832 | tf_op jit(solution)/shard_map/ppermute | solution.py:393
  82.3 17.5 %collective-permute-start.18 = (f32[128,256]{1,0:T(8,128)S(1)}, f32[128,256]{1,0:T(8,128)S(1)}, u32[]{:S(2)}, u32[]{:S(2)}) collective-permute-start(f32[128,256]{1,0:T(8,128)S(1)} %get-tuple-element.174), channel_id=1, source_target_pairs={{4,6},{5,7},{12,14},{13,15},{20,22},{21,23},{28,30},{29,31}} | collective-permute-start | bytes 393224 | tf_op jit(solution)/shard_map/ppermute | solution.py:392
  84.0 15.7 %collective-permute-start.21 = (f32[128,256]{1,0:T(8,128)S(1)}, f32[128,256]{1,0:T(8,128)S(1)}, u32[]{:S(2)}, u32[]{:S(2)}) collective-permute-start(f32[128,256]{1,0:T(8,128)S(1)} %get-tuple-element.154), channel_id=1, source_target_pairs={{2,0},{3,1},{10,8},{11,9},{18,16},{19,17},{26,24},{27,25}} | collective-permute-start | bytes 393224 | tf_op jit(solution)/shard_map/ppermute | solution.py:393
  115.3 13.8 %collective-permute-start.24 = (f32[128,256]{1,0:T(8,128)S(1)}, f32[128,256]{1,0:T(8,128)S(1)}, u32[]{:S(2)}, u32[]{:S(2)}) collective-permute-start(f32[128,256]{1,0:T(8,128)S(1)} %get-tuple-element.143), channel_id=1, source_target_pairs={{0,1},{1,0},{2,3},{3,2},{4,5},{5,4},{6,7},{7,6},{8,9},{9,8},{10,11... | collective-permute-start | bytes 393224 | tf_op jit(solution)/shard_map/ppermute | solution.py:318
  116.8 14.1 %collective-permute-start.22 = (f32[128,384]{1,0:T(8,128)S(1)}, f32[128,384]{1,0:T(8,128)S(1)}, u32[]{:S(2)}, u32[]{:S(2)}) collective-permute-start(f32[128,384]{1,0:T(8,128)S(1)} %get-tuple-element.141), channel_id=1, source_target_pairs={{0,1},{1,0},{2,3},{3,2},{4,5},{5,4},{6,7},{7,6},{8,9},{9,8},{10,11... | collective-permute-start | bytes 589832 | tf_op jit(solution)/shard_map/ppermute | solution.py:318
  117.3 13.6 %collective-permute-start.23 = (f32[128,384]{1,0:T(8,128)S(1)}, f32[128,384]{1,0:T(8,128)S(1)}, u32[]{:S(2)}, u32[]{:S(2)}) collective-permute-start(f32[128,384]{1,0:T(8,128)S(1)} %get-tuple-element.142), channel_id=1, source_target_pairs={{0,1},{1,0},{2,3},{3,2},{4,5},{5,4},{6,7},{7,6},{8,9},{9,8},{10,11... | collective-permute-start | bytes 589832 | tf_op jit(solution)/shard_map/ppermute | solution.py:318
  120.7 12.2 %collective-permute-start.35 = (f32[128,256]{1,0:T(8,128)S(1)}, f32[128,256]{1,0:T(8,128)S(1)}, u32[]{:S(2)}, u32[]{:S(2)}) collective-permute-start(f32[128,256]{1,0:T(8,128)S(1)} %get-tuple-element.153), channel_id=1, source_target_pairs={{0,6},{1,7},{2,0},{3,1},{4,2},{5,3},{6,4},{7,5},{8,14},{9,15},{10,... | collective-permute-start | bytes 393224 | tf_op jit(solution)/shard_map/ppermute | solution.py:438
  121.8 18.8 %collective-permute-start.34 = (f32[128,256]{1,0:T(8,128)S(1)}, f32[128,256]{1,0:T(8,128)S(1)}, u32[]{:S(2)}, u32[]{:S(2)}) collective-permute-start(f32[128,256]{1,0:T(8,128)S(1)} %get-tuple-element.152), channel_id=1, source_target_pairs={{0,4},{1,5},{2,6},{3,7},{4,0},{5,1},{6,2},{7,3},{8,12},{9,13},{10,... | collective-permute-start | bytes 393224 | tf_op jit(solution)/shard_map/ppermute | solution.py:438
  129.1 11.5 %collective-permute-start.33 = (f32[128,256]{1,0:T(8,128)S(1)}, f32[128,256]{1,0:T(8,128)S(1)}, u32[]{:S(2)}, u32[]{:S(2)}) collective-permute-start(f32[128,256]{1,0:T(8,128)S(1)} %get-tuple-element.151), channel_id=1, source_target_pairs={{0,2},{1,3},{2,4},{3,5},{4,6},{5,7},{6,0},{7,1},{8,10},{9,11},{10,... | collective-permute-start | bytes 393224 | tf_op jit(solution)/shard_map/ppermute | solution.py:438
  (15 other events, 95.4 us)

commit v5 on v4

v5 whole, which is shorter than its diff:
```python
import functools

import jax
import jax.numpy as jnp
from jax import lax
from jax.experimental import pallas as pl
from jax.experimental.pallas import tpu as pltpu
from jax.sharding import PartitionSpec as P

HEADS = 32
HEAD_DIM = 64
STATE = 128
SPAN = 128
PARTS = 2
F32 = jnp.float32
BF16 = jnp.bfloat16
VMEM_LIMIT = 16 * 1024 * 1024


def group_size(n_seq):
    q = 1
    while n_seq % (2 * q) == 0 and 4 * q * q <= n_seq:
        q *= 2
    return q


def nn(a, b):
    return lax.dot_general(a, b, (((1,), (0,)), ((), ())), preferred_element_type=F32)


def nt(a, b):
    return lax.dot_general(a, b, (((1,), (1,)), ((), ())), preferred_element_type=F32)


def tn(a, b):
    return lax.dot_general(a, b, (((0,), (0,)), ((), ())), preferred_element_type=F32)


def terms(a):
    high = a.astype(BF16)
    rest = a - high.astype(F32)
    mid = rest.astype(BF16)
    return high, mid, (rest - mid.astype(F32)).astype(BF16)


def head_chunks(heads):
    first = 2 * (heads * 5 // 16)
    return [(0, first), (first, heads - first)]


def call(body, outs, scratch=(), name=None, smem=0):
    def run(*args):
        specs = [pl.BlockSpec(memory_space=pltpu.SMEM)] * smem
        specs += [pl.BlockSpec(memory_space=pltpu.VMEM)] * (len(args) - smem)
        return pl.pallas_call(
            body,
            out_shape=tuple(outs),
            in_specs=specs,
            out_specs=tuple(pl.BlockSpec(memory_space=pltpu.VMEM) for _ in outs),
            scratch_shapes=scratch,
            compiler_params=pltpu.CompilerParams(vmem_limit_bytes=VMEM_LIMIT),
            name=name,
        )(*args)

    return run


def whole(shape):
    return pl.BlockSpec(shape, lambda i, rank=len(shape): (0,) * rank)


def staged(body, outs, scratch=(), name=None, smem=0, hbm=0):
    def run(*args):
        args = list(args)
        for k in range(smem, len(args)):
            if isinstance(args[k], list):
                args[k] = args[k][0]
            else:
                args[k] = pltpu.with_memory_space_constraint(args[k], pltpu.HBM)
        specs = [pl.BlockSpec(memory_space=pltpu.SMEM)] * smem
        specs += [pl.BlockSpec(memory_space=pltpu.HBM)] * hbm
        specs += [whole(a.shape) for a in args[smem + hbm :]]
        shapes = [o[0] if isinstance(o, list) else pltpu.HBM(o.shape, o.dtype) for o in outs]
        return pl.pallas_call(
            body,
            out_shape=tuple(shapes),
            grid=(1,),
            in_specs=specs,
            out_specs=tuple(whole(o.shape) for o in shapes),
            scratch_shapes=scratch,
            compiler_params=pltpu.CompilerParams(vmem_limit_bytes=VMEM_LIMIT),
            name=name,
        )(*args)

    return run


def loose(values):
    return [[value] for value in values]


def in_group(q):
    return lax.rem(lax.axis_index("seq"), q)


def out(shape, dtype=F32):
    return jax.ShapeDtypeStruct(shape, dtype)


def iotas():
    rows = lax.broadcasted_iota(jnp.int32, (SPAN, SPAN), 0)
    cols = lax.broadcasted_iota(jnp.int32, (SPAN, SPAN), 1)
    return rows, cols


def columns(ref, start, width):
    return ref[:, pl.ds(pl.multiple_of(start, 128), width)]


def pack_body(q, group, first, width, x, g, *refs):
    packed, (stage, sems) = refs[: q - 1], refs[q - 1 :]
    y = in_group(q)
    copies = {}
    for r in range(1, q):
        at = pl.multiple_of(lax.rem(y + r, q) * group + first, 128)
        for k, source in enumerate((x, g)):
            copies[r, k] = pltpu.make_async_copy(
                source.at[:, pl.ds(at, width)], stage.at[r - 1, k], sems.at[r - 1, k]
            )
            copies[r, k].start()
    for r in range(1, q):
        for k in range(2):
            copies[r, k].wait()
            packed[r - 1][k] = stage[r - 1, k].astype(F32)


def deal_body(rows, q, planes, tokens, *outs):
    n_dp = len(outs)
    each = q * planes * rows
    dp = lax.axis_index("dp")
    for r in range(n_dp - 1, -1, -1):
        cut = columns(tokens, lax.bitwise_xor(dp, r) * each, each).astype(F32)
        for k in range(q * planes):
            at = (k % planes * q + k // planes) * rows
            outs[r][:, k * rows : (k + 1) * rows] = cut[:, at : at + rows]


def hand_body(q, part, *refs):
    tokens, outs = refs[: 1 - q], refs[1 - q :]
    y = in_group(q)
    for r in range(1, q):
        for k, ref in enumerate(tokens):
            outs[r - 1][k] = columns(ref, lax.rem(y + r, q) * part, part)


def project_body(q, tokens, weight, decay, step, *bundles):
    proj = nn(tokens[...], weight[...]).astype(BF16).astype(F32)
    heads = HEADS // q
    y = in_group(q)
    for r in range(q):
        at = pl.multiple_of(lax.rem(y + r, q) * heads, heads)
        bundles[r][:SPAN, :] = proj
        bundles[r][SPAN:, :SPAN] = decay[pl.ds(at, heads), :]
        bundles[r][SPAN:, SPAN:] = step[pl.ds(at, heads), :]


def states_body(q, first, hc, *refs):
    it = iter(refs)
    x_ref, g_ref = next(it), next(it)
    xg_in = [next(it) for _ in range(q - 1)]
    bundles = [next(it) for _ in range(q)]
    rows16, states, f1s, ds, total_s, total_g, plane, bcs, cums, a_cols, steps = it
    width = hc * HEAD_DIM
    y = in_group(q)
    at = pl.multiple_of(y * (HEADS // q * HEAD_DIM) + first * HEAD_DIM, 128)
    for k, ref in enumerate((x_ref, g_ref)):
        rows16[k, y] = ref[:, pl.ds(at, width)]
    low = SPAN + first
    for r in range(q):
        block = lax.rem(y - r + q, q)
        if r > 0:
            for k in range(2):
                rows16[k, block] = xg_in[r - 1][k].astype(BF16)
        bcs[block] = bundles[r][:SPAN, :].astype(BF16)
        cums[block] = bundles[r][low : low + hc, :SPAN]
        steps[block] = bundles[r][low : low + hc, SPAN:]
    rows, cols = iotas()
    tri = jnp.where(rows <= cols, 1.0, 0.0).astype(BF16)
    head_of = lax.broadcasted_iota(jnp.int32, (hc, width), 1) // HEAD_DIM
    spread = head_of == lax.broadcasted_iota(jnp.int32, (hc, width), 0)
    spread = jnp.where(spread, 1.0, 0.0).astype(BF16)
    for b in range(q):
        cum = sum(nn(term, tri) for term in terms(cums[b]))
        a = cum - jnp.log(steps[b])
        cums[b] = cum
        cum_c, a_c = cum.T, a.T
        a_cols[b] = a_c
        cum_x = sum(nn(term, spread) for term in terms(cum_c))
        a_x = sum(nn(term, spread) for term in terms(a_c))
        total = cum_x[SPAN - 1 : SPAN, :]
        f1 = jnp.exp(total - a_x)
        f1s[b] = f1
        ds[b] = jnp.exp(total)
        weighted = (rows16[0, b].astype(F32) * f1).astype(BF16)
        scaled = (rows16[1, b].astype(F32) * jnp.exp(cum_x)).astype(BF16)
        rows16[2, b] = weighted
        rows16[3, b] = scaled
        states[0, b] = tn(bcs[b, :, :STATE], weighted)
        states[1, b] = tn(bcs[b, :, STATE:], scaled)
    forward, backward, through = states[0, 0], states[1, q - 1], ds[0]
    for b in range(1, q):
        forward = ds[b] * forward + states[0, b]
        backward = ds[q - 1 - b] * backward + states[1, q - 1 - b]
        through = through * ds[b]
    total_s[...] = forward
    total_g[...] = backward
    plane[...] = through


def local_body(q, first, hc, skip, rows16, bcs, cums, a_cols, gx, gp):
    rows, cols = iotas()
    causal = rows <= cols
    low = lax.broadcasted_iota(jnp.int32, (SPAN, 128), 1) < HEAD_DIM
    skip_at = in_group(q) * (HEADS // q) + first
    for b in range(q):
        b_cols, c_cols = bcs[b, :, :STATE], bcs[b, :, STATE:]
        kernel = nt(b_cols, c_cols)
        mixing = jnp.zeros((SPAN, SPAN), F32)
        for pair in range(hc // 2):
            at = slice(pair * 128, pair * 128 + 128)
            x, g = rows16[0, b, :, at], rows16[1, b, :, at]
            parts = []
            for half in range(2):
                h = 2 * pair + half
                gap = cums[b, h : h + 1, :] - a_cols[b, :, h : h + 1]
                decay = jnp.exp(jnp.where(causal, gap, -jnp.inf))
                picked = jnp.where(low if half == 0 else ~low, x, jnp.zeros_like(x))
                mixing += decay * nt(picked, g)
                parts.append(nn((decay * kernel).astype(BF16), g))
            gains = jnp.where(low, skip[skip_at + 2 * pair], skip[skip_at + 2 * pair + 1])
            gx[b, :, at] = jnp.where(low, parts[0], parts[1]) + gains * g.astype(F32)
        mixed = mixing.astype(BF16)
        gp[b, :, :STATE] = nn(mixed, c_cols)
        gp[b, :, STATE:] = tn(mixed, b_cols)


def final_body(q, planes, more, *refs):
    it = iter(refs)
    got = [next(it) for _ in range(planes - 1)]
    rows16, states, f1s, ds, bcs, gx, gp = [next(it) for _ in range(7)]
    before = next(it) if more else None
    gx_out = [next(it) for _ in range(q)]
    gp_out, gx_all = it
    y = in_group(q)
    z = lax.div(lax.axis_index("seq"), q)
    start = after = jnp.zeros(got[0].shape, F32)
    for t in range(planes - 1):
        came = got[t][...]
        start += jnp.where(z == t + 1, 1.0, 0.0) * came
        after += jnp.where(z == planes - 2 - t, 1.0, 0.0) * came
    for b in range(q):
        part = gp[b, :, STATE:] + nt(rows16[3, b], start.astype(BF16))
        gp_out[b, :, STATE:] = part if before is None else part + before[b, :, STATE:]
        if b < q - 1:
            start = ds[b] * start + states[0, b]
    for b in range(q - 1, -1, -1):
        rounded = after.astype(BF16)
        gx_all[b] = gx[b] + f1s[b] * nn(bcs[b, :, :STATE], rounded)
        part = gp[b, :, :STATE] + nt(rows16[2, b], rounded)
        gp_out[b, :, :STATE] = part if before is None else part + before[b, :, :STATE]
        if b > 0:
            after = ds[b] * after + states[1, b]
    for r in range(q):
        gx_out[r][...] = gx_all[lax.rem(y + r, q)]


def assemble_body(q, group, spans, *refs):
    parts, result = refs[:-1], refs[-1]
    y = in_group(q)
    for r in range(q):
        base = lax.rem(y - r + q, q) * group
        for c, (first, width) in enumerate(spans):
            at = pl.multiple_of(base + first, 128)
            result[:, pl.ds(at, width)] = parts[r * len(spans) + c][...].astype(BF16)


def weight_body(n_dp, q, planes, rows, scale, *refs):
    it = iter(refs)
    tokens = [next(it) for _ in range(n_dp)]
    swapped = [next(it) for _ in range(q - 1)]
    grads = [next(it) for _ in range(n_dp)]
    outs = [next(it) for _ in range(planes)]
    held, factors, products = it
    width = planes * rows
    seq = lax.axis_index("seq")
    y, z = lax.rem(seq, q), lax.div(seq, q)
    for r in range(n_dp):
        held[y, r] = columns(tokens[r], y * width, width).astype(BF16)
        for b in range(q):
            factors[b, r] = grads[r][b].astype(BF16)
    for k in range(1, q):
        at = lax.rem(y - k + q, q)
        for r in range(n_dp):
            held[at, r] = swapped[k - 1][r].astype(BF16)
    total = tn(
        held[...].reshape(q * n_dp * SPAN, width), factors[...].reshape(q * n_dp * SPAN, 2 * STATE)
    )
    products[...] = (total * scale).reshape(planes, rows, 2 * STATE)
    for r in range(planes):
        outs[r][...] = products[lax.rem(z + r, planes)]


def behind(value, *others):
    return lax.optimization_barrier((value,) + others)[0]


def on_device(layer_input, proj_weight, inputs, step_size, log_decay, skip_gain, grad_out):
    n_seq, n_dp = lax.axis_size("seq"), lax.axis_size("dp")
    q = group_size(n_seq)
    planes = n_seq // q
    heads = HEADS // q
    group = heads * HEAD_DIM
    chunks = head_chunks(heads)
    spans = [(first * HEAD_DIM, count * HEAD_DIM) for first, count in chunks]
    tokens, x, g = layer_input[0], inputs[0], grad_out[0]
    length, features = tokens.shape
    seq = lax.axis_index("seq")

    def swap(value, r):
        pairs = [(z * q + i, z * q + (i + r) % q) for z in range(planes) for i in range(q)]
        return lax.ppermute(value, "seq", pairs)

    def across(value, r):
        return lax.ppermute(value, "dp", [(i, i ^ r) for i in range(n_dp)])

    def pack(first, width):
        scratch = (pltpu.VMEM((q - 1, 2, SPAN, width), BF16), pltpu.SemaphoreType.DMA((q - 1, 2)))
        outs = loose([out((2, SPAN, width))] * (q - 1))
        body = functools.partial(pack_body, q, group, first, width)
        return staged(body, outs, scratch, name="pack", hbm=2)(x, g)

    packed = pack(*spans[0])
    xg_in = [[swap(packed[r - 1], r) for r in range(1, q)]]
    bundles = call(
        functools.partial(project_body, q), [out((SPAN + heads, 2 * STATE))] * q, name="project"
    )(tokens, proj_weight, log_decay[0], step_size[0])
    projected = bundles[0]
    bundles = [projected] + [swap(bundles[r], r) for r in range(1, q)]
    packed = pack(*spans[1])
    got = [behind(packed[r - 1], projected) for r in range(1, q)]
    xg_in.append([swap(got[r - 1], r) for r in range(1, q)])
    columns_each = features // n_dp
    rows = columns_each // n_seq
    part = planes * rows

    shapes = [out((length, columns_each))] + loose([out((length, columns_each))] * (n_dp - 1))
    token_parts = list(
        staged(functools.partial(deal_body, rows, q, planes), shapes, name="deal")(tokens)
    )
    for r in range(n_dp - 1, 0, -1):
        token_parts[r] = across(token_parts[r], r)

    held, local = [], []
    for c, (first, count) in enumerate(chunks):
        wide = (q, SPAN, count * HEAD_DIM)
        state = out((STATE, wide[2]))
        outs = [
            out((4,) + wide, BF16), out((2,) + wide), out(wide), out((q, 1, wide[2])),
            state, state, out((1, wide[2])),
            out((q, SPAN, 2 * STATE), BF16), out((q, count, SPAN)), out((q, SPAN, count)),
        ]
        scratch = (pltpu.VMEM((q, count, SPAN), F32),)
        body = functools.partial(states_body, q, first, count)
        held.append(call(body, outs, scratch, name="states")(x, g, *xg_in[c], *bundles))
        body = functools.partial(local_body, q, first, count)
        rows16, bcs, cums, a_cols = (held[c][k] for k in (0, 7, 8, 9))
        outs = [out(wide), out((q, SPAN, 2 * STATE))]
        local.append(call(body, outs, smem=1, name="local")(skip_gain, rows16, bcs, cums, a_cols))

    ready = behind(tuple(token_parts), held[-1][6])
    handed = staged(
        functools.partial(hand_body, q, part), loose([out((n_dp, length, part))] * (q - 1)), name="hand"
    )(ready[0], *loose(ready[1:]))
    swapped = [swap(handed[r - 1], r) for r in range(1, q)]

    z = seq // q
    sent = [jnp.where(z < planes // 2, h[4], h[5]) for h in held]
    arrived = [[] for _ in held]
    for t in range(planes - 1):
        top = planes - 1 - t
        pairs = [(t * q + i, (t + 1) * q + i) for i in range(q)]
        pairs += [(top * q + i, (top - 1) * q + i) for i in range(q)]
        for c in range(PARTS):
            if c == 0 and t == planes - 2:
                sent[c] = behind(sent[c], *handed)
            came = lax.ppermute(sent[c], "seq", pairs)
            if t == max(planes - 3, 0):
                came = behind(came, local[c])
            if c == PARTS - 1 and t == planes - 2:
                came = behind(came, *swapped)
            arrived[c].append(came)
            if t < planes - 2:
                sent[c] = jnp.where(z == t + 1, held[c][4], held[c][5]) + held[c][6] * came

    before, gx_parts = [], {}
    for c, (first, width) in enumerate(spans):
        rows16, states, f1s, ds, bcs = (held[c][k] for k in (0, 1, 2, 3, 7))
        outs = [out((SPAN, width))] * q + [out((q, SPAN, 2 * STATE))]
        scratch = (pltpu.VMEM((q, SPAN, width), F32),)
        body = functools.partial(final_body, q, planes, bool(before))
        done = call(body, outs, scratch, name="final")(
            *arrived[c], rows16, states, f1s, ds, bcs, *local[c], *before
        )
        for r in range(q):
            gx_parts[r, c] = done[r]
        before = [done[q]]

    gp = before[0]
    for r in range(1, q):
        gp = gp + swap(before[0], r)
    grads = {0: gp}
    bit = n_dp // 2
    while bit:
        for r in list(grads):
            grads[r ^ bit] = across(grads[r], bit)
        bit //= 2
    scale = 1.0 / (length * n_seq)
    outs = [out((rows, 2 * STATE))] * planes
    args = token_parts + swapped + [grads[r] for r in range(n_dp)]
    scratch = (
        pltpu.VMEM((q, n_dp, SPAN, part), BF16),
        pltpu.VMEM((q, n_dp, SPAN, 2 * STATE), BF16),
        pltpu.VMEM((planes, rows, 2 * STATE), F32),
    )
    body = functools.partial(weight_body, n_dp, q, planes, rows, scale)
    pieces = call(body, outs, scratch, name="weight")(*args)
    grad_weight = pieces[0]
    for r in range(1, planes):
        pairs = [(z * q + i, (z + r) % planes * q + i) for z in range(planes) for i in range(q)]
        grad_weight = grad_weight + lax.ppermute(pieces[r], "seq", pairs)

    parts = [gx_parts[0, c] for c in range(PARTS)]
    for r in range(1, q):
        parts += [swap(gx_parts[r, c], r) for c in range(PARTS)]
    body = functools.partial(assemble_body, q, group, spans)
    (grad_x,) = call(body, [out((length, q * group), BF16)], name="assemble")(*parts)
    return grad_x[None], grad_weight


def solution(mesh):
    return jax.shard_map(
        on_device,
        mesh=mesh,
        in_specs=(
            P("dp", "seq", None),
            P(),
            P("dp", "seq", None),
            P("dp", None, "seq"),
            P("dp", None, "seq"),
            P(),
            P("dp", "seq", None),
        ),
        out_specs=(P("dp", "seq", None), P(("dp", "seq"), None)),
        check_vma=False,
    )
```

time: 142 us -> 119 us (0.84)
  starting transfers between devices: 49.9 us -> 25.5 us
  Pallas kernels: 43.2 us -> 22.2 us
  local copies, waits for them, and re-layouts: 0.01 us -> 16.3 us
  waiting for transfers between devices: 42.1 us -> 46.7 us
  other arithmetic: 5.04 us -> 6.74 us
    pallas_call x18 -> x4, Pallas kernels: 43.2 us -> 8.16 us  [run(): pl.pallas_call(body, out_shape=tuple(shapes), grid=(1,), in_specs=specs,...]
    unnamed x6 -> x80, local copies, waits for them, and re-layouts: 0.01 us -> 16.3 us
    pallas_call x0 -> x9, Pallas kernels: none -> 14.1 us  [run(): pl.pallas_call(body, out_shape=tuple(outs), in_specs=specs, out_specs=tup...]
    ppermute x18 -> x6, starting transfers between devices: 24 us -> 11.5 us  [on_device(): came = lax.ppermute(sent[c], 'seq', pairs)]
    ppermute x18 -> x6, waiting for transfers between devices: 4.65 us -> 14.1 us  [on_device(): came = lax.ppermute(sent[c], 'seq', pairs)]
    ppermute x3, starting transfers between devices: 10.2 us -> 3.19 us  [on_device(): grad_weight = grad_weight + lax.ppermute(pieces[r], 'seq', pairs)]
    ppermute x6, waiting for transfers between devices: 12.3 us -> 7.06 us  [across(): return lax.ppermute(value, 'dp', [(i, i ^ r) for i in range(n_dp)])]
    ppermute x9 -> x7, waiting for transfers between devices: 17.4 us -> 22.2 us  [swap(): return lax.ppermute(value, 'seq', pairs)]
  transfers between devices with their start and end apart: 36 -> 22, of which waited for: 8 -> 6; matrix products, arithmetic and copies ran while one was open for 3% -> 5% of each run, Pallas kernels for 29% -> 15%
where the time goes in v5:
time: 119 us
  waiting for transfers between devices  46.7 us (39%)
  starting transfers between devices  25.5 us (21%)
  Pallas kernels  22.2 us (19%)
  local copies, waits for them, and re-layouts  16.3 us (14%)
  other arithmetic  6.74 us (6%)
    ppermute x7, waiting for transfers between devices, swap(): return lax.ppermute(value, 'seq', pairs)  22.2 us
    unnamed x80, local copies, waits for them, and re-layouts  16.3 us
    ppermute x6, waiting for transfers between devices, on_device(): came = lax.ppermute(sent[c], 'seq', pairs)  14.1 us
    pallas_call x9, Pallas kernels, run(): pl.pallas_call(body, out_shape=tuple(outs), in_specs=specs, out_specs=tup...  14.1 us
    ppermute x6, starting transfers between devices, on_device(): came = lax.ppermute(sent[c], 'seq', pairs)  11.5 us
    ppermute x7, starting transfers between devices, swap(): return lax.ppermute(value, 'seq', pairs)  9.22 us
    pallas_call x4, Pallas kernels, run(): pl.pallas_call(body, out_shape=tuple(shapes), grid=(1,), in_specs=specs,...  8.16 us
    ppermute x6, waiting for transfers between devices, across(): return lax.ppermute(value, 'dp', [(i, i ^ r) for i in range(n_dp)])  7.06 us
  transfers between devices with their start and end apart: 22, of which 6 were waited for; matrix products, arithmetic and copies ran while one was open for 5% of the time, Pallas kernels for 15%

profile of v5, /device:TPU:0, one launch (start us, length us, event | category | flops | bytes accessed | tf_op | source)
XLA Modules:
  0.0 118.6 jit_solution(16767197560832631329)
XLA Ops:
  1.8 3.0 %collective-permute-start = (f32[2,128,640]{2,1,0:T(8,128)S(1)}, f32[2,128,640]{2,1,0:T(8,128)S(1)}, u32[]{:S(2)}, u32[]{:S(2)}) collective-permute-start(f32[2,128,640]{2,1,0:T(8,128)S(1)} %pack.2), channel_id=1, source_target_pairs={{0,1},{1,0},{2,3},{3,2},{4,5},{5,4},{6,7},{7,6},{8,9},{9,8},{10,11... | collective-permute-start | bytes 1966088 | tf_op jit(solution)/shard_map/ppermute | solution.py:331
  4.8 1.6 %copy-done.5 = bf16[4096,256]{1,0:T(8,128)(2,1)S(1)} copy-done((bf16[4096,256]{1,0:T(8,128)(2,1)S(1)}, bf16[4096,256]{1,0:T(8,128)(2,1)}, u32[]{:S(2)}) %copy-start.5) | copy-done | bytes 2097176
  7.7 1.8 %pack.3 = f32[2,128,384]{2,1,0:T(8,128)} custom-call(bf16[128,2048]{1,0:T(8,128)(2,1)} %bitcast.7, bf16[128,2048]{1,0:T(8,128)(2,1)} %bitcast.11), custom_call_target="tpu_custom_call" | custom-call | tf_op jit(solution)/shard_map/pack/pallas_call | solution.py:84
  9.5 1.9 %collective-permute-start.7 = (f32[2,128,384]{2,1,0:T(8,128)}, f32[2,128,384]{2,1,0:T(8,128)}, u32[]{:S(2)}, u32[]{:S(2)}) collective-permute-start(f32[2,128,384]{2,1,0:T(8,128)} %pack.3), channel_id=1, source_target_pairs={{0,1},{1,0},{2,3},{3,2},{4,5},{5,4},{6,7},{7,6},{8,9},{9,8},{10,11... | collective-permute-start | bytes 1179656 | tf_op jit(solution)/shard_map/ppermute | solution.py:331
  11.4 2.6 %deal.1 = (f32[128,1024]{1,0:T(8,128)}, f32[128,1024]{1,0:T(8,128)}, f32[128,1024]{1,0:T(8,128)}, f32[128,1024]{1,0:T(8,128)}) custom-call(bf16[128,4096]{1,0:T(8,128)(2,1)} %bitcast.14), custom_call_target="tpu_custom_call" | custom-call | tf_op jit(solution)/shard_map/deal/pallas_call | solution.py:84
  15.5 8.1 %collective-permute-done.1.refs_4_ = f32[144,256]{1,0:T(8,128)S(1)} collective-permute-done((f32[144,256]{1,0:T(8,128)S(1)}, f32[144,256]{1,0:T(8,128)S(1)}, u32[]{:S(2)}, u32[]{:S(2)}) %collective-permute-start.1) | collective-permute-done | bytes 147488 | tf_op jit(solution)/shard_map/ppermute | solution.py:331
  32.1 4.7 %collective-permute-start.2 = (f32[128,640]{1,0:T(8,128)}, f32[128,640]{1,0:T(8,128)}, u32[]{:S(2)}, u32[]{:S(2)}) collective-permute-start(f32[128,640]{1,0:T(8,128)} %broadcast_select_fusion), channel_id=1, source_target_pairs={{0,2},{1,3},{6,4},{7,5},{8,10},{9,11},{14,12},{15,13},{16,18},{17,... | collective-permute-start | bytes 983048 | tf_op jit(solution)/shard_map/ppermute | solution.py:396
  38.7 2.3 %states.3 = (bf16[4,2,128,384]{3,2,1,0:T(8,128)(2,1)S(1)}, f32[2,2,128,384]{3,2,1,0:T(8,128)S(1)}, f32[2,128,384]{2,1,0:T(8,128)S(1)}, f32[2,1,384]{2,1,0:T(1,12...) custom-call(bf16[128,2048]{1,0:T(8,128)(2,1)S(1)} %bitcast.9, ...), custom_call_target="tpu_custom_call" | custom-call | tf_op jit(solution)/shard_map/states/pallas_call | solution.py:55
  44.0 2.0 %collective-permute-start.9 = (f32[128,384]{1,0:T(8,128)}, f32[128,384]{1,0:T(8,128)}, u32[]{:S(2)}, u32[]{:S(2)}) collective-permute-start(f32[128,384]{1,0:T(8,128)} %broadcast_select_fusion.1), channel_id=1, source_target_pairs={{0,2},{1,3},{6,4},{7,5},{8,10},{9,11},{14,12},{15,13},{16,18},{17,... | collective-permute-start | bytes 589832 | tf_op jit(solution)/shard_map/ppermute | solution.py:396
  46.0 2.6 %hand.1 = f32[4,128,512]{2,1,0:T(8,128)} custom-call(f32[128,1024]{1,0:T(8,128)} %get-tuple-element.69.refs_0_, f32[128,1024]{1,0:T(8,128)} %collective-permute-done.4.refs_1_, f32[128,1024]{1,0:T(8,128)} %collective-permute-done.5.refs_2_, f32[128,1024]{1,0:T(8,128)} %collective-permute-done.6.refs_3_), custom_call_target="tpu_custom_call" | custom-call | tf_op jit(solution)/shard_map/hand/pallas_call | solution.py:84
  48.7 1.6 %collective-permute-start.12 = (f32[4,128,512]{2,1,0:T(8,128)}, f32[4,128,512]{2,1,0:T(8,128)}, u32[]{:S(2)}, u32[]{:S(2)}) collective-permute-start(f32[4,128,512]{2,1,0:T(8,128)} %hand.1), channel_id=1, source_target_pairs={{0,1},{1,0},{2,3},{3,2},{4,5},{5,4},{6,7},{7,6},{8,9},{9,8},{10,11... | collective-permute-start | bytes 3145736 | tf_op jit(solution)/shard_map/ppermute | solution.py:331
  50.3 1.8 %multiply_add_fusion.1 = f32[128,640]{1,0:T(8,128)} fusion(f32[128,640]{1,0:T(8,128)} %collective-permute-done.2.refs_0_, f32[128,640]{1,0:T(8,128)S(1)} %get-tuple-element.53, f32[128,640]{1,0:T(8,128)S(1)} %copy-done.4, f32[640]{0:T(1024)S(1)} %reduce, pred[]{:T(512)S(6)} %eq.8), kind=kLoop, calls=%fused_computation.1 | loop fusion | flops 245760 | bytes 1313281 | tf_op jit(solution)/shard_map/add | solution.py:403
  52.8 1.6 %multiply_add_fusion.3 = f32[128,384]{1,0:T(8,128)} fusion(f32[128,384]{1,0:T(8,128)} %collective-permute-done.9.refs_0_, f32[128,384]{1,0:T(8,128)S(1)} %copy-done.8, f32[128,384]{1,0:T(8,128)S(1)} %copy-done.10, f32[384]{0:T(512)S(1)} %reduce.1, pred[]{:T(512)S(6)} %eq.8), kind=kLoop, calls=%fused_computation.3 | loop fusion | flops 147456 | bytes 787969 | tf_op jit(solution)/shard_map/add | solution.py:403
  57.6 1.5 %local.3 = (f32[2,128,384]{2,1,0:T(8,128)S(1)}, f32[2,128,256]{2,1,0:T(8,128)S(1)}) custom-call(f32[32]{0:T(128)S(1)} %copy-done.39, bf16[4,2,128,384]{3,2,1,0:T(8,128)(2,1)S(1)} %get-tuple-element.80.rows16.refs_3_, bf16[2,128,256]{2,1,0:T(8,128)(2,1)S(1)} %copy-done.29, f32[2,6,128]{2,1,0:T(8,128)S(1)} %get-tuple-element.82.cums, f32[2,128,6]{2,1,0:T(8,128)S(1)} %copy-done.36), custom_call_target="tpu_custom_call" | custom-call | tf_op jit(solution)/shard_map/local/pallas_call | solution.py:55
  61.0 1.8 %local.2 = (f32[2,128,640]{2,1,0:T(8,128)S(1)}, f32[2,128,256]{2,1,0:T(8,128)S(1)}) custom-call(f32[32]{0:T(128)S(1)} %copy-done.39, bf16[4,2,128,640]{3,2,1,0:T(8,128)(2,1)S(1)} %get-tuple-element.56.rows16.refs_3_, bf16[2,128,256]{2,1,0:T(8,128)(2,1)S(1)} %copy-done.26, f32[2,10,128]{2,1,0:T(8,128)S(1)} %get-tuple-element.58.cums, f32[2,128,10]{2,1,0:T(8,128)S(1)} %copy-done.34), custom_call_target="tpu_custom_call" | custom-call | tf_op jit(solution)/shard_map/local/pallas_call | solution.py:55
  66.6 14.1 %collective-permute-done.11.refs_2_ = f32[128,384]{1,0:T(8,128)S(1)} collective-permute-done((f32[128,384]{1,0:T(8,128)S(1)}, f32[128,384]{1,0:T(8,128)S(1)}, u32[]{:S(2)}, u32[]{:S(2)}) %collective-permute-start.11) | collective-permute-done | bytes 196640 | tf_op jit(solution)/shard_map/ppermute | solution.py:396
  80.7 1.7 %final.2 = (f32[128,640]{1,0:T(8,128)S(1)}, f32[128,640]{1,0:T(8,128)S(1)}, f32[2,128,256]{2,1,0:T(8,128)S(1)}) custom-call(f32[128,640]{1,0:T(8,128)} %collective-permute-done.2.refs_0_, f32[128,640]{1,0:T(8,128)S(1)} %collective-permute-done.3.refs_1_, f32[128,640]{1,0:T(8,128)S(1)} %collective-permute-done.8.refs_2_, ...), custom_call_target="tpu_custom_call" | custom-call | tf_op jit(solution)/shard_map/final/pallas_call | solution.py:55
  82.4 1.5 %final.3 = (f32[128,384]{1,0:T(8,128)S(1)}, f32[128,384]{1,0:T(8,128)S(1)}, f32[2,128,256]{2,1,0:T(8,128)S(1)}) custom-call(f32[128,384]{1,0:T(8,128)} %collective-permute-done.9.refs_0_, f32[128,384]{1,0:T(8,128)} %collective-permute-done.10.refs_1_, f32[128,384]{1,0:T(8,128)S(1)} %collective-permute-done.11.refs_2_, ...), custom_call_target="tpu_custom_call" | custom-call | tf_op jit(solution)/shard_map/final/pallas_call | solution.py:55
  84.5 7.5 %collective-permute-done.15 = f32[2,128,256]{2,1,0:T(8,128)S(1)} collective-permute-done((f32[2,128,256]{2,1,0:T(8,128)S(1)}, f32[2,128,256]{2,1,0:T(8,128)S(1)}, u32[]{:S(2)}, u32[]{:S(2)}) %collective-permute-start.15) | collective-permute-done | bytes 262176 | tf_op jit(solution)/shard_map/ppermute | solution.py:331
  92.2 7.0 %collective-permute-done.17.refs_7_ = f32[2,128,256]{2,1,0:T(8,128)S(1)} collective-permute-done((f32[2,128,256]{2,1,0:T(8,128)S(1)}, f32[2,128,256]{2,1,0:T(8,128)S(1)}, u32[]{:S(2)}, u32[]{:S(2)}) %collective-permute-start.17) | collective-permute-done | bytes 262176 | tf_op jit(solution)/shard_map/ppermute | solution.py:334
  101.3 2.5 %weight.3 = (f32[128,256]{1,0:T(8,128)S(1)}, f32[128,256]{1,0:T(8,128)S(1)}, f32[128,256]{1,0:T(8,128)S(1)}, f32[128,256]{1,0:T(8,128)S(1)}) custom-call(f32[128,1024]{1,0:T(8,128)S(1)} %copy-done.6, f32[128,1024]{1,0:T(8,128)} %collective-permute-done.4.refs_1_, f32[128,1024]{1,0:T(8,128)} %collective-permute-done.5.refs_2_, ...), custom_call_target="tpu_custom_call" | custom-call | tf_op jit(solution)/shard_map/weight/pallas_call | solution.py:55
  103.9 2.5 %collective-permute-start.21 = (f32[128,256]{1,0:T(8,128)S(1)}, f32[128,256]{1,0:T(8,128)S(1)}, u32[]{:S(2)}, u32[]{:S(2)}) collective-permute-start(f32[128,256]{1,0:T(8,128)S(1)} %get-tuple-element.99), channel_id=1, source_target_pairs={{0,6},{1,7},{2,0},{3,1},{4,2},{5,3},{6,4},{7,5},{8,14},{9,15},{10,... | collective-permute-start | bytes 393224 | tf_op jit(solution)/shard_map/ppermute | solution.py:440
  107.1 6.6 %collective-permute-done.14.refs_3_ = f32[128,384]{1,0:T(8,128)S(1)} collective-permute-done((f32[128,384]{1,0:T(8,128)S(1)}, f32[128,384]{1,0:T(8,128)S(1)}, u32[]{:S(2)}, u32[]{:S(2)}) %collective-permute-start.14) | collective-permute-done | bytes 196640 | tf_op jit(solution)/shard_map/ppermute | solution.py:331
  114.5 3.4 %collective-permute-done.20 = f32[128,256]{1,0:T(8,128)S(1)} collective-permute-done((f32[128,256]{1,0:T(8,128)S(1)}, f32[128,256]{1,0:T(8,128)S(1)}, u32[]{:S(2)}, u32[]{:S(2)}) %collective-permute-start.20) | collective-permute-done | bytes 131104 | tf_op jit(solution)/shard_map/ppermute | solution.py:440
  (123 shorter events, 31.7 us)
Async XLA Ops:
  1.8 22.4 %collective-permute-start = (f32[2,128,640]{2,1,0:T(8,128)S(1)}, f32[2,128,640]{2,1,0:T(8,128)S(1)}, u32[]{:S(2)}, u32[]{:S(2)}) collective-permute-start(f32[2,128,640]{2,1,0:T(8,128)S(1)} %pack.2), channel_id=1, source_target_pairs={{0,1},{1,0},{2,3},{3,2},{4,5},{5,4},{6,7},{7,6},{8,9},{9,8},{10,11... | collective-permute-start | bytes 1966088 | tf_op jit(solution)/shard_map/ppermute | solution.py:331
  7.5 16.0 %collective-permute-start.1 = (f32[144,256]{1,0:T(8,128)S(1)}, f32[144,256]{1,0:T(8,128)S(1)}, u32[]{:S(2)}, u32[]{:S(2)}) collective-permute-start(f32[144,256]{1,0:T(8,128)S(1)} %get-tuple-element.52), channel_id=1, source_target_pairs={{0,1},{1,0},{2,3},{3,2},{4,5},{5,4},{6,7},{7,6},{8,9},{9,8},{10,11... | collective-permute-start | bytes 442376 | tf_op jit(solution)/shard_map/ppermute | solution.py:331
  9.5 27.4 %collective-permute-start.7 = (f32[2,128,384]{2,1,0:T(8,128)}, f32[2,128,384]{2,1,0:T(8,128)}, u32[]{:S(2)}, u32[]{:S(2)}) collective-permute-start(f32[2,128,384]{2,1,0:T(8,128)} %pack.3), channel_id=1, source_target_pairs={{0,1},{1,0},{2,3},{3,2},{4,5},{5,4},{6,7},{7,6},{8,9},{9,8},{10,11... | collective-permute-start | bytes 1179656 | tf_op jit(solution)/shard_map/ppermute | solution.py:331
  14.0 32.0 %collective-permute-start.4 = (f32[128,1024]{1,0:T(8,128)}, f32[128,1024]{1,0:T(8,128)}, u32[]{:S(2)}, u32[]{:S(2)}) collective-permute-start(f32[128,1024]{1,0:T(8,128)} %get-tuple-element.64), channel_id=1, source_target_pairs={{0,8},{8,0},{16,24},{24,16},{1,9},{9,1},{17,25},{25,17},{2,10},{10... | collective-permute-start | bytes 1572872 | tf_op jit(solution)/shard_map/ppermute | solution.py:334
  14.0 32.0 %collective-permute-start.5 = (f32[128,1024]{1,0:T(8,128)}, f32[128,1024]{1,0:T(8,128)}, u32[]{:S(2)}, u32[]{:S(2)}) collective-permute-start(f32[128,1024]{1,0:T(8,128)} %get-tuple-element.65), channel_id=1, source_target_pairs={{0,16},{8,24},{16,0},{24,8},{1,17},{9,25},{17,1},{25,9},{2,18},{10... | collective-permute-start | bytes 1572872 | tf_op jit(solution)/shard_map/ppermute | solution.py:334
  24.2 21.8 %collective-permute-start.6 = (f32[128,1024]{1,0:T(8,128)}, f32[128,1024]{1,0:T(8,128)}, u32[]{:S(2)}, u32[]{:S(2)}) collective-permute-start(f32[128,1024]{1,0:T(8,128)} %get-tuple-element.66), channel_id=1, source_target_pairs={{0,24},{8,16},{16,8},{24,0},{1,25},{9,17},{17,9},{25,1},{2,26},{10... | collective-permute-start | bytes 1572872 | tf_op jit(solution)/shard_map/ppermute | solution.py:334
  32.1 18.2 %collective-permute-start.2 = (f32[128,640]{1,0:T(8,128)}, f32[128,640]{1,0:T(8,128)}, u32[]{:S(2)}, u32[]{:S(2)}) collective-permute-start(f32[128,640]{1,0:T(8,128)} %broadcast_select_fusion), channel_id=1, source_target_pairs={{0,2},{1,3},{6,4},{7,5},{8,10},{9,11},{14,12},{15,13},{16,18},{17,... | collective-permute-start | bytes 983048 | tf_op jit(solution)/shard_map/ppermute | solution.py:396
  44.0 8.8 %collective-permute-start.9 = (f32[128,384]{1,0:T(8,128)}, f32[128,384]{1,0:T(8,128)}, u32[]{:S(2)}, u32[]{:S(2)}) collective-permute-start(f32[128,384]{1,0:T(8,128)} %broadcast_select_fusion.1), channel_id=1, source_target_pairs={{0,2},{1,3},{6,4},{7,5},{8,10},{9,11},{14,12},{15,13},{16,18},{17,... | collective-permute-start | bytes 589832 | tf_op jit(solution)/shard_map/ppermute | solution.py:396
  48.7 32.0 %collective-permute-start.12 = (f32[4,128,512]{2,1,0:T(8,128)}, f32[4,128,512]{2,1,0:T(8,128)}, u32[]{:S(2)}, u32[]{:S(2)}) collective-permute-start(f32[4,128,512]{2,1,0:T(8,128)} %hand.1), channel_id=1, source_target_pairs={{0,1},{1,0},{2,3},{3,2},{4,5},{5,4},{6,7},{7,6},{8,9},{9,8},{10,11... | collective-permute-start | bytes 3145736 | tf_op jit(solution)/shard_map/ppermute | solution.py:331
  52.1 10.7 %collective-permute-start.3 = (f32[128,640]{1,0:T(8,128)}, f32[128,640]{1,0:T(8,128)S(1)}, u32[]{:S(2)}, u32[]{:S(2)}) collective-permute-start(f32[128,640]{1,0:T(8,128)} %multiply_add_fusion.1), channel_id=1, source_target_pairs={{2,4},{3,5},{4,2},{5,3},{10,12},{11,13},{12,10},{13,11},{18,20},{1... | collective-permute-start | bytes 983048 | tf_op jit(solution)/shard_map/ppermute | solution.py:396
  54.5 8.3 %collective-permute-start.10 = (f32[128,384]{1,0:T(8,128)}, f32[128,384]{1,0:T(8,128)}, u32[]{:S(2)}, u32[]{:S(2)}) collective-permute-start(f32[128,384]{1,0:T(8,128)} %multiply_add_fusion.3), channel_id=1, source_target_pairs={{2,4},{3,5},{4,2},{5,3},{10,12},{11,13},{12,10},{13,11},{18,20},{1... | collective-permute-start | bytes 589832 | tf_op jit(solution)/shard_map/ppermute | solution.py:396
  62.7 17.9 %copy-start.12 = (f32[2,2,128,640]{3,2,1,0:T(8,128)S(1)}, f32[2,2,128,640]{3,2,1,0:T(8,128)}, u32[]{:S(2)}) copy-start(f32[2,2,128,640]{3,2,1,0:T(8,128)} %copy-done.11) | copy-start | bytes 3932164
  62.9 17.8 %collective-permute-start.8 = (f32[128,640]{1,0:T(8,128)S(1)}, f32[128,640]{1,0:T(8,128)S(1)}, u32[]{:S(2)}, u32[]{:S(2)}) collective-permute-start(f32[128,640]{1,0:T(8,128)S(1)} %multiply_add_fusion), channel_id=1, source_target_pairs={{4,6},{5,7},{2,0},{3,1},{12,14},{13,15},{10,8},{11,9},{20,22},{21,... | collective-permute-start | bytes 983048 | tf_op jit(solution)/shard_map/ppermute | solution.py:396
  65.3 15.4 %collective-permute-start.11 = (f32[128,384]{1,0:T(8,128)S(1)}, f32[128,384]{1,0:T(8,128)S(1)}, u32[]{:S(2)}, u32[]{:S(2)}) collective-permute-start(f32[128,384]{1,0:T(8,128)S(1)} %multiply_add_fusion.2), channel_id=1, source_target_pairs={{4,6},{5,7},{2,0},{3,1},{12,14},{13,15},{10,8},{11,9},{20,22},{21,... | collective-permute-start | bytes 589832 | tf_op jit(solution)/shard_map/ppermute | solution.py:396
  82.4 18.9 %copy-start.6 = (f32[128,1024]{1,0:T(8,128)S(1)}, f32[128,1024]{1,0:T(8,128)}, u32[]{:S(2)}) copy-start(f32[128,1024]{1,0:T(8,128)} %get-tuple-element.69.refs_0_) | copy-start | bytes 1572868
  84.0 8.1 %collective-permute-start.15 = (f32[2,128,256]{2,1,0:T(8,128)S(1)}, f32[2,128,256]{2,1,0:T(8,128)S(1)}, u32[]{:S(2)}, u32[]{:S(2)}) collective-permute-start(f32[2,128,256]{2,1,0:T(8,128)S(1)} %get-tuple-element.95), channel_id=1, source_target_pairs={{0,1},{1,0},{2,3},{3,2},{4,5},{5,4},{6,7},{7,6},{8,9},{9,8},{10,11... | collective-permute-start | bytes 786440 | tf_op jit(solution)/shard_map/ppermute | solution.py:331
  92.1 7.2 %collective-permute-start.17 = (f32[2,128,256]{2,1,0:T(8,128)S(1)}, f32[2,128,256]{2,1,0:T(8,128)S(1)}, u32[]{:S(2)}, u32[]{:S(2)}) collective-permute-start(f32[2,128,256]{2,1,0:T(8,128)S(1)} %add.29.refs_5_), channel_id=1, source_target_pairs={{0,16},{8,24},{16,0},{24,8},{1,17},{9,25},{17,1},{25,9},{2,18},{10... | collective-permute-start | bytes 786440 | tf_op jit(solution)/shard_map/ppermute | solution.py:334
  92.2 9.2 %collective-permute-start.16 = (f32[2,128,256]{2,1,0:T(8,128)S(1)}, f32[2,128,256]{2,1,0:T(8,128)S(1)}, u32[]{:S(2)}, u32[]{:S(2)}) collective-permute-start(f32[2,128,256]{2,1,0:T(8,128)S(1)} %add.29.refs_5_), channel_id=1, source_target_pairs={{0,8},{8,0},{16,24},{24,16},{1,9},{9,1},{17,25},{25,17},{2,10},{10... | collective-permute-start | bytes 786440 | tf_op jit(solution)/shard_map/ppermute | solution.py:334
  99.3 2.0 %collective-permute-start.18 = (f32[2,128,256]{2,1,0:T(8,128)S(1)}, f32[2,128,256]{2,1,0:T(8,128)S(1)}, u32[]{:S(2)}, u32[]{:S(2)}) collective-permute-start(f32[2,128,256]{2,1,0:T(8,128)S(1)} %collective-permute-done.17.refs_7_), channel_id=1, source_target_pairs={{0,8},{8,0},{16,24},{24,16},{1,9},{9,1},{17,25},{25,17},{2,10},{10... | collective-permute-start | bytes 786440 | tf_op jit(solution)/shard_map/ppermute | solution.py:334
  99.3 14.3 %collective-permute-start.13 = (f32[128,640]{1,0:T(8,128)S(1)}, f32[128,640]{1,0:T(8,128)S(1)}, u32[]{:S(2)}, u32[]{:S(2)}) collective-permute-start(f32[128,640]{1,0:T(8,128)S(1)} %get-tuple-element.93), channel_id=1, source_target_pairs={{0,1},{1,0},{2,3},{3,2},{4,5},{5,4},{6,7},{7,6},{8,9},{9,8},{10,11... | collective-permute-start | bytes 983048 | tf_op jit(solution)/shard_map/ppermute | solution.py:331
  99.8 13.8 %collective-permute-start.14 = (f32[128,384]{1,0:T(8,128)S(1)}, f32[128,384]{1,0:T(8,128)S(1)}, u32[]{:S(2)}, u32[]{:S(2)}) collective-permute-start(f32[128,384]{1,0:T(8,128)S(1)} %get-tuple-element.94), channel_id=1, source_target_pairs={{0,1},{1,0},{2,3},{3,2},{4,5},{5,4},{6,7},{7,6},{8,9},{9,8},{10,11... | collective-permute-start | bytes 589832 | tf_op jit(solution)/shard_map/ppermute | solution.py:331
  103.9 10.6 %collective-permute-start.21 = (f32[128,256]{1,0:T(8,128)S(1)}, f32[128,256]{1,0:T(8,128)S(1)}, u32[]{:S(2)}, u32[]{:S(2)}) collective-permute-start(f32[128,256]{1,0:T(8,128)S(1)} %get-tuple-element.99), channel_id=1, source_target_pairs={{0,6},{1,7},{2,0},{3,1},{4,2},{5,3},{6,4},{7,5},{8,14},{9,15},{10,... | collective-permute-start | bytes 393224 | tf_op jit(solution)/shard_map/ppermute | solution.py:440
  106.4 11.5 %collective-permute-start.20 = (f32[128,256]{1,0:T(8,128)S(1)}, f32[128,256]{1,0:T(8,128)S(1)}, u32[]{:S(2)}, u32[]{:S(2)}) collective-permute-start(f32[128,256]{1,0:T(8,128)S(1)} %get-tuple-element.98), channel_id=1, source_target_pairs={{0,4},{1,5},{2,6},{3,7},{4,0},{5,1},{6,2},{7,3},{8,12},{9,13},{10,... | collective-permute-start | bytes 393224 | tf_op jit(solution)/shard_map/ppermute | solution.py:440
  106.4 11.5 %collective-permute-start.19 = (f32[128,256]{1,0:T(8,128)S(1)}, f32[128,256]{1,0:T(8,128)S(1)}, u32[]{:S(2)}, u32[]{:S(2)}) collective-permute-start(f32[128,256]{1,0:T(8,128)S(1)} %get-tuple-element.97), channel_id=1, source_target_pairs={{0,2},{1,3},{2,4},{3,5},{4,6},{5,7},{6,0},{7,1},{8,10},{9,11},{10,... | collective-permute-start | bytes 393224 | tf_op jit(solution)/shard_map/ppermute | solution.py:440
  (38 other events, 146.9 us)

commit v6 on v5

--- a/solution.py
+++ b/solution.py
@@ -48,13 +48,21 @@
     return [(0, first), (first, heads - first)]
 
 
-def call(body, outs, scratch=(), name=None, smem=0):
+def call(body, outs, scratch=(), name=None, smem=0, hbm=0):
     def run(*args):
+        args = list(args)
+        for k in range(smem, len(args)):
+            if isinstance(args[k], list):
+                args[k] = args[k][0]
+            else:
+                place = pltpu.HBM if k < smem + hbm else pltpu.VMEM
+                args[k] = pltpu.with_memory_space_constraint(args[k], place)
         specs = [pl.BlockSpec(memory_space=pltpu.SMEM)] * smem
-        specs += [pl.BlockSpec(memory_space=pltpu.VMEM)] * (len(args) - smem)
+        specs += [pl.BlockSpec(memory_space=pltpu.HBM)] * hbm
+        specs += [pl.BlockSpec(memory_space=pltpu.VMEM)] * (len(args) - smem - hbm)
         return pl.pallas_call(
             body,
-            out_shape=tuple(outs),
+            out_shape=tuple(o[0] if isinstance(o, list) else pltpu.VMEM(o.shape, o.dtype) for o in outs),
             in_specs=specs,
             out_specs=tuple(pl.BlockSpec(memory_space=pltpu.VMEM) for _ in outs),
             scratch_shapes=scratch,
@@ -65,36 +73,6 @@
     return run
 
 
-def whole(shape):
-    return pl.BlockSpec(shape, lambda i, rank=len(shape): (0,) * rank)
-
-
-def staged(body, outs, scratch=(), name=None, smem=0, hbm=0):
-    def run(*args):
-        args = list(args)
-        for k in range(smem, len(args)):
-            if isinstance(args[k], list):
-                args[k] = args[k][0]
-            else:
-                args[k] = pltpu.with_memory_space_constraint(args[k], pltpu.HBM)
-        specs = [pl.BlockSpec(memory_space=pltpu.SMEM)] * smem
-        specs += [pl.BlockSpec(memory_space=pltpu.HBM)] * hbm
-        specs += [whole(a.shape) for a in args[smem + hbm :]]
-        shapes = [o[0] if isinstance(o, list) else pltpu.HBM(o.shape, o.dtype) for o in outs]
-        return pl.pallas_call(
-            body,
-            out_shape=tuple(shapes),
-            grid=(1,),
-            in_specs=specs,
-            out_specs=tuple(whole(o.shape) for o in shapes),
-            scratch_shapes=scratch,
-            compiler_params=pltpu.CompilerParams(vmem_limit_bytes=VMEM_LIMIT),
-            name=name,
-        )(*args)
-
-    return run
-
-
 def loose(values):
     return [[value] for value in values]
 
@@ -117,21 +95,31 @@
     return ref[:, pl.ds(pl.multiple_of(start, 128), width)]
 
 
-def pack_body(q, group, first, width, x, g, *refs):
-    packed, (stage, sems) = refs[: q - 1], refs[q - 1 :]
+def pack_body(q, group, first, width, keep, x, g, *refs):
+    packed, rest = refs[: q - 1], list(refs[q - 1 :])
+    own = rest.pop(0) if keep else None
+    stage, sems = rest
     y = in_group(q)
     copies = {}
     for r in range(1, q):
         at = pl.multiple_of(lax.rem(y + r, q) * group + first, 128)
         for k, source in enumerate((x, g)):
             copies[r, k] = pltpu.make_async_copy(
-                source.at[:, pl.ds(at, width)], stage.at[r - 1, k], sems.at[r - 1, k]
+                source.at[:, pl.ds(at, width)], stage.at[r - 1, k], sems.at[r, k]
             )
             copies[r, k].start()
+    if keep:
+        at = pl.multiple_of(y * group, 128)
+        for k, source in enumerate((x, g)):
+            copies[0, k] = pltpu.make_async_copy(source.at[:, pl.ds(at, group)], own.at[k], sems.at[0, k])
+            copies[0, k].start()
     for r in range(1, q):
         for k in range(2):
             copies[r, k].wait()
             packed[r - 1][k] = stage[r - 1, k].astype(F32)
+    if keep:
+        for k in range(2):
+            copies[0, k].wait()
 
 
 def deal_body(rows, q, planes, tokens, *outs):
@@ -164,17 +152,16 @@
         bundles[r][SPAN:, SPAN:] = step[pl.ds(at, heads), :]
 
 
-def states_body(q, first, hc, *refs):
+def states_body(q, planes, first, hc, *refs):
     it = iter(refs)
-    x_ref, g_ref = next(it), next(it)
+    own = next(it)
     xg_in = [next(it) for _ in range(q - 1)]
     bundles = [next(it) for _ in range(q)]
-    rows16, states, f1s, ds, total_s, total_g, plane, bcs, cums, a_cols, steps = it
+    rows16, states, f1s, ds, totals, sent, plane, bcs, cums, a_cols, steps = it
     width = hc * HEAD_DIM
     y = in_group(q)
-    at = pl.multiple_of(y * (HEADS // q * HEAD_DIM) + first * HEAD_DIM, 128)
-    for k, ref in enumerate((x_ref, g_ref)):
-        rows16[k, y] = ref[:, pl.ds(at, width)]
+    for k in range(2):
+        rows16[k, y] = own[k, :, first * HEAD_DIM : first * HEAD_DIM + width]
     low = SPAN + first
     for r in range(q):
         block = lax.rem(y - r + q, q)
@@ -212,9 +199,15 @@
         forward = ds[b] * forward + states[0, b]
         backward = ds[q - 1 - b] * backward + states[1, q - 1 - b]
         through = through * ds[b]
-    total_s[...] = forward
-    total_g[...] = backward
+    totals[0] = forward
+    totals[1] = backward
     plane[...] = through
+    sent[...] = jnp.where(lax.div(lax.axis_index("seq"), q) < planes // 2, forward, backward)
+
+
+def relay_body(q, hop, came, totals, plane, sent):
+    up = lax.div(lax.axis_index("seq"), q) == hop + 1
+    sent[...] = jnp.where(up, totals[0], totals[1]) + plane[...] * came[...]
 
 
 def local_body(q, first, hc, skip, rows16, bcs, cums, a_cols, gx, gp):
@@ -333,29 +326,32 @@
     def across(value, r):
         return lax.ppermute(value, "dp", [(i, i ^ r) for i in range(n_dp)])
 
-    def pack(first, width):
-        scratch = (pltpu.VMEM((q - 1, 2, SPAN, width), BF16), pltpu.SemaphoreType.DMA((q - 1, 2)))
-        outs = loose([out((2, SPAN, width))] * (q - 1))
-        body = functools.partial(pack_body, q, group, first, width)
-        return staged(body, outs, scratch, name="pack", hbm=2)(x, g)
-
-    packed = pack(*spans[0])
+    def pack(first, width, keep):
+        scratch = (pltpu.VMEM((q - 1, 2, SPAN, width), BF16), pltpu.SemaphoreType.DMA((q, 2)))
+        outs = [out((2, SPAN, width))] * (q - 1) + [out((2, SPAN, group), BF16)] * keep
+        body = functools.partial(pack_body, q, group, first, width, keep)
+        return call(body, outs, scratch, name="pack", hbm=2)(x, g)
+
+    packed = pack(*spans[0], False)
     xg_in = [[swap(packed[r - 1], r) for r in range(1, q)]]
     bundles = call(
         functools.partial(project_body, q), [out((SPAN + heads, 2 * STATE))] * q, name="project"
-    )(tokens, proj_weight, log_decay[0], step_size[0])
+    )(*loose([tokens, proj_weight, log_decay[0], step_size[0]]))
     projected = bundles[0]
     bundles = [projected] + [swap(bundles[r], r) for r in range(1, q)]
-    packed = pack(*spans[1])
+    packed = pack(*spans[1], True)
+    own = packed[q - 1]
     got = [behind(packed[r - 1], projected) for r in range(1, q)]
     xg_in.append([swap(got[r - 1], r) for r in range(1, q)])
     columns_each = features // n_dp
     rows = columns_each // n_seq
     part = planes * rows
 
-    shapes = [out((length, columns_each))] + loose([out((length, columns_each))] * (n_dp - 1))
+    shapes = [out((length, columns_each))] * n_dp
     token_parts = list(
-        staged(functools.partial(deal_body, rows, q, planes), shapes, name="deal")(tokens)
+        call(functools.partial(deal_body, rows, q, planes), shapes, name="deal")(
+            [behind(tokens, own)]
+        )
     )
     for r in range(n_dp - 1, 0, -1):
         token_parts[r] = across(token_parts[r], r)
@@ -366,41 +362,46 @@
         state = out((STATE, wide[2]))
         outs = [
             out((4,) + wide, BF16), out((2,) + wide), out(wide), out((q, 1, wide[2])),
-            state, state, out((1, wide[2])),
+            out((2, STATE, wide[2])), state, out((1, wide[2])),
             out((q, SPAN, 2 * STATE), BF16), out((q, count, SPAN)), out((q, SPAN, count)),
         ]
         scratch = (pltpu.VMEM((q, count, SPAN), F32),)
-        body = functools.partial(states_body, q, first, count)
-        held.append(call(body, outs, scratch, name="states")(x, g, *xg_in[c], *bundles))
+        body = functools.partial(states_body, q, planes, first, count)
+        if c > 0:
+            xg_in[c] = [behind(v, held[c - 1][5]) for v in xg_in[c]]
+        held.append(call(body, outs, scratch, name="states")(own, *xg_in[c], *bundles))
         body = functools.partial(local_body, q, first, count)
         rows16, bcs, cums, a_cols = (held[c][k] for k in (0, 7, 8, 9))
         outs = [out(wide), out((q, SPAN, 2 * STATE))]
         local.append(call(body, outs, smem=1, name="local")(skip_gain, rows16, bcs, cums, a_cols))
 
-    ready = behind(tuple(token_parts), held[-1][6])
-    handed = staged(
-        functools.partial(hand_body, q, part), loose([out((n_dp, length, part))] * (q - 1)), name="hand"
-    )(ready[0], *loose(ready[1:]))
-    swapped = [swap(handed[r - 1], r) for r in range(1, q)]
-
-    z = seq // q
-    sent = [jnp.where(z < planes // 2, h[4], h[5]) for h in held]
+    sent = [h[5] for h in held]
     arrived = [[] for _ in held]
     for t in range(planes - 1):
         top = planes - 1 - t
         pairs = [(t * q + i, (t + 1) * q + i) for i in range(q)]
         pairs += [(top * q + i, (top - 1) * q + i) for i in range(q)]
         for c in range(PARTS):
-            if c == 0 and t == planes - 2:
+            if c == 0 and t == planes - 2 and t > 0:
                 sent[c] = behind(sent[c], *handed)
             came = lax.ppermute(sent[c], "seq", pairs)
             if t == max(planes - 3, 0):
                 came = behind(came, local[c])
-            if c == PARTS - 1 and t == planes - 2:
+            if c == PARTS - 1 and t == planes - 2 and t > 0:
                 came = behind(came, *swapped)
+            if c > 0 and t < planes - 2:
+                came = behind(came, sent[c - 1])
             arrived[c].append(came)
             if t < planes - 2:
-                sent[c] = jnp.where(z == t + 1, held[c][4], held[c][5]) + held[c][6] * came
+                (sent[c],) = call(
+                    functools.partial(relay_body, q, t), [out(came.shape)], name="relay"
+                )(came, held[c][4], held[c][6])
+        if t == 0:
+            ready = behind(tuple(token_parts), sent[0], sent[-1])
+            handed = call(
+                functools.partial(hand_body, q, part), [out((n_dp, length, part))] * (q - 1), name="hand"
+            )(*ready)
+            swapped = [swap(handed[r - 1], r) for r in range(1, q)]
 
     before, gx_parts = [], {}
     for c, (first, width) in enumerate(spans):
@@ -443,7 +444,7 @@
     for r in range(1, q):
         parts += [swap(gx_parts[r, c], r) for c in range(PARTS)]
     body = functools.partial(assemble_body, q, group, spans)
-    (grad_x,) = call(body, [out((length, q * group), BF16)], name="assemble")(*parts)
+    (grad_x,) = call(body, [[out((length, q * group), BF16)]], name="assemble")(*parts)
     return grad_x[None], grad_weight
 
 

time: 119 us -> 99.3 us (0.83)
  local copies, waits for them, and re-layouts: 16.3 us -> 1.61 us
  Pallas kernels: 22.2 us -> 12.1 us
  waiting for transfers between devices: 46.7 us -> 54.7 us
  other arithmetic: 6.74 us -> 0.73 us
  starting transfers between devices: 25.5 us -> 28.8 us
    unnamed x80 -> x10, local copies, waits for them, and re-layouts: 16.3 us -> 1.61 us
    pallas_call x13 -> x17, Pallas kernels: 22.2 us -> 12.1 us  [run(): pl.pallas_call(body, out_shape=tuple((o[0] if isinstance(o, list) else pl...]
    ppermute x6, waiting for transfers between devices: 14.1 us -> 22.8 us  [on_device(): came = lax.ppermute(sent[c], 'seq', pairs)]
    add x4 -> x0, other arithmetic: 4.46 us -> none  [on_device(): sent[c] = jnp.where(z == t + 1, held[c][4], held[c][5]) + held[c][6] * came]
    ppermute x7, waiting for transfers between devices: 22.2 us -> 25.8 us  [swap(): return lax.ppermute(value, 'seq', pairs)]
    ppermute x3, waiting for transfers between devices: 3.37 us -> 0.6 us  [on_device(): grad_weight = grad_weight + lax.ppermute(pieces[r], 'seq', pairs)]
    ppermute x3, starting transfers between devices: 3.19 us -> 5.05 us  [on_device(): grad_weight = grad_weight + lax.ppermute(pieces[r], 'seq', pairs)]
    ppermute x6, waiting for transfers between devices: 7.06 us -> 5.42 us  [across(): return lax.ppermute(value, 'dp', [(i, i ^ r) for i in range(n_dp)])]
  transfers between devices with their start and end apart: 22 -> 22, of which waited for: 6 -> 11; matrix products, arithmetic and copies ran while one was open for 5% -> 0% of each run, Pallas kernels for 15% -> 11%
where the time goes in v6:
time: 99.3 us; the launch traced here: 98.8 us
  waiting for transfers between devices  54.7 us (55%)
  starting transfers between devices  28.8 us (29%)
  Pallas kernels  12.1 us (12%)
  local copies, waits for them, and re-layouts  1.61 us (2%)
    ppermute x7, waiting for transfers between devices, swap(): return lax.ppermute(value, 'seq', pairs)  25.8 us
    ppermute x6, waiting for transfers between devices, on_device(): came = lax.ppermute(sent[c], 'seq', pairs)  22.8 us
    pallas_call x17, Pallas kernels, run(): pl.pallas_call(body, out_shape=tuple((o[0] if isinstance(o, list) else pl...  12.1 us
    ppermute x6, starting transfers between devices, on_device(): came = lax.ppermute(sent[c], 'seq', pairs)  11.7 us
    ppermute x7, starting transfers between devices, swap(): return lax.ppermute(value, 'seq', pairs)  9.39 us
    ppermute x6, waiting for transfers between devices, across(): return lax.ppermute(value, 'dp', [(i, i ^ r) for i in range(n_dp)])  5.42 us
    ppermute x3, starting transfers between devices, on_device(): grad_weight = grad_weight + lax.ppermute(pieces[r], 'seq', pairs)  5.05 us
    ppermute x6, starting transfers between devices, across(): return lax.ppermute(value, 'dp', [(i, i ^ r) for i in range(n_dp)])  2.65 us
  transfers between devices with their start and end apart: 22, of which 11 were waited for; matrix products, arithmetic and copies ran while one was open for 0% of the time, Pallas kernels for 11%

profile of v6, /device:TPU:0, one launch (start us, length us, event | category | flops | bytes accessed | tf_op | source)
XLA Modules:
  0.0 98.8 jit_solution(14056066993713270601)
XLA Ops:
  1.8 3.0 %collective-permute-start = (f32[2,128,640]{2,1,0:T(8,128)S(1)}, f32[2,128,640]{2,1,0:T(8,128)S(1)}, u32[]{:S(2)}, u32[]{:S(2)}) collective-permute-start(f32[2,128,640]{2,1,0:T(8,128)S(1)} %pack.3), channel_id=1, source_target_pairs={{0,1},{1,0},{2,3},{3,2},{4,5},{5,4},{6,7},{7,6},{8,9},{9,8},{10,11... | collective-permute-start | bytes 1966088 | tf_op jit(solution)/shard_map/ppermute | solution.py:324
  4.9 1.6 %copy-done.1 = bf16[4096,256]{1,0:T(8,128)(2,1)S(1)} copy-done((bf16[4096,256]{1,0:T(8,128)(2,1)S(1)}, bf16[4096,256]{1,0:T(8,128)(2,1)}, u32[]{:S(2)}) %copy-start.1) | copy-done | bytes 2097176
  8.3 1.9 %collective-permute-start.7 = (f32[2,128,384]{2,1,0:T(8,128)S(1)}, f32[2,128,384]{2,1,0:T(8,128)S(1)}, u32[]{:S(2)}, u32[]{:S(2)}) collective-permute-start(f32[2,128,384]{2,1,0:T(8,128)S(1)} %get-tuple-element.76), channel_id=1, source_target_pairs={{0,1},{1,0},{2,3},{3,2},{4,5},{5,4},{6,7},{7,6},{8,9},{9,8},{10,11... | collective-permute-start | bytes 1179656 | tf_op jit(solution)/shard_map/ppermute | solution.py:324
  10.5 1.6 %collective-permute-start.5 = (f32[128,1024]{1,0:T(8,128)S(1)}, f32[128,1024]{1,0:T(8,128)S(1)}, u32[]{:S(2)}, u32[]{:S(2)}) collective-permute-start(f32[128,1024]{1,0:T(8,128)S(1)} %get-tuple-element.73), channel_id=1, source_target_pairs={{0,16},{8,24},{16,0},{24,8},{1,17},{9,25},{17,1},{25,9},{2,18},{10... | collective-permute-start | bytes 1572872 | tf_op jit(solution)/shard_map/ppermute | solution.py:327
  12.1 11.5 %collective-permute-done.1.refs_3_ = f32[144,256]{1,0:T(8,128)S(1)} collective-permute-done((f32[144,256]{1,0:T(8,128)S(1)}, f32[144,256]{1,0:T(8,128)S(1)}, u32[]{:S(2)}, u32[]{:S(2)}) %collective-permute-start.1) | collective-permute-done | bytes 147488 | tf_op jit(solution)/shard_map/ppermute | solution.py:324
  23.6 1.4 %states.2 = (bf16[4,2,128,640]{3,2,1,0:T(8,128)(2,1)S(1)}, f32[2,2,128,640]{3,2,1,0:T(8,128)S(1)}, f32[2,128,640]{2,1,0:T(8,128)S(1)}, f32[2,1,640]{2,1,0:T(1,12...) custom-call(bf16[2,128,1024]{2,1,0:T(8,128)(2,1)S(1)} %get-tuple-ele, ...), custom_call_target="tpu_custom_call" | custom-call | tf_op jit(solution)/shard_map/states/pallas_call | solution.py:63
  25.0 4.0 %collective-permute-start.2 = (f32[128,640]{1,0:T(8,128)S(1)}, f32[128,640]{1,0:T(8,128)S(1)}, u32[]{:S(2)}, u32[]{:S(2)}) collective-permute-start(f32[128,640]{1,0:T(8,128)S(1)} %get-tuple-element.60), channel_id=1, source_target_pairs={{0,2},{1,3},{6,4},{7,5},{8,10},{9,11},{14,12},{15,13},{16,18},{17,... | collective-permute-start | bytes 983048 | tf_op jit(solution)/shard_map/ppermute | solution.py:387
  29.1 2.1 %collective-permute-done.7.refs_1_ = f32[2,128,384]{2,1,0:T(8,128)S(1)} collective-permute-done((f32[2,128,384]{2,1,0:T(8,128)S(1)}, f32[2,128,384]{2,1,0:T(8,128)S(1)}, u32[]{:S(2)}, u32[]{:S(2)}) %collective-permute-start.7) | collective-permute-done | bytes 393248 | tf_op jit(solution)/shard_map/ppermute | solution.py:324
  32.5 3.7 %collective-permute-start.8 = (f32[128,384]{1,0:T(8,128)S(1)}, f32[128,384]{1,0:T(8,128)S(1)}, u32[]{:S(2)}, u32[]{:S(2)}) collective-permute-start(f32[128,384]{1,0:T(8,128)S(1)} %get-tuple-element.78), channel_id=1, source_target_pairs={{0,2},{1,3},{6,4},{7,5},{8,10},{9,11},{14,12},{15,13},{16,18},{17,... | collective-permute-start | bytes 589832 | tf_op jit(solution)/shard_map/ppermute | solution.py:387
  36.6 4.7 %collective-permute-done.8.came.refs_0_ = f32[128,384]{1,0:T(8,128)S(1)} collective-permute-done((f32[128,384]{1,0:T(8,128)S(1)}, f32[128,384]{1,0:T(8,128)S(1)}, u32[]{:S(2)}, u32[]{:S(2)}) %collective-permute-start.8) | collective-permute-done | bytes 196640 | tf_op jit(solution)/shard_map/ppermute | solution.py:387
  41.5 1.6 %collective-permute-start.12 = (f32[4,128,512]{2,1,0:T(8,128)S(1)}, f32[4,128,512]{2,1,0:T(8,128)S(1)}, u32[]{:S(2)}, u32[]{:S(2)}) collective-permute-start(f32[4,128,512]{2,1,0:T(8,128)S(1)} %hand.1), channel_id=1, source_target_pairs={{0,1},{1,0},{2,3},{3,2},{4,5},{5,4},{6,7},{7,6},{8,9},{9,8},{10,11... | collective-permute-start | bytes 3145736 | tf_op jit(solution)/shard_map/ppermute | solution.py:324
  44.5 1.8 %local.2 = (f32[2,128,640]{2,1,0:T(8,128)S(1)}, f32[2,128,256]{2,1,0:T(8,128)S(1)}) custom-call(f32[32]{0:T(128)S(1)} %copy-done.4, bf16[4,2,128,640]{3,2,1,0:T(8,128)(2,1)S(1)} %get-tuple-element.63.rows16.refs_3_, bf16[2,128,256]{2,1,0:T(8,128)(2,1)S(1)} %get-tuple-element.64.bcs.refs_7_, f32[2,10,128]{2,1,0:T(8,128)S(1)} %get-tuple-element.65.cums, ...), custom_call_target="tpu_custom_call" | custom-call | tf_op jit(solution)/shard_map/local/pallas_call | solution.py:63
  46.4 1.3 %collective-permute-start.9 = (f32[128,640]{1,0:T(8,128)S(1)}, f32[128,640]{1,0:T(8,128)S(1)}, u32[]{:S(2)}, u32[]{:S(2)}) collective-permute-start(f32[128,640]{1,0:T(8,128)S(1)} %relay.5), channel_id=1, source_target_pairs={{4,6},{5,7},{2,0},{3,1},{12,14},{13,15},{10,8},{11,9},{20,22},{21,... | collective-permute-start | bytes 983048 | tf_op jit(solution)/shard_map/ppermute | solution.py:387
  47.7 1.6 %local.3 = (f32[2,128,384]{2,1,0:T(8,128)S(1)}, f32[2,128,256]{2,1,0:T(8,128)S(1)}) custom-call(f32[32]{0:T(128)S(1)} %copy-done.4, bf16[4,2,128,384]{3,2,1,0:T(8,128)(2,1)S(1)} %get-tuple-element.91.rows16.refs_3_, bf16[2,128,256]{2,1,0:T(8,128)(2,1)S(1)} %get-tuple-element.92.bcs.refs_7_, f32[2,6,128]{2,1,0:T(8,128)S(1)} %get-tuple-element.93.cums, ...), custom_call_target="tpu_custom_call" | custom-call | tf_op jit(solution)/shard_map/local/pallas_call | solution.py:63
  49.3 1.3 %collective-permute-start.11 = (f32[128,384]{1,0:T(8,128)S(1)}, f32[128,384]{1,0:T(8,128)S(1)}, u32[]{:S(2)}, u32[]{:S(2)}) collective-permute-start(f32[128,384]{1,0:T(8,128)S(1)} %relay.7), channel_id=1, source_target_pairs={{4,6},{5,7},{2,0},{3,1},{12,14},{13,15},{10,8},{11,9},{20,22},{21,... | collective-permute-start | bytes 589832 | tf_op jit(solution)/shard_map/ppermute | solution.py:387
  50.6 16.2 %collective-permute-done.9.refs_2_ = f32[128,640]{1,0:T(8,128)S(1)} collective-permute-done((f32[128,640]{1,0:T(8,128)S(1)}, f32[128,640]{1,0:T(8,128)S(1)}, u32[]{:S(2)}, u32[]{:S(2)}) %collective-permute-start.9) | collective-permute-done | bytes 327712 | tf_op jit(solution)/shard_map/ppermute | solution.py:387
  67.5 1.5 %collective-permute-done.11.refs_2_ = f32[128,384]{1,0:T(8,128)S(1)} collective-permute-done((f32[128,384]{1,0:T(8,128)S(1)}, f32[128,384]{1,0:T(8,128)S(1)}, u32[]{:S(2)}, u32[]{:S(2)}) %collective-permute-start.11) | collective-permute-done | bytes 196640 | tf_op jit(solution)/shard_map/ppermute | solution.py:387
  70.0 5.9 %collective-permute-done.15 = f32[2,128,256]{2,1,0:T(8,128)S(1)} collective-permute-done((f32[2,128,256]{2,1,0:T(8,128)S(1)}, f32[2,128,256]{2,1,0:T(8,128)S(1)}, u32[]{:S(2)}, u32[]{:S(2)}) %collective-permute-start.15) | collective-permute-done | bytes 262176 | tf_op jit(solution)/shard_map/ppermute | solution.py:324
  76.9 5.4 %collective-permute-done.17.refs_7_ = f32[2,128,256]{2,1,0:T(8,128)S(1)} collective-permute-done((f32[2,128,256]{2,1,0:T(8,128)S(1)}, f32[2,128,256]{2,1,0:T(8,128)S(1)}, u32[]{:S(2)}, u32[]{:S(2)}) %collective-permute-start.17) | collective-permute-done | bytes 262176 | tf_op jit(solution)/shard_map/ppermute | solution.py:327
  82.8 1.5 %collective-permute-start.14 = (f32[128,384]{1,0:T(8,128)S(1)}, f32[128,384]{1,0:T(8,128)S(1)}, u32[]{:S(2)}, u32[]{:S(2)}) collective-permute-start(f32[128,384]{1,0:T(8,128)S(1)} %get-tuple-element.106), channel_id=1, source_target_pairs={{0,1},{1,0},{2,3},{3,2},{4,5},{5,4},{6,7},{7,6},{8,9},{9,8},{10,11... | collective-permute-start | bytes 589832 | tf_op jit(solution)/shard_map/ppermute | solution.py:324
  86.3 2.0 %collective-permute-start.20 = (f32[128,256]{1,0:T(8,128)S(1)}, f32[128,256]{1,0:T(8,128)S(1)}, u32[]{:S(2)}, u32[]{:S(2)}) collective-permute-start(f32[128,256]{1,0:T(8,128)S(1)} %get-tuple-element.110), channel_id=1, source_target_pairs={{0,4},{1,5},{2,6},{3,7},{4,0},{5,1},{6,2},{7,3},{8,12},{9,13},{10,... | collective-permute-start | bytes 393224 | tf_op jit(solution)/shard_map/ppermute | solution.py:441
  88.3 2.0 %collective-permute-start.21 = (f32[128,256]{1,0:T(8,128)S(1)}, f32[128,256]{1,0:T(8,128)S(1)}, u32[]{:S(2)}, u32[]{:S(2)}) collective-permute-start(f32[128,256]{1,0:T(8,128)S(1)} %get-tuple-element.111), channel_id=1, source_target_pairs={{0,6},{1,7},{2,0},{3,1},{4,2},{5,3},{6,4},{7,5},{8,14},{9,15},{10,... | collective-permute-start | bytes 393224 | tf_op jit(solution)/shard_map/ppermute | solution.py:441
  90.3 2.6 %collective-permute-done.13.refs_2_ = f32[128,640]{1,0:T(8,128)S(1)} collective-permute-done((f32[128,640]{1,0:T(8,128)S(1)}, f32[128,640]{1,0:T(8,128)S(1)}, u32[]{:S(2)}, u32[]{:S(2)}) %collective-permute-start.13) | collective-permute-done | bytes 327712 | tf_op jit(solution)/shard_map/ppermute | solution.py:324
  92.8 3.8 %collective-permute-done.14.refs_3_ = f32[128,384]{1,0:T(8,128)S(1)} collective-permute-done((f32[128,384]{1,0:T(8,128)S(1)}, f32[128,384]{1,0:T(8,128)S(1)}, u32[]{:S(2)}, u32[]{:S(2)}) %collective-permute-start.14) | collective-permute-done | bytes 196640 | tf_op jit(solution)/shard_map/ppermute | solution.py:324
  (49 shorter events, 14.0 us)
Async XLA Ops:
  0.6 4.2 %copy-start.2 = (f32[1,32,128]{2,1,0:T(8,128)S(1)}, f32[1,32,128]{2,1,0:T(8,128)}, u32[]{:S(2)}) copy-start(f32[1,32,128]{2,1,0:T(8,128)} %param.11) | copy-start | bytes 49156
  0.6 4.2 %copy-start.3 = (f32[1,32,128]{2,1,0:T(8,128)S(1)}, f32[1,32,128]{2,1,0:T(8,128)}, u32[]{:S(2)}) copy-start(f32[1,32,128]{2,1,0:T(8,128)} %param.10) | copy-start | bytes 49156
  1.8 21.8 %collective-permute-start = (f32[2,128,640]{2,1,0:T(8,128)S(1)}, f32[2,128,640]{2,1,0:T(8,128)S(1)}, u32[]{:S(2)}, u32[]{:S(2)}) collective-permute-start(f32[2,128,640]{2,1,0:T(8,128)S(1)} %pack.3), channel_id=1, source_target_pairs={{0,1},{1,0},{2,3},{3,2},{4,5},{5,4},{6,7},{7,6},{8,9},{9,8},{10,11... | collective-permute-start | bytes 1966088 | tf_op jit(solution)/shard_map/ppermute | solution.py:324
  6.9 16.7 %collective-permute-start.1 = (f32[144,256]{1,0:T(8,128)S(1)}, f32[144,256]{1,0:T(8,128)S(1)}, u32[]{:S(2)}, u32[]{:S(2)}) collective-permute-start(f32[144,256]{1,0:T(8,128)S(1)} %get-tuple-element.59), channel_id=1, source_target_pairs={{0,1},{1,0},{2,3},{3,2},{4,5},{5,4},{6,7},{7,6},{8,9},{9,8},{10,11... | collective-permute-start | bytes 442376 | tf_op jit(solution)/shard_map/ppermute | solution.py:324
  8.3 22.9 %collective-permute-start.7 = (f32[2,128,384]{2,1,0:T(8,128)S(1)}, f32[2,128,384]{2,1,0:T(8,128)S(1)}, u32[]{:S(2)}, u32[]{:S(2)}) collective-permute-start(f32[2,128,384]{2,1,0:T(8,128)S(1)} %get-tuple-element.76), channel_id=1, source_target_pairs={{0,1},{1,0},{2,3},{3,2},{4,5},{5,4},{6,7},{7,6},{8,9},{9,8},{10,11... | collective-permute-start | bytes 1179656 | tf_op jit(solution)/shard_map/ppermute | solution.py:324
  10.5 30.9 %collective-permute-start.4 = (f32[128,1024]{1,0:T(8,128)S(1)}, f32[128,1024]{1,0:T(8,128)S(1)}, u32[]{:S(2)}, u32[]{:S(2)}) collective-permute-start(f32[128,1024]{1,0:T(8,128)S(1)} %get-tuple-element.72), channel_id=1, source_target_pairs={{0,8},{8,0},{16,24},{24,16},{1,9},{9,1},{17,25},{25,17},{2,10},{10... | collective-permute-start | bytes 1572872 | tf_op jit(solution)/shard_map/ppermute | solution.py:327
  10.5 30.9 %collective-permute-start.5 = (f32[128,1024]{1,0:T(8,128)S(1)}, f32[128,1024]{1,0:T(8,128)S(1)}, u32[]{:S(2)}, u32[]{:S(2)}) collective-permute-start(f32[128,1024]{1,0:T(8,128)S(1)} %get-tuple-element.73), channel_id=1, source_target_pairs={{0,16},{8,24},{16,0},{24,8},{1,17},{9,25},{17,1},{25,9},{2,18},{10... | collective-permute-start | bytes 1572872 | tf_op jit(solution)/shard_map/ppermute | solution.py:327
  23.6 17.8 %collective-permute-start.6 = (f32[128,1024]{1,0:T(8,128)S(1)}, f32[128,1024]{1,0:T(8,128)S(1)}, u32[]{:S(2)}, u32[]{:S(2)}) collective-permute-start(f32[128,1024]{1,0:T(8,128)S(1)} %get-tuple-element.74), channel_id=1, source_target_pairs={{0,24},{8,16},{16,8},{24,0},{1,25},{9,17},{17,9},{25,1},{2,26},{10... | collective-permute-start | bytes 1572872 | tf_op jit(solution)/shard_map/ppermute | solution.py:327
  25.0 11.5 %collective-permute-start.2 = (f32[128,640]{1,0:T(8,128)S(1)}, f32[128,640]{1,0:T(8,128)S(1)}, u32[]{:S(2)}, u32[]{:S(2)}) collective-permute-start(f32[128,640]{1,0:T(8,128)S(1)} %get-tuple-element.60), channel_id=1, source_target_pairs={{0,2},{1,3},{6,4},{7,5},{8,10},{9,11},{14,12},{15,13},{16,18},{17,... | collective-permute-start | bytes 983048 | tf_op jit(solution)/shard_map/ppermute | solution.py:387
  32.5 8.9 %collective-permute-start.8 = (f32[128,384]{1,0:T(8,128)S(1)}, f32[128,384]{1,0:T(8,128)S(1)}, u32[]{:S(2)}, u32[]{:S(2)}) collective-permute-start(f32[128,384]{1,0:T(8,128)S(1)} %get-tuple-element.78), channel_id=1, source_target_pairs={{0,2},{1,3},{6,4},{7,5},{8,10},{9,11},{14,12},{15,13},{16,18},{17,... | collective-permute-start | bytes 589832 | tf_op jit(solution)/shard_map/ppermute | solution.py:387
  41.5 27.4 %collective-permute-start.12 = (f32[4,128,512]{2,1,0:T(8,128)S(1)}, f32[4,128,512]{2,1,0:T(8,128)S(1)}, u32[]{:S(2)}, u32[]{:S(2)}) collective-permute-start(f32[4,128,512]{2,1,0:T(8,128)S(1)} %hand.1), channel_id=1, source_target_pairs={{0,1},{1,0},{2,3},{3,2},{4,5},{5,4},{6,7},{7,6},{8,9},{9,8},{10,11... | collective-permute-start | bytes 3145736 | tf_op jit(solution)/shard_map/ppermute | solution.py:324
  43.1 3.2 %collective-permute-start.3 = (f32[128,640]{1,0:T(8,128)S(1)}, f32[128,640]{1,0:T(8,128)S(1)}, u32[]{:S(2)}, u32[]{:S(2)}) collective-permute-start(f32[128,640]{1,0:T(8,128)S(1)} %relay.4), channel_id=1, source_target_pairs={{2,4},{3,5},{4,2},{5,3},{10,12},{11,13},{12,10},{13,11},{18,20},{1... | collective-permute-start | bytes 983048 | tf_op jit(solution)/shard_map/ppermute | solution.py:387
  43.8 5.4 %collective-permute-start.10 = (f32[128,384]{1,0:T(8,128)S(1)}, f32[128,384]{1,0:T(8,128)S(1)}, u32[]{:S(2)}, u32[]{:S(2)}) collective-permute-start(f32[128,384]{1,0:T(8,128)S(1)} %relay.6), channel_id=1, source_target_pairs={{2,4},{3,5},{4,2},{5,3},{10,12},{11,13},{12,10},{13,11},{18,20},{1... | collective-permute-start | bytes 589832 | tf_op jit(solution)/shard_map/ppermute | solution.py:387
  46.4 20.5 %collective-permute-start.9 = (f32[128,640]{1,0:T(8,128)S(1)}, f32[128,640]{1,0:T(8,128)S(1)}, u32[]{:S(2)}, u32[]{:S(2)}) collective-permute-start(f32[128,640]{1,0:T(8,128)S(1)} %relay.5), channel_id=1, source_target_pairs={{4,6},{5,7},{2,0},{3,1},{12,14},{13,15},{10,8},{11,9},{20,22},{21,... | collective-permute-start | bytes 983048 | tf_op jit(solution)/shard_map/ppermute | solution.py:387
  49.3 19.7 %collective-permute-start.11 = (f32[128,384]{1,0:T(8,128)S(1)}, f32[128,384]{1,0:T(8,128)S(1)}, u32[]{:S(2)}, u32[]{:S(2)}) collective-permute-start(f32[128,384]{1,0:T(8,128)S(1)} %relay.7), channel_id=1, source_target_pairs={{4,6},{5,7},{2,0},{3,1},{12,14},{13,15},{10,8},{11,9},{20,22},{21,... | collective-permute-start | bytes 589832 | tf_op jit(solution)/shard_map/ppermute | solution.py:387
  69.4 6.4 %collective-permute-start.15 = (f32[2,128,256]{2,1,0:T(8,128)S(1)}, f32[2,128,256]{2,1,0:T(8,128)S(1)}, u32[]{:S(2)}, u32[]{:S(2)}) collective-permute-start(f32[2,128,256]{2,1,0:T(8,128)S(1)} %get-tuple-element.107), channel_id=1, source_target_pairs={{0,1},{1,0},{2,3},{3,2},{4,5},{5,4},{6,7},{7,6},{8,9},{9,8},{10,11... | collective-permute-start | bytes 786440 | tf_op jit(solution)/shard_map/ppermute | solution.py:324
  75.9 6.4 %collective-permute-start.17 = (f32[2,128,256]{2,1,0:T(8,128)S(1)}, f32[2,128,256]{2,1,0:T(8,128)S(1)}, u32[]{:S(2)}, u32[]{:S(2)}) collective-permute-start(f32[2,128,256]{2,1,0:T(8,128)S(1)} %add.12.refs_5_), channel_id=1, source_target_pairs={{0,16},{8,24},{16,0},{24,8},{1,17},{9,25},{17,1},{25,9},{2,18},{10... | collective-permute-start | bytes 786440 | tf_op jit(solution)/shard_map/ppermute | solution.py:327
  76.9 7.4 %collective-permute-start.16 = (f32[2,128,256]{2,1,0:T(8,128)S(1)}, f32[2,128,256]{2,1,0:T(8,128)S(1)}, u32[]{:S(2)}, u32[]{:S(2)}) collective-permute-start(f32[2,128,256]{2,1,0:T(8,128)S(1)} %add.12.refs_5_), channel_id=1, source_target_pairs={{0,8},{8,0},{16,24},{24,16},{1,9},{9,1},{17,25},{25,17},{2,10},{10... | collective-permute-start | bytes 786440 | tf_op jit(solution)/shard_map/ppermute | solution.py:327
  82.3 2.0 %collective-permute-start.18 = (f32[2,128,256]{2,1,0:T(8,128)S(1)}, f32[2,128,256]{2,1,0:T(8,128)S(1)}, u32[]{:S(2)}, u32[]{:S(2)}) collective-permute-start(f32[2,128,256]{2,1,0:T(8,128)S(1)} %collective-permute-done.17.refs_7_), channel_id=1, source_target_pairs={{0,8},{8,0},{16,24},{24,16},{1,9},{9,1},{17,25},{25,17},{2,10},{10... | collective-permute-start | bytes 786440 | tf_op jit(solution)/shard_map/ppermute | solution.py:327
  82.3 10.5 %collective-permute-start.13 = (f32[128,640]{1,0:T(8,128)S(1)}, f32[128,640]{1,0:T(8,128)S(1)}, u32[]{:S(2)}, u32[]{:S(2)}) collective-permute-start(f32[128,640]{1,0:T(8,128)S(1)} %get-tuple-element.105), channel_id=1, source_target_pairs={{0,1},{1,0},{2,3},{3,2},{4,5},{5,4},{6,7},{7,6},{8,9},{9,8},{10,11... | collective-permute-start | bytes 983048 | tf_op jit(solution)/shard_map/ppermute | solution.py:324
  82.8 13.8 %collective-permute-start.14 = (f32[128,384]{1,0:T(8,128)S(1)}, f32[128,384]{1,0:T(8,128)S(1)}, u32[]{:S(2)}, u32[]{:S(2)}) collective-permute-start(f32[128,384]{1,0:T(8,128)S(1)} %get-tuple-element.106), channel_id=1, source_target_pairs={{0,1},{1,0},{2,3},{3,2},{4,5},{5,4},{6,7},{7,6},{8,9},{9,8},{10,11... | collective-permute-start | bytes 589832 | tf_op jit(solution)/shard_map/ppermute | solution.py:324
  85.2 12.3 %collective-permute-start.19 = (f32[128,256]{1,0:T(8,128)S(1)}, f32[128,256]{1,0:T(8,128)S(1)}, u32[]{:S(2)}, u32[]{:S(2)}) collective-permute-start(f32[128,256]{1,0:T(8,128)S(1)} %get-tuple-element.109), channel_id=1, source_target_pairs={{0,2},{1,3},{2,4},{3,5},{4,6},{5,7},{6,0},{7,1},{8,10},{9,11},{10,... | collective-permute-start | bytes 393224 | tf_op jit(solution)/shard_map/ppermute | solution.py:441
  86.3 11.8 %collective-permute-start.20 = (f32[128,256]{1,0:T(8,128)S(1)}, f32[128,256]{1,0:T(8,128)S(1)}, u32[]{:S(2)}, u32[]{:S(2)}) collective-permute-start(f32[128,256]{1,0:T(8,128)S(1)} %get-tuple-element.110), channel_id=1, source_target_pairs={{0,4},{1,5},{2,6},{3,7},{4,0},{5,1},{6,2},{7,3},{8,12},{9,13},{10,... | collective-permute-start | bytes 393224 | tf_op jit(solution)/shard_map/ppermute | solution.py:441
  88.3 9.8 %collective-permute-start.21 = (f32[128,256]{1,0:T(8,128)S(1)}, f32[128,256]{1,0:T(8,128)S(1)}, u32[]{:S(2)}, u32[]{:S(2)}) collective-permute-start(f32[128,256]{1,0:T(8,128)S(1)} %get-tuple-element.111), channel_id=1, source_target_pairs={{0,6},{1,7},{2,0},{3,1},{4,2},{5,3},{6,4},{7,5},{8,14},{9,15},{10,... | collective-permute-start | bytes 393224 | tf_op jit(solution)/shard_map/ppermute | solution.py:441
  (3 other events, 8.9 us)

commit v7 on v6

v7 whole, which is shorter than its diff:
```python
import functools

import jax
import jax.numpy as jnp
from jax import lax
from jax.experimental import pallas as pl
from jax.experimental.pallas import tpu as pltpu
from jax.sharding import PartitionSpec as P

HEADS = 32
HEAD_DIM = 64
STATE = 128
SPAN = 128
PARTS = 2
F32 = jnp.float32
BF16 = jnp.bfloat16
VMEM_LIMIT = 16 * 1024 * 1024


def group_size(n_seq):
    q = 1
    while n_seq % (4 * q) == 0 and HEADS // (2 * q) >= 4:
        q *= 2
    return q


def nn(a, b):
    return lax.dot_general(a, b, (((1,), (0,)), ((), ())), preferred_element_type=F32)


def nt(a, b):
    return lax.dot_general(a, b, (((1,), (1,)), ((), ())), preferred_element_type=F32)


def tn(a, b):
    return lax.dot_general(a, b, (((0,), (0,)), ((), ())), preferred_element_type=F32)


def terms(a):
    high = a.astype(BF16)
    rest = a - high.astype(F32)
    mid = rest.astype(BF16)
    return high, mid, (rest - mid.astype(F32)).astype(BF16)


def head_chunks(heads):
    first = 2 * (heads * 5 // 16)
    return [(0, first), (first, heads - first)]


def call(body, outs, scratch=(), name=None, smem=0, hbm=0):
    def run(*args):
        args = list(args)
        for k in range(smem, len(args)):
            if isinstance(args[k], list):
                args[k] = args[k][0]
            else:
                place = pltpu.HBM if k < smem + hbm else pltpu.VMEM
                args[k] = pltpu.with_memory_space_constraint(args[k], place)
        specs = [pl.BlockSpec(memory_space=pltpu.SMEM)] * smem
        specs += [pl.BlockSpec(memory_space=pltpu.HBM)] * hbm
        specs += [pl.BlockSpec(memory_space=pltpu.VMEM)] * (len(args) - smem - hbm)
        return pl.pallas_call(
            body,
            out_shape=tuple(o[0] if isinstance(o, list) else pltpu.VMEM(o.shape, o.dtype) for o in outs),
            in_specs=specs,
            out_specs=tuple(pl.BlockSpec(memory_space=pltpu.VMEM) for _ in outs),
            scratch_shapes=scratch,
            compiler_params=pltpu.CompilerParams(vmem_limit_bytes=VMEM_LIMIT),
            name=name,
        )(*args)

    return run


def loose(values):
    return [[value] for value in values]


def in_group(q):
    return lax.rem(lax.axis_index("seq"), q)


def out(shape, dtype=F32):
    return jax.ShapeDtypeStruct(shape, dtype)


def iotas():
    rows = lax.broadcasted_iota(jnp.int32, (SPAN, SPAN), 0)
    cols = lax.broadcasted_iota(jnp.int32, (SPAN, SPAN), 1)
    return rows, cols


def columns(ref, start, width):
    return ref[:, pl.ds(pl.multiple_of(start, 128), width)]


def pack_body(q, group, first, width, x, g, *refs):
    packed, own, (stage, sems) = refs[: q - 1], refs[q - 1], refs[q:]
    y = in_group(q)
    copies = {}
    for r in range(1, q):
        at = pl.multiple_of(lax.bitwise_xor(y, r) * group + first, 128)
        for k, source in enumerate((x, g)):
            copies[r, k] = pltpu.make_async_copy(
                source.at[:, pl.ds(at, width)], stage.at[r - 1, k], sems.at[r, k]
            )
            copies[r, k].start()
    at = pl.multiple_of(y * group, 128)
    for k, source in enumerate((x, g)):
        copies[0, k] = pltpu.make_async_copy(source.at[:, pl.ds(at, group)], own.at[k], sems.at[0, k])
        copies[0, k].start()
    blocks = width // 128
    for r in range(1, q):
        for k in range(2):
            copies[r, k].wait()
            for b in range(blocks):
                at = (k * blocks + b) * SPAN
                packed[r - 1][at : at + SPAN, :] = stage[r - 1, k, :, b * 128 : b * 128 + 128].astype(F32)
    for k in range(2):
        copies[0, k].wait()


def deal_body(bit, offsets, *refs):
    sent = refs[-1]
    for k, (ref, offset) in enumerate(zip(refs, offsets)):
        sent[k * bit : (k + 1) * bit] = ref[offset + bit : offset + 2 * bit]


def open_body(q, n_dp, group, width, tokens, weight, x, g, decay, step, *refs):
    firsts, (bundle, kept, dealt, held_t, held_w, stage, sems) = refs[: q - 1], refs[q - 1 :]
    heads = HEADS // q
    y = in_group(q)
    copies = {}
    for r in range(1, q):
        at = pl.multiple_of(lax.bitwise_xor(y, r) * group, 128)
        for k, source in enumerate((x, g)):
            copies[r, k] = pltpu.make_async_copy(
                source.at[:, pl.ds(at, width)], stage.at[r - 1, k], sems.at[r, k]
            )
    copies[0, 0] = pltpu.make_async_copy(tokens, held_t, sems.at[0, 0])
    copies[0, 1] = pltpu.make_async_copy(weight, held_w, sems.at[0, 1])
    for copy in copies.values():
        copy.start()
    blocks = width // 128
    for r in range(1, q):
        for k in range(2):
            copies[r, k].wait()
            for b in range(blocks):
                at = (k * blocks + b) * SPAN
                firsts[r - 1][at : at + SPAN, :] = stage[r - 1, k, :, b * 128 : b * 128 + 128].astype(F32)
    copies[0, 0].wait()
    copies[0, 1].wait()
    proj = nn(held_t[...], held_w[...]).astype(BF16).astype(F32)
    base = 2 * blocks * SPAN
    for r in range(q):
        own = pl.multiple_of(lax.bitwise_xor(y, r) * heads, heads)
        target, at = (firsts[r - 1], base) if r else (bundle, 0)
        target[at : at + SPAN, :] = proj[:, :STATE]
        target[at + SPAN : at + 2 * SPAN, :] = proj[:, STATE:]
        target[at + 2 * SPAN : at + 2 * SPAN + heads, :] = decay[pl.ds(own, heads), :]
        target[at + 2 * SPAN + heads :, :] = step[pl.ds(own, heads), :]
    each = tokens.shape[1] // n_dp
    dp = lax.axis_index("dp")
    for r in range(n_dp):
        to, at = (kept, r) if r < n_dp // 2 else (dealt, r - n_dp // 2)
        to[at] = columns(held_t, lax.bitwise_xor(dp, r) * each, each).astype(F32)


def states_body(q, planes, first, hc, base, *refs):
    it = iter(refs)
    own = next(it)
    bundles = [next(it) for _ in range(q)]
    xg_in = [next(it) for _ in range(q - 1)] if first else bundles[1:]
    rows16, states, f1s, ds, totals, sent, plane, bcs, cums, a_cols, steps = it
    width = hc * HEAD_DIM
    heads = HEADS // q
    blocks = width // 128
    y = in_group(q)
    for k in range(2):
        rows16[k, y] = own[k, :, first * HEAD_DIM : first * HEAD_DIM + width]
    for r in range(q):
        block = lax.bitwise_xor(y, r)
        if r > 0:
            for k in range(2):
                for b in range(blocks):
                    at = (k * blocks + b) * SPAN
                    rows16[k, block, :, b * 128 : b * 128 + 128] = xg_in[r - 1][at : at + SPAN, :].astype(BF16)
        low = base if r else 0
        bcs[block, :, :STATE] = bundles[r][low : low + SPAN, :].astype(BF16)
        bcs[block, :, STATE:] = bundles[r][low + SPAN : low + 2 * SPAN, :].astype(BF16)
        low += 2 * SPAN + first
        cums[block] = bundles[r][low : low + hc, :]
        steps[block] = bundles[r][low + heads : low + heads + hc, :]
    rows, cols = iotas()
    tri = jnp.where(rows <= cols, 1.0, 0.0).astype(BF16)
    head_of = lax.broadcasted_iota(jnp.int32, (hc, width), 1) // HEAD_DIM
    spread = head_of == lax.broadcasted_iota(jnp.int32, (hc, width), 0)
    spread = jnp.where(spread, 1.0, 0.0).astype(BF16)
    for b in range(q):
        cum = sum(nn(term, tri) for term in terms(cums[b]))
        a = cum - jnp.log(steps[b])
        cums[b] = cum
        cum_c, a_c = cum.T, a.T
        a_cols[b] = a_c
        cum_x = sum(nn(term, spread) for term in terms(cum_c))
        a_x = sum(nn(term, spread) for term in terms(a_c))
        total = cum_x[SPAN - 1 : SPAN, :]
        f1 = jnp.exp(total - a_x)
        f1s[b] = f1
        ds[b] = jnp.exp(total)
        weighted = (rows16[0, b].astype(F32) * f1).astype(BF16)
        scaled = (rows16[1, b].astype(F32) * jnp.exp(cum_x)).astype(BF16)
        rows16[2, b] = weighted
        rows16[3, b] = scaled
        states[0, b] = tn(bcs[b, :, :STATE], weighted)
        states[1, b] = tn(bcs[b, :, STATE:], scaled)
    forward, backward, through = states[0, 0], states[1, q - 1], ds[0]
    for b in range(1, q):
        forward = ds[b] * forward + states[0, b]
        backward = ds[q - 1 - b] * backward + states[1, q - 1 - b]
        through = through * ds[b]
    totals[0] = forward
    totals[1] = backward
    plane[...] = through
    sent[...] = jnp.where(lax.div(lax.axis_index("seq"), q) < planes // 2, forward, backward)


def relay_body(q, hop, came, totals, plane, sent):
    up = lax.div(lax.axis_index("seq"), q) == hop + 1
    sent[...] = jnp.where(up, totals[0], totals[1]) + plane[...] * came[...]


def local_body(q, first, hc, skip, rows16, bcs, cums, a_cols, gx, gp):
    rows, cols = iotas()
    causal = rows <= cols
    low = lax.broadcasted_iota(jnp.int32, (SPAN, 128), 1) < HEAD_DIM
    skip_at = in_group(q) * (HEADS // q) + first
    for b in range(q):
        b_cols, c_cols = bcs[b, :, :STATE], bcs[b, :, STATE:]
        kernel = nt(b_cols, c_cols)
        mixing = jnp.zeros((SPAN, SPAN), F32)
        for pair in range(hc // 2):
            at = slice(pair * 128, pair * 128 + 128)
            x, g = rows16[0, b, :, at], rows16[1, b, :, at]
            parts = []
            for half in range(2):
                h = 2 * pair + half
                gap = cums[b, h : h + 1, :] - a_cols[b, :, h : h + 1]
                decay = jnp.exp(jnp.where(causal, gap, -jnp.inf))
                picked = jnp.where(low if half == 0 else ~low, x, jnp.zeros_like(x))
                mixing += decay * nt(picked, g)
                parts.append(nn((decay * kernel).astype(BF16), g))
            gains = jnp.where(low, skip[skip_at + 2 * pair], skip[skip_at + 2 * pair + 1])
            gx[b, :, at] = jnp.where(low, parts[0], parts[1]) + gains * g.astype(F32)
        mixed = mixing.astype(BF16)
        gp[b, :, :STATE] = nn(mixed, c_cols)
        gp[b, :, STATE:] = tn(mixed, b_cols)


def final_body(q, planes, more, *refs):
    it = iter(refs)
    got = [next(it) for _ in range(planes - 1)]
    rows16, states, f1s, ds, bcs, gx, gp = [next(it) for _ in range(7)]
    before = next(it) if more else None
    gx_out = [next(it) for _ in range(q)]
    gp_sent = [next(it) for _ in range(q)] if more else []
    gp_out, gx_all = it
    y = in_group(q)
    z = lax.div(lax.axis_index("seq"), q)
    start = after = jnp.zeros(got[0].shape, F32)
    for t in range(planes - 1):
        came = got[t][...]
        start += jnp.where(z == t + 1, 1.0, 0.0) * came
        after += jnp.where(z == planes - 2 - t, 1.0, 0.0) * came
    for b in range(q):
        part = gp[b, :, STATE:] + nt(rows16[3, b], start.astype(BF16))
        gp_out[b, :, STATE:] = part if before is None else part + before[b, :, STATE:]
        if b < q - 1:
            start = ds[b] * start + states[0, b]
    for b in range(q - 1, -1, -1):
        rounded = after.astype(BF16)
        gx_all[b] = gx[b] + f1s[b] * nn(bcs[b, :, :STATE], rounded)
        part = gp[b, :, :STATE] + nt(rows16[2, b], rounded)
        gp_out[b, :, :STATE] = part if before is None else part + before[b, :, :STATE]
        if b > 0:
            after = ds[b] * after + states[1, b]
    for r in range(q):
        gx_out[r][...] = gx_all[lax.bitwise_xor(y, r)]
        if more:
            gp_sent[r][...] = gp_out[lax.bitwise_xor(y, r)]


def assemble_body(q, group, spans, *refs):
    parts, result = refs[:-1], refs[-1]
    y = in_group(q)
    for r in range(q):
        for c, (first, width) in enumerate(spans):
            at = pl.multiple_of(lax.bitwise_xor(y, r) * group + first, 128)
            result[:, pl.ds(at, width)] = parts[c * q + r][...].astype(BF16)


def weight_body(n_dp, n_seq, rows, scale, places, *refs):
    arrays = 1 + max(k for k, _ in places)
    tokens, grads, refs = refs[:arrays], refs[arrays : arrays + n_dp], refs[arrays + n_dp :]
    outs, (held, factors, products) = refs[:4], refs[4:]
    width = n_seq * rows
    half = n_seq // 4
    seq = lax.axis_index("seq")
    for r in range(n_dp):
        held[r] = tokens[places[r][0]][places[r][1]].astype(BF16)
        factors[r] = grads[r][...].astype(BF16)
    total = tn(held[...].reshape(n_dp * SPAN, width), factors[...].reshape(n_dp * SPAN, 2 * STATE))
    products[...] = (total * scale).reshape(n_seq, rows, 2 * STATE)
    for k in range(2 * half):
        near, at = 1 - k // half, k % half
        for other in range(2):
            outs[2 * near + other][at] = products[lax.bitwise_xor(seq, 2 * k + other)]


def behind(value, *others):
    return lax.optimization_barrier((value,) + others)[0]


def on_device(layer_input, proj_weight, inputs, step_size, log_decay, skip_gain, grad_out):
    n_seq, n_dp = lax.axis_size("seq"), lax.axis_size("dp")
    q = group_size(n_seq)
    planes = n_seq // q
    heads = HEADS // q
    group = heads * HEAD_DIM
    chunks = head_chunks(heads)
    spans = [(first * HEAD_DIM, count * HEAD_DIM) for first, count in chunks]
    tokens, x, g = layer_input[0], inputs[0], grad_out[0]
    length, features = tokens.shape
    seq = lax.axis_index("seq")

    def swap(value, r):
        return lax.ppermute(value, "seq", [(i, i ^ r) for i in range(n_seq)])

    def across(value, r):
        return lax.ppermute(value, "dp", [(i, i ^ r) for i in range(n_dp)])

    widths = [width for _, width in spans]
    base = 2 * widths[0]
    tail = 2 * SPAN + 2 * heads
    columns_each = features // n_dp
    rows = columns_each // n_seq
    body = functools.partial(open_body, q, n_dp, group, widths[0])
    scratch = (
        pltpu.VMEM(tokens.shape, BF16), pltpu.VMEM(proj_weight.shape, BF16),
        pltpu.VMEM((q - 1, 2, SPAN, widths[0]), BF16), pltpu.SemaphoreType.DMA((q, 2)),
    )
    outs = [out((base + tail, 128))] * (q - 1) + [out((tail, 128))]
    outs += [out((n_dp // 2, length, columns_each))] * 2
    opened = call(body, outs, scratch, name="open", hbm=4)(
        tokens, proj_weight, x, g, [log_decay[0]], [step_size[0]]
    )
    bundles = [opened[q - 1]] + [swap(opened[r - 1], r) for r in range(1, q)]
    body = functools.partial(pack_body, q, group, *spans[1])
    scratch = (pltpu.VMEM((q - 1, 2, SPAN, widths[1]), BF16), pltpu.SemaphoreType.DMA((q, 2)))
    outs = [out((2 * widths[1], 128))] * (q - 1) + [out((2, SPAN, group), BF16)]
    packed = call(body, outs, scratch, name="pack", hbm=2)(x, g)
    own = packed[q - 1]
    bit = n_dp // 2
    sources = {0: (opened[q], 0), bit: (across(opened[q + 1], bit), 0)}
    second = [swap(behind(packed[r - 1], opened[q - 1]), r) for r in range(1, q)]

    def hop(value, t):
        top = planes - 1 - t
        pairs = [(t * q + i, (t + 1) * q + i) for i in range(q)]
        pairs += [(top * q + i, (top - 1) * q + i) for i in range(q)]
        return lax.ppermute(value, "seq", pairs)

    held, local, extra = [], [], []
    for c, (first, count) in enumerate(chunks):
        wide = (q, SPAN, count * HEAD_DIM)
        state = out((STATE, wide[2]))
        outs = [
            out((4,) + wide, BF16), out((2,) + wide), out(wide), out((q, 1, wide[2])),
            out((2, STATE, wide[2])), state, out((1, wide[2])),
            out((q, SPAN, 2 * STATE), BF16), out((q, count, SPAN)), out((q, SPAN, count)),
        ]
        scratch = (pltpu.VMEM((q, count, SPAN), F32),)
        body = functools.partial(states_body, q, planes, first, count, base)
        if c > 0:
            ahead = hop(held[0][5], 0)
            extra = [behind(v, *local[0]) for v in second]
        held.append(call(body, outs, scratch, name="states")(own, *bundles, *extra))
        body = functools.partial(local_body, q, first, count)
        rows16, bcs, cums, a_cols = (held[c][k] for k in (0, 7, 8, 9))
        outs = [out(wide), out((q, SPAN, 2 * STATE))]
        local.append(call(body, outs, smem=1, name="local")(skip_gain, rows16, bcs, cums, a_cols))

    sent = [h[5] for h in held]
    arrived = [[] for _ in held]
    for t in range(planes - 1):
        for c in range(PARTS):
            if c == 1 and t == 0:
                sent[c] = behind(sent[c], ahead)
            came = ahead if c == t == 0 else hop(sent[c], t)
            if t == max(planes - 3, 0):
                came = behind(came, local[c])
            if c > 0 and t < planes - 2:
                came = behind(came, sent[c - 1])
            arrived[c].append(came)
            if t < planes - 2:
                (sent[c],) = call(
                    functools.partial(relay_body, q, t), [out(came.shape)], name="relay"
                )(came, held[c][4], held[c][6])

    before, gx_parts, returned = [], [], []
    for c, (first, width) in enumerate(spans):
        rows16, states, f1s, ds, bcs = (held[c][k] for k in (0, 1, 2, 3, 7))
        block, all_blocks = (SPAN, 2 * STATE), (q, SPAN, 2 * STATE)
        outs = [out((SPAN, width))] * q + ([out(block)] * q if before else [out(all_blocks)])
        scratch = (pltpu.VMEM((q, SPAN, width), F32),)
        if before:
            scratch = (pltpu.VMEM(all_blocks, F32),) + scratch
        body = functools.partial(final_body, q, planes, bool(before))
        done = call(body, outs, scratch, name="final")(
            *arrived[c], rows16, states, f1s, ds, bcs, *local[c], *before
        )
        gx_parts.append(list(done[:q]))
        before = list(done[q:])
        if c == 0:
            returned.append([swap(done[r], r) for r in range(1, q)])
            arrived[1][-1] = behind(arrived[1][-1], *returned[0])

    while bit > 1:
        bit //= 2
        order = list(sources)
        arrays = behind(tuple(sources[r][0] for r in order), before[0])
        body = functools.partial(deal_body, bit, [sources[r][1] for r in order])
        shape = (len(order) * bit, length, columns_each)
        (dealt,) = call(body, [out(shape)], name="deal")(*arrays)
        got = across(dealt, bit)
        for k, r in enumerate(order):
            sources[r ^ bit] = got, k * bit

    gp = before[0]
    for r in range(1, q):
        gp = gp + swap(before[r], r)
    returned.append([swap(behind(gx_parts[1][r], gp), r) for r in range(1, q)])
    grads = {0: behind(gp, *(v for v, _ in sources.values()))}
    bit = n_dp // 2
    while bit:
        for r in list(grads):
            grads[r ^ bit] = across(grads[r], bit)
        bit //= 2
    scale = 1.0 / (length * n_seq)
    arrays = list({id(v): v for v, _ in sources.values()}.values())
    places = [([v is a for a in arrays].index(True), at) for v, at in (sources[r] for r in range(n_dp))]
    args = arrays + [behind(grads[0], *returned[1])] + [grads[r] for r in range(1, n_dp)]
    scratch = (
        pltpu.VMEM((n_dp, SPAN, columns_each), BF16),
        pltpu.VMEM((n_dp, SPAN, 2 * STATE), BF16),
        pltpu.VMEM((n_seq, rows, 2 * STATE), F32),
    )
    body = functools.partial(weight_body, n_dp, n_seq, rows, scale, places)
    half = n_seq // 4
    far, far_sent, near, near_sent = call(body, [out((half, rows, 2 * STATE))] * 4, scratch, name="weight")(*args)
    far_in = swap(far_sent, 1)
    near_in = swap(behind(near_sent, far_sent), 1)
    far = far + far_in
    came = [swap(far[k], 2 * (half + k)) for k in range(half)]
    near = near + near_in
    came += [swap(near[k], 2 * k) for k in range(1, half)]
    grad_weight = near[0]
    for part in came:
        grad_weight = grad_weight + part

    body = functools.partial(assemble_body, q, group, spans)
    parts = [v for c in range(PARTS) for v in (gx_parts[c][0], *returned[c])]
    (grad_x,) = call(body, [[out((length, q * group), BF16)]], name="assemble")(*parts)
    return grad_x[None], grad_weight


def solution(mesh):
    return jax.shard_map(
        on_device,
        mesh=mesh,
        in_specs=(
            P("dp", "seq", None),
            P(),
            P("dp", "seq", None),
            P("dp", None, "seq"),
            P("dp", None, "seq"),
            P(),
            P("dp", "seq", None),
        ),
        out_specs=(P("dp", "seq", None), P(("dp", "seq"), None)),
        check_vma=False,
    )
```

time: 99.3 us -> 100 us (level)
  waiting for transfers between devices: 54.7 us -> 46.7 us
  starting transfers between devices: 28.8 us -> 33.7 us
  Pallas kernels: 12.1 us -> 16.7 us
    ppermute x6 -> x5, waiting for transfers between devices: 5.42 us -> 0.84 us  [across(): return lax.ppermute(value, 'dp', [(i, i ^ r) for i in range(n_dp)])]
    pallas_call x17 -> x11, Pallas kernels: 12.1 us -> 16.7 us  [run(): pl.pallas_call(body, out_shape=tuple((o[0] if isinstance(o, list) else pl...]
    ppermute x16 -> x22, starting transfers between devices: 26.1 us -> 29.9 us  [the longest x20 25.6 us: swap(): return lax.ppermute(value, 'seq', [(i, i ^ r) for i in range(n_seq)])]
    ppermute x16 -> x22, waiting for transfers between devices: 49.3 us -> 45.8 us  [the longest x20 45.8 us: swap(): return lax.ppermute(value, 'seq', [(i, i ^ r) for i in range(n_seq)])]
    ppermute x6 -> x5, starting transfers between devices: 2.65 us -> 3.79 us  [across(): return lax.ppermute(value, 'dp', [(i, i ^ r) for i in range(n_dp)])]
  transfers between devices with their start and end apart: 22 -> 27, of which waited for: 11 -> 16; matrix products, arithmetic and copies ran while one was open for 0% -> 0% of each run, Pallas kernels for 11% -> 13%
where the time goes in v7:
time: 100 us
  waiting for transfers between devices  46.7 us (47%)
  starting transfers between devices  33.7 us (34%)
  Pallas kernels  16.7 us (17%)
  local copies, waits for them, and re-layouts  1.46 us (1%)
    ppermute x20, waiting for transfers between devices, swap(): return lax.ppermute(value, 'seq', [(i, i ^ r) for i in range(n_seq)])  45.8 us
    ppermute x20, starting transfers between devices, swap(): return lax.ppermute(value, 'seq', [(i, i ^ r) for i in range(n_seq)])  25.6 us
    pallas_call x11, Pallas kernels, run(): pl.pallas_call(body, out_shape=tuple((o[0] if isinstance(o, list) else pl...  16.7 us
    ppermute x2, starting transfers between devices, hop(): return lax.ppermute(value, 'seq', pairs)  4.27 us
    ppermute x5, starting transfers between devices, across(): return lax.ppermute(value, 'dp', [(i, i ^ r) for i in range(n_dp)])  3.79 us
  transfers between devices with their start and end apart: 27, of which 16 were waited for; matrix products, arithmetic and copies ran while one was open for 0% of the time, Pallas kernels for 13%

profile of v7, /device:TPU:0, one launch (start us, length us, event | category | flops | bytes accessed | tf_op | source)
XLA Modules:
  0.0 100.0 jit_solution(12602603821379803482)
XLA Ops:
  2.1 2.8 %open.1 = (f32[784,128]{1,0:T(8,128)S(1)}, f32[784,128]{1,0:T(8,128)S(1)}, f32[784,128]{1,0:T(8,128)S(1)}, f32[272,128]{1,0:T(8,128)S(1)}, f32[2,128,1024]{2,1,0:T(8,128)S(1)}, /*index=5*/f32[2,128,1024]{2,1,0:T(8,128)S(1)}) custom-call(bf16[128,4096]{1,0:T(8,128)(2,1)} %bitcast.26, bf16[4096,256]{1,0:T(8,128)(2,1)} %weight.2, bf16[128,2048]{1,0:T(8,128)(2,1)} %bitcast.22, ...), custom_call_target="tpu_custom_call" | custom-call | tf_op jit(solution)/shard_map/open/pallas_call | solution.py:63
  4.9 3.0 %collective-permute-start.17 = (f32[2,128,1024]{2,1,0:T(8,128)S(1)}, f32[2,128,1024]{2,1,0:T(8,128)S(1)}, u32[]{:S(2)}, u32[]{:S(2)}) collective-permute-start(f32[2,128,1024]{2,1,0:T(8,128)S(1)} %get-tuple-element.122), channel_id=1, source_target_pairs={{0,16},{8,24},{16,0},{24,8},{1,17},{9,25},{17,1},{25,9},{2,18},{10... | collective-permute-start | bytes 3145736 | tf_op jit(solution)/shard_map/ppermute | solution.py:341
  9.4 1.6 %collective-permute-start.1 = (f32[784,128]{1,0:T(8,128)S(1)}, f32[784,128]{1,0:T(8,128)S(1)}, u32[]{:S(2)}, u32[]{:S(2)}) collective-permute-start(f32[784,128]{1,0:T(8,128)S(1)} %get-tuple-element.70), channel_id=1, source_target_pairs={{0,2},{1,3},{2,0},{3,1},{4,6},{5,7},{6,4},{7,5},{8,10},{9,11},{10,... | collective-permute-start | bytes 1204232 | tf_op jit(solution)/shard_map/ppermute | solution.py:338
  12.6 2.6 %collective-permute-start.9 = (f32[512,128]{1,0:T(8,128)S(1)}, f32[512,128]{1,0:T(8,128)S(1)}, u32[]{:S(2)}, u32[]{:S(2)}) collective-permute-start(f32[512,128]{1,0:T(8,128)S(1)} %get-tuple-element.94), channel_id=1, source_target_pairs={{0,3},{1,2},{2,1},{3,0},{4,7},{5,6},{6,5},{7,4},{8,11},{9,10},{10,... | collective-permute-start | bytes 786440 | tf_op jit(solution)/shard_map/ppermute | solution.py:338
  15.2 4.0 %collective-permute-done.refs_2_ = f32[784,128]{1,0:T(8,128)S(1)} collective-permute-done((f32[784,128]{1,0:T(8,128)S(1)}, f32[784,128]{1,0:T(8,128)S(1)}, u32[]{:S(2)}, u32[]{:S(2)}) %collective-permute-start) | collective-permute-done | bytes 401440 | tf_op jit(solution)/shard_map/ppermute | solution.py:338
  19.2 1.6 %collective-permute-start.8 = (f32[512,128]{1,0:T(8,128)S(1)}, f32[512,128]{1,0:T(8,128)S(1)}, u32[]{:S(2)}, u32[]{:S(2)}) collective-permute-start(f32[512,128]{1,0:T(8,128)S(1)} %get-tuple-element.91), channel_id=1, source_target_pairs={{0,2},{1,3},{2,0},{3,1},{4,6},{5,7},{6,4},{7,5},{8,10},{9,11},{10,... | collective-permute-start | bytes 786440 | tf_op jit(solution)/shard_map/ppermute | solution.py:338
  22.3 8.0 %collective-permute-done.2.refs_4_ = f32[784,128]{1,0:T(8,128)S(1)} collective-permute-done((f32[784,128]{1,0:T(8,128)S(1)}, f32[784,128]{1,0:T(8,128)S(1)}, u32[]{:S(2)}, u32[]{:S(2)}) %collective-permute-start.2) | collective-permute-done | bytes 401440 | tf_op jit(solution)/shard_map/ppermute | solution.py:338
  30.3 3.0 %states.2 = (bf16[4,4,128,256]{3,2,1,0:T(8,128)(2,1)S(1)}, f32[2,4,128,256]{3,2,1,0:T(8,128)S(1)}, f32[4,128,256]{2,1,0:T(8,128)S(1)}, f32[4,1,256]{2,1,0:T(1,12...) custom-call(bf16[2,128,512]{2,1,0:T(8,128)(2,1)S(1)} %get-tuple-elem, ...), custom_call_target="tpu_custom_call" | custom-call | tf_op jit(solution)/shard_map/states/pallas_call | solution.py:63
  33.2 2.6 %collective-permute-start.3 = (f32[128,256]{1,0:T(8,128)S(1)}, f32[128,256]{1,0:T(8,128)S(1)}, u32[]{:S(2)}, u32[]{:S(2)}) collective-permute-start(f32[128,256]{1,0:T(8,128)S(1)} %get-tuple-element.72), channel_id=1, source_target_pairs={{0,4},{1,5},{2,6},{3,7},{4,0},{5,1},{6,2},{7,3},{8,12},{9,13},{10,... | collective-permute-start | bytes 393224 | tf_op jit(solution)/shard_map/ppermute | solution.py:372
  35.8 2.1 %local.2 = (f32[4,128,256]{2,1,0:T(8,128)S(1)}, f32[4,128,256]{2,1,0:T(8,128)S(1)}) custom-call(f32[32]{0:T(128)S(1)} %copy-done.2, bf16[4,4,128,256]{3,2,1,0:T(8,128)(2,1)S(1)} %get-tuple-element.73.rows16.refs_1_, bf16[4,128,256]{2,1,0:T(8,128)(2,1)S(1)} %get-tuple-element.74.bcs.refs_5_, f32[4,4,128]{2,1,0:T(4,128)S(1)} %get-tuple-element.75.cums, ...), custom_call_target="tpu_custom_call" | custom-call | tf_op jit(solution)/shard_map/local/pallas_call | solution.py:63
  37.9 4.6 %collective-permute-done.8.refs_6_ = f32[512,128]{1,0:T(8,128)S(1)} collective-permute-done((f32[512,128]{1,0:T(8,128)S(1)}, f32[512,128]{1,0:T(8,128)S(1)}, u32[]{:S(2)}, u32[]{:S(2)}) %collective-permute-start.8) | collective-permute-done | bytes 262176 | tf_op jit(solution)/shard_map/ppermute | solution.py:338
  42.5 2.9 %states.3 = (bf16[4,4,128,256]{3,2,1,0:T(8,128)(2,1)S(1)}, f32[2,4,128,256]{3,2,1,0:T(8,128)S(1)}, f32[4,128,256]{2,1,0:T(8,128)S(1)}, f32[4,1,256]{2,1,0:T(1,12...) custom-call(bf16[2,128,512]{2,1,0:T(8,128)(2,1)S(1)} %get-tuple-elem, ...), custom_call_target="tpu_custom_call" | custom-call | tf_op jit(solution)/shard_map/states/pallas_call | solution.py:63
  45.5 1.7 %collective-permute-start.10 = (f32[128,256]{1,0:T(8,128)S(1)}, f32[128,256]{1,0:T(8,128)S(1)}, u32[]{:S(2)}, u32[]{:S(2)}) collective-permute-start(f32[128,256]{1,0:T(8,128)S(1)} %get-tuple-element.97), channel_id=1, source_target_pairs={{0,4},{1,5},{2,6},{3,7},{4,0},{5,1},{6,2},{7,3},{8,12},{9,13},{10,... | collective-permute-start | bytes 393224 | tf_op jit(solution)/shard_map/ppermute | solution.py:372
  48.3 2.4 %collective-permute-start.5 = (f32[128,256]{1,0:T(8,128)S(1)}, f32[128,256]{1,0:T(8,128)S(1)}, u32[]{:S(2)}, u32[]{:S(2)}) collective-permute-start(f32[128,256]{1,0:T(8,128)S(1)} %get-tuple-element.85), channel_id=1, source_target_pairs={{0,2},{1,3},{2,0},{3,1},{4,6},{5,7},{6,4},{7,5},{8,10},{9,11},{10,... | collective-permute-start | bytes 393224 | tf_op jit(solution)/shard_map/ppermute | solution.py:338
  51.7 2.1 %local.3 = (f32[4,128,256]{2,1,0:T(8,128)S(1)}, f32[4,128,256]{2,1,0:T(8,128)S(1)}) custom-call(f32[32]{0:T(128)S(1)} %copy-done.2, bf16[4,4,128,256]{3,2,1,0:T(8,128)(2,1)S(1)} %get-tuple-element.98.rows16.refs_1_, bf16[4,128,256]{2,1,0:T(8,128)(2,1)S(1)} %get-tuple-element.99.bcs.refs_5_, f32[4,4,128]{2,1,0:T(4,128)S(1)} %get-tuple-element.100.cums, ...), custom_call_target="tpu_custom_call" | custom-call | tf_op jit(solution)/shard_map/local/pallas_call | solution.py:63
  55.2 1.9 %collective-permute-done.6.refs_3_ = f32[128,256]{1,0:T(8,128)S(1)} collective-permute-done((f32[128,256]{1,0:T(8,128)S(1)}, f32[128,256]{1,0:T(8,128)S(1)}, u32[]{:S(2)}, u32[]{:S(2)}) %collective-permute-start.6) | collective-permute-done | bytes 131104 | tf_op jit(solution)/shard_map/ppermute | solution.py:338
  61.4 2.4 %collective-permute-done.11 = f32[128,256]{1,0:T(8,128)S(1)} collective-permute-done((f32[128,256]{1,0:T(8,128)S(1)}, f32[128,256]{1,0:T(8,128)S(1)}, u32[]{:S(2)}, u32[]{:S(2)}) %collective-permute-start.11) | collective-permute-done | bytes 131104 | tf_op jit(solution)/shard_map/ppermute | solution.py:338
  65.2 2.5 %collective-permute-done.13 = f32[128,256]{1,0:T(8,128)S(1)} collective-permute-done((f32[128,256]{1,0:T(8,128)S(1)}, f32[128,256]{1,0:T(8,128)S(1)}, u32[]{:S(2)}, u32[]{:S(2)}) %collective-permute-start.13) | collective-permute-done | bytes 131104 | tf_op jit(solution)/shard_map/ppermute | solution.py:338
  72.8 2.0 %collective-permute-done.14.refs_5_ = f32[128,256]{1,0:T(8,128)S(1)} collective-permute-done((f32[128,256]{1,0:T(8,128)S(1)}, f32[128,256]{1,0:T(8,128)S(1)}, u32[]{:S(2)}, u32[]{:S(2)}) %collective-permute-start.14) | collective-permute-done | bytes 131104 | tf_op jit(solution)/shard_map/ppermute | solution.py:338
  74.9 2.0 %collective-permute-done.16.refs_7_ = f32[128,256]{1,0:T(8,128)S(1)} collective-permute-done((f32[128,256]{1,0:T(8,128)S(1)}, f32[128,256]{1,0:T(8,128)S(1)}, u32[]{:S(2)}, u32[]{:S(2)}) %collective-permute-start.16) | collective-permute-done | bytes 131104 | tf_op jit(solution)/shard_map/ppermute | solution.py:338
  79.6 6.6 %collective-permute-done.22 = f32[2,128,256]{2,1,0:T(8,128)S(1)} collective-permute-done((f32[2,128,256]{2,1,0:T(8,128)S(1)}, f32[2,128,256]{2,1,0:T(8,128)S(1)}, u32[]{:S(2)}, u32[]{:S(2)}) %collective-permute-start.22) | collective-permute-done | bytes 262176 | tf_op jit(solution)/shard_map/ppermute | solution.py:338
  87.1 1.9 %collective-permute-done.23 = f32[2,128,256]{2,1,0:T(8,128)S(1)} collective-permute-done((f32[2,128,256]{2,1,0:T(8,128)S(1)}, f32[2,128,256]{2,1,0:T(8,128)S(1)}, u32[]{:S(2)}, u32[]{:S(2)}) %collective-permute-start.23) | collective-permute-done | bytes 262176 | tf_op jit(solution)/shard_map/ppermute | solution.py:338
  89.0 2.5 %collective-permute-start.24 = (f32[128,256]{1,0:T(8,128)S(1)}, f32[128,256]{1,0:T(8,128)S(1)}, u32[]{:S(2)}, u32[]{:S(2)}) collective-permute-start(f32[128,256]{1,0:T(8,128)S(1)} %get-tuple-element.132), channel_id=1, source_target_pairs={{0,4},{1,5},{2,6},{3,7},{4,0},{5,1},{6,2},{7,3},{8,12},{9,13},{10,... | collective-permute-start | bytes 393224 | tf_op jit(solution)/shard_map/ppermute | solution.py:338
  93.1 6.2 %collective-permute-done.24 = f32[128,256]{1,0:T(8,128)S(1)} collective-permute-done((f32[128,256]{1,0:T(8,128)S(1)}, f32[128,256]{1,0:T(8,128)S(1)}, u32[]{:S(2)}, u32[]{:S(2)}) %collective-permute-start.24) | collective-permute-done | bytes 131104 | tf_op jit(solution)/shard_map/ppermute | solution.py:338
  (53 shorter events, 26.3 us)
Async XLA Ops:
  4.9 52.8 %collective-permute-start.17 = (f32[2,128,1024]{2,1,0:T(8,128)S(1)}, f32[2,128,1024]{2,1,0:T(8,128)S(1)}, u32[]{:S(2)}, u32[]{:S(2)}) collective-permute-start(f32[2,128,1024]{2,1,0:T(8,128)S(1)} %get-tuple-element.122), channel_id=1, source_target_pairs={{0,16},{8,24},{16,0},{24,8},{1,17},{9,25},{17,1},{25,9},{2,18},{10... | collective-permute-start | bytes 3145736 | tf_op jit(solution)/shard_map/ppermute | solution.py:341
  7.9 11.3 %collective-permute-start = (f32[784,128]{1,0:T(8,128)S(1)}, f32[784,128]{1,0:T(8,128)S(1)}, u32[]{:S(2)}, u32[]{:S(2)}) collective-permute-start(f32[784,128]{1,0:T(8,128)S(1)} %get-tuple-element.69), channel_id=1, source_target_pairs={{0,1},{1,0},{2,3},{3,2},{4,5},{5,4},{6,7},{7,6},{8,9},{9,8},{10,11... | collective-permute-start | bytes 1204232 | tf_op jit(solution)/shard_map/ppermute | solution.py:338
  9.4 12.2 %collective-permute-start.1 = (f32[784,128]{1,0:T(8,128)S(1)}, f32[784,128]{1,0:T(8,128)S(1)}, u32[]{:S(2)}, u32[]{:S(2)}) collective-permute-start(f32[784,128]{1,0:T(8,128)S(1)} %get-tuple-element.70), channel_id=1, source_target_pairs={{0,2},{1,3},{2,0},{3,1},{4,6},{5,7},{6,4},{7,5},{8,10},{9,11},{10,... | collective-permute-start | bytes 1204232 | tf_op jit(solution)/shard_map/ppermute | solution.py:338
  11.0 19.3 %collective-permute-start.2 = (f32[784,128]{1,0:T(8,128)S(1)}, f32[784,128]{1,0:T(8,128)S(1)}, u32[]{:S(2)}, u32[]{:S(2)}) collective-permute-start(f32[784,128]{1,0:T(8,128)S(1)} %get-tuple-element.71), channel_id=1, source_target_pairs={{0,3},{1,2},{2,1},{3,0},{4,7},{5,6},{6,5},{7,4},{8,11},{9,10},{10,... | collective-permute-start | bytes 1204232 | tf_op jit(solution)/shard_map/ppermute | solution.py:338
  12.6 25.3 %collective-permute-start.9 = (f32[512,128]{1,0:T(8,128)S(1)}, f32[512,128]{1,0:T(8,128)S(1)}, u32[]{:S(2)}, u32[]{:S(2)}) collective-permute-start(f32[512,128]{1,0:T(8,128)S(1)} %get-tuple-element.94), channel_id=1, source_target_pairs={{0,3},{1,2},{2,1},{3,0},{4,7},{5,6},{6,5},{7,4},{8,11},{9,10},{10,... | collective-permute-start | bytes 786440 | tf_op jit(solution)/shard_map/ppermute | solution.py:338
  19.2 23.4 %collective-permute-start.8 = (f32[512,128]{1,0:T(8,128)S(1)}, f32[512,128]{1,0:T(8,128)S(1)}, u32[]{:S(2)}, u32[]{:S(2)}) collective-permute-start(f32[512,128]{1,0:T(8,128)S(1)} %get-tuple-element.91), channel_id=1, source_target_pairs={{0,2},{1,3},{2,0},{3,1},{4,6},{5,7},{6,4},{7,5},{8,10},{9,11},{10,... | collective-permute-start | bytes 786440 | tf_op jit(solution)/shard_map/ppermute | solution.py:338
  21.6 20.9 %collective-permute-start.7 = (f32[512,128]{1,0:T(8,128)S(1)}, f32[512,128]{1,0:T(8,128)S(1)}, u32[]{:S(2)}, u32[]{:S(2)}) collective-permute-start(f32[512,128]{1,0:T(8,128)S(1)} %get-tuple-element.88), channel_id=1, source_target_pairs={{0,1},{1,0},{2,3},{3,2},{4,5},{5,4},{6,7},{7,6},{8,9},{9,8},{10,11... | collective-permute-start | bytes 786440 | tf_op jit(solution)/shard_map/ppermute | solution.py:338
  33.2 12.3 %collective-permute-start.3 = (f32[128,256]{1,0:T(8,128)S(1)}, f32[128,256]{1,0:T(8,128)S(1)}, u32[]{:S(2)}, u32[]{:S(2)}) collective-permute-start(f32[128,256]{1,0:T(8,128)S(1)} %get-tuple-element.72), channel_id=1, source_target_pairs={{0,4},{1,5},{2,6},{3,7},{4,0},{5,1},{6,2},{7,3},{8,12},{9,13},{10,... | collective-permute-start | bytes 393224 | tf_op jit(solution)/shard_map/ppermute | solution.py:372
  45.5 8.3 %collective-permute-start.10 = (f32[128,256]{1,0:T(8,128)S(1)}, f32[128,256]{1,0:T(8,128)S(1)}, u32[]{:S(2)}, u32[]{:S(2)}) collective-permute-start(f32[128,256]{1,0:T(8,128)S(1)} %get-tuple-element.97), channel_id=1, source_target_pairs={{0,4},{1,5},{2,6},{3,7},{4,0},{5,1},{6,2},{7,3},{8,12},{9,13},{10,... | collective-permute-start | bytes 393224 | tf_op jit(solution)/shard_map/ppermute | solution.py:372
  47.7 6.1 %collective-permute-start.4 = (f32[128,256]{1,0:T(8,128)S(1)}, f32[128,256]{1,0:T(8,128)S(1)}, u32[]{:S(2)}, u32[]{:S(2)}) collective-permute-start(f32[128,256]{1,0:T(8,128)S(1)} %get-tuple-element.84), channel_id=1, source_target_pairs={{0,1},{1,0},{2,3},{3,2},{4,5},{5,4},{6,7},{7,6},{8,9},{9,8},{10,11... | collective-permute-start | bytes 393224 | tf_op jit(solution)/shard_map/ppermute | solution.py:338
  48.3 6.9 %collective-permute-start.5 = (f32[128,256]{1,0:T(8,128)S(1)}, f32[128,256]{1,0:T(8,128)S(1)}, u32[]{:S(2)}, u32[]{:S(2)}) collective-permute-start(f32[128,256]{1,0:T(8,128)S(1)} %get-tuple-element.85), channel_id=1, source_target_pairs={{0,2},{1,3},{2,0},{3,1},{4,6},{5,7},{6,4},{7,5},{8,10},{9,11},{10,... | collective-permute-start | bytes 393224 | tf_op jit(solution)/shard_map/ppermute | solution.py:338
  50.7 6.4 %collective-permute-start.6 = (f32[128,256]{1,0:T(8,128)S(1)}, f32[128,256]{1,0:T(8,128)S(1)}, u32[]{:S(2)}, u32[]{:S(2)}) collective-permute-start(f32[128,256]{1,0:T(8,128)S(1)} %get-tuple-element.86), channel_id=1, source_target_pairs={{0,3},{1,2},{2,1},{3,0},{4,7},{5,6},{6,5},{7,4},{8,11},{9,10},{10,... | collective-permute-start | bytes 393224 | tf_op jit(solution)/shard_map/ppermute | solution.py:338
  57.7 10.0 %collective-permute-start.18 = (f32[2,128,1024]{2,1,0:T(8,128)S(1)}, f32[2,128,1024]{2,1,0:T(8,128)S(1)}, u32[]{:S(2)}, u32[]{:S(2)}) collective-permute-start(f32[2,128,1024]{2,1,0:T(8,128)S(1)} %deal.1), channel_id=1, source_target_pairs={{0,8},{8,0},{16,24},{24,16},{1,9},{9,1},{17,25},{25,17},{2,10},{10... | collective-permute-start | bytes 3145736 | tf_op jit(solution)/shard_map/ppermute | solution.py:341
  57.8 5.9 %collective-permute-start.11 = (f32[128,256]{1,0:T(8,128)S(1)}, f32[128,256]{1,0:T(8,128)S(1)}, u32[]{:S(2)}, u32[]{:S(2)}) collective-permute-start(f32[128,256]{1,0:T(8,128)S(1)} %get-tuple-element.113), channel_id=1, source_target_pairs={{0,1},{1,0},{2,3},{3,2},{4,5},{5,4},{6,7},{7,6},{8,9},{9,8},{10,11... | collective-permute-start | bytes 393224 | tf_op jit(solution)/shard_map/ppermute | solution.py:338
  58.8 6.3 %collective-permute-start.12 = (f32[128,256]{1,0:T(8,128)S(1)}, f32[128,256]{1,0:T(8,128)S(1)}, u32[]{:S(2)}, u32[]{:S(2)}) collective-permute-start(f32[128,256]{1,0:T(8,128)S(1)} %get-tuple-element.114), channel_id=1, source_target_pairs={{0,2},{1,3},{2,0},{3,1},{4,6},{5,7},{6,4},{7,5},{8,10},{9,11},{10,... | collective-permute-start | bytes 393224 | tf_op jit(solution)/shard_map/ppermute | solution.py:338
  60.0 7.7 %collective-permute-start.13 = (f32[128,256]{1,0:T(8,128)S(1)}, f32[128,256]{1,0:T(8,128)S(1)}, u32[]{:S(2)}, u32[]{:S(2)}) collective-permute-start(f32[128,256]{1,0:T(8,128)S(1)} %get-tuple-element.115), channel_id=1, source_target_pairs={{0,3},{1,2},{2,1},{3,0},{4,7},{5,6},{6,5},{7,4},{8,11},{9,10},{10,... | collective-permute-start | bytes 393224 | tf_op jit(solution)/shard_map/ppermute | solution.py:338
  68.5 6.4 %collective-permute-start.14 = (f32[128,256]{1,0:T(8,128)S(1)}, f32[128,256]{1,0:T(8,128)S(1)}, u32[]{:S(2)}, u32[]{:S(2)}) collective-permute-start(f32[128,256]{1,0:T(8,128)S(1)} %get-tuple-element.116), channel_id=1, source_target_pairs={{0,1},{1,0},{2,3},{3,2},{4,5},{5,4},{6,7},{7,6},{8,9},{9,8},{10,11... | collective-permute-start | bytes 393224 | tf_op jit(solution)/shard_map/ppermute | solution.py:338
  69.3 5.6 %collective-permute-start.15 = (f32[128,256]{1,0:T(8,128)S(1)}, f32[128,256]{1,0:T(8,128)S(1)}, u32[]{:S(2)}, u32[]{:S(2)}) collective-permute-start(f32[128,256]{1,0:T(8,128)S(1)} %get-tuple-element.118), channel_id=1, source_target_pairs={{0,2},{1,3},{2,0},{3,1},{4,6},{5,7},{6,4},{7,5},{8,10},{9,11},{10,... | collective-permute-start | bytes 393224 | tf_op jit(solution)/shard_map/ppermute | solution.py:338
  70.5 6.5 %collective-permute-start.16 = (f32[128,256]{1,0:T(8,128)S(1)}, f32[128,256]{1,0:T(8,128)S(1)}, u32[]{:S(2)}, u32[]{:S(2)}) collective-permute-start(f32[128,256]{1,0:T(8,128)S(1)} %get-tuple-element.120), channel_id=1, source_target_pairs={{0,3},{1,2},{2,1},{3,0},{4,7},{5,6},{6,5},{7,4},{8,11},{9,10},{10,... | collective-permute-start | bytes 393224 | tf_op jit(solution)/shard_map/ppermute | solution.py:338
  77.5 8.7 %collective-permute-start.22 = (f32[2,128,256]{2,1,0:T(8,128)S(1)}, f32[2,128,256]{2,1,0:T(8,128)S(1)}, u32[]{:S(2)}, u32[]{:S(2)}) collective-permute-start(f32[2,128,256]{2,1,0:T(8,128)S(1)} %get-tuple-element.130), channel_id=1, source_target_pairs={{0,1},{1,0},{2,3},{3,2},{4,5},{5,4},{6,7},{7,6},{8,9},{9,8},{10,11... | collective-permute-start | bytes 786440 | tf_op jit(solution)/shard_map/ppermute | solution.py:338
  78.4 10.5 %collective-permute-start.23 = (f32[2,128,256]{2,1,0:T(8,128)S(1)}, f32[2,128,256]{2,1,0:T(8,128)S(1)}, u32[]{:S(2)}, u32[]{:S(2)}) collective-permute-start(f32[2,128,256]{2,1,0:T(8,128)S(1)} %get-tuple-element.129), channel_id=1, source_target_pairs={{0,1},{1,0},{2,3},{3,2},{4,5},{5,4},{6,7},{7,6},{8,9},{9,8},{10,11... | collective-permute-start | bytes 786440 | tf_op jit(solution)/shard_map/ppermute | solution.py:338
  86.2 6.9 %collective-permute-start.26 = (f32[128,256]{1,0:T(8,128)S(1)}, f32[128,256]{1,0:T(8,128)S(1)}, u32[]{:S(2)}, u32[]{:S(2)}) collective-permute-start(f32[128,256]{1,0:T(8,128)S(1)} %slice_bitcast_fusion), channel_id=1, source_target_pairs={{0,2},{1,3},{2,0},{3,1},{4,6},{5,7},{6,4},{7,5},{8,10},{9,11},{10,... | collective-permute-start | bytes 393224 | tf_op jit(solution)/shard_map/ppermute | solution.py:338
  89.0 10.3 %collective-permute-start.24 = (f32[128,256]{1,0:T(8,128)S(1)}, f32[128,256]{1,0:T(8,128)S(1)}, u32[]{:S(2)}, u32[]{:S(2)}) collective-permute-start(f32[128,256]{1,0:T(8,128)S(1)} %get-tuple-element.132), channel_id=1, source_target_pairs={{0,4},{1,5},{2,6},{3,7},{4,0},{5,1},{6,2},{7,3},{8,12},{9,13},{10,... | collective-permute-start | bytes 393224 | tf_op jit(solution)/shard_map/ppermute | solution.py:338
  91.5 7.8 %collective-permute-start.25 = (f32[128,256]{1,0:T(8,128)S(1)}, f32[128,256]{1,0:T(8,128)S(1)}, u32[]{:S(2)}, u32[]{:S(2)}) collective-permute-start(f32[128,256]{1,0:T(8,128)S(1)} %get-tuple-element.133), channel_id=1, source_target_pairs={{0,6},{1,7},{2,4},{3,5},{4,2},{5,3},{6,0},{7,1},{8,14},{9,15},{10,... | collective-permute-start | bytes 393224 | tf_op jit(solution)/shard_map/ppermute | solution.py:338
  (6 other events, 46.5 us)

commit v8 on v7

--- a/solution.py
+++ b/solution.py
@@ -95,8 +95,10 @@
     return ref[:, pl.ds(pl.multiple_of(start, 128), width)]
 
 
-def pack_body(q, group, first, width, x, g, *refs):
-    packed, own, (stage, sems) = refs[: q - 1], refs[q - 1], refs[q:]
+def pack_body(q, group, first, width, keep, x, g, *refs):
+    packed, rest = refs[: q - 1], list(refs[q - 1 :])
+    own = rest.pop(0) if keep else None
+    stage, sems = rest
     y = in_group(q)
     copies = {}
     for r in range(1, q):
@@ -106,19 +108,18 @@
                 source.at[:, pl.ds(at, width)], stage.at[r - 1, k], sems.at[r, k]
             )
             copies[r, k].start()
-    at = pl.multiple_of(y * group, 128)
-    for k, source in enumerate((x, g)):
-        copies[0, k] = pltpu.make_async_copy(source.at[:, pl.ds(at, group)], own.at[k], sems.at[0, k])
-        copies[0, k].start()
-    blocks = width // 128
+    if keep:
+        at = pl.multiple_of(y * group, 128)
+        for k, source in enumerate((x, g)):
+            copies[0, k] = pltpu.make_async_copy(source.at[:, pl.ds(at, group)], own.at[k], sems.at[0, k])
+            copies[0, k].start()
     for r in range(1, q):
         for k in range(2):
             copies[r, k].wait()
-            for b in range(blocks):
-                at = (k * blocks + b) * SPAN
-                packed[r - 1][at : at + SPAN, :] = stage[r - 1, k, :, b * 128 : b * 128 + 128].astype(F32)
-    for k in range(2):
-        copies[0, k].wait()
+            packed[r - 1][k] = stage[r - 1, k].astype(F32)
+    if keep:
+        for k in range(2):
+            copies[0, k].wait()
 
 
 def deal_body(bit, offsets, *refs):
@@ -127,39 +128,26 @@
         sent[k * bit : (k + 1) * bit] = ref[offset + bit : offset + 2 * bit]
 
 
-def open_body(q, n_dp, group, width, tokens, weight, x, g, decay, step, *refs):
-    firsts, (bundle, kept, dealt, held_t, held_w, stage, sems) = refs[: q - 1], refs[q - 1 :]
+def project_body(q, n_dp, tokens, weight, decay, step, *refs):
+    bundles, (kept, dealt, held_t, held_w, held_d, held_s, sems) = refs[:q], refs[q:]
+    copies = [
+        pltpu.make_async_copy(source, target, sems.at[k])
+        for k, (source, target) in enumerate(
+            ((tokens, held_t), (weight, held_w), (decay, held_d), (step, held_s))
+        )
+    ]
+    for copy in copies:
+        copy.start()
+    for copy in copies:
+        copy.wait()
     heads = HEADS // q
     y = in_group(q)
-    copies = {}
-    for r in range(1, q):
-        at = pl.multiple_of(lax.bitwise_xor(y, r) * group, 128)
-        for k, source in enumerate((x, g)):
-            copies[r, k] = pltpu.make_async_copy(
-                source.at[:, pl.ds(at, width)], stage.at[r - 1, k], sems.at[r, k]
-            )
-    copies[0, 0] = pltpu.make_async_copy(tokens, held_t, sems.at[0, 0])
-    copies[0, 1] = pltpu.make_async_copy(weight, held_w, sems.at[0, 1])
-    for copy in copies.values():
-        copy.start()
-    blocks = width // 128
-    for r in range(1, q):
-        for k in range(2):
-            copies[r, k].wait()
-            for b in range(blocks):
-                at = (k * blocks + b) * SPAN
-                firsts[r - 1][at : at + SPAN, :] = stage[r - 1, k, :, b * 128 : b * 128 + 128].astype(F32)
-    copies[0, 0].wait()
-    copies[0, 1].wait()
     proj = nn(held_t[...], held_w[...]).astype(BF16).astype(F32)
-    base = 2 * blocks * SPAN
     for r in range(q):
-        own = pl.multiple_of(lax.bitwise_xor(y, r) * heads, heads)
-        target, at = (firsts[r - 1], base) if r else (bundle, 0)
-        target[at : at + SPAN, :] = proj[:, :STATE]
-        target[at + SPAN : at + 2 * SPAN, :] = proj[:, STATE:]
-        target[at + 2 * SPAN : at + 2 * SPAN + heads, :] = decay[pl.ds(own, heads), :]
-        target[at + 2 * SPAN + heads :, :] = step[pl.ds(own, heads), :]
+        at = pl.multiple_of(lax.bitwise_xor(y, r) * heads, heads)
+        bundles[r][:SPAN, :] = proj
+        bundles[r][SPAN:, :SPAN] = held_d[pl.ds(at, heads), :]
+        bundles[r][SPAN:, SPAN:] = held_s[pl.ds(at, heads), :]
     each = tokens.shape[1] // n_dp
     dp = lax.axis_index("dp")
     for r in range(n_dp):
@@ -167,35 +155,20 @@
         to[at] = columns(held_t, lax.bitwise_xor(dp, r) * each, each).astype(F32)
 
 
-def states_body(q, planes, first, hc, base, *refs):
-    it = iter(refs)
-    own = next(it)
-    bundles = [next(it) for _ in range(q)]
-    xg_in = [next(it) for _ in range(q - 1)] if first else bundles[1:]
-    rows16, states, f1s, ds, totals, sent, plane, bcs, cums, a_cols, steps = it
-    width = hc * HEAD_DIM
-    heads = HEADS // q
-    blocks = width // 128
-    y = in_group(q)
-    for k in range(2):
-        rows16[k, y] = own[k, :, first * HEAD_DIM : first * HEAD_DIM + width]
+def decays_body(q, heads, *refs):
+    bundles = refs[:q]
+    bcs, cums, a_cols, f1s, f2s, ds, steps = refs[q:]
+    width = heads * HEAD_DIM
+    y = in_group(q)
     for r in range(q):
-        block = lax.bitwise_xor(y, r)
-        if r > 0:
-            for k in range(2):
-                for b in range(blocks):
-                    at = (k * blocks + b) * SPAN
-                    rows16[k, block, :, b * 128 : b * 128 + 128] = xg_in[r - 1][at : at + SPAN, :].astype(BF16)
-        low = base if r else 0
-        bcs[block, :, :STATE] = bundles[r][low : low + SPAN, :].astype(BF16)
-        bcs[block, :, STATE:] = bundles[r][low + SPAN : low + 2 * SPAN, :].astype(BF16)
-        low += 2 * SPAN + first
-        cums[block] = bundles[r][low : low + hc, :]
-        steps[block] = bundles[r][low + heads : low + heads + hc, :]
+        at = lax.bitwise_xor(y, r)
+        bcs[at] = bundles[r][:SPAN, :].astype(BF16)
+        cums[at] = bundles[r][SPAN:, :SPAN]
+        steps[at] = bundles[r][SPAN:, SPAN:]
     rows, cols = iotas()
     tri = jnp.where(rows <= cols, 1.0, 0.0).astype(BF16)
-    head_of = lax.broadcasted_iota(jnp.int32, (hc, width), 1) // HEAD_DIM
-    spread = head_of == lax.broadcasted_iota(jnp.int32, (hc, width), 0)
+    head_of = lax.broadcasted_iota(jnp.int32, (heads, width), 1) // HEAD_DIM
+    spread = head_of == lax.broadcasted_iota(jnp.int32, (heads, width), 0)
     spread = jnp.where(spread, 1.0, 0.0).astype(BF16)
     for b in range(q):
         cum = sum(nn(term, tri) for term in terms(cums[b]))
@@ -206,20 +179,31 @@
         cum_x = sum(nn(term, spread) for term in terms(cum_c))
         a_x = sum(nn(term, spread) for term in terms(a_c))
         total = cum_x[SPAN - 1 : SPAN, :]
-        f1 = jnp.exp(total - a_x)
-        f1s[b] = f1
+        f1s[b] = jnp.exp(total - a_x)
+        f2s[b] = jnp.exp(cum_x)
         ds[b] = jnp.exp(total)
-        weighted = (rows16[0, b].astype(F32) * f1).astype(BF16)
-        scaled = (rows16[1, b].astype(F32) * jnp.exp(cum_x)).astype(BF16)
-        rows16[2, b] = weighted
-        rows16[3, b] = scaled
-        states[0, b] = tn(bcs[b, :, :STATE], weighted)
-        states[1, b] = tn(bcs[b, :, STATE:], scaled)
-    forward, backward, through = states[0, 0], states[1, q - 1], ds[0]
+
+
+def states_body(q, planes, at, *refs):
+    it = iter(refs)
+    own = next(it)
+    xg_in = [next(it) for _ in range(q - 1)]
+    bcs, f1s, f2s, ds, rows16, states, totals, sent, plane = it
+    y = in_group(q)
+    for k in range(2):
+        rows16[k, y] = own[k, :, at]
+        for r in range(1, q):
+            rows16[k, lax.bitwise_xor(y, r)] = xg_in[r - 1][k].astype(BF16)
+    for b in range(q):
+        rows16[2, b] = (rows16[0, b].astype(F32) * f1s[b, :, at]).astype(BF16)
+        rows16[3, b] = (rows16[1, b].astype(F32) * f2s[b, :, at]).astype(BF16)
+        states[0, b] = tn(bcs[b, :, :STATE], rows16[2, b])
+        states[1, b] = tn(bcs[b, :, STATE:], rows16[3, b])
+    forward, backward, through = states[0, 0], states[1, q - 1], ds[0, :, at]
     for b in range(1, q):
-        forward = ds[b] * forward + states[0, b]
-        backward = ds[q - 1 - b] * backward + states[1, q - 1 - b]
-        through = through * ds[b]
+        forward = ds[b, :, at] * forward + states[0, b]
+        backward = ds[q - 1 - b, :, at] * backward + states[1, q - 1 - b]
+        through = through * ds[b, :, at]
     totals[0] = forward
     totals[1] = backward
     plane[...] = through
@@ -245,7 +229,7 @@
             x, g = rows16[0, b, :, at], rows16[1, b, :, at]
             parts = []
             for half in range(2):
-                h = 2 * pair + half
+                h = first + 2 * pair + half
                 gap = cums[b, h : h + 1, :] - a_cols[b, :, h : h + 1]
                 decay = jnp.exp(jnp.where(causal, gap, -jnp.inf))
                 picked = jnp.where(low if half == 0 else ~low, x, jnp.zeros_like(x))
@@ -258,7 +242,7 @@
         gp[b, :, STATE:] = tn(mixed, b_cols)
 
 
-def final_body(q, planes, more, *refs):
+def final_body(q, planes, at, more, *refs):
     it = iter(refs)
     got = [next(it) for _ in range(planes - 1)]
     rows16, states, f1s, ds, bcs, gx, gp = [next(it) for _ in range(7)]
@@ -277,14 +261,14 @@
         part = gp[b, :, STATE:] + nt(rows16[3, b], start.astype(BF16))
         gp_out[b, :, STATE:] = part if before is None else part + before[b, :, STATE:]
         if b < q - 1:
-            start = ds[b] * start + states[0, b]
+            start = ds[b, :, at] * start + states[0, b]
     for b in range(q - 1, -1, -1):
         rounded = after.astype(BF16)
-        gx_all[b] = gx[b] + f1s[b] * nn(bcs[b, :, :STATE], rounded)
+        gx_all[b] = gx[b] + f1s[b, :, at] * nn(bcs[b, :, :STATE], rounded)
         part = gp[b, :, :STATE] + nt(rows16[2, b], rounded)
         gp_out[b, :, :STATE] = part if before is None else part + before[b, :, :STATE]
         if b > 0:
-            after = ds[b] * after + states[1, b]
+            after = ds[b, :, at] * after + states[1, b]
     for r in range(q):
         gx_out[r][...] = gx_all[lax.bitwise_xor(y, r)]
         if more:
@@ -340,30 +324,41 @@
     def across(value, r):
         return lax.ppermute(value, "dp", [(i, i ^ r) for i in range(n_dp)])
 
-    widths = [width for _, width in spans]
-    base = 2 * widths[0]
-    tail = 2 * SPAN + 2 * heads
     columns_each = features // n_dp
     rows = columns_each // n_seq
-    body = functools.partial(open_body, q, n_dp, group, widths[0])
+
+    def pack(first, width, keep):
+        scratch = (pltpu.VMEM((q - 1, 2, SPAN, width), BF16), pltpu.SemaphoreType.DMA((q, 2)))
+        outs = [out((2, SPAN, width))] * (q - 1) + [out((2, SPAN, group), BF16)] * keep
+        body = functools.partial(pack_body, q, group, first, width, keep)
+        return call(body, outs, scratch, name="pack", hbm=2)(x, g)
+
+    packed = pack(*spans[0], False)
+    xg_in = [[swap(packed[r - 1], r) for r in range(1, q)]]
     scratch = (
         pltpu.VMEM(tokens.shape, BF16), pltpu.VMEM(proj_weight.shape, BF16),
-        pltpu.VMEM((q - 1, 2, SPAN, widths[0]), BF16), pltpu.SemaphoreType.DMA((q, 2)),
+        pltpu.VMEM((HEADS, SPAN), F32), pltpu.VMEM((HEADS, SPAN), F32), pltpu.SemaphoreType.DMA((4,)),
     )
-    outs = [out((base + tail, 128))] * (q - 1) + [out((tail, 128))]
-    outs += [out((n_dp // 2, length, columns_each))] * 2
-    opened = call(body, outs, scratch, name="open", hbm=4)(
-        tokens, proj_weight, x, g, [log_decay[0]], [step_size[0]]
+    outs = [out((SPAN + heads, 2 * STATE))] * q + [out((n_dp // 2, length, columns_each))] * 2
+    opened = call(functools.partial(project_body, q, n_dp), outs, scratch, name="project", hbm=4)(
+        behind(tokens, packed[0]), proj_weight, log_decay[0], step_size[0]
     )
-    bundles = [opened[q - 1]] + [swap(opened[r - 1], r) for r in range(1, q)]
-    body = functools.partial(pack_body, q, group, *spans[1])
-    scratch = (pltpu.VMEM((q - 1, 2, SPAN, widths[1]), BF16), pltpu.SemaphoreType.DMA((q, 2)))
-    outs = [out((2 * widths[1], 128))] * (q - 1) + [out((2, SPAN, group), BF16)]
-    packed = call(body, outs, scratch, name="pack", hbm=2)(x, g)
+    bundles = [opened[0]] + [swap(opened[r], r) for r in range(1, q)]
+    packed = pack(*spans[1], True)
     own = packed[q - 1]
+    xg_in.append([swap(behind(packed[r - 1], opened[0]), r) for r in range(1, q)])
     bit = n_dp // 2
-    sources = {0: (opened[q], 0), bit: (across(opened[q + 1], bit), 0)}
-    second = [swap(behind(packed[r - 1], opened[q - 1]), r) for r in range(1, q)]
+    sources = {0: (opened[q], 0), bit: (across(behind(opened[q + 1], *xg_in[0]), bit), 0)}
+
+    rows_of = (q, SPAN, group)
+    outs = [
+        out((q, SPAN, 2 * STATE), BF16), out((q, heads, SPAN)), out((q, SPAN, heads)),
+        out(rows_of), out(rows_of), out((q, 1, group)),
+    ]
+    body = functools.partial(decays_body, q, heads)
+    bcs, cums, a_cols, f1s, f2s, ds = call(body, outs, (pltpu.VMEM((q, heads, SPAN), F32),), name="decays")(
+        behind(bundles[0], *xg_in[0]), *bundles[1:]
+    )
 
     def hop(value, t):
         top = planes - 1 - t
@@ -371,27 +366,22 @@
         pairs += [(top * q + i, (top - 1) * q + i) for i in range(q)]
         return lax.ppermute(value, "seq", pairs)
 
-    held, local, extra = [], [], []
+    held, local = [], []
     for c, (first, count) in enumerate(chunks):
         wide = (q, SPAN, count * HEAD_DIM)
         state = out((STATE, wide[2]))
-        outs = [
-            out((4,) + wide, BF16), out((2,) + wide), out(wide), out((q, 1, wide[2])),
-            out((2, STATE, wide[2])), state, out((1, wide[2])),
-            out((q, SPAN, 2 * STATE), BF16), out((q, count, SPAN)), out((q, SPAN, count)),
-        ]
-        scratch = (pltpu.VMEM((q, count, SPAN), F32),)
-        body = functools.partial(states_body, q, planes, first, count, base)
+        at = slice(first * HEAD_DIM, (first + count) * HEAD_DIM)
         if c > 0:
-            ahead = hop(held[0][5], 0)
-            extra = [behind(v, *local[0]) for v in second]
-        held.append(call(body, outs, scratch, name="states")(own, *bundles, *extra))
+            ahead = hop(held[0][3], 0)
+            xg_in[c] = [behind(v, *local[0]) for v in xg_in[c]]
+        outs = [out((4,) + wide, BF16), out((2,) + wide), out((2, STATE, wide[2])), state, out((1, wide[2]))]
+        body = functools.partial(states_body, q, planes, at)
+        held.append(call(body, outs, name="states")(own, *xg_in[c], bcs, f1s, f2s, ds))
         body = functools.partial(local_body, q, first, count)
-        rows16, bcs, cums, a_cols = (held[c][k] for k in (0, 7, 8, 9))
         outs = [out(wide), out((q, SPAN, 2 * STATE))]
-        local.append(call(body, outs, smem=1, name="local")(skip_gain, rows16, bcs, cums, a_cols))
-
-    sent = [h[5] for h in held]
+        local.append(call(body, outs, smem=1, name="local")(skip_gain, held[c][0], bcs, cums, a_cols))
+
+    sent = [h[3] for h in held]
     arrived = [[] for _ in held]
     for t in range(planes - 1):
         for c in range(PARTS):
@@ -406,17 +396,17 @@
             if t < planes - 2:
                 (sent[c],) = call(
                     functools.partial(relay_body, q, t), [out(came.shape)], name="relay"
-                )(came, held[c][4], held[c][6])
+                )(came, held[c][2], held[c][4])
 
     before, gx_parts, returned = [], [], []
     for c, (first, width) in enumerate(spans):
-        rows16, states, f1s, ds, bcs = (held[c][k] for k in (0, 1, 2, 3, 7))
+        rows16, states = held[c][:2]
         block, all_blocks = (SPAN, 2 * STATE), (q, SPAN, 2 * STATE)
         outs = [out((SPAN, width))] * q + ([out(block)] * q if before else [out(all_blocks)])
         scratch = (pltpu.VMEM((q, SPAN, width), F32),)
         if before:
             scratch = (pltpu.VMEM(all_blocks, F32),) + scratch
-        body = functools.partial(final_body, q, planes, bool(before))
+        body = functools.partial(final_body, q, planes, slice(first, first + width), bool(before))
         done = call(body, outs, scratch, name="final")(
             *arrived[c], rows16, states, f1s, ds, bcs, *local[c], *before
         )

time: 100 us -> 100 us (level)
  starting transfers between devices: 33.7 us -> 41.5 us
  waiting for transfers between devices: 46.7 us -> 41.3 us
  local copies, waits for them, and re-layouts: 1.46 us -> 0.03 us
  Pallas kernels: 16.7 us -> 15.7 us
    ppermute x20 -> x23, starting transfers between devices: 25.6 us -> 33.5 us  [swap(): return lax.ppermute(value, 'seq', [(i, i ^ r) for i in range(n_seq)])]
    ppermute x20 -> x23, waiting for transfers between devices: 45.8 us -> 40.4 us  [swap(): return lax.ppermute(value, 'seq', [(i, i ^ r) for i in range(n_seq)])]
    ppermute x5, starting transfers between devices: 3.79 us -> 2.16 us  [across(): return lax.ppermute(value, 'dp', [(i, i ^ r) for i in range(n_dp)])]
    ppermute x2, starting transfers between devices: 4.27 us -> 5.86 us  [hop(): return lax.ppermute(value, 'seq', pairs)]
    unnamed x6 -> x2, local copies, waits for them, and re-layouts: 1.43 us -> 0.01 us
    pallas_call x11 -> x13, Pallas kernels: 16.7 us -> 15.7 us  [run(): pl.pallas_call(body, out_shape=tuple((o[0] if isinstance(o, list) else pl...]
  transfers between devices with their start and end apart: 27 -> 30, of which waited for: 16 -> 15; matrix products, arithmetic and copies ran while one was open for 0% -> 0% of each run, Pallas kernels for 13% -> 14%
where the time goes in v8:
time: 100 us
  starting transfers between devices  41.5 us (42%)
  waiting for transfers between devices  41.3 us (41%)
  Pallas kernels  15.7 us (16%)
    ppermute x23, waiting for transfers between devices, swap(): return lax.ppermute(value, 'seq', [(i, i ^ r) for i in range(n_seq)])  40.4 us
    ppermute x23, starting transfers between devices, swap(): return lax.ppermute(value, 'seq', [(i, i ^ r) for i in range(n_seq)])  33.5 us
    pallas_call x13, Pallas kernels, run(): pl.pallas_call(body, out_shape=tuple((o[0] if isinstance(o, list) else pl...  15.7 us
    ppermute x2, starting transfers between devices, hop(): return lax.ppermute(value, 'seq', pairs)  5.86 us
    ppermute x5, starting transfers between devices, across(): return lax.ppermute(value, 'dp', [(i, i ^ r) for i in range(n_dp)])  2.16 us
  transfers between devices with their start and end apart: 30, of which 15 were waited for; matrix products, arithmetic and copies ran while one was open for 0% of the time, Pallas kernels for 14%

profile of v8, /device:TPU:0, one launch (start us, length us, event | category | flops | bytes accessed | tf_op | source)
XLA Modules:
  0.0 100.2 jit_solution(17981361617984578139)
XLA Ops:
  1.7 3.1 %collective-permute-start.1 = (f32[2,128,256]{2,1,0:T(8,128)S(1)}, f32[2,128,256]{2,1,0:T(8,128)S(1)}, u32[]{:S(2)}, u32[]{:S(2)}) collective-permute-start(f32[2,128,256]{2,1,0:T(8,128)S(1)} %get-tuple-element.71), channel_id=1, source_target_pairs={{0,2},{1,3},{2,0},{3,1},{4,6},{5,7},{6,4},{7,5},{8,10},{9,11},{10,... | collective-permute-start | bytes 786440 | tf_op jit(solution)/shard_map/ppermute | solution.py:322
  6.4 2.5 %project.1 = (f32[136,256]{1,0:T(8,128)S(1)}, f32[136,256]{1,0:T(8,128)S(1)}, f32[136,256]{1,0:T(8,128)S(1)}, f32[136,256]{1,0:T(8,128)S(1)}, f32[2,128,1024]{2,1,0:T(8,128)S(1)}, /*index=5*/f32[2,128,1024]{2,1,0:T(8,128)S(1)}) custom-call(bf16[128,4096]{1,0:T(8,128)(2,1)} %bitcast.24, bf16[4096,256]{1,0:T(8,128)(2,1)} %weight.2, f32[32,128]{1,0:T(8,128)} %bitcast.26, ...), custom_call_target="tpu_custom_call" | custom-call | tf_op jit(solution)/shard_map/project/pallas_call | solution.py:63
  8.9 3.1 %collective-permute-done.1.refs_2_ = f32[2,128,256]{2,1,0:T(8,128)S(1)} collective-permute-done((f32[2,128,256]{2,1,0:T(8,128)S(1)}, f32[2,128,256]{2,1,0:T(8,128)S(1)}, u32[]{:S(2)}, u32[]{:S(2)}) %collective-permute-start.1) | collective-permute-done | bytes 262176 | tf_op jit(solution)/shard_map/ppermute | solution.py:322
  12.0 6.0 %collective-permute-done.2.refs_3_ = f32[2,128,256]{2,1,0:T(8,128)S(1)} collective-permute-done((f32[2,128,256]{2,1,0:T(8,128)S(1)}, f32[2,128,256]{2,1,0:T(8,128)S(1)}, u32[]{:S(2)}, u32[]{:S(2)}) %collective-permute-start.2) | collective-permute-done | bytes 262176 | tf_op jit(solution)/shard_map/ppermute | solution.py:322
  27.2 3.0 %collective-permute-done.3.refs_1_ = f32[136,256]{1,0:T(8,128)S(1)} collective-permute-done((f32[136,256]{1,0:T(8,128)S(1)}, f32[136,256]{1,0:T(8,128)S(1)}, u32[]{:S(2)}, u32[]{:S(2)}) %collective-permute-start.3) | collective-permute-done | bytes 139296 | tf_op jit(solution)/shard_map/ppermute | solution.py:322
  30.2 2.8 %collective-permute-start.10 = (f32[2,128,256]{2,1,0:T(8,128)S(1)}, f32[2,128,256]{2,1,0:T(8,128)S(1)}, u32[]{:S(2)}, u32[]{:S(2)}) collective-permute-start(f32[2,128,256]{2,1,0:T(8,128)S(1)} %get-tuple-element.96), channel_id=1, source_target_pairs={{0,1},{1,0},{2,3},{3,2},{4,5},{5,4},{6,7},{7,6},{8,9},{9,8},{10,11... | collective-permute-start | bytes 786440 | tf_op jit(solution)/shard_map/ppermute | solution.py:322
  33.0 1.9 %decays.1 = (bf16[4,128,256]{2,1,0:T(8,128)(2,1)S(1)}, f32[4,8,128]{2,1,0:T(8,128)S(1)}, f32[4,128,8]{2,1,0:T(8,128)S(1)}, f32[4,128,512]{2,1,0:T(8,128)S(1)}, f...) custom-call(f32[136,256]{1,0:T(8,128)S(1)} %get-tuple-element.75.refs_0_, ...), custom_call_target="tpu_custom_call" | custom-call | tf_op jit(solution)/shard_map/decays/pallas_call | solution.py:63
  36.0 2.7 %collective-permute-start.6 = (f32[128,256]{1,0:T(8,128)S(1)}, f32[128,256]{1,0:T(8,128)S(1)}, u32[]{:S(2)}, u32[]{:S(2)}) collective-permute-start(f32[128,256]{1,0:T(8,128)S(1)} %get-tuple-element.83), channel_id=1, source_target_pairs={{0,4},{1,5},{2,6},{3,7},{4,0},{5,1},{6,2},{7,3},{8,12},{9,13},{10,... | collective-permute-start | bytes 393224 | tf_op jit(solution)/shard_map/ppermute | solution.py:367
  38.7 2.1 %local.2 = (f32[4,128,256]{2,1,0:T(8,128)S(1)}, f32[4,128,256]{2,1,0:T(8,128)S(1)}) custom-call(f32[32]{0:T(128)S(1)} %copy-done, bf16[4,4,128,256]{3,2,1,0:T(8,128)(2,1)S(1)} %get-tuple-element.84.rows16.refs_1_, bf16[4,128,256]{2,1,0:T(8,128)(2,1)S(1)} %get-tuple-element.79.refs_4_.bcs.refs_5_, f32[4,8,128]{2,1,0:T(8,128)S(1)} %get-tuple-element.85.cums, ...), custom_call_target="tpu_custom_call" | custom-call | tf_op jit(solution)/shard_map/local/pallas_call | solution.py:63
  42.0 3.1 %collective-permute-start.13 = (f32[128,256]{1,0:T(8,128)S(1)}, f32[128,256]{1,0:T(8,128)S(1)}, u32[]{:S(2)}, u32[]{:S(2)}) collective-permute-start(f32[128,256]{1,0:T(8,128)S(1)} %get-tuple-element.105), channel_id=1, source_target_pairs={{0,4},{1,5},{2,6},{3,7},{4,0},{5,1},{6,2},{7,3},{8,12},{9,13},{10,... | collective-permute-start | bytes 393224 | tf_op jit(solution)/shard_map/ppermute | solution.py:367
  46.3 4.7 %collective-permute-start.8 = (f32[128,256]{1,0:T(8,128)S(1)}, f32[128,256]{1,0:T(8,128)S(1)}, u32[]{:S(2)}, u32[]{:S(2)}) collective-permute-start(f32[128,256]{1,0:T(8,128)S(1)} %get-tuple-element.93), channel_id=1, source_target_pairs={{0,2},{1,3},{2,0},{3,1},{4,6},{5,7},{6,4},{7,5},{8,10},{9,11},{10,... | collective-permute-start | bytes 393224 | tf_op jit(solution)/shard_map/ppermute | solution.py:322
  52.3 2.1 %local.3 = (f32[4,128,256]{2,1,0:T(8,128)S(1)}, f32[4,128,256]{2,1,0:T(8,128)S(1)}) custom-call(f32[32]{0:T(128)S(1)} %copy-done, bf16[4,4,128,256]{3,2,1,0:T(8,128)(2,1)S(1)} %get-tuple-element.106.rows16.refs_1_, bf16[4,128,256]{2,1,0:T(8,128)(2,1)S(1)} %get-tuple-element.79.refs_4_.bcs.refs_5_, f32[4,8,128]{2,1,0:T(8,128)S(1)} %get-tuple-element.85.cums, ...), custom_call_target="tpu_custom_call" | custom-call | tf_op jit(solution)/shard_map/local/pallas_call | solution.py:63
  54.5 2.3 %collective-permute-done.9.refs_3_ = f32[128,256]{1,0:T(8,128)S(1)} collective-permute-done((f32[128,256]{1,0:T(8,128)S(1)}, f32[128,256]{1,0:T(8,128)S(1)}, u32[]{:S(2)}, u32[]{:S(2)}) %collective-permute-start.9) | collective-permute-done | bytes 131104 | tf_op jit(solution)/shard_map/ppermute | solution.py:322
  57.4 2.0 %collective-permute-start.14 = (f32[128,256]{1,0:T(8,128)S(1)}, f32[128,256]{1,0:T(8,128)S(1)}, u32[]{:S(2)}, u32[]{:S(2)}) collective-permute-start(f32[128,256]{1,0:T(8,128)S(1)} %get-tuple-element.116), channel_id=1, source_target_pairs={{0,1},{1,0},{2,3},{3,2},{4,5},{5,4},{6,7},{7,6},{8,9},{9,8},{10,11... | collective-permute-start | bytes 393224 | tf_op jit(solution)/shard_map/ppermute | solution.py:322
  61.0 2.5 %collective-permute-done.14 = f32[128,256]{1,0:T(8,128)S(1)} collective-permute-done((f32[128,256]{1,0:T(8,128)S(1)}, f32[128,256]{1,0:T(8,128)S(1)}, u32[]{:S(2)}, u32[]{:S(2)}) %collective-permute-start.14) | collective-permute-done | bytes 131104 | tf_op jit(solution)/shard_map/ppermute | solution.py:322
  63.5 2.3 %collective-permute-done.15 = f32[128,256]{1,0:T(8,128)S(1)} collective-permute-done((f32[128,256]{1,0:T(8,128)S(1)}, f32[128,256]{1,0:T(8,128)S(1)}, u32[]{:S(2)}, u32[]{:S(2)}) %collective-permute-start.15) | collective-permute-done | bytes 131104 | tf_op jit(solution)/shard_map/ppermute | solution.py:322
  65.8 1.7 %collective-permute-done.16 = f32[128,256]{1,0:T(8,128)S(1)} collective-permute-done((f32[128,256]{1,0:T(8,128)S(1)}, f32[128,256]{1,0:T(8,128)S(1)}, u32[]{:S(2)}, u32[]{:S(2)}) %collective-permute-start.16) | collective-permute-done | bytes 131104 | tf_op jit(solution)/shard_map/ppermute | solution.py:322
  68.2 1.8 %collective-permute-start.17 = (f32[128,256]{1,0:T(8,128)S(1)}, f32[128,256]{1,0:T(8,128)S(1)}, u32[]{:S(2)}, u32[]{:S(2)}) collective-permute-start(f32[128,256]{1,0:T(8,128)S(1)} %get-tuple-element.119), channel_id=1, source_target_pairs={{0,1},{1,0},{2,3},{3,2},{4,5},{5,4},{6,7},{7,6},{8,9},{9,8},{10,11... | collective-permute-start | bytes 393224 | tf_op jit(solution)/shard_map/ppermute | solution.py:322
  72.6 1.7 %collective-permute-done.17.refs_5_ = f32[128,256]{1,0:T(8,128)S(1)} collective-permute-done((f32[128,256]{1,0:T(8,128)S(1)}, f32[128,256]{1,0:T(8,128)S(1)}, u32[]{:S(2)}, u32[]{:S(2)}) %collective-permute-start.17) | collective-permute-done | bytes 131104 | tf_op jit(solution)/shard_map/ppermute | solution.py:322
  77.4 1.6 %collective-permute-start.25 = (f32[2,128,256]{2,1,0:T(8,128)S(1)}, f32[2,128,256]{2,1,0:T(8,128)S(1)}, u32[]{:S(2)}, u32[]{:S(2)}) collective-permute-start(f32[2,128,256]{2,1,0:T(8,128)S(1)} %get-tuple-element.134), channel_id=1, source_target_pairs={{0,1},{1,0},{2,3},{3,2},{4,5},{5,4},{6,7},{7,6},{8,9},{9,8},{10,11... | collective-permute-start | bytes 786440 | tf_op jit(solution)/shard_map/ppermute | solution.py:322
  79.5 6.8 %collective-permute-done.25 = f32[2,128,256]{2,1,0:T(8,128)S(1)} collective-permute-done((f32[2,128,256]{2,1,0:T(8,128)S(1)}, f32[2,128,256]{2,1,0:T(8,128)S(1)}, u32[]{:S(2)}, u32[]{:S(2)}) %collective-permute-start.25) | collective-permute-done | bytes 262176 | tf_op jit(solution)/shard_map/ppermute | solution.py:322
  89.1 1.8 %collective-permute-start.27 = (f32[128,256]{1,0:T(8,128)S(1)}, f32[128,256]{1,0:T(8,128)S(1)}, u32[]{:S(2)}, u32[]{:S(2)}) collective-permute-start(f32[128,256]{1,0:T(8,128)S(1)} %get-tuple-element.136), channel_id=1, source_target_pairs={{0,4},{1,5},{2,6},{3,7},{4,0},{5,1},{6,2},{7,3},{8,12},{9,13},{10,... | collective-permute-start | bytes 393224 | tf_op jit(solution)/shard_map/ppermute | solution.py:322
  90.9 2.0 %collective-permute-start.28 = (f32[128,256]{1,0:T(8,128)S(1)}, f32[128,256]{1,0:T(8,128)S(1)}, u32[]{:S(2)}, u32[]{:S(2)}) collective-permute-start(f32[128,256]{1,0:T(8,128)S(1)} %get-tuple-element.137), channel_id=1, source_target_pairs={{0,6},{1,7},{2,4},{3,5},{4,2},{5,3},{6,0},{7,1},{8,14},{9,15},{10,... | collective-permute-start | bytes 393224 | tf_op jit(solution)/shard_map/ppermute | solution.py:322
  93.8 5.8 %collective-permute-done.27 = f32[128,256]{1,0:T(8,128)S(1)} collective-permute-done((f32[128,256]{1,0:T(8,128)S(1)}, f32[128,256]{1,0:T(8,128)S(1)}, u32[]{:S(2)}, u32[]{:S(2)}) %collective-permute-start.27) | collective-permute-done | bytes 131104 | tf_op jit(solution)/shard_map/ppermute | solution.py:322
  (57 shorter events, 30.1 us)
Async XLA Ops:
  1.7 10.2 %collective-permute-start.1 = (f32[2,128,256]{2,1,0:T(8,128)S(1)}, f32[2,128,256]{2,1,0:T(8,128)S(1)}, u32[]{:S(2)}, u32[]{:S(2)}) collective-permute-start(f32[2,128,256]{2,1,0:T(8,128)S(1)} %get-tuple-element.71), channel_id=1, source_target_pairs={{0,2},{1,3},{2,0},{3,1},{4,6},{5,7},{6,4},{7,5},{8,10},{9,11},{10,... | collective-permute-start | bytes 786440 | tf_op jit(solution)/shard_map/ppermute | solution.py:322
  4.8 13.1 %collective-permute-start.2 = (f32[2,128,256]{2,1,0:T(8,128)S(1)}, f32[2,128,256]{2,1,0:T(8,128)S(1)}, u32[]{:S(2)}, u32[]{:S(2)}) collective-permute-start(f32[2,128,256]{2,1,0:T(8,128)S(1)} %get-tuple-element.72), channel_id=1, source_target_pairs={{0,3},{1,2},{2,1},{3,0},{4,7},{5,6},{6,5},{7,4},{8,11},{9,10},{10,... | collective-permute-start | bytes 786440 | tf_op jit(solution)/shard_map/ppermute | solution.py:322
  6.2 13.1 %collective-permute-start = (f32[2,128,256]{2,1,0:T(8,128)S(1)}, f32[2,128,256]{2,1,0:T(8,128)S(1)}, u32[]{:S(2)}, u32[]{:S(2)}) collective-permute-start(f32[2,128,256]{2,1,0:T(8,128)S(1)} %get-tuple-element.70), channel_id=1, source_target_pairs={{0,1},{1,0},{2,3},{3,2},{4,5},{5,4},{6,7},{7,6},{8,9},{9,8},{10,11... | collective-permute-start | bytes 786440 | tf_op jit(solution)/shard_map/ppermute | solution.py:322
  19.3 37.9 %collective-permute-start.20 = (f32[2,128,1024]{2,1,0:T(8,128)S(1)}, f32[2,128,1024]{2,1,0:T(8,128)S(1)}, u32[]{:S(2)}, u32[]{:S(2)}) collective-permute-start(f32[2,128,1024]{2,1,0:T(8,128)S(1)} %get-tuple-element.126), channel_id=1, source_target_pairs={{0,16},{8,24},{16,0},{24,8},{1,17},{9,25},{17,1},{25,9},{2,18},{10... | collective-permute-start | bytes 3145736 | tf_op jit(solution)/shard_map/ppermute | solution.py:325
  20.8 9.3 %collective-permute-start.3 = (f32[136,256]{1,0:T(8,128)S(1)}, f32[136,256]{1,0:T(8,128)S(1)}, u32[]{:S(2)}, u32[]{:S(2)}) collective-permute-start(f32[136,256]{1,0:T(8,128)S(1)} %get-tuple-element.76), channel_id=1, source_target_pairs={{0,1},{1,0},{2,3},{3,2},{4,5},{5,4},{6,7},{7,6},{8,9},{9,8},{10,11... | collective-permute-start | bytes 417800 | tf_op jit(solution)/shard_map/ppermute | solution.py:322
  21.3 8.9 %collective-permute-start.4 = (f32[136,256]{1,0:T(8,128)S(1)}, f32[136,256]{1,0:T(8,128)S(1)}, u32[]{:S(2)}, u32[]{:S(2)}) collective-permute-start(f32[136,256]{1,0:T(8,128)S(1)} %get-tuple-element.77), channel_id=1, source_target_pairs={{0,2},{1,3},{2,0},{3,1},{4,6},{5,7},{6,4},{7,5},{8,10},{9,11},{10,... | collective-permute-start | bytes 417800 | tf_op jit(solution)/shard_map/ppermute | solution.py:322
  22.9 10.1 %collective-permute-start.5 = (f32[136,256]{1,0:T(8,128)S(1)}, f32[136,256]{1,0:T(8,128)S(1)}, u32[]{:S(2)}, u32[]{:S(2)}) collective-permute-start(f32[136,256]{1,0:T(8,128)S(1)} %get-tuple-element.78), channel_id=1, source_target_pairs={{0,3},{1,2},{2,1},{3,0},{4,7},{5,6},{6,5},{7,4},{8,11},{9,10},{10,... | collective-permute-start | bytes 417800 | tf_op jit(solution)/shard_map/ppermute | solution.py:322
  25.6 15.3 %collective-permute-start.12 = (f32[2,128,256]{2,1,0:T(8,128)S(1)}, f32[2,128,256]{2,1,0:T(8,128)S(1)}, u32[]{:S(2)}, u32[]{:S(2)}) collective-permute-start(f32[2,128,256]{2,1,0:T(8,128)S(1)} %get-tuple-element.102), channel_id=1, source_target_pairs={{0,3},{1,2},{2,1},{3,0},{4,7},{5,6},{6,5},{7,4},{8,11},{9,10},{10,... | collective-permute-start | bytes 786440 | tf_op jit(solution)/shard_map/ppermute | solution.py:322
  30.1 10.8 %collective-permute-start.11 = (f32[2,128,256]{2,1,0:T(8,128)S(1)}, f32[2,128,256]{2,1,0:T(8,128)S(1)}, u32[]{:S(2)}, u32[]{:S(2)}) collective-permute-start(f32[2,128,256]{2,1,0:T(8,128)S(1)} %get-tuple-element.99), channel_id=1, source_target_pairs={{0,2},{1,3},{2,0},{3,1},{4,6},{5,7},{6,4},{7,5},{8,10},{9,11},{10,... | collective-permute-start | bytes 786440 | tf_op jit(solution)/shard_map/ppermute | solution.py:322
  30.2 10.7 %collective-permute-start.10 = (f32[2,128,256]{2,1,0:T(8,128)S(1)}, f32[2,128,256]{2,1,0:T(8,128)S(1)}, u32[]{:S(2)}, u32[]{:S(2)}) collective-permute-start(f32[2,128,256]{2,1,0:T(8,128)S(1)} %get-tuple-element.96), channel_id=1, source_target_pairs={{0,1},{1,0},{2,3},{3,2},{4,5},{5,4},{6,7},{7,6},{8,9},{9,8},{10,11... | collective-permute-start | bytes 786440 | tf_op jit(solution)/shard_map/ppermute | solution.py:322
  42.0 12.4 %collective-permute-start.13 = (f32[128,256]{1,0:T(8,128)S(1)}, f32[128,256]{1,0:T(8,128)S(1)}, u32[]{:S(2)}, u32[]{:S(2)}) collective-permute-start(f32[128,256]{1,0:T(8,128)S(1)} %get-tuple-element.105), channel_id=1, source_target_pairs={{0,4},{1,5},{2,6},{3,7},{4,0},{5,1},{6,2},{7,3},{8,12},{9,13},{10,... | collective-permute-start | bytes 393224 | tf_op jit(solution)/shard_map/ppermute | solution.py:367
  45.6 8.9 %collective-permute-start.7 = (f32[128,256]{1,0:T(8,128)S(1)}, f32[128,256]{1,0:T(8,128)S(1)}, u32[]{:S(2)}, u32[]{:S(2)}) collective-permute-start(f32[128,256]{1,0:T(8,128)S(1)} %get-tuple-element.92), channel_id=1, source_target_pairs={{0,1},{1,0},{2,3},{3,2},{4,5},{5,4},{6,7},{7,6},{8,9},{9,8},{10,11... | collective-permute-start | bytes 393224 | tf_op jit(solution)/shard_map/ppermute | solution.py:322
  46.3 8.2 %collective-permute-start.8 = (f32[128,256]{1,0:T(8,128)S(1)}, f32[128,256]{1,0:T(8,128)S(1)}, u32[]{:S(2)}, u32[]{:S(2)}) collective-permute-start(f32[128,256]{1,0:T(8,128)S(1)} %get-tuple-element.93), channel_id=1, source_target_pairs={{0,2},{1,3},{2,0},{3,1},{4,6},{5,7},{6,4},{7,5},{8,10},{9,11},{10,... | collective-permute-start | bytes 393224 | tf_op jit(solution)/shard_map/ppermute | solution.py:322
  57.4 10.2 %collective-permute-start.21 = (f32[2,128,1024]{2,1,0:T(8,128)S(1)}, f32[2,128,1024]{2,1,0:T(8,128)S(1)}, u32[]{:S(2)}, u32[]{:S(2)}) collective-permute-start(f32[2,128,1024]{2,1,0:T(8,128)S(1)} %deal.1), channel_id=1, source_target_pairs={{0,8},{8,0},{16,24},{24,16},{1,9},{9,1},{17,25},{25,17},{2,10},{10... | collective-permute-start | bytes 3145736 | tf_op jit(solution)/shard_map/ppermute | solution.py:325
  57.4 6.1 %collective-permute-start.14 = (f32[128,256]{1,0:T(8,128)S(1)}, f32[128,256]{1,0:T(8,128)S(1)}, u32[]{:S(2)}, u32[]{:S(2)}) collective-permute-start(f32[128,256]{1,0:T(8,128)S(1)} %get-tuple-element.116), channel_id=1, source_target_pairs={{0,1},{1,0},{2,3},{3,2},{4,5},{5,4},{6,7},{7,6},{8,9},{9,8},{10,11... | collective-permute-start | bytes 393224 | tf_op jit(solution)/shard_map/ppermute | solution.py:322
  59.4 6.3 %collective-permute-start.15 = (f32[128,256]{1,0:T(8,128)S(1)}, f32[128,256]{1,0:T(8,128)S(1)}, u32[]{:S(2)}, u32[]{:S(2)}) collective-permute-start(f32[128,256]{1,0:T(8,128)S(1)} %get-tuple-element.117), channel_id=1, source_target_pairs={{0,2},{1,3},{2,0},{3,1},{4,6},{5,7},{6,4},{7,5},{8,10},{9,11},{10,... | collective-permute-start | bytes 393224 | tf_op jit(solution)/shard_map/ppermute | solution.py:322
  59.5 8.1 %collective-permute-start.16 = (f32[128,256]{1,0:T(8,128)S(1)}, f32[128,256]{1,0:T(8,128)S(1)}, u32[]{:S(2)}, u32[]{:S(2)}) collective-permute-start(f32[128,256]{1,0:T(8,128)S(1)} %get-tuple-element.118), channel_id=1, source_target_pairs={{0,3},{1,2},{2,1},{3,0},{4,7},{5,6},{6,5},{7,4},{8,11},{9,10},{10,... | collective-permute-start | bytes 393224 | tf_op jit(solution)/shard_map/ppermute | solution.py:322
  68.2 6.1 %collective-permute-start.17 = (f32[128,256]{1,0:T(8,128)S(1)}, f32[128,256]{1,0:T(8,128)S(1)}, u32[]{:S(2)}, u32[]{:S(2)}) collective-permute-start(f32[128,256]{1,0:T(8,128)S(1)} %get-tuple-element.119), channel_id=1, source_target_pairs={{0,1},{1,0},{2,3},{3,2},{4,5},{5,4},{6,7},{7,6},{8,9},{9,8},{10,11... | collective-permute-start | bytes 393224 | tf_op jit(solution)/shard_map/ppermute | solution.py:322
  70.2 6.6 %collective-permute-start.19 = (f32[128,256]{1,0:T(8,128)S(1)}, f32[128,256]{1,0:T(8,128)S(1)}, u32[]{:S(2)}, u32[]{:S(2)}) collective-permute-start(f32[128,256]{1,0:T(8,128)S(1)} %get-tuple-element.123), channel_id=1, source_target_pairs={{0,3},{1,2},{2,1},{3,0},{4,7},{5,6},{6,5},{7,4},{8,11},{9,10},{10,... | collective-permute-start | bytes 393224 | tf_op jit(solution)/shard_map/ppermute | solution.py:322
  77.4 8.8 %collective-permute-start.25 = (f32[2,128,256]{2,1,0:T(8,128)S(1)}, f32[2,128,256]{2,1,0:T(8,128)S(1)}, u32[]{:S(2)}, u32[]{:S(2)}) collective-permute-start(f32[2,128,256]{2,1,0:T(8,128)S(1)} %get-tuple-element.134), channel_id=1, source_target_pairs={{0,1},{1,0},{2,3},{3,2},{4,5},{5,4},{6,7},{7,6},{8,9},{9,8},{10,11... | collective-permute-start | bytes 786440 | tf_op jit(solution)/shard_map/ppermute | solution.py:322
  79.0 10.0 %collective-permute-start.26 = (f32[2,128,256]{2,1,0:T(8,128)S(1)}, f32[2,128,256]{2,1,0:T(8,128)S(1)}, u32[]{:S(2)}, u32[]{:S(2)}) collective-permute-start(f32[2,128,256]{2,1,0:T(8,128)S(1)} %get-tuple-element.133), channel_id=1, source_target_pairs={{0,1},{1,0},{2,3},{3,2},{4,5},{5,4},{6,7},{7,6},{8,9},{9,8},{10,11... | collective-permute-start | bytes 786440 | tf_op jit(solution)/shard_map/ppermute | solution.py:322
  86.3 7.4 %collective-permute-start.29 = (f32[128,256]{1,0:T(8,128)S(1)}, f32[128,256]{1,0:T(8,128)S(1)}, u32[]{:S(2)}, u32[]{:S(2)}) collective-permute-start(f32[128,256]{1,0:T(8,128)S(1)} %slice_bitcast_fusion), channel_id=1, source_target_pairs={{0,2},{1,3},{2,0},{3,1},{4,6},{5,7},{6,4},{7,5},{8,10},{9,11},{10,... | collective-permute-start | bytes 393224 | tf_op jit(solution)/shard_map/ppermute | solution.py:322
  89.1 10.4 %collective-permute-start.27 = (f32[128,256]{1,0:T(8,128)S(1)}, f32[128,256]{1,0:T(8,128)S(1)}, u32[]{:S(2)}, u32[]{:S(2)}) collective-permute-start(f32[128,256]{1,0:T(8,128)S(1)} %get-tuple-element.136), channel_id=1, source_target_pairs={{0,4},{1,5},{2,6},{3,7},{4,0},{5,1},{6,2},{7,3},{8,12},{9,13},{10,... | collective-permute-start | bytes 393224 | tf_op jit(solution)/shard_map/ppermute | solution.py:322
  90.9 8.6 %collective-permute-start.28 = (f32[128,256]{1,0:T(8,128)S(1)}, f32[128,256]{1,0:T(8,128)S(1)}, u32[]{:S(2)}, u32[]{:S(2)}) collective-permute-start(f32[128,256]{1,0:T(8,128)S(1)} %get-tuple-element.137), channel_id=1, source_target_pairs={{0,6},{1,7},{2,4},{3,5},{4,2},{5,3},{6,0},{7,1},{8,14},{9,15},{10,... | collective-permute-start | bytes 393224 | tf_op jit(solution)/shard_map/ppermute | solution.py:322
  (7 other events, 45.0 us)

commit v9 on v8

--- a/solution.py
+++ b/solution.py
@@ -128,8 +128,19 @@
         sent[k * bit : (k + 1) * bit] = ref[offset + bit : offset + 2 * bit]
 
 
-def project_body(q, n_dp, tokens, weight, decay, step, *refs):
-    bundles, (kept, dealt, held_t, held_w, held_d, held_s, sems) = refs[:q], refs[q:]
+def split_body(tokens, kept, dealt, held, sem):
+    copy = pltpu.make_async_copy(tokens, held, sem)
+    copy.start()
+    copy.wait()
+    half, _, each = kept.shape
+    dp = lax.axis_index("dp")
+    for r in range(2 * half):
+        to, at = (kept, r) if r < half else (dealt, r - half)
+        to[at] = columns(held, lax.bitwise_xor(dp, r) * each, each).astype(F32)
+
+
+def project_body(q, tokens, weight, decay, step, *refs):
+    bundles, (held_t, held_w, held_d, held_s, sems) = refs[:q], refs[q:]
     copies = [
         pltpu.make_async_copy(source, target, sems.at[k])
         for k, (source, target) in enumerate(
@@ -148,11 +159,6 @@
         bundles[r][:SPAN, :] = proj
         bundles[r][SPAN:, :SPAN] = held_d[pl.ds(at, heads), :]
         bundles[r][SPAN:, SPAN:] = held_s[pl.ds(at, heads), :]
-    each = tokens.shape[1] // n_dp
-    dp = lax.axis_index("dp")
-    for r in range(n_dp):
-        to, at = (kept, r) if r < n_dp // 2 else (dealt, r - n_dp // 2)
-        to[at] = columns(held_t, lax.bitwise_xor(dp, r) * each, each).astype(F32)
 
 
 def decays_body(q, heads, *refs):
@@ -339,8 +345,8 @@
         pltpu.VMEM(tokens.shape, BF16), pltpu.VMEM(proj_weight.shape, BF16),
         pltpu.VMEM((HEADS, SPAN), F32), pltpu.VMEM((HEADS, SPAN), F32), pltpu.SemaphoreType.DMA((4,)),
     )
-    outs = [out((SPAN + heads, 2 * STATE))] * q + [out((n_dp // 2, length, columns_each))] * 2
-    opened = call(functools.partial(project_body, q, n_dp), outs, scratch, name="project", hbm=4)(
+    outs = [out((SPAN + heads, 2 * STATE))] * q
+    opened = call(functools.partial(project_body, q), outs, scratch, name="project", hbm=4)(
         behind(tokens, packed[0]), proj_weight, log_decay[0], step_size[0]
     )
     bundles = [opened[0]] + [swap(opened[r], r) for r in range(1, q)]
@@ -348,8 +354,6 @@
     own = packed[q - 1]
     xg_in.append([swap(behind(packed[r - 1], opened[0]), r) for r in range(1, q)])
     bit = n_dp // 2
-    sources = {0: (opened[q], 0), bit: (across(behind(opened[q + 1], *xg_in[0]), bit), 0)}
-
     rows_of = (q, SPAN, group)
     outs = [
         out((q, SPAN, 2 * STATE), BF16), out((q, heads, SPAN)), out((q, SPAN, heads)),
@@ -357,7 +361,7 @@
     ]
     body = functools.partial(decays_body, q, heads)
     bcs, cums, a_cols, f1s, f2s, ds = call(body, outs, (pltpu.VMEM((q, heads, SPAN), F32),), name="decays")(
-        behind(bundles[0], *xg_in[0]), *bundles[1:]
+        *bundles
     )
 
     def hop(value, t):
@@ -380,6 +384,11 @@
         body = functools.partial(local_body, q, first, count)
         outs = [out(wide), out((q, SPAN, 2 * STATE))]
         local.append(call(body, outs, smem=1, name="local")(skip_gain, held[c][0], bcs, cums, a_cols))
+
+    outs = [out((bit, length, columns_each))] * 2
+    scratch = (pltpu.VMEM(tokens.shape, BF16), pltpu.SemaphoreType.DMA)
+    kept, dealt = call(split_body, outs, scratch, name="split", hbm=1)(behind(tokens, ahead, held[1][3]))
+    sources = {0: (kept, 0), bit: (across(dealt, bit), 0)}
 
     sent = [h[3] for h in held]
     arrived = [[] for _ in held]
@@ -416,10 +425,13 @@
             returned.append([swap(done[r], r) for r in range(1, q)])
             arrived[1][-1] = behind(arrived[1][-1], *returned[0])
 
+    gp = before[0]
+    for r in range(1, q):
+        gp = gp + swap(before[r], r)
     while bit > 1:
         bit //= 2
         order = list(sources)
-        arrays = behind(tuple(sources[r][0] for r in order), before[0])
+        arrays = behind(tuple(sources[r][0] for r in order), gp)
         body = functools.partial(deal_body, bit, [sources[r][1] for r in order])
         shape = (len(order) * bit, length, columns_each)
         (dealt,) = call(body, [out(shape)], name="deal")(*arrays)
@@ -427,11 +439,8 @@
         for k, r in enumerate(order):
             sources[r ^ bit] = got, k * bit
 
-    gp = before[0]
-    for r in range(1, q):
-        gp = gp + swap(before[r], r)
     returned.append([swap(behind(gx_parts[1][r], gp), r) for r in range(1, q)])
-    grads = {0: behind(gp, *(v for v, _ in sources.values()))}
+    grads = {0: gp}
     bit = n_dp // 2
     while bit:
         for r in list(grads):
@@ -450,7 +459,7 @@
     half = n_seq // 4
     far, far_sent, near, near_sent = call(body, [out((half, rows, 2 * STATE))] * 4, scratch, name="weight")(*args)
     far_in = swap(far_sent, 1)
-    near_in = swap(behind(near_sent, far_sent), 1)
+    near_in = swap(behind(near_sent, far_in), 1)
     far = far + far_in
     came = [swap(far[k], 2 * (half + k)) for k in range(half)]
     near = near + near_in

time: 100 us -> 99.7 us (level)
  starting transfers between devices: 41.5 us -> 38 us
  waiting for transfers between devices: 41.3 us -> 42.8 us
  Pallas kernels: 15.7 us -> 17 us
    ppermute x2, waiting for transfers between devices: 0.01 us -> 2.73 us  [hop(): return lax.ppermute(value, 'seq', pairs)]
    ppermute x23, waiting for transfers between devices: 40.4 us -> 38 us  [swap(): return lax.ppermute(value, 'seq', [(i, i ^ r) for i in range(n_seq)])]
    ppermute x2, starting transfers between devices: 5.86 us -> 3.61 us  [hop(): return lax.ppermute(value, 'seq', pairs)]
    ppermute x23, starting transfers between devices: 33.5 us -> 31.3 us  [swap(): return lax.ppermute(value, 'seq', [(i, i ^ r) for i in range(n_seq)])]
    pallas_call x13 -> x14, Pallas kernels: 15.7 us -> 17 us  [run(): pl.pallas_call(body, out_shape=tuple((o[0] if isinstance(o, list) else pl...]
    ppermute x5, waiting for transfers between devices: 0.96 us -> 2 us  [across(): return lax.ppermute(value, 'dp', [(i, i ^ r) for i in range(n_dp)])]
  transfers between devices with their start and end apart: 30 -> 30, of which waited for: 15 -> 19; matrix products, arithmetic and copies ran while one was open for 0% -> 0% of each run, Pallas kernels for 14% -> 12%
where the time goes in v9:
time: 99.7 us; the launch traced here: 99.5 us
  waiting for transfers between devices  42.8 us (43%)
  starting transfers between devices  38 us (38%)
  Pallas kernels  17 us (17%)
    ppermute x23, waiting for transfers between devices, swap(): return lax.ppermute(value, 'seq', [(i, i ^ r) for i in range(n_seq)])  38 us
    ppermute x23, starting transfers between devices, swap(): return lax.ppermute(value, 'seq', [(i, i ^ r) for i in range(n_seq)])  31.3 us
    pallas_call x14, Pallas kernels, run(): pl.pallas_call(body, out_shape=tuple((o[0] if isinstance(o, list) else pl...  17 us
    ppermute x2, starting transfers between devices, hop(): return lax.ppermute(value, 'seq', pairs)  3.61 us
    ppermute x5, starting transfers between devices, across(): return lax.ppermute(value, 'dp', [(i, i ^ r) for i in range(n_dp)])  3.12 us
    ppermute x2, waiting for transfers between devices, hop(): return lax.ppermute(value, 'seq', pairs)  2.73 us
    ppermute x5, waiting for transfers between devices, across(): return lax.ppermute(value, 'dp', [(i, i ^ r) for i in range(n_dp)])  2 us
  transfers between devices with their start and end apart: 30, of which 19 were waited for; matrix products, arithmetic and copies ran while one was open for 0% of the time, Pallas kernels for 12%

profile of v9, /device:TPU:0, one launch (start us, length us, event | category | flops | bytes accessed | tf_op | source)
XLA Modules:
  0.0 99.5 jit_solution(10486910487341215612)
XLA Ops:
  1.7 2.4 %project.1 = (f32[136,256]{1,0:T(8,128)S(1)}, f32[136,256]{1,0:T(8,128)S(1)}, f32[136,256]{1,0:T(8,128)S(1)}, f32[136,256]{1,0:T(8,128)S(1)}) custom-call(bf16[128,4096]{1,0:T(8,128)(2,1)} %bitcast.20, bf16[4096,256]{1,0:T(8,128)(2,1)} %weight.2, f32[32,128]{1,0:T(8,128)} %bitcast.27, f32[32,128]{1,0:T(8,128)} %bitcast.28), custom_call_target="tpu_custom_call" | custom-call | tf_op jit(solution)/shard_map/project/pallas_call | solution.py:63
  4.2 3.0 %collective-permute-start.3 = (f32[136,256]{1,0:T(8,128)S(1)}, f32[136,256]{1,0:T(8,128)S(1)}, u32[]{:S(2)}, u32[]{:S(2)}) collective-permute-start(f32[136,256]{1,0:T(8,128)S(1)} %get-tuple-element.73), channel_id=1, source_target_pairs={{0,1},{1,0},{2,3},{3,2},{4,5},{5,4},{6,7},{7,6},{8,9},{9,8},{10,11... | collective-permute-start | bytes 417800 | tf_op jit(solution)/shard_map/ppermute | solution.py:328
  7.2 1.6 %collective-permute-start.1 = (f32[2,128,256]{2,1,0:T(8,128)S(1)}, f32[2,128,256]{2,1,0:T(8,128)S(1)}, u32[]{:S(2)}, u32[]{:S(2)}) collective-permute-start(f32[2,128,256]{2,1,0:T(8,128)S(1)} %get-tuple-element.69), channel_id=1, source_target_pairs={{0,2},{1,3},{2,0},{3,1},{4,6},{5,7},{6,4},{7,5},{8,10},{9,11},{10,... | collective-permute-start | bytes 786440 | tf_op jit(solution)/shard_map/ppermute | solution.py:328
  13.9 5.5 %collective-permute-done.4.refs_2_ = f32[136,256]{1,0:T(8,128)S(1)} collective-permute-done((f32[136,256]{1,0:T(8,128)S(1)}, f32[136,256]{1,0:T(8,128)S(1)}, u32[]{:S(2)}, u32[]{:S(2)}) %collective-permute-start.4) | collective-permute-done | bytes 139296 | tf_op jit(solution)/shard_map/ppermute | solution.py:328
  22.0 2.0 %collective-permute-start.11 = (f32[2,128,256]{2,1,0:T(8,128)S(1)}, f32[2,128,256]{2,1,0:T(8,128)S(1)}, u32[]{:S(2)}, u32[]{:S(2)}) collective-permute-start(f32[2,128,256]{2,1,0:T(8,128)S(1)} %get-tuple-element.96), channel_id=1, source_target_pairs={{0,2},{1,3},{2,0},{3,1},{4,6},{5,7},{6,4},{7,5},{8,10},{9,11},{10,... | collective-permute-start | bytes 786440 | tf_op jit(solution)/shard_map/ppermute | solution.py:328
  25.5 1.9 %decays.1 = (bf16[4,128,256]{2,1,0:T(8,128)(2,1)S(1)}, f32[4,8,128]{2,1,0:T(8,128)S(1)}, f32[4,128,8]{2,1,0:T(8,128)S(1)}, f32[4,128,512]{2,1,0:T(8,128)S(1)}, f...) custom-call(f32[136,256]{1,0:T(8,128)S(1)} %get-tuple-element.72.refs_0_, ...), custom_call_target="tpu_custom_call" | custom-call | tf_op jit(solution)/shard_map/decays/pallas_call | solution.py:63
  27.6 5.7 %collective-permute-done.refs_1_ = f32[2,128,256]{2,1,0:T(8,128)S(1)} collective-permute-done((f32[2,128,256]{2,1,0:T(8,128)S(1)}, f32[2,128,256]{2,1,0:T(8,128)S(1)}, u32[]{:S(2)}, u32[]{:S(2)}) %collective-permute-start) | collective-permute-done | bytes 262176 | tf_op jit(solution)/shard_map/ppermute | solution.py:328
  34.3 3.1 %collective-permute-start.6 = (f32[128,256]{1,0:T(8,128)S(1)}, f32[128,256]{1,0:T(8,128)S(1)}, u32[]{:S(2)}, u32[]{:S(2)}) collective-permute-start(f32[128,256]{1,0:T(8,128)S(1)} %get-tuple-element.80), channel_id=1, source_target_pairs={{0,4},{1,5},{2,6},{3,7},{4,0},{5,1},{6,2},{7,3},{8,12},{9,13},{10,... | collective-permute-start | bytes 393224 | tf_op jit(solution)/shard_map/ppermute | solution.py:371
  37.4 2.1 %local.2 = (f32[4,128,256]{2,1,0:T(8,128)S(1)}, f32[4,128,256]{2,1,0:T(8,128)S(1)}) custom-call(f32[32]{0:T(128)S(1)} %copy-done, bf16[4,4,128,256]{3,2,1,0:T(8,128)(2,1)S(1)} %get-tuple-element.81.rows16.refs_1_, bf16[4,128,256]{2,1,0:T(8,128)(2,1)S(1)} %get-tuple-element.76.refs_4_.bcs.refs_5_, f32[4,8,128]{2,1,0:T(8,128)S(1)} %get-tuple-element.82.cums, ...), custom_call_target="tpu_custom_call" | custom-call | tf_op jit(solution)/shard_map/local/pallas_call | solution.py:63
  40.7 2.2 %collective-permute-done.6.refs_0_ = f32[128,256]{1,0:T(8,128)S(1)} collective-permute-done((f32[128,256]{1,0:T(8,128)S(1)}, f32[128,256]{1,0:T(8,128)S(1)}, u32[]{:S(2)}, u32[]{:S(2)}) %collective-permute-start.6) | collective-permute-done | bytes 131104 | tf_op jit(solution)/shard_map/ppermute | solution.py:371
  44.3 1.6 %collective-permute-start.20 = (f32[2,128,1024]{2,1,0:T(8,128)S(1)}, f32[2,128,1024]{2,1,0:T(8,128)S(1)}, u32[]{:S(2)}, u32[]{:S(2)}) collective-permute-start(f32[2,128,1024]{2,1,0:T(8,128)S(1)} %get-tuple-element.123), channel_id=1, source_target_pairs={{0,16},{8,24},{16,0},{24,8},{1,17},{9,25},{17,1},{25,9},{2,18},{10... | collective-permute-start | bytes 3145736 | tf_op jit(solution)/shard_map/ppermute | solution.py:331
  47.2 2.4 %collective-permute-start.8 = (f32[128,256]{1,0:T(8,128)S(1)}, f32[128,256]{1,0:T(8,128)S(1)}, u32[]{:S(2)}, u32[]{:S(2)}) collective-permute-start(f32[128,256]{1,0:T(8,128)S(1)} %get-tuple-element.90), channel_id=1, source_target_pairs={{0,2},{1,3},{2,0},{3,1},{4,6},{5,7},{6,4},{7,5},{8,10},{9,11},{10,... | collective-permute-start | bytes 393224 | tf_op jit(solution)/shard_map/ppermute | solution.py:328
  50.4 2.1 %local.3 = (f32[4,128,256]{2,1,0:T(8,128)S(1)}, f32[4,128,256]{2,1,0:T(8,128)S(1)}) custom-call(f32[32]{0:T(128)S(1)} %copy-done, bf16[4,4,128,256]{3,2,1,0:T(8,128)(2,1)S(1)} %get-tuple-element.103.rows16.refs_1_, bf16[4,128,256]{2,1,0:T(8,128)(2,1)S(1)} %get-tuple-element.76.refs_4_.bcs.refs_5_, f32[4,8,128]{2,1,0:T(8,128)S(1)} %get-tuple-element.82.cums, ...), custom_call_target="tpu_custom_call" | custom-call | tf_op jit(solution)/shard_map/local/pallas_call | solution.py:63
  54.0 1.7 %collective-permute-done.9.refs_3_ = f32[128,256]{1,0:T(8,128)S(1)} collective-permute-done((f32[128,256]{1,0:T(8,128)S(1)}, f32[128,256]{1,0:T(8,128)S(1)}, u32[]{:S(2)}, u32[]{:S(2)}) %collective-permute-start.9) | collective-permute-done | bytes 131104 | tf_op jit(solution)/shard_map/ppermute | solution.py:328
  59.7 2.8 %collective-permute-done.14 = f32[128,256]{1,0:T(8,128)S(1)} collective-permute-done((f32[128,256]{1,0:T(8,128)S(1)}, f32[128,256]{1,0:T(8,128)S(1)}, u32[]{:S(2)}, u32[]{:S(2)}) %collective-permute-start.14) | collective-permute-done | bytes 131104 | tf_op jit(solution)/shard_map/ppermute | solution.py:328
  62.6 2.2 %collective-permute-done.16 = f32[128,256]{1,0:T(8,128)S(1)} collective-permute-done((f32[128,256]{1,0:T(8,128)S(1)}, f32[128,256]{1,0:T(8,128)S(1)}, u32[]{:S(2)}, u32[]{:S(2)}) %collective-permute-start.16) | collective-permute-done | bytes 131104 | tf_op jit(solution)/shard_map/ppermute | solution.py:328
  65.6 1.7 %collective-permute-start.17 = (f32[128,256]{1,0:T(8,128)S(1)}, f32[128,256]{1,0:T(8,128)S(1)}, u32[]{:S(2)}, u32[]{:S(2)}) collective-permute-start(f32[128,256]{1,0:T(8,128)S(1)} %get-tuple-element.116), channel_id=1, source_target_pairs={{0,1},{1,0},{2,3},{3,2},{4,5},{5,4},{6,7},{7,6},{8,9},{9,8},{10,11... | collective-permute-start | bytes 393224 | tf_op jit(solution)/shard_map/ppermute | solution.py:328
  68.8 1.6 %collective-permute-start.18 = (f32[128,256]{1,0:T(8,128)S(1)}, f32[128,256]{1,0:T(8,128)S(1)}, u32[]{:S(2)}, u32[]{:S(2)}) collective-permute-start(f32[128,256]{1,0:T(8,128)S(1)} %get-tuple-element.118), channel_id=1, source_target_pairs={{0,2},{1,3},{2,0},{3,1},{4,6},{5,7},{6,4},{7,5},{8,10},{9,11},{10,... | collective-permute-start | bytes 393224 | tf_op jit(solution)/shard_map/ppermute | solution.py:328
  72.9 1.9 %collective-permute-done.18.refs_6_ = f32[128,256]{1,0:T(8,128)S(1)} collective-permute-done((f32[128,256]{1,0:T(8,128)S(1)}, f32[128,256]{1,0:T(8,128)S(1)}, u32[]{:S(2)}, u32[]{:S(2)}) %collective-permute-start.18) | collective-permute-done | bytes 131104 | tf_op jit(solution)/shard_map/ppermute | solution.py:328
  74.8 2.8 %collective-permute-done.19.refs_7_ = f32[128,256]{1,0:T(8,128)S(1)} collective-permute-done((f32[128,256]{1,0:T(8,128)S(1)}, f32[128,256]{1,0:T(8,128)S(1)}, u32[]{:S(2)}, u32[]{:S(2)}) %collective-permute-start.19) | collective-permute-done | bytes 131104 | tf_op jit(solution)/shard_map/ppermute | solution.py:328
  79.1 6.8 %collective-permute-done.25 = f32[2,128,256]{2,1,0:T(8,128)S(1)} collective-permute-done((f32[2,128,256]{2,1,0:T(8,128)S(1)}, f32[2,128,256]{2,1,0:T(8,128)S(1)}, u32[]{:S(2)}, u32[]{:S(2)}) %collective-permute-start.25) | collective-permute-done | bytes 262176 | tf_op jit(solution)/shard_map/ppermute | solution.py:328
  86.7 2.3 %collective-permute-start.27 = (f32[128,256]{1,0:T(8,128)S(1)}, f32[128,256]{1,0:T(8,128)S(1)}, u32[]{:S(2)}, u32[]{:S(2)}) collective-permute-start(f32[128,256]{1,0:T(8,128)S(1)} %get-tuple-element.132), channel_id=1, source_target_pairs={{0,4},{1,5},{2,6},{3,7},{4,0},{5,1},{6,2},{7,3},{8,12},{9,13},{10,... | collective-permute-start | bytes 393224 | tf_op jit(solution)/shard_map/ppermute | solution.py:328
  90.4 2.1 %collective-permute-done.26 = f32[2,128,256]{2,1,0:T(8,128)S(1)} collective-permute-done((f32[2,128,256]{2,1,0:T(8,128)S(1)}, f32[2,128,256]{2,1,0:T(8,128)S(1)}, u32[]{:S(2)}, u32[]{:S(2)}) %collective-permute-start.26) | collective-permute-done | bytes 262176 | tf_op jit(solution)/shard_map/ppermute | solution.py:328
  94.6 3.5 %collective-permute-done.27 = f32[128,256]{1,0:T(8,128)S(1)} collective-permute-done((f32[128,256]{1,0:T(8,128)S(1)}, f32[128,256]{1,0:T(8,128)S(1)}, u32[]{:S(2)}, u32[]{:S(2)}) %collective-permute-start.27) | collective-permute-done | bytes 131104 | tf_op jit(solution)/shard_map/ppermute | solution.py:328
  (58 shorter events, 33.6 us)
Async XLA Ops:
  4.2 8.0 %collective-permute-start.3 = (f32[136,256]{1,0:T(8,128)S(1)}, f32[136,256]{1,0:T(8,128)S(1)}, u32[]{:S(2)}, u32[]{:S(2)}) collective-permute-start(f32[136,256]{1,0:T(8,128)S(1)} %get-tuple-element.73), channel_id=1, source_target_pairs={{0,1},{1,0},{2,3},{3,2},{4,5},{5,4},{6,7},{7,6},{8,9},{9,8},{10,11... | collective-permute-start | bytes 417800 | tf_op jit(solution)/shard_map/ppermute | solution.py:328
  7.2 16.8 %collective-permute-start.1 = (f32[2,128,256]{2,1,0:T(8,128)S(1)}, f32[2,128,256]{2,1,0:T(8,128)S(1)}, u32[]{:S(2)}, u32[]{:S(2)}) collective-permute-start(f32[2,128,256]{2,1,0:T(8,128)S(1)} %get-tuple-element.69), channel_id=1, source_target_pairs={{0,2},{1,3},{2,0},{3,1},{4,6},{5,7},{6,4},{7,5},{8,10},{9,11},{10,... | collective-permute-start | bytes 786440 | tf_op jit(solution)/shard_map/ppermute | solution.py:328
  8.8 10.6 %collective-permute-start.4 = (f32[136,256]{1,0:T(8,128)S(1)}, f32[136,256]{1,0:T(8,128)S(1)}, u32[]{:S(2)}, u32[]{:S(2)}) collective-permute-start(f32[136,256]{1,0:T(8,128)S(1)} %get-tuple-element.74), channel_id=1, source_target_pairs={{0,2},{1,3},{2,0},{3,1},{4,6},{5,7},{6,4},{7,5},{8,10},{9,11},{10,... | collective-permute-start | bytes 417800 | tf_op jit(solution)/shard_map/ppermute | solution.py:328
  9.2 12.8 %collective-permute-start.5 = (f32[136,256]{1,0:T(8,128)S(1)}, f32[136,256]{1,0:T(8,128)S(1)}, u32[]{:S(2)}, u32[]{:S(2)}) collective-permute-start(f32[136,256]{1,0:T(8,128)S(1)} %get-tuple-element.75), channel_id=1, source_target_pairs={{0,3},{1,2},{2,1},{3,0},{4,7},{5,6},{6,5},{7,4},{8,11},{9,10},{10,... | collective-permute-start | bytes 417800 | tf_op jit(solution)/shard_map/ppermute | solution.py:328
  10.7 16.8 %collective-permute-start.2 = (f32[2,128,256]{2,1,0:T(8,128)S(1)}, f32[2,128,256]{2,1,0:T(8,128)S(1)}, u32[]{:S(2)}, u32[]{:S(2)}) collective-permute-start(f32[2,128,256]{2,1,0:T(8,128)S(1)} %get-tuple-element.70), channel_id=1, source_target_pairs={{0,3},{1,2},{2,1},{3,0},{4,7},{5,6},{6,5},{7,4},{8,11},{9,10},{10,... | collective-permute-start | bytes 786440 | tf_op jit(solution)/shard_map/ppermute | solution.py:328
  12.1 21.1 %collective-permute-start = (f32[2,128,256]{2,1,0:T(8,128)S(1)}, f32[2,128,256]{2,1,0:T(8,128)S(1)}, u32[]{:S(2)}, u32[]{:S(2)}) collective-permute-start(f32[2,128,256]{2,1,0:T(8,128)S(1)} %get-tuple-element.68), channel_id=1, source_target_pairs={{0,1},{1,0},{2,3},{3,2},{4,5},{5,4},{6,7},{7,6},{8,9},{9,8},{10,11... | collective-permute-start | bytes 786440 | tf_op jit(solution)/shard_map/ppermute | solution.py:328
  19.4 20.2 %collective-permute-start.12 = (f32[2,128,256]{2,1,0:T(8,128)S(1)}, f32[2,128,256]{2,1,0:T(8,128)S(1)}, u32[]{:S(2)}, u32[]{:S(2)}) collective-permute-start(f32[2,128,256]{2,1,0:T(8,128)S(1)} %get-tuple-element.99), channel_id=1, source_target_pairs={{0,3},{1,2},{2,1},{3,0},{4,7},{5,6},{6,5},{7,4},{8,11},{9,10},{10,... | collective-permute-start | bytes 786440 | tf_op jit(solution)/shard_map/ppermute | solution.py:328
  22.0 17.6 %collective-permute-start.11 = (f32[2,128,256]{2,1,0:T(8,128)S(1)}, f32[2,128,256]{2,1,0:T(8,128)S(1)}, u32[]{:S(2)}, u32[]{:S(2)}) collective-permute-start(f32[2,128,256]{2,1,0:T(8,128)S(1)} %get-tuple-element.96), channel_id=1, source_target_pairs={{0,2},{1,3},{2,0},{3,1},{4,6},{5,7},{6,4},{7,5},{8,10},{9,11},{10,... | collective-permute-start | bytes 786440 | tf_op jit(solution)/shard_map/ppermute | solution.py:328
  24.0 15.6 %collective-permute-start.10 = (f32[2,128,256]{2,1,0:T(8,128)S(1)}, f32[2,128,256]{2,1,0:T(8,128)S(1)}, u32[]{:S(2)}, u32[]{:S(2)}) collective-permute-start(f32[2,128,256]{2,1,0:T(8,128)S(1)} %get-tuple-element.93), channel_id=1, source_target_pairs={{0,1},{1,0},{2,3},{3,2},{4,5},{5,4},{6,7},{7,6},{8,9},{9,8},{10,11... | collective-permute-start | bytes 786440 | tf_op jit(solution)/shard_map/ppermute | solution.py:328
  34.3 8.6 %collective-permute-start.6 = (f32[128,256]{1,0:T(8,128)S(1)}, f32[128,256]{1,0:T(8,128)S(1)}, u32[]{:S(2)}, u32[]{:S(2)}) collective-permute-start(f32[128,256]{1,0:T(8,128)S(1)} %get-tuple-element.80), channel_id=1, source_target_pairs={{0,4},{1,5},{2,6},{3,7},{4,0},{5,1},{6,2},{7,3},{8,12},{9,13},{10,... | collective-permute-start | bytes 393224 | tf_op jit(solution)/shard_map/ppermute | solution.py:371
  44.3 21.2 %collective-permute-start.20 = (f32[2,128,1024]{2,1,0:T(8,128)S(1)}, f32[2,128,1024]{2,1,0:T(8,128)S(1)}, u32[]{:S(2)}, u32[]{:S(2)}) collective-permute-start(f32[2,128,1024]{2,1,0:T(8,128)S(1)} %get-tuple-element.123), channel_id=1, source_target_pairs={{0,16},{8,24},{16,0},{24,8},{1,17},{9,25},{17,1},{25,9},{2,18},{10... | collective-permute-start | bytes 3145736 | tf_op jit(solution)/shard_map/ppermute | solution.py:331
  45.8 7.2 %collective-permute-start.13 = (f32[128,256]{1,0:T(8,128)S(1)}, f32[128,256]{1,0:T(8,128)S(1)}, u32[]{:S(2)}, u32[]{:S(2)}) collective-permute-start(f32[128,256]{1,0:T(8,128)S(1)} %get-tuple-element.102), channel_id=1, source_target_pairs={{0,4},{1,5},{2,6},{3,7},{4,0},{5,1},{6,2},{7,3},{8,12},{9,13},{10,... | collective-permute-start | bytes 393224 | tf_op jit(solution)/shard_map/ppermute | solution.py:371
  46.8 6.2 %collective-permute-start.7 = (f32[128,256]{1,0:T(8,128)S(1)}, f32[128,256]{1,0:T(8,128)S(1)}, u32[]{:S(2)}, u32[]{:S(2)}) collective-permute-start(f32[128,256]{1,0:T(8,128)S(1)} %get-tuple-element.89), channel_id=1, source_target_pairs={{0,1},{1,0},{2,3},{3,2},{4,5},{5,4},{6,7},{7,6},{8,9},{9,8},{10,11... | collective-permute-start | bytes 393224 | tf_op jit(solution)/shard_map/ppermute | solution.py:328
  47.2 6.9 %collective-permute-start.8 = (f32[128,256]{1,0:T(8,128)S(1)}, f32[128,256]{1,0:T(8,128)S(1)}, u32[]{:S(2)}, u32[]{:S(2)}) collective-permute-start(f32[128,256]{1,0:T(8,128)S(1)} %get-tuple-element.90), channel_id=1, source_target_pairs={{0,2},{1,3},{2,0},{3,1},{4,6},{5,7},{6,4},{7,5},{8,10},{9,11},{10,... | collective-permute-start | bytes 393224 | tf_op jit(solution)/shard_map/ppermute | solution.py:328
  49.6 6.1 %collective-permute-start.9 = (f32[128,256]{1,0:T(8,128)S(1)}, f32[128,256]{1,0:T(8,128)S(1)}, u32[]{:S(2)}, u32[]{:S(2)}) collective-permute-start(f32[128,256]{1,0:T(8,128)S(1)} %get-tuple-element.91), channel_id=1, source_target_pairs={{0,3},{1,2},{2,1},{3,0},{4,7},{5,6},{6,5},{7,4},{8,11},{9,10},{10,... | collective-permute-start | bytes 393224 | tf_op jit(solution)/shard_map/ppermute | solution.py:328
  56.2 6.4 %collective-permute-start.14 = (f32[128,256]{1,0:T(8,128)S(1)}, f32[128,256]{1,0:T(8,128)S(1)}, u32[]{:S(2)}, u32[]{:S(2)}) collective-permute-start(f32[128,256]{1,0:T(8,128)S(1)} %get-tuple-element.113), channel_id=1, source_target_pairs={{0,1},{1,0},{2,3},{3,2},{4,5},{5,4},{6,7},{7,6},{8,9},{9,8},{10,11... | collective-permute-start | bytes 393224 | tf_op jit(solution)/shard_map/ppermute | solution.py:328
  65.6 12.1 %collective-permute-start.21 = (f32[2,128,1024]{2,1,0:T(8,128)S(1)}, f32[2,128,1024]{2,1,0:T(8,128)S(1)}, u32[]{:S(2)}, u32[]{:S(2)}) collective-permute-start(f32[2,128,1024]{2,1,0:T(8,128)S(1)} %deal.1), channel_id=1, source_target_pairs={{0,8},{8,0},{16,24},{24,16},{1,9},{9,1},{17,25},{25,17},{2,10},{10... | collective-permute-start | bytes 3145736 | tf_op jit(solution)/shard_map/ppermute | solution.py:331
  70.4 7.2 %collective-permute-start.19 = (f32[128,256]{1,0:T(8,128)S(1)}, f32[128,256]{1,0:T(8,128)S(1)}, u32[]{:S(2)}, u32[]{:S(2)}) collective-permute-start(f32[128,256]{1,0:T(8,128)S(1)} %get-tuple-element.120), channel_id=1, source_target_pairs={{0,3},{1,2},{2,1},{3,0},{4,7},{5,6},{6,5},{7,4},{8,11},{9,10},{10,... | collective-permute-start | bytes 393224 | tf_op jit(solution)/shard_map/ppermute | solution.py:328
  71.5 6.1 %collective-permute-start.22 = (f32[128,256]{1,0:T(8,128)S(1)}, f32[128,256]{1,0:T(8,128)S(1)}, u32[]{:S(2)}, u32[]{:S(2)}) collective-permute-start(f32[128,256]{1,0:T(8,128)S(1)} %add_add_fusion.refs_3_), channel_id=1, source_target_pairs={{0,8},{8,0},{16,24},{24,16},{1,9},{9,1},{17,25},{25,17},{2,10},{10... | collective-permute-start | bytes 393224 | tf_op jit(solution)/shard_map/ppermute | solution.py:331
  78.2 7.6 %collective-permute-start.25 = (f32[2,128,256]{2,1,0:T(8,128)S(1)}, f32[2,128,256]{2,1,0:T(8,128)S(1)}, u32[]{:S(2)}, u32[]{:S(2)}) collective-permute-start(f32[2,128,256]{2,1,0:T(8,128)S(1)} %get-tuple-element.129), channel_id=1, source_target_pairs={{0,1},{1,0},{2,3},{3,2},{4,5},{5,4},{6,7},{7,6},{8,9},{9,8},{10,11... | collective-permute-start | bytes 786440 | tf_op jit(solution)/shard_map/ppermute | solution.py:328
  85.8 6.6 %collective-permute-start.26 = (f32[2,128,256]{2,1,0:T(8,128)S(1)}, f32[2,128,256]{2,1,0:T(8,128)S(1)}, u32[]{:S(2)}, u32[]{:S(2)}) collective-permute-start(f32[2,128,256]{2,1,0:T(8,128)S(1)} %get-tuple-element.130), channel_id=1, source_target_pairs={{0,1},{1,0},{2,3},{3,2},{4,5},{5,4},{6,7},{7,6},{8,9},{9,8},{10,11... | collective-permute-start | bytes 786440 | tf_op jit(solution)/shard_map/ppermute | solution.py:328
  86.7 11.4 %collective-permute-start.27 = (f32[128,256]{1,0:T(8,128)S(1)}, f32[128,256]{1,0:T(8,128)S(1)}, u32[]{:S(2)}, u32[]{:S(2)}) collective-permute-start(f32[128,256]{1,0:T(8,128)S(1)} %get-tuple-element.132), channel_id=1, source_target_pairs={{0,4},{1,5},{2,6},{3,7},{4,0},{5,1},{6,2},{7,3},{8,12},{9,13},{10,... | collective-permute-start | bytes 393224 | tf_op jit(solution)/shard_map/ppermute | solution.py:328
  89.0 9.1 %collective-permute-start.28 = (f32[128,256]{1,0:T(8,128)S(1)}, f32[128,256]{1,0:T(8,128)S(1)}, u32[]{:S(2)}, u32[]{:S(2)}) collective-permute-start(f32[128,256]{1,0:T(8,128)S(1)} %get-tuple-element.133), channel_id=1, source_target_pairs={{0,6},{1,7},{2,4},{3,5},{4,2},{5,3},{6,0},{7,1},{8,14},{9,15},{10,... | collective-permute-start | bytes 393224 | tf_op jit(solution)/shard_map/ppermute | solution.py:328
  92.5 6.2 %collective-permute-start.29 = (f32[128,256]{1,0:T(8,128)S(1)}, f32[128,256]{1,0:T(8,128)S(1)}, u32[]{:S(2)}, u32[]{:S(2)}) collective-permute-start(f32[128,256]{1,0:T(8,128)S(1)} %slice_bitcast_fusion), channel_id=1, source_target_pairs={{0,2},{1,3},{2,0},{3,1},{4,6},{5,7},{6,4},{7,5},{8,10},{9,11},{10,... | collective-permute-start | bytes 393224 | tf_op jit(solution)/shard_map/ppermute | solution.py:328
  (7 other events, 56.7 us)

commit v10 on v9

--- a/solution.py
+++ b/solution.py
@@ -11,7 +11,6 @@
 HEAD_DIM = 64
 STATE = 128
 SPAN = 128
-PARTS = 2
 F32 = jnp.float32
 BF16 = jnp.bfloat16
 VMEM_LIMIT = 16 * 1024 * 1024
@@ -41,11 +40,6 @@
     rest = a - high.astype(F32)
     mid = rest.astype(BF16)
     return high, mid, (rest - mid.astype(F32)).astype(BF16)
-
-
-def head_chunks(heads):
-    first = 2 * (heads * 5 // 16)
-    return [(0, first), (first, heads - first)]
 
 
 def call(body, outs, scratch=(), name=None, smem=0, hbm=0):
@@ -95,31 +89,27 @@
     return ref[:, pl.ds(pl.multiple_of(start, 128), width)]
 
 
-def pack_body(q, group, first, width, keep, x, g, *refs):
-    packed, rest = refs[: q - 1], list(refs[q - 1 :])
-    own = rest.pop(0) if keep else None
-    stage, sems = rest
+def pack_body(q, group, x, g, *refs):
+    packed, own, (stage, sems) = refs[: q - 1], refs[q - 1], refs[q:]
     y = in_group(q)
     copies = {}
     for r in range(1, q):
-        at = pl.multiple_of(lax.bitwise_xor(y, r) * group + first, 128)
+        at = pl.multiple_of(lax.bitwise_xor(y, r) * group, 128)
         for k, source in enumerate((x, g)):
             copies[r, k] = pltpu.make_async_copy(
-                source.at[:, pl.ds(at, width)], stage.at[r - 1, k], sems.at[r, k]
+                source.at[:, pl.ds(at, group)], stage.at[r - 1, k], sems.at[r, k]
             )
             copies[r, k].start()
-    if keep:
-        at = pl.multiple_of(y * group, 128)
-        for k, source in enumerate((x, g)):
-            copies[0, k] = pltpu.make_async_copy(source.at[:, pl.ds(at, group)], own.at[k], sems.at[0, k])
-            copies[0, k].start()
+    at = pl.multiple_of(y * group, 128)
+    for k, source in enumerate((x, g)):
+        copies[0, k] = pltpu.make_async_copy(source.at[:, pl.ds(at, group)], own.at[k], sems.at[0, k])
+        copies[0, k].start()
     for r in range(1, q):
         for k in range(2):
             copies[r, k].wait()
             packed[r - 1][k] = stage[r - 1, k].astype(F32)
-    if keep:
-        for k in range(2):
-            copies[0, k].wait()
+    for k in range(2):
+        copies[0, k].wait()
 
 
 def deal_body(bit, offsets, *refs):
@@ -190,26 +180,26 @@
         ds[b] = jnp.exp(total)
 
 
-def states_body(q, planes, at, *refs):
+def states_body(q, planes, *refs):
     it = iter(refs)
     own = next(it)
     xg_in = [next(it) for _ in range(q - 1)]
     bcs, f1s, f2s, ds, rows16, states, totals, sent, plane = it
     y = in_group(q)
     for k in range(2):
-        rows16[k, y] = own[k, :, at]
+        rows16[k, y] = own[k]
         for r in range(1, q):
             rows16[k, lax.bitwise_xor(y, r)] = xg_in[r - 1][k].astype(BF16)
     for b in range(q):
-        rows16[2, b] = (rows16[0, b].astype(F32) * f1s[b, :, at]).astype(BF16)
-        rows16[3, b] = (rows16[1, b].astype(F32) * f2s[b, :, at]).astype(BF16)
+        rows16[2, b] = (rows16[0, b].astype(F32) * f1s[b]).astype(BF16)
+        rows16[3, b] = (rows16[1, b].astype(F32) * f2s[b]).astype(BF16)
         states[0, b] = tn(bcs[b, :, :STATE], rows16[2, b])
         states[1, b] = tn(bcs[b, :, STATE:], rows16[3, b])
-    forward, backward, through = states[0, 0], states[1, q - 1], ds[0, :, at]
+    forward, backward, through = states[0, 0], states[1, q - 1], ds[0]
     for b in range(1, q):
-        forward = ds[b, :, at] * forward + states[0, b]
-        backward = ds[q - 1 - b, :, at] * backward + states[1, q - 1 - b]
-        through = through * ds[b, :, at]
+        forward = ds[b] * forward + states[0, b]
+        backward = ds[q - 1 - b] * backward + states[1, q - 1 - b]
+        through = through * ds[b]
     totals[0] = forward
     totals[1] = backward
     plane[...] = through
@@ -221,11 +211,11 @@
     sent[...] = jnp.where(up, totals[0], totals[1]) + plane[...] * came[...]
 
 
-def local_body(q, first, hc, skip, rows16, bcs, cums, a_cols, gx, gp):
+def local_body(q, hc, skip, rows16, bcs, cums, a_cols, gx, gp):
     rows, cols = iotas()
     causal = rows <= cols
     low = lax.broadcasted_iota(jnp.int32, (SPAN, 128), 1) < HEAD_DIM
-    skip_at = in_group(q) * (HEADS // q) + first
+    skip_at = in_group(q) * hc
     for b in range(q):
         b_cols, c_cols = bcs[b, :, :STATE], bcs[b, :, STATE:]
         kernel = nt(b_cols, c_cols)
@@ -235,7 +225,7 @@
             x, g = rows16[0, b, :, at], rows16[1, b, :, at]
             parts = []
             for half in range(2):
-                h = first + 2 * pair + half
+                h = 2 * pair + half
                 gap = cums[b, h : h + 1, :] - a_cols[b, :, h : h + 1]
                 decay = jnp.exp(jnp.where(causal, gap, -jnp.inf))
                 picked = jnp.where(low if half == 0 else ~low, x, jnp.zeros_like(x))
@@ -248,13 +238,12 @@
         gp[b, :, STATE:] = tn(mixed, b_cols)
 
 
-def final_body(q, planes, at, more, *refs):
+def final_body(q, planes, *refs):
     it = iter(refs)
     got = [next(it) for _ in range(planes - 1)]
     rows16, states, f1s, ds, bcs, gx, gp = [next(it) for _ in range(7)]
-    before = next(it) if more else None
     gx_out = [next(it) for _ in range(q)]
-    gp_sent = [next(it) for _ in range(q)] if more else []
+    gp_sent = [next(it) for _ in range(q)]
     gp_out, gx_all = it
     y = in_group(q)
     z = lax.div(lax.axis_index("seq"), q)
@@ -265,29 +254,27 @@
         after += jnp.where(z == planes - 2 - t, 1.0, 0.0) * came
     for b in range(q):
         part = gp[b, :, STATE:] + nt(rows16[3, b], start.astype(BF16))
-        gp_out[b, :, STATE:] = part if before is None else part + before[b, :, STATE:]
+        gp_out[b, :, STATE:] = part
         if b < q - 1:
-            start = ds[b, :, at] * start + states[0, b]
+            start = ds[b] * start + states[0, b]
     for b in range(q - 1, -1, -1):
         rounded = after.astype(BF16)
-        gx_all[b] = gx[b] + f1s[b, :, at] * nn(bcs[b, :, :STATE], rounded)
+        gx_all[b] = gx[b] + f1s[b] * nn(bcs[b, :, :STATE], rounded)
         part = gp[b, :, :STATE] + nt(rows16[2, b], rounded)
-        gp_out[b, :, :STATE] = part if before is None else part + before[b, :, :STATE]
+        gp_out[b, :, :STATE] = part
         if b > 0:
-            after = ds[b, :, at] * after + states[1, b]
+            after = ds[b] * after + states[1, b]
     for r in range(q):
         gx_out[r][...] = gx_all[lax.bitwise_xor(y, r)]
-        if more:
-            gp_sent[r][...] = gp_out[lax.bitwise_xor(y, r)]
-
-
-def assemble_body(q, group, spans, *refs):
+        gp_sent[r][...] = gp_out[lax.bitwise_xor(y, r)]
+
+
+def assemble_body(q, group, *refs):
     parts, result = refs[:-1], refs[-1]
     y = in_group(q)
     for r in range(q):
-        for c, (first, width) in enumerate(spans):
-            at = pl.multiple_of(lax.bitwise_xor(y, r) * group + first, 128)
-            result[:, pl.ds(at, width)] = parts[c * q + r][...].astype(BF16)
+        at = pl.multiple_of(lax.bitwise_xor(y, r) * group, 128)
+        result[:, pl.ds(at, group)] = parts[r][...].astype(BF16)
 
 
 def weight_body(n_dp, n_seq, rows, scale, places, *refs):
@@ -318,8 +305,6 @@
     planes = n_seq // q
     heads = HEADS // q
     group = heads * HEAD_DIM
-    chunks = head_chunks(heads)
-    spans = [(first * HEAD_DIM, count * HEAD_DIM) for first, count in chunks]
     tokens, x, g = layer_input[0], inputs[0], grad_out[0]
     length, features = tokens.shape
     seq = lax.axis_index("seq")
@@ -333,14 +318,11 @@
     columns_each = features // n_dp
     rows = columns_each // n_seq
 
-    def pack(first, width, keep):
-        scratch = (pltpu.VMEM((q - 1, 2, SPAN, width), BF16), pltpu.SemaphoreType.DMA((q, 2)))
-        outs = [out((2, SPAN, width))] * (q - 1) + [out((2, SPAN, group), BF16)] * keep
-        body = functools.partial(pack_body, q, group, first, width, keep)
-        return call(body, outs, scratch, name="pack", hbm=2)(x, g)
-
-    packed = pack(*spans[0], False)
-    xg_in = [[swap(packed[r - 1], r) for r in range(1, q)]]
+    scratch = (pltpu.VMEM((q - 1, 2, SPAN, group), BF16), pltpu.SemaphoreType.DMA((q, 2)))
+    outs = [out((2, SPAN, group))] * (q - 1) + [out((2, SPAN, group), BF16)]
+    packed = call(functools.partial(pack_body, q, group), outs, scratch, name="pack", hbm=2)(x, g)
+    own = packed[q - 1]
+    xg_in = [swap(packed[r - 1], r) for r in range(1, q)]
     scratch = (
         pltpu.VMEM(tokens.shape, BF16), pltpu.VMEM(proj_weight.shape, BF16),
         pltpu.VMEM((HEADS, SPAN), F32), pltpu.VMEM((HEADS, SPAN), F32), pltpu.SemaphoreType.DMA((4,)),
@@ -350,9 +332,6 @@
         behind(tokens, packed[0]), proj_weight, log_decay[0], step_size[0]
     )
     bundles = [opened[0]] + [swap(opened[r], r) for r in range(1, q)]
-    packed = pack(*spans[1], True)
-    own = packed[q - 1]
-    xg_in.append([swap(behind(packed[r - 1], opened[0]), r) for r in range(1, q)])
     bit = n_dp // 2
     rows_of = (q, SPAN, group)
     outs = [
@@ -370,60 +349,31 @@
         pairs += [(top * q + i, (top - 1) * q + i) for i in range(q)]
         return lax.ppermute(value, "seq", pairs)
 
-    held, local = [], []
-    for c, (first, count) in enumerate(chunks):
-        wide = (q, SPAN, count * HEAD_DIM)
-        state = out((STATE, wide[2]))
-        at = slice(first * HEAD_DIM, (first + count) * HEAD_DIM)
-        if c > 0:
-            ahead = hop(held[0][3], 0)
-            xg_in[c] = [behind(v, *local[0]) for v in xg_in[c]]
-        outs = [out((4,) + wide, BF16), out((2,) + wide), out((2, STATE, wide[2])), state, out((1, wide[2]))]
-        body = functools.partial(states_body, q, planes, at)
-        held.append(call(body, outs, name="states")(own, *xg_in[c], bcs, f1s, f2s, ds))
-        body = functools.partial(local_body, q, first, count)
-        outs = [out(wide), out((q, SPAN, 2 * STATE))]
-        local.append(call(body, outs, smem=1, name="local")(skip_gain, held[c][0], bcs, cums, a_cols))
+    state = (STATE, group)
+    outs = [out((4,) + rows_of, BF16), out((2,) + rows_of), out((2,) + state), out(state), out((1, group))]
+    body = functools.partial(states_body, q, planes)
+    rows16, states, totals, sent, through = call(body, outs, name="states")(own, *xg_in, bcs, f1s, f2s, ds)
+    arrived = []
+    for t in range(planes - 1):
+        arrived.append(hop(sent, t))
+        if t < planes - 2:
+            body = functools.partial(relay_body, q, t)
+            (sent,) = call(body, [out(state)], name="relay")(arrived[t], totals, through)
+    body = functools.partial(local_body, q, heads)
+    outs = [out(rows_of), out((q, SPAN, 2 * STATE))]
+    local = call(body, outs, smem=1, name="local")(skip_gain, rows16, bcs, cums, a_cols)
 
     outs = [out((bit, length, columns_each))] * 2
     scratch = (pltpu.VMEM(tokens.shape, BF16), pltpu.SemaphoreType.DMA)
-    kept, dealt = call(split_body, outs, scratch, name="split", hbm=1)(behind(tokens, ahead, held[1][3]))
+    kept, dealt = call(split_body, outs, scratch, name="split", hbm=1)(behind(tokens, bcs))
     sources = {0: (kept, 0), bit: (across(dealt, bit), 0)}
 
-    sent = [h[3] for h in held]
-    arrived = [[] for _ in held]
-    for t in range(planes - 1):
-        for c in range(PARTS):
-            if c == 1 and t == 0:
-                sent[c] = behind(sent[c], ahead)
-            came = ahead if c == t == 0 else hop(sent[c], t)
-            if t == max(planes - 3, 0):
-                came = behind(came, local[c])
-            if c > 0 and t < planes - 2:
-                came = behind(came, sent[c - 1])
-            arrived[c].append(came)
-            if t < planes - 2:
-                (sent[c],) = call(
-                    functools.partial(relay_body, q, t), [out(came.shape)], name="relay"
-                )(came, held[c][2], held[c][4])
-
-    before, gx_parts, returned = [], [], []
-    for c, (first, width) in enumerate(spans):
-        rows16, states = held[c][:2]
-        block, all_blocks = (SPAN, 2 * STATE), (q, SPAN, 2 * STATE)
-        outs = [out((SPAN, width))] * q + ([out(block)] * q if before else [out(all_blocks)])
-        scratch = (pltpu.VMEM((q, SPAN, width), F32),)
-        if before:
-            scratch = (pltpu.VMEM(all_blocks, F32),) + scratch
-        body = functools.partial(final_body, q, planes, slice(first, first + width), bool(before))
-        done = call(body, outs, scratch, name="final")(
-            *arrived[c], rows16, states, f1s, ds, bcs, *local[c], *before
-        )
-        gx_parts.append(list(done[:q]))
-        before = list(done[q:])
-        if c == 0:
-            returned.append([swap(done[r], r) for r in range(1, q)])
-            arrived[1][-1] = behind(arrived[1][-1], *returned[0])
+    all_blocks = (q, SPAN, 2 * STATE)
+    outs = [out((SPAN, group))] * q + [out(all_blocks[1:])] * q
+    scratch = (pltpu.VMEM(all_blocks, F32), pltpu.VMEM(rows_of, F32))
+    body = functools.partial(final_body, q, planes)
+    done = call(body, outs, scratch, name="final")(*arrived, rows16, states, f1s, ds, bcs, *local)
+    gx_parts, before = done[:q], done[q:]
 
     gp = before[0]
     for r in range(1, q):
@@ -439,7 +389,7 @@
         for k, r in enumerate(order):
             sources[r ^ bit] = got, k * bit
 
-    returned.append([swap(behind(gx_parts[1][r], gp), r) for r in range(1, q)])
+    returned = [swap(gx_parts[r], r) for r in range(1, q)]
     grads = {0: gp}
     bit = n_dp // 2
     while bit:
@@ -449,7 +399,7 @@
     scale = 1.0 / (length * n_seq)
     arrays = list({id(v): v for v, _ in sources.values()}.values())
     places = [([v is a for a in arrays].index(True), at) for v, at in (sources[r] for r in range(n_dp))]
-    args = arrays + [behind(grads[0], *returned[1])] + [grads[r] for r in range(1, n_dp)]
+    args = arrays + [behind(grads[0], *returned)] + [grads[r] for r in range(1, n_dp)]
     scratch = (
         pltpu.VMEM((n_dp, SPAN, columns_each), BF16),
         pltpu.VMEM((n_dp, SPAN, 2 * STATE), BF16),
@@ -468,8 +418,8 @@
     for part in came:
         grad_weight = grad_weight + part
 
-    body = functools.partial(assemble_body, q, group, spans)
-    parts = [v for c in range(PARTS) for v in (gx_parts[c][0], *returned[c])]
+    body = functools.partial(assemble_body, q, group)
+    parts = [gx_parts[0], *returned]
     (grad_x,) = call(body, [[out((length, q * group), BF16)]], name="assemble")(*parts)
     return grad_x[None], grad_weight
 

time: 99.7 us -> 101 us (1.013)
  waiting for transfers between devices: 42.8 us -> 56.1 us
  starting transfers between devices: 38 us -> 29.9 us
  Pallas kernels: 17 us -> 13.5 us
    ppermute x23 -> x17, starting transfers between devices: 31.3 us -> 23.8 us  [swap(): return lax.ppermute(value, 'seq', [(i, i ^ r) for i in range(n_seq)])]
    ppermute x23 -> x17, waiting for transfers between devices: 38 us -> 44.1 us  [swap(): return lax.ppermute(value, 'seq', [(i, i ^ r) for i in range(n_seq)])]
    ppermute x2 -> x1, waiting for transfers between devices: 2.73 us -> 8.53 us  [hop(): return lax.ppermute(value, 'seq', pairs)]
    pallas_call x14 -> x10, Pallas kernels: 17 us -> 13.5 us  [run(): pl.pallas_call(body, out_shape=tuple((o[0] if isinstance(o, list) else pl...]
    ppermute x5, waiting for transfers between devices: 2 us -> 3.52 us  [across(): return lax.ppermute(value, 'dp', [(i, i ^ r) for i in range(n_dp)])]
    ppermute x2 -> x1, starting transfers between devices: 3.61 us -> 2.69 us  [hop(): return lax.ppermute(value, 'seq', pairs)]
  transfers between devices with their start and end apart: 30 -> 23, of which waited for: 19 -> 16; matrix products, arithmetic and copies ran while one was open for 0% -> 0% of each run, Pallas kernels for 12% -> 9%
where the time goes in v10:
time: 101 us
  waiting for transfers between devices  56.1 us (56%)
  starting transfers between devices  29.9 us (30%)
  Pallas kernels  13.5 us (13%)
    ppermute x17, waiting for transfers between devices, swap(): return lax.ppermute(value, 'seq', [(i, i ^ r) for i in range(n_seq)])  44.1 us
    ppermute x17, starting transfers between devices, swap(): return lax.ppermute(value, 'seq', [(i, i ^ r) for i in range(n_seq)])  23.8 us
    pallas_call x10, Pallas kernels, run(): pl.pallas_call(body, out_shape=tuple((o[0] if isinstance(o, list) else pl...  13.5 us
    ppermute x1, waiting for transfers between devices, hop(): return lax.ppermute(value, 'seq', pairs)  8.53 us
    ppermute x5, waiting for transfers between devices, across(): return lax.ppermute(value, 'dp', [(i, i ^ r) for i in range(n_dp)])  3.52 us
    ppermute x5, starting transfers between devices, across(): return lax.ppermute(value, 'dp', [(i, i ^ r) for i in range(n_dp)])  3.44 us
    ppermute x1, starting transfers between devices, hop(): return lax.ppermute(value, 'seq', pairs)  2.69 us
  transfers between devices with their start and end apart: 23, of which 16 were waited for; matrix products, arithmetic and copies ran while one was open for 0% of the time, Pallas kernels for 9%

profile of v10, /device:TPU:0, one launch (start us, length us, event | category | flops | bytes accessed | tf_op | source)
XLA Modules:
  0.0 101.1 jit_solution(6710018700457987246)
XLA Ops:
  2.0 2.4 %project.1 = (f32[136,256]{1,0:T(8,128)S(1)}, f32[136,256]{1,0:T(8,128)S(1)}, f32[136,256]{1,0:T(8,128)S(1)}, f32[136,256]{1,0:T(8,128)S(1)}) custom-call(bf16[128,4096]{1,0:T(8,128)(2,1)} %bitcast.20, bf16[4096,256]{1,0:T(8,128)(2,1)} %weight.2, f32[32,128]{1,0:T(8,128)} %bitcast.25, f32[32,128]{1,0:T(8,128)} %bitcast.26), custom_call_target="tpu_custom_call" | custom-call | tf_op jit(solution)/shard_map/project/pallas_call | solution.py:57
  4.4 3.0 %collective-permute-start.3 = (f32[136,256]{1,0:T(8,128)S(1)}, f32[136,256]{1,0:T(8,128)S(1)}, u32[]{:S(2)}, u32[]{:S(2)}) collective-permute-start(f32[136,256]{1,0:T(8,128)S(1)} %get-tuple-element.47), channel_id=1, source_target_pairs={{0,1},{1,0},{2,3},{3,2},{4,5},{5,4},{6,7},{7,6},{8,9},{9,8},{10,11... | collective-permute-start | bytes 417800 | tf_op jit(solution)/shard_map/ppermute | solution.py:313
  7.5 1.6 %collective-permute-start.4 = (f32[136,256]{1,0:T(8,128)S(1)}, f32[136,256]{1,0:T(8,128)S(1)}, u32[]{:S(2)}, u32[]{:S(2)}) collective-permute-start(f32[136,256]{1,0:T(8,128)S(1)} %get-tuple-element.48), channel_id=1, source_target_pairs={{0,2},{1,3},{2,0},{3,1},{4,6},{5,7},{6,4},{7,5},{8,10},{9,11},{10,... | collective-permute-start | bytes 417800 | tf_op jit(solution)/shard_map/ppermute | solution.py:313
  9.0 1.9 %collective-permute-start = (f32[2,128,512]{2,1,0:T(8,128)S(1)}, f32[2,128,512]{2,1,0:T(8,128)S(1)}, u32[]{:S(2)}, u32[]{:S(2)}) collective-permute-start(f32[2,128,512]{2,1,0:T(8,128)S(1)} %get-tuple-element.42), channel_id=1, source_target_pairs={{0,1},{1,0},{2,3},{3,2},{4,5},{5,4},{6,7},{7,6},{8,9},{9,8},{10,11... | collective-permute-start | bytes 1572872 | tf_op jit(solution)/shard_map/ppermute | solution.py:313
  11.0 1.6 %collective-permute-start.1 = (f32[2,128,512]{2,1,0:T(8,128)S(1)}, f32[2,128,512]{2,1,0:T(8,128)S(1)}, u32[]{:S(2)}, u32[]{:S(2)}) collective-permute-start(f32[2,128,512]{2,1,0:T(8,128)S(1)} %get-tuple-element.43), channel_id=1, source_target_pairs={{0,2},{1,3},{2,0},{3,1},{4,6},{5,7},{6,4},{7,5},{8,10},{9,11},{10,... | collective-permute-start | bytes 1572872 | tf_op jit(solution)/shard_map/ppermute | solution.py:313
  12.5 2.2 %collective-permute-start.2 = (f32[2,128,512]{2,1,0:T(8,128)S(1)}, f32[2,128,512]{2,1,0:T(8,128)S(1)}, u32[]{:S(2)}, u32[]{:S(2)}) collective-permute-start(f32[2,128,512]{2,1,0:T(8,128)S(1)} %get-tuple-element.44), channel_id=1, source_target_pairs={{0,3},{1,2},{2,1},{3,0},{4,7},{5,6},{6,5},{7,4},{8,11},{9,10},{10,... | collective-permute-start | bytes 1572872 | tf_op jit(solution)/shard_map/ppermute | solution.py:313
  14.7 1.9 %collective-permute-done.5.refs_3_ = f32[136,256]{1,0:T(8,128)S(1)} collective-permute-done((f32[136,256]{1,0:T(8,128)S(1)}, f32[136,256]{1,0:T(8,128)S(1)}, u32[]{:S(2)}, u32[]{:S(2)}) %collective-permute-start.5) | collective-permute-done | bytes 139296 | tf_op jit(solution)/shard_map/ppermute | solution.py:313
  16.6 1.9 %decays.1 = (bf16[4,128,256]{2,1,0:T(8,128)(2,1)S(1)}, f32[4,8,128]{2,1,0:T(8,128)S(1)}, f32[4,128,8]{2,1,0:T(8,128)S(1)}, f32[4,128,512]{2,1,0:T(8,128)S(1)}, f...) custom-call(f32[136,256]{1,0:T(8,128)S(1)} %get-tuple-element.46.refs_0_, ...), custom_call_target="tpu_custom_call" | custom-call | tf_op jit(solution)/shard_map/decays/pallas_call | solution.py:57
  19.9 1.5 %collective-permute-start.10 = (f32[2,128,1024]{2,1,0:T(8,128)S(1)}, f32[2,128,1024]{2,1,0:T(8,128)S(1)}, u32[]{:S(2)}, u32[]{:S(2)}) collective-permute-start(f32[2,128,1024]{2,1,0:T(8,128)S(1)} %get-tuple-element.67), channel_id=1, source_target_pairs={{0,16},{8,24},{16,0},{24,8},{1,17},{9,25},{17,1},{25,9},{2,18},{10... | collective-permute-start | bytes 3145736 | tf_op jit(solution)/shard_map/ppermute | solution.py:316
  21.4 3.9 %collective-permute-done.refs_1_ = f32[2,128,512]{2,1,0:T(8,128)S(1)} collective-permute-done((f32[2,128,512]{2,1,0:T(8,128)S(1)}, f32[2,128,512]{2,1,0:T(8,128)S(1)}, u32[]{:S(2)}, u32[]{:S(2)}) %collective-permute-start) | collective-permute-done | bytes 524320 | tf_op jit(solution)/shard_map/ppermute | solution.py:313
  25.4 2.9 %collective-permute-done.1.refs_2_ = f32[2,128,512]{2,1,0:T(8,128)S(1)} collective-permute-done((f32[2,128,512]{2,1,0:T(8,128)S(1)}, f32[2,128,512]{2,1,0:T(8,128)S(1)}, u32[]{:S(2)}, u32[]{:S(2)}) %collective-permute-start.1) | collective-permute-done | bytes 524320 | tf_op jit(solution)/shard_map/ppermute | solution.py:313
  28.3 9.6 %collective-permute-done.2.refs_3_ = f32[2,128,512]{2,1,0:T(8,128)S(1)} collective-permute-done((f32[2,128,512]{2,1,0:T(8,128)S(1)}, f32[2,128,512]{2,1,0:T(8,128)S(1)}, u32[]{:S(2)}, u32[]{:S(2)}) %collective-permute-start.2) | collective-permute-done | bytes 524320 | tf_op jit(solution)/shard_map/ppermute | solution.py:313
  39.4 2.7 %collective-permute-start.6 = (f32[128,512]{1,0:T(8,128)S(1)}, f32[128,512]{1,0:T(8,128)S(1)}, u32[]{:S(2)}, u32[]{:S(2)}) collective-permute-start(f32[128,512]{1,0:T(8,128)S(1)} %get-tuple-element.54), channel_id=1, source_target_pairs={{0,4},{1,5},{2,6},{3,7},{4,0},{5,1},{6,2},{7,3},{8,12},{9,13},{10,... | collective-permute-start | bytes 786440 | tf_op jit(solution)/shard_map/ppermute | solution.py:350
  42.0 2.6 %local.1 = (f32[4,128,512]{2,1,0:T(8,128)S(1)}, f32[4,128,256]{2,1,0:T(8,128)S(1)}) custom-call(f32[32]{0:T(128)S(1)} %copy-done, bf16[4,4,128,512]{3,2,1,0:T(8,128)(2,1)S(1)} %get-tuple-element.55.rows16.refs_1_, bf16[4,128,256]{2,1,0:T(8,128)(2,1)S(1)} %get-tuple-element.50.refs_4_.bcs.refs_5_, f32[4,8,128]{2,1,0:T(8,128)S(1)} %get-tuple-element.57.cums, ...), custom_call_target="tpu_custom_call" | custom-call | tf_op jit(solution)/shard_map/local/pallas_call | solution.py:57
  44.7 8.5 %collective-permute-done.6.refs_0_ = f32[128,512]{1,0:T(8,128)S(1)} collective-permute-done((f32[128,512]{1,0:T(8,128)S(1)}, f32[128,512]{1,0:T(8,128)S(1)}, u32[]{:S(2)}, u32[]{:S(2)}) %collective-permute-start.6) | collective-permute-done | bytes 262176 | tf_op jit(solution)/shard_map/ppermute | solution.py:350
  55.9 1.7 %collective-permute-start.13 = (f32[128,256]{1,0:T(8,128)S(1)}, f32[128,256]{1,0:T(8,128)S(1)}, u32[]{:S(2)}, u32[]{:S(2)}) collective-permute-start(f32[128,256]{1,0:T(8,128)S(1)} %get-tuple-element.71), channel_id=1, source_target_pairs={{0,3},{1,2},{2,1},{3,0},{4,7},{5,6},{6,5},{7,4},{8,11},{9,10},{10,... | collective-permute-start | bytes 393224 | tf_op jit(solution)/shard_map/ppermute | solution.py:313
  57.6 1.9 %collective-permute-done.11 = f32[128,256]{1,0:T(8,128)S(1)} collective-permute-done((f32[128,256]{1,0:T(8,128)S(1)}, f32[128,256]{1,0:T(8,128)S(1)}, u32[]{:S(2)}, u32[]{:S(2)}) %collective-permute-start.11) | collective-permute-done | bytes 131104 | tf_op jit(solution)/shard_map/ppermute | solution.py:313
  60.8 2.3 %collective-permute-done.13 = f32[128,256]{1,0:T(8,128)S(1)} collective-permute-done((f32[128,256]{1,0:T(8,128)S(1)}, f32[128,256]{1,0:T(8,128)S(1)}, u32[]{:S(2)}, u32[]{:S(2)}) %collective-permute-start.13) | collective-permute-done | bytes 131104 | tf_op jit(solution)/shard_map/ppermute | solution.py:313
  63.9 1.7 %collective-permute-start.8 = (f32[128,512]{1,0:T(8,128)S(1)}, f32[128,512]{1,0:T(8,128)S(1)}, u32[]{:S(2)}, u32[]{:S(2)}) collective-permute-start(f32[128,512]{1,0:T(8,128)S(1)} %get-tuple-element.63), channel_id=1, source_target_pairs={{0,2},{1,3},{2,0},{3,1},{4,6},{5,7},{6,4},{7,5},{8,10},{9,11},{10,... | collective-permute-start | bytes 786440 | tf_op jit(solution)/shard_map/ppermute | solution.py:313
  68.3 3.5 %collective-permute-done.16.refs_5_ = f32[128,256]{1,0:T(8,128)S(1)} collective-permute-done((f32[128,256]{1,0:T(8,128)S(1)}, f32[128,256]{1,0:T(8,128)S(1)}, u32[]{:S(2)}, u32[]{:S(2)}) %collective-permute-start.16) | collective-permute-done | bytes 131104 | tf_op jit(solution)/shard_map/ppermute | solution.py:316
  73.0 5.8 %collective-permute-done.9.refs_3_ = f32[128,512]{1,0:T(8,128)S(1)} collective-permute-done((f32[128,512]{1,0:T(8,128)S(1)}, f32[128,512]{1,0:T(8,128)S(1)}, u32[]{:S(2)}, u32[]{:S(2)}) %collective-permute-start.9) | collective-permute-done | bytes 262176 | tf_op jit(solution)/shard_map/ppermute | solution.py:313
  80.0 7.0 %collective-permute-done.18 = f32[2,128,256]{2,1,0:T(8,128)S(1)} collective-permute-done((f32[2,128,256]{2,1,0:T(8,128)S(1)}, f32[2,128,256]{2,1,0:T(8,128)S(1)}, u32[]{:S(2)}, u32[]{:S(2)}) %collective-permute-start.18) | collective-permute-done | bytes 262176 | tf_op jit(solution)/shard_map/ppermute | solution.py:313
  87.6 3.4 %collective-permute-start.20 = (f32[128,256]{1,0:T(8,128)S(1)}, f32[128,256]{1,0:T(8,128)S(1)}, u32[]{:S(2)}, u32[]{:S(2)}) collective-permute-start(f32[128,256]{1,0:T(8,128)S(1)} %get-tuple-element.80), channel_id=1, source_target_pairs={{0,4},{1,5},{2,6},{3,7},{4,0},{5,1},{6,2},{7,3},{8,12},{9,13},{10,... | collective-permute-start | bytes 393224 | tf_op jit(solution)/shard_map/ppermute | solution.py:313
  95.2 4.6 %collective-permute-done.20 = f32[128,256]{1,0:T(8,128)S(1)} collective-permute-done((f32[128,256]{1,0:T(8,128)S(1)}, f32[128,256]{1,0:T(8,128)S(1)}, u32[]{:S(2)}, u32[]{:S(2)}) %collective-permute-start.20) | collective-permute-done | bytes 131104 | tf_op jit(solution)/shard_map/ppermute | solution.py:313
  (40 shorter events, 20.2 us)
Async XLA Ops:
  4.4 8.1 %collective-permute-start.3 = (f32[136,256]{1,0:T(8,128)S(1)}, f32[136,256]{1,0:T(8,128)S(1)}, u32[]{:S(2)}, u32[]{:S(2)}) collective-permute-start(f32[136,256]{1,0:T(8,128)S(1)} %get-tuple-element.47), channel_id=1, source_target_pairs={{0,1},{1,0},{2,3},{3,2},{4,5},{5,4},{6,7},{7,6},{8,9},{9,8},{10,11... | collective-permute-start | bytes 417800 | tf_op jit(solution)/shard_map/ppermute | solution.py:313
  7.5 7.2 %collective-permute-start.4 = (f32[136,256]{1,0:T(8,128)S(1)}, f32[136,256]{1,0:T(8,128)S(1)}, u32[]{:S(2)}, u32[]{:S(2)}) collective-permute-start(f32[136,256]{1,0:T(8,128)S(1)} %get-tuple-element.48), channel_id=1, source_target_pairs={{0,2},{1,3},{2,0},{3,1},{4,6},{5,7},{6,4},{7,5},{8,10},{9,11},{10,... | collective-permute-start | bytes 417800 | tf_op jit(solution)/shard_map/ppermute | solution.py:313
  9.0 7.6 %collective-permute-start.5 = (f32[136,256]{1,0:T(8,128)S(1)}, f32[136,256]{1,0:T(8,128)S(1)}, u32[]{:S(2)}, u32[]{:S(2)}) collective-permute-start(f32[136,256]{1,0:T(8,128)S(1)} %get-tuple-element.49), channel_id=1, source_target_pairs={{0,3},{1,2},{2,1},{3,0},{4,7},{5,6},{6,5},{7,4},{8,11},{9,10},{10,... | collective-permute-start | bytes 417800 | tf_op jit(solution)/shard_map/ppermute | solution.py:313
  9.0 16.3 %collective-permute-start = (f32[2,128,512]{2,1,0:T(8,128)S(1)}, f32[2,128,512]{2,1,0:T(8,128)S(1)}, u32[]{:S(2)}, u32[]{:S(2)}) collective-permute-start(f32[2,128,512]{2,1,0:T(8,128)S(1)} %get-tuple-element.42), channel_id=1, source_target_pairs={{0,1},{1,0},{2,3},{3,2},{4,5},{5,4},{6,7},{7,6},{8,9},{9,8},{10,11... | collective-permute-start | bytes 1572872 | tf_op jit(solution)/shard_map/ppermute | solution.py:313
  11.0 17.3 %collective-permute-start.1 = (f32[2,128,512]{2,1,0:T(8,128)S(1)}, f32[2,128,512]{2,1,0:T(8,128)S(1)}, u32[]{:S(2)}, u32[]{:S(2)}) collective-permute-start(f32[2,128,512]{2,1,0:T(8,128)S(1)} %get-tuple-element.43), channel_id=1, source_target_pairs={{0,2},{1,3},{2,0},{3,1},{4,6},{5,7},{6,4},{7,5},{8,10},{9,11},{10,... | collective-permute-start | bytes 1572872 | tf_op jit(solution)/shard_map/ppermute | solution.py:313
  12.5 25.4 %collective-permute-start.2 = (f32[2,128,512]{2,1,0:T(8,128)S(1)}, f32[2,128,512]{2,1,0:T(8,128)S(1)}, u32[]{:S(2)}, u32[]{:S(2)}) collective-permute-start(f32[2,128,512]{2,1,0:T(8,128)S(1)} %get-tuple-element.44), channel_id=1, source_target_pairs={{0,3},{1,2},{2,1},{3,0},{4,7},{5,6},{6,5},{7,4},{8,11},{9,10},{10,... | collective-permute-start | bytes 1572872 | tf_op jit(solution)/shard_map/ppermute | solution.py:313
  19.9 43.2 %collective-permute-start.10 = (f32[2,128,1024]{2,1,0:T(8,128)S(1)}, f32[2,128,1024]{2,1,0:T(8,128)S(1)}, u32[]{:S(2)}, u32[]{:S(2)}) collective-permute-start(f32[2,128,1024]{2,1,0:T(8,128)S(1)} %get-tuple-element.67), channel_id=1, source_target_pairs={{0,16},{8,24},{16,0},{24,8},{1,17},{9,25},{17,1},{25,9},{2,18},{10... | collective-permute-start | bytes 3145736 | tf_op jit(solution)/shard_map/ppermute | solution.py:316
  37.9 4.2 %copy-start = (f32[32]{0:T(128)S(1)}, f32[32]{0:T(128)}, u32[]{:S(2)}) copy-start(f32[32]{0:T(128)} %skip.1) | copy-start | bytes 388
  39.4 13.9 %collective-permute-start.6 = (f32[128,512]{1,0:T(8,128)S(1)}, f32[128,512]{1,0:T(8,128)S(1)}, u32[]{:S(2)}, u32[]{:S(2)}) collective-permute-start(f32[128,512]{1,0:T(8,128)S(1)} %get-tuple-element.54), channel_id=1, source_target_pairs={{0,4},{1,5},{2,6},{3,7},{4,0},{5,1},{6,2},{7,3},{8,12},{9,13},{10,... | collective-permute-start | bytes 786440 | tf_op jit(solution)/shard_map/ppermute | solution.py:350
  54.0 5.5 %collective-permute-start.11 = (f32[128,256]{1,0:T(8,128)S(1)}, f32[128,256]{1,0:T(8,128)S(1)}, u32[]{:S(2)}, u32[]{:S(2)}) collective-permute-start(f32[128,256]{1,0:T(8,128)S(1)} %get-tuple-element.69), channel_id=1, source_target_pairs={{0,1},{1,0},{2,3},{3,2},{4,5},{5,4},{6,7},{7,6},{8,9},{9,8},{10,11... | collective-permute-start | bytes 393224 | tf_op jit(solution)/shard_map/ppermute | solution.py:313
  55.2 5.5 %collective-permute-start.12 = (f32[128,256]{1,0:T(8,128)S(1)}, f32[128,256]{1,0:T(8,128)S(1)}, u32[]{:S(2)}, u32[]{:S(2)}) collective-permute-start(f32[128,256]{1,0:T(8,128)S(1)} %get-tuple-element.70), channel_id=1, source_target_pairs={{0,2},{1,3},{2,0},{3,1},{4,6},{5,7},{6,4},{7,5},{8,10},{9,11},{10,... | collective-permute-start | bytes 393224 | tf_op jit(solution)/shard_map/ppermute | solution.py:313
  55.9 7.2 %collective-permute-start.13 = (f32[128,256]{1,0:T(8,128)S(1)}, f32[128,256]{1,0:T(8,128)S(1)}, u32[]{:S(2)}, u32[]{:S(2)}) collective-permute-start(f32[128,256]{1,0:T(8,128)S(1)} %get-tuple-element.71), channel_id=1, source_target_pairs={{0,3},{1,2},{2,1},{3,0},{4,7},{5,6},{6,5},{7,4},{8,11},{9,10},{10,... | collective-permute-start | bytes 393224 | tf_op jit(solution)/shard_map/ppermute | solution.py:313
  63.2 15.6 %collective-permute-start.14 = (f32[2,128,1024]{2,1,0:T(8,128)S(1)}, f32[2,128,1024]{2,1,0:T(8,128)S(1)}, u32[]{:S(2)}, u32[]{:S(2)}) collective-permute-start(f32[2,128,1024]{2,1,0:T(8,128)S(1)} %deal.1), channel_id=1, source_target_pairs={{0,8},{8,0},{16,24},{24,16},{1,9},{9,1},{17,25},{25,17},{2,10},{10... | collective-permute-start | bytes 3145736 | tf_op jit(solution)/shard_map/ppermute | solution.py:316
  63.3 8.7 %collective-permute-start.7 = (f32[128,512]{1,0:T(8,128)S(1)}, f32[128,512]{1,0:T(8,128)S(1)}, u32[]{:S(2)}, u32[]{:S(2)}) collective-permute-start(f32[128,512]{1,0:T(8,128)S(1)} %get-tuple-element.62), channel_id=1, source_target_pairs={{0,1},{1,0},{2,3},{3,2},{4,5},{5,4},{6,7},{7,6},{8,9},{9,8},{10,11... | collective-permute-start | bytes 786440 | tf_op jit(solution)/shard_map/ppermute | solution.py:313
  63.9 9.2 %collective-permute-start.8 = (f32[128,512]{1,0:T(8,128)S(1)}, f32[128,512]{1,0:T(8,128)S(1)}, u32[]{:S(2)}, u32[]{:S(2)}) collective-permute-start(f32[128,512]{1,0:T(8,128)S(1)} %get-tuple-element.63), channel_id=1, source_target_pairs={{0,2},{1,3},{2,0},{3,1},{4,6},{5,7},{6,4},{7,5},{8,10},{9,11},{10,... | collective-permute-start | bytes 786440 | tf_op jit(solution)/shard_map/ppermute | solution.py:313
  65.6 13.2 %collective-permute-start.9 = (f32[128,512]{1,0:T(8,128)S(1)}, f32[128,512]{1,0:T(8,128)S(1)}, u32[]{:S(2)}, u32[]{:S(2)}) collective-permute-start(f32[128,512]{1,0:T(8,128)S(1)} %get-tuple-element.64), channel_id=1, source_target_pairs={{0,3},{1,2},{2,1},{3,0},{4,7},{5,6},{6,5},{7,4},{8,11},{9,10},{10,... | collective-permute-start | bytes 786440 | tf_op jit(solution)/shard_map/ppermute | solution.py:313
  66.8 5.0 %collective-permute-start.16 = (f32[128,256]{1,0:T(8,128)S(1)}, f32[128,256]{1,0:T(8,128)S(1)}, u32[]{:S(2)}, u32[]{:S(2)}) collective-permute-start(f32[128,256]{1,0:T(8,128)S(1)} %add_add_fusion.refs_3_), channel_id=1, source_target_pairs={{0,16},{8,24},{16,0},{24,8},{1,17},{9,25},{17,1},{25,9},{2,18},{10... | collective-permute-start | bytes 393224 | tf_op jit(solution)/shard_map/ppermute | solution.py:316
  71.8 7.0 %collective-permute-start.15 = (f32[128,256]{1,0:T(8,128)S(1)}, f32[128,256]{1,0:T(8,128)S(1)}, u32[]{:S(2)}, u32[]{:S(2)}) collective-permute-start(f32[128,256]{1,0:T(8,128)S(1)} %add_add_fusion.refs_3_), channel_id=1, source_target_pairs={{0,8},{8,0},{16,24},{24,16},{1,9},{9,1},{17,25},{25,17},{2,10},{10... | collective-permute-start | bytes 393224 | tf_op jit(solution)/shard_map/ppermute | solution.py:316
  72.0 6.8 %collective-permute-start.17 = (f32[128,256]{1,0:T(8,128)S(1)}, f32[128,256]{1,0:T(8,128)S(1)}, u32[]{:S(2)}, u32[]{:S(2)}) collective-permute-start(f32[128,256]{1,0:T(8,128)S(1)} %collective-permute-done.16.refs_5_), channel_id=1, source_target_pairs={{0,8},{8,0},{16,24},{24,16},{1,9},{9,1},{17,25},{25,17},{2,10},{10... | collective-permute-start | bytes 393224 | tf_op jit(solution)/shard_map/ppermute | solution.py:316
  79.4 7.6 %collective-permute-start.18 = (f32[2,128,256]{2,1,0:T(8,128)S(1)}, f32[2,128,256]{2,1,0:T(8,128)S(1)}, u32[]{:S(2)}, u32[]{:S(2)}) collective-permute-start(f32[2,128,256]{2,1,0:T(8,128)S(1)} %get-tuple-element.77), channel_id=1, source_target_pairs={{0,1},{1,0},{2,3},{3,2},{4,5},{5,4},{6,7},{7,6},{8,9},{9,8},{10,11... | collective-permute-start | bytes 786440 | tf_op jit(solution)/shard_map/ppermute | solution.py:313
  87.0 6.6 %collective-permute-start.19 = (f32[2,128,256]{2,1,0:T(8,128)S(1)}, f32[2,128,256]{2,1,0:T(8,128)S(1)}, u32[]{:S(2)}, u32[]{:S(2)}) collective-permute-start(f32[2,128,256]{2,1,0:T(8,128)S(1)} %get-tuple-element.78), channel_id=1, source_target_pairs={{0,1},{1,0},{2,3},{3,2},{4,5},{5,4},{6,7},{7,6},{8,9},{9,8},{10,11... | collective-permute-start | bytes 786440 | tf_op jit(solution)/shard_map/ppermute | solution.py:313
  87.6 12.2 %collective-permute-start.20 = (f32[128,256]{1,0:T(8,128)S(1)}, f32[128,256]{1,0:T(8,128)S(1)}, u32[]{:S(2)}, u32[]{:S(2)}) collective-permute-start(f32[128,256]{1,0:T(8,128)S(1)} %get-tuple-element.80), channel_id=1, source_target_pairs={{0,4},{1,5},{2,6},{3,7},{4,0},{5,1},{6,2},{7,3},{8,12},{9,13},{10,... | collective-permute-start | bytes 393224 | tf_op jit(solution)/shard_map/ppermute | solution.py:313
  91.0 8.8 %collective-permute-start.21 = (f32[128,256]{1,0:T(8,128)S(1)}, f32[128,256]{1,0:T(8,128)S(1)}, u32[]{:S(2)}, u32[]{:S(2)}) collective-permute-start(f32[128,256]{1,0:T(8,128)S(1)} %get-tuple-element.81), channel_id=1, source_target_pairs={{0,6},{1,7},{2,4},{3,5},{4,2},{5,3},{6,0},{7,1},{8,14},{9,15},{10,... | collective-permute-start | bytes 393224 | tf_op jit(solution)/shard_map/ppermute | solution.py:313
  93.7 6.8 %collective-permute-start.22 = (f32[128,256]{1,0:T(8,128)S(1)}, f32[128,256]{1,0:T(8,128)S(1)}, u32[]{:S(2)}, u32[]{:S(2)}) collective-permute-start(f32[128,256]{1,0:T(8,128)S(1)} %slice_bitcast_fusion), channel_id=1, source_target_pairs={{0,2},{1,3},{2,0},{3,1},{4,6},{5,7},{6,4},{7,5},{8,10},{9,11},{10,... | collective-permute-start | bytes 393224 | tf_op jit(solution)/shard_map/ppermute | solution.py:313

commit v11 on v6

--- a/solution.py
+++ b/solution.py
@@ -382,22 +382,22 @@
         pairs = [(t * q + i, (t + 1) * q + i) for i in range(q)]
         pairs += [(top * q + i, (top - 1) * q + i) for i in range(q)]
         for c in range(PARTS):
-            if c == 0 and t == planes - 2 and t > 0:
-                sent[c] = behind(sent[c], *handed)
             came = lax.ppermute(sent[c], "seq", pairs)
             if t == max(planes - 3, 0):
                 came = behind(came, local[c])
-            if c == PARTS - 1 and t == planes - 2 and t > 0:
-                came = behind(came, *swapped)
             if c > 0 and t < planes - 2:
                 came = behind(came, sent[c - 1])
+            if c == 0 and t > 0:
+                came = behind(came, sent[PARTS - 1])
+            if c == 0 and t == 0:
+                came = behind(came, held[-1][5], *token_parts[1:])
             arrived[c].append(came)
             if t < planes - 2:
                 (sent[c],) = call(
                     functools.partial(relay_body, q, t), [out(came.shape)], name="relay"
                 )(came, held[c][4], held[c][6])
-        if t == 0:
-            ready = behind(tuple(token_parts), sent[0], sent[-1])
+        if t == max(planes - 3, 0):
+            ready = behind(tuple(token_parts), sent[0])
             handed = call(
                 functools.partial(hand_body, q, part), [out((n_dp, length, part))] * (q - 1), name="hand"
             )(*ready)
@@ -418,7 +418,7 @@
 
     gp = before[0]
     for r in range(1, q):
-        gp = gp + swap(before[0], r)
+        gp = gp + behind(swap(before[0], r), swapped[r - 1])
     grads = {0: gp}
     bit = n_dp // 2
     while bit:

time: 99.3 us -> 98.7 us (level)
  waiting for transfers between devices: 54.7 us -> 49.5 us
  starting transfers between devices: 28.8 us -> 32.9 us
    ppermute x6, waiting for transfers between devices: 22.8 us -> 13.6 us  [on_device(): came = lax.ppermute(sent[c], 'seq', pairs)]
    ppermute x7, waiting for transfers between devices: 25.8 us -> 30.4 us  [swap(): return lax.ppermute(value, 'seq', pairs)]
    ppermute x6, starting transfers between devices: 11.7 us -> 14.6 us  [on_device(): came = lax.ppermute(sent[c], 'seq', pairs)]
    ppermute x3, starting transfers between devices: 5.05 us -> 6.29 us  [on_device(): grad_weight = grad_weight + lax.ppermute(pieces[r], 'seq', pairs)]
    ppermute x7, starting transfers between devices: 9.39 us -> 8.36 us  [swap(): return lax.ppermute(value, 'seq', pairs)]
  transfers between devices with their start and end apart: 22 -> 22, of which waited for: 11 -> 10; matrix products, arithmetic and copies ran while one was open for 0% -> 0% of each run, Pallas kernels for 11% -> 11%
where the time goes in v11:
time: 98.7 us; the launch traced here: 97.8 us
  waiting for transfers between devices  49.5 us (50%)
  starting transfers between devices  32.9 us (33%)
  Pallas kernels  12.2 us (12%)
  local copies, waits for them, and re-layouts  1.61 us (2%)
    ppermute x7, waiting for transfers between devices, swap(): return lax.ppermute(value, 'seq', pairs)  30.4 us
    ppermute x6, starting transfers between devices, on_device(): came = lax.ppermute(sent[c], 'seq', pairs)  14.6 us
    ppermute x6, waiting for transfers between devices, on_device(): came = lax.ppermute(sent[c], 'seq', pairs)  13.6 us
    pallas_call x17, Pallas kernels, run(): pl.pallas_call(body, out_shape=tuple((o[0] if isinstance(o, list) else pl...  12.2 us
    ppermute x7, starting transfers between devices, swap(): return lax.ppermute(value, 'seq', pairs)  8.36 us
    ppermute x3, starting transfers between devices, on_device(): grad_weight = grad_weight + lax.ppermute(pieces[r], 'seq', pairs)  6.29 us
    ppermute x6, waiting for transfers between devices, across(): return lax.ppermute(value, 'dp', [(i, i ^ r) for i in range(n_dp)])  4.89 us
    ppermute x6, starting transfers between devices, across(): return lax.ppermute(value, 'dp', [(i, i ^ r) for i in range(n_dp)])  3.61 us
  transfers between devices with their start and end apart: 22, of which 10 were waited for; matrix products, arithmetic and copies ran while one was open for 0% of the time, Pallas kernels for 11%

profile of v11, /device:TPU:0, one launch (start us, length us, event | category | flops | bytes accessed | tf_op | source)
XLA Modules:
  0.0 97.8 jit_solution(258123800485022841)
XLA Ops:
  1.8 3.0 %collective-permute-start = (f32[2,128,640]{2,1,0:T(8,128)S(1)}, f32[2,128,640]{2,1,0:T(8,128)S(1)}, u32[]{:S(2)}, u32[]{:S(2)}) collective-permute-start(f32[2,128,640]{2,1,0:T(8,128)S(1)} %pack.3), channel_id=1, source_target_pairs={{0,1},{1,0},{2,3},{3,2},{4,5},{5,4},{6,7},{7,6},{8,9},{9,8},{10,11... | collective-permute-start | bytes 1966088 | tf_op jit(solution)/shard_map/ppermute | solution.py:324
  4.9 1.6 %copy-done.1 = bf16[4096,256]{1,0:T(8,128)(2,1)S(1)} copy-done((bf16[4096,256]{1,0:T(8,128)(2,1)S(1)}, bf16[4096,256]{1,0:T(8,128)(2,1)}, u32[]{:S(2)}) %copy-start.1) | copy-done | bytes 2097176
  8.6 1.9 %collective-permute-start.5 = (f32[128,1024]{1,0:T(8,128)S(1)}, f32[128,1024]{1,0:T(8,128)S(1)}, u32[]{:S(2)}, u32[]{:S(2)}) collective-permute-start(f32[128,1024]{1,0:T(8,128)S(1)} %get-tuple-element.69), channel_id=1, source_target_pairs={{0,16},{8,24},{16,0},{24,8},{1,17},{9,25},{17,1},{25,9},{2,18},{10... | collective-permute-start | bytes 1572872 | tf_op jit(solution)/shard_map/ppermute | solution.py:327
  10.6 12.2 %collective-permute-done.1.refs_3_ = f32[144,256]{1,0:T(8,128)S(1)} collective-permute-done((f32[144,256]{1,0:T(8,128)S(1)}, f32[144,256]{1,0:T(8,128)S(1)}, u32[]{:S(2)}, u32[]{:S(2)}) %collective-permute-start.1) | collective-permute-done | bytes 147488 | tf_op jit(solution)/shard_map/ppermute | solution.py:324
  22.7 1.7 %collective-permute-start.3 = (f32[2,128,384]{2,1,0:T(8,128)S(1)}, f32[2,128,384]{2,1,0:T(8,128)S(1)}, u32[]{:S(2)}, u32[]{:S(2)}) collective-permute-start(f32[2,128,384]{2,1,0:T(8,128)S(1)} %get-tuple-element.64), channel_id=1, source_target_pairs={{0,1},{1,0},{2,3},{3,2},{4,5},{5,4},{6,7},{7,6},{8,9},{9,8},{10,11... | collective-permute-start | bytes 1179656 | tf_op jit(solution)/shard_map/ppermute | solution.py:324
  24.5 1.4 %states.2 = (bf16[4,2,128,640]{3,2,1,0:T(8,128)(2,1)S(1)}, f32[2,2,128,640]{3,2,1,0:T(8,128)S(1)}, f32[2,128,640]{2,1,0:T(8,128)S(1)}, f32[2,1,640]{2,1,0:T(1,12...) custom-call(bf16[2,128,1024]{2,1,0:T(8,128)(2,1)S(1)} %get-tuple-ele, ...), custom_call_target="tpu_custom_call" | custom-call | tf_op jit(solution)/shard_map/states/pallas_call | solution.py:63
  25.9 3.5 %collective-permute-start.2 = (f32[128,640]{1,0:T(8,128)S(1)}, f32[128,640]{1,0:T(8,128)S(1)}, u32[]{:S(2)}, u32[]{:S(2)}) collective-permute-start(f32[128,640]{1,0:T(8,128)S(1)} %get-tuple-element.62), channel_id=1, source_target_pairs={{0,2},{1,3},{6,4},{7,5},{8,10},{9,11},{14,12},{15,13},{16,18},{17,... | collective-permute-start | bytes 983048 | tf_op jit(solution)/shard_map/ppermute | solution.py:385
  29.5 3.6 %collective-permute-done.3.refs_1_ = f32[2,128,384]{2,1,0:T(8,128)S(1)} collective-permute-done((f32[2,128,384]{2,1,0:T(8,128)S(1)}, f32[2,128,384]{2,1,0:T(8,128)S(1)}, u32[]{:S(2)}, u32[]{:S(2)}) %collective-permute-start.3) | collective-permute-done | bytes 393248 | tf_op jit(solution)/shard_map/ppermute | solution.py:324
  33.0 1.3 %states.3 = (bf16[4,2,128,384]{3,2,1,0:T(8,128)(2,1)S(1)}, f32[2,2,128,384]{3,2,1,0:T(8,128)S(1)}, f32[2,128,384]{2,1,0:T(8,128)S(1)}, f32[2,1,384]{2,1,0:T(1,12...) custom-call(bf16[2,128,1024]{2,1,0:T(8,128)(2,1)S(1)} %get-tuple-ele, ...), custom_call_target="tpu_custom_call" | custom-call | tf_op jit(solution)/shard_map/states/pallas_call | solution.py:63
  36.0 7.2 %collective-permute-start.8 = (f32[128,384]{1,0:T(8,128)S(1)}, f32[128,384]{1,0:T(8,128)S(1)}, u32[]{:S(2)}, u32[]{:S(2)}) collective-permute-start(f32[128,384]{1,0:T(8,128)S(1)} %get-tuple-element.66), channel_id=1, source_target_pairs={{0,2},{1,3},{6,4},{7,5},{8,10},{9,11},{14,12},{15,13},{16,18},{17,... | collective-permute-start | bytes 589832 | tf_op jit(solution)/shard_map/ppermute | solution.py:385
  43.2 1.8 %local.2 = (f32[2,128,640]{2,1,0:T(8,128)S(1)}, f32[2,128,256]{2,1,0:T(8,128)S(1)}) custom-call(f32[32]{0:T(128)S(1)} %copy-done.4, bf16[4,2,128,640]{3,2,1,0:T(8,128)(2,1)S(1)} %get-tuple-element.74.rows16.refs_3_, bf16[2,128,256]{2,1,0:T(8,128)(2,1)S(1)} %get-tuple-element.75.bcs.refs_7_, f32[2,10,128]{2,1,0:T(8,128)S(1)} %get-tuple-element.76.cums, ...), custom_call_target="tpu_custom_call" | custom-call | tf_op jit(solution)/shard_map/local/pallas_call | solution.py:63
  45.0 1.3 %collective-permute-done.8.came.refs_0_ = f32[128,384]{1,0:T(8,128)S(1)} collective-permute-done((f32[128,384]{1,0:T(8,128)S(1)}, f32[128,384]{1,0:T(8,128)S(1)}, u32[]{:S(2)}, u32[]{:S(2)}) %collective-permute-start.8) | collective-permute-done | bytes 196640 | tf_op jit(solution)/shard_map/ppermute | solution.py:385
  48.2 1.3 %collective-permute-start.9 = (f32[128,640]{1,0:T(8,128)S(1)}, f32[128,640]{1,0:T(8,128)S(1)}, u32[]{:S(2)}, u32[]{:S(2)}) collective-permute-start(f32[128,640]{1,0:T(8,128)S(1)} %relay.6), channel_id=1, source_target_pairs={{4,6},{5,7},{2,0},{3,1},{12,14},{13,15},{10,8},{11,9},{20,22},{21,... | collective-permute-start | bytes 983048 | tf_op jit(solution)/shard_map/ppermute | solution.py:385
  49.5 1.6 %local.3 = (f32[2,128,384]{2,1,0:T(8,128)S(1)}, f32[2,128,256]{2,1,0:T(8,128)S(1)}) custom-call(f32[32]{0:T(128)S(1)} %copy-done.4, bf16[4,2,128,384]{3,2,1,0:T(8,128)(2,1)S(1)} %get-tuple-element.85.rows16.refs_3_, bf16[2,128,256]{2,1,0:T(8,128)(2,1)S(1)} %get-tuple-element.86.bcs.refs_7_, f32[2,6,128]{2,1,0:T(8,128)S(1)} %get-tuple-element.87.cums, ...), custom_call_target="tpu_custom_call" | custom-call | tf_op jit(solution)/shard_map/local/pallas_call | solution.py:63
  51.1 1.3 %collective-permute-start.11 = (f32[128,384]{1,0:T(8,128)S(1)}, f32[128,384]{1,0:T(8,128)S(1)}, u32[]{:S(2)}, u32[]{:S(2)}) collective-permute-start(f32[128,384]{1,0:T(8,128)S(1)} %relay.7), channel_id=1, source_target_pairs={{4,6},{5,7},{2,0},{3,1},{12,14},{13,15},{10,8},{11,9},{20,22},{21,... | collective-permute-start | bytes 589832 | tf_op jit(solution)/shard_map/ppermute | solution.py:385
  52.4 9.9 %collective-permute-done.9.refs_2_ = f32[128,640]{1,0:T(8,128)S(1)} collective-permute-done((f32[128,640]{1,0:T(8,128)S(1)}, f32[128,640]{1,0:T(8,128)S(1)}, u32[]{:S(2)}, u32[]{:S(2)}) %collective-permute-start.9) | collective-permute-done | bytes 327712 | tf_op jit(solution)/shard_map/ppermute | solution.py:385
  63.0 1.5 %collective-permute-done.11.refs_2_ = f32[128,384]{1,0:T(8,128)S(1)} collective-permute-done((f32[128,384]{1,0:T(8,128)S(1)}, f32[128,384]{1,0:T(8,128)S(1)}, u32[]{:S(2)}, u32[]{:S(2)}) %collective-permute-start.11) | collective-permute-done | bytes 196640 | tf_op jit(solution)/shard_map/ppermute | solution.py:385
  65.3 9.5 %collective-permute-done.15 = f32[2,128,256]{2,1,0:T(8,128)S(1)} collective-permute-done((f32[2,128,256]{2,1,0:T(8,128)S(1)}, f32[2,128,256]{2,1,0:T(8,128)S(1)}, u32[]{:S(2)}, u32[]{:S(2)}) %collective-permute-start.15) | collective-permute-done | bytes 262176 | tf_op jit(solution)/shard_map/ppermute | solution.py:324
  74.8 1.6 %collective-permute-start.17 = (f32[2,128,256]{2,1,0:T(8,128)S(1)}, f32[2,128,256]{2,1,0:T(8,128)S(1)}, u32[]{:S(2)}, u32[]{:S(2)}) collective-permute-start(f32[2,128,256]{2,1,0:T(8,128)S(1)} %add.12.refs_5_), channel_id=1, source_target_pairs={{0,16},{8,24},{16,0},{24,8},{1,17},{9,25},{17,1},{25,9},{2,18},{10... | collective-permute-start | bytes 786440 | tf_op jit(solution)/shard_map/ppermute | solution.py:327
  76.4 4.9 %collective-permute-done.17.refs_7_ = f32[2,128,256]{2,1,0:T(8,128)S(1)} collective-permute-done((f32[2,128,256]{2,1,0:T(8,128)S(1)}, f32[2,128,256]{2,1,0:T(8,128)S(1)}, u32[]{:S(2)}, u32[]{:S(2)}) %collective-permute-start.17) | collective-permute-done | bytes 262176 | tf_op jit(solution)/shard_map/ppermute | solution.py:327
  81.3 1.7 %collective-permute-start.12 = (f32[128,640]{1,0:T(8,128)S(1)}, f32[128,640]{1,0:T(8,128)S(1)}, u32[]{:S(2)}, u32[]{:S(2)}) collective-permute-start(f32[128,640]{1,0:T(8,128)S(1)} %get-tuple-element.103), channel_id=1, source_target_pairs={{0,1},{1,0},{2,3},{3,2},{4,5},{5,4},{6,7},{7,6},{8,9},{9,8},{10,11... | collective-permute-start | bytes 983048 | tf_op jit(solution)/shard_map/ppermute | solution.py:324
  84.2 2.5 %collective-permute-start.19 = (f32[128,256]{1,0:T(8,128)S(1)}, f32[128,256]{1,0:T(8,128)S(1)}, u32[]{:S(2)}, u32[]{:S(2)}) collective-permute-start(f32[128,256]{1,0:T(8,128)S(1)} %get-tuple-element.113), channel_id=1, source_target_pairs={{0,2},{1,3},{2,4},{3,5},{4,6},{5,7},{6,0},{7,1},{8,10},{9,11},{10,... | collective-permute-start | bytes 393224 | tf_op jit(solution)/shard_map/ppermute | solution.py:441
  87.6 2.8 %collective-permute-start.21 = (f32[128,256]{1,0:T(8,128)S(1)}, f32[128,256]{1,0:T(8,128)S(1)}, u32[]{:S(2)}, u32[]{:S(2)}) collective-permute-start(f32[128,256]{1,0:T(8,128)S(1)} %get-tuple-element.115), channel_id=1, source_target_pairs={{0,6},{1,7},{2,0},{3,1},{4,2},{5,3},{6,4},{7,5},{8,14},{9,15},{10,... | collective-permute-start | bytes 393224 | tf_op jit(solution)/shard_map/ppermute | solution.py:441
  90.5 5.2 %collective-permute-done.13.refs_3_ = f32[128,384]{1,0:T(8,128)S(1)} collective-permute-done((f32[128,384]{1,0:T(8,128)S(1)}, f32[128,384]{1,0:T(8,128)S(1)}, u32[]{:S(2)}, u32[]{:S(2)}) %collective-permute-start.13) | collective-permute-done | bytes 196640 | tf_op jit(solution)/shard_map/ppermute | solution.py:324
  (49 shorter events, 12.6 us)
Async XLA Ops:
  0.6 4.2 %copy-start.2 = (f32[1,32,128]{2,1,0:T(8,128)S(1)}, f32[1,32,128]{2,1,0:T(8,128)}, u32[]{:S(2)}) copy-start(f32[1,32,128]{2,1,0:T(8,128)} %param.11) | copy-start | bytes 49156
  1.8 22.7 %collective-permute-start = (f32[2,128,640]{2,1,0:T(8,128)S(1)}, f32[2,128,640]{2,1,0:T(8,128)S(1)}, u32[]{:S(2)}, u32[]{:S(2)}) collective-permute-start(f32[2,128,640]{2,1,0:T(8,128)S(1)} %pack.3), channel_id=1, source_target_pairs={{0,1},{1,0},{2,3},{3,2},{4,5},{5,4},{6,7},{7,6},{8,9},{9,8},{10,11... | collective-permute-start | bytes 1966088 | tf_op jit(solution)/shard_map/ppermute | solution.py:324
  6.9 15.8 %collective-permute-start.1 = (f32[144,256]{1,0:T(8,128)S(1)}, f32[144,256]{1,0:T(8,128)S(1)}, u32[]{:S(2)}, u32[]{:S(2)}) collective-permute-start(f32[144,256]{1,0:T(8,128)S(1)} %get-tuple-element.61), channel_id=1, source_target_pairs={{0,1},{1,0},{2,3},{3,2},{4,5},{5,4},{6,7},{7,6},{8,9},{9,8},{10,11... | collective-permute-start | bytes 442376 | tf_op jit(solution)/shard_map/ppermute | solution.py:324
  8.5 25.8 %collective-permute-start.4 = (f32[128,1024]{1,0:T(8,128)S(1)}, f32[128,1024]{1,0:T(8,128)S(1)}, u32[]{:S(2)}, u32[]{:S(2)}) collective-permute-start(f32[128,1024]{1,0:T(8,128)S(1)} %get-tuple-element.68), channel_id=1, source_target_pairs={{0,8},{8,0},{16,24},{24,16},{1,9},{9,1},{17,25},{25,17},{2,10},{10... | collective-permute-start | bytes 1572872 | tf_op jit(solution)/shard_map/ppermute | solution.py:327
  8.6 25.8 %collective-permute-start.5 = (f32[128,1024]{1,0:T(8,128)S(1)}, f32[128,1024]{1,0:T(8,128)S(1)}, u32[]{:S(2)}, u32[]{:S(2)}) collective-permute-start(f32[128,1024]{1,0:T(8,128)S(1)} %get-tuple-element.69), channel_id=1, source_target_pairs={{0,16},{8,24},{16,0},{24,8},{1,17},{9,25},{17,1},{25,9},{2,18},{10... | collective-permute-start | bytes 1572872 | tf_op jit(solution)/shard_map/ppermute | solution.py:327
  10.5 23.8 %collective-permute-start.6 = (f32[128,1024]{1,0:T(8,128)S(1)}, f32[128,1024]{1,0:T(8,128)S(1)}, u32[]{:S(2)}, u32[]{:S(2)}) collective-permute-start(f32[128,1024]{1,0:T(8,128)S(1)} %get-tuple-element.70), channel_id=1, source_target_pairs={{0,24},{8,16},{16,8},{24,0},{1,25},{9,17},{17,9},{25,1},{2,26},{10... | collective-permute-start | bytes 1572872 | tf_op jit(solution)/shard_map/ppermute | solution.py:327
  22.7 10.3 %collective-permute-start.3 = (f32[2,128,384]{2,1,0:T(8,128)S(1)}, f32[2,128,384]{2,1,0:T(8,128)S(1)}, u32[]{:S(2)}, u32[]{:S(2)}) collective-permute-start(f32[2,128,384]{2,1,0:T(8,128)S(1)} %get-tuple-element.64), channel_id=1, source_target_pairs={{0,1},{1,0},{2,3},{3,2},{4,5},{5,4},{6,7},{7,6},{8,9},{9,8},{10,11... | collective-permute-start | bytes 1179656 | tf_op jit(solution)/shard_map/ppermute | solution.py:324
  25.9 17.3 %copy-start.4 = (f32[32]{0:T(128)S(1)}, f32[32]{0:T(128)}, u32[]{:S(2)}) copy-start(f32[32]{0:T(128)} %skip.3) | copy-start | bytes 388
  25.9 9.3 %collective-permute-start.2 = (f32[128,640]{1,0:T(8,128)S(1)}, f32[128,640]{1,0:T(8,128)S(1)}, u32[]{:S(2)}, u32[]{:S(2)}) collective-permute-start(f32[128,640]{1,0:T(8,128)S(1)} %get-tuple-element.62), channel_id=1, source_target_pairs={{0,2},{1,3},{6,4},{7,5},{8,10},{9,11},{14,12},{15,13},{16,18},{17,... | collective-permute-start | bytes 983048 | tf_op jit(solution)/shard_map/ppermute | solution.py:385
  35.3 11.1 %collective-permute-start.7 = (f32[128,640]{1,0:T(8,128)S(1)}, f32[128,640]{1,0:T(8,128)S(1)}, u32[]{:S(2)}, u32[]{:S(2)}) collective-permute-start(f32[128,640]{1,0:T(8,128)S(1)} %relay.4), channel_id=1, source_target_pairs={{2,4},{3,5},{4,2},{5,3},{10,12},{11,13},{12,10},{13,11},{18,20},{1... | collective-permute-start | bytes 983048 | tf_op jit(solution)/shard_map/ppermute | solution.py:385
  36.0 10.4 %collective-permute-start.8 = (f32[128,384]{1,0:T(8,128)S(1)}, f32[128,384]{1,0:T(8,128)S(1)}, u32[]{:S(2)}, u32[]{:S(2)}) collective-permute-start(f32[128,384]{1,0:T(8,128)S(1)} %get-tuple-element.66), channel_id=1, source_target_pairs={{0,2},{1,3},{6,4},{7,5},{8,10},{9,11},{14,12},{15,13},{16,18},{17,... | collective-permute-start | bytes 589832 | tf_op jit(solution)/shard_map/ppermute | solution.py:385
  46.6 28.3 %collective-permute-start.14 = (f32[4,128,512]{2,1,0:T(8,128)S(1)}, f32[4,128,512]{2,1,0:T(8,128)S(1)}, u32[]{:S(2)}, u32[]{:S(2)}) collective-permute-start(f32[4,128,512]{2,1,0:T(8,128)S(1)} %hand.1), channel_id=1, source_target_pairs={{0,1},{1,0},{2,3},{3,2},{4,5},{5,4},{6,7},{7,6},{8,9},{9,8},{10,11... | collective-permute-start | bytes 3145736 | tf_op jit(solution)/shard_map/ppermute | solution.py:324
  47.5 3.5 %collective-permute-start.10 = (f32[128,384]{1,0:T(8,128)S(1)}, f32[128,384]{1,0:T(8,128)S(1)}, u32[]{:S(2)}, u32[]{:S(2)}) collective-permute-start(f32[128,384]{1,0:T(8,128)S(1)} %relay.5), channel_id=1, source_target_pairs={{2,4},{3,5},{4,2},{5,3},{10,12},{11,13},{12,10},{13,11},{18,20},{1... | collective-permute-start | bytes 589832 | tf_op jit(solution)/shard_map/ppermute | solution.py:385
  48.2 14.1 %collective-permute-start.9 = (f32[128,640]{1,0:T(8,128)S(1)}, f32[128,640]{1,0:T(8,128)S(1)}, u32[]{:S(2)}, u32[]{:S(2)}) collective-permute-start(f32[128,640]{1,0:T(8,128)S(1)} %relay.6), channel_id=1, source_target_pairs={{4,6},{5,7},{2,0},{3,1},{12,14},{13,15},{10,8},{11,9},{20,22},{21,... | collective-permute-start | bytes 983048 | tf_op jit(solution)/shard_map/ppermute | solution.py:385
  51.1 13.3 %collective-permute-start.11 = (f32[128,384]{1,0:T(8,128)S(1)}, f32[128,384]{1,0:T(8,128)S(1)}, u32[]{:S(2)}, u32[]{:S(2)}) collective-permute-start(f32[128,384]{1,0:T(8,128)S(1)} %relay.7), channel_id=1, source_target_pairs={{4,6},{5,7},{2,0},{3,1},{12,14},{13,15},{10,8},{11,9},{20,22},{21,... | collective-permute-start | bytes 589832 | tf_op jit(solution)/shard_map/ppermute | solution.py:385
  64.9 9.9 %collective-permute-start.15 = (f32[2,128,256]{2,1,0:T(8,128)S(1)}, f32[2,128,256]{2,1,0:T(8,128)S(1)}, u32[]{:S(2)}, u32[]{:S(2)}) collective-permute-start(f32[2,128,256]{2,1,0:T(8,128)S(1)} %get-tuple-element.110), channel_id=1, source_target_pairs={{0,1},{1,0},{2,3},{3,2},{4,5},{5,4},{6,7},{7,6},{8,9},{9,8},{10,11... | collective-permute-start | bytes 786440 | tf_op jit(solution)/shard_map/ppermute | solution.py:324
  74.8 6.4 %collective-permute-start.17 = (f32[2,128,256]{2,1,0:T(8,128)S(1)}, f32[2,128,256]{2,1,0:T(8,128)S(1)}, u32[]{:S(2)}, u32[]{:S(2)}) collective-permute-start(f32[2,128,256]{2,1,0:T(8,128)S(1)} %add.12.refs_5_), channel_id=1, source_target_pairs={{0,16},{8,24},{16,0},{24,8},{1,17},{9,25},{17,1},{25,9},{2,18},{10... | collective-permute-start | bytes 786440 | tf_op jit(solution)/shard_map/ppermute | solution.py:327
  76.4 6.9 %collective-permute-start.16 = (f32[2,128,256]{2,1,0:T(8,128)S(1)}, f32[2,128,256]{2,1,0:T(8,128)S(1)}, u32[]{:S(2)}, u32[]{:S(2)}) collective-permute-start(f32[2,128,256]{2,1,0:T(8,128)S(1)} %add.12.refs_5_), channel_id=1, source_target_pairs={{0,8},{8,0},{16,24},{24,16},{1,9},{9,1},{17,25},{25,17},{2,10},{10... | collective-permute-start | bytes 786440 | tf_op jit(solution)/shard_map/ppermute | solution.py:327
  81.3 2.0 %collective-permute-start.18 = (f32[2,128,256]{2,1,0:T(8,128)S(1)}, f32[2,128,256]{2,1,0:T(8,128)S(1)}, u32[]{:S(2)}, u32[]{:S(2)}) collective-permute-start(f32[2,128,256]{2,1,0:T(8,128)S(1)} %collective-permute-done.17.refs_7_), channel_id=1, source_target_pairs={{0,8},{8,0},{16,24},{24,16},{1,9},{9,1},{17,25},{25,17},{2,10},{10... | collective-permute-start | bytes 786440 | tf_op jit(solution)/shard_map/ppermute | solution.py:327
  81.3 14.3 %collective-permute-start.12 = (f32[128,640]{1,0:T(8,128)S(1)}, f32[128,640]{1,0:T(8,128)S(1)}, u32[]{:S(2)}, u32[]{:S(2)}) collective-permute-start(f32[128,640]{1,0:T(8,128)S(1)} %get-tuple-element.103), channel_id=1, source_target_pairs={{0,1},{1,0},{2,3},{3,2},{4,5},{5,4},{6,7},{7,6},{8,9},{9,8},{10,11... | collective-permute-start | bytes 983048 | tf_op jit(solution)/shard_map/ppermute | solution.py:324
  83.0 12.6 %collective-permute-start.13 = (f32[128,384]{1,0:T(8,128)S(1)}, f32[128,384]{1,0:T(8,128)S(1)}, u32[]{:S(2)}, u32[]{:S(2)}) collective-permute-start(f32[128,384]{1,0:T(8,128)S(1)} %get-tuple-element.104), channel_id=1, source_target_pairs={{0,1},{1,0},{2,3},{3,2},{4,5},{5,4},{6,7},{7,6},{8,9},{9,8},{10,11... | collective-permute-start | bytes 589832 | tf_op jit(solution)/shard_map/ppermute | solution.py:324
  84.2 12.3 %collective-permute-start.19 = (f32[128,256]{1,0:T(8,128)S(1)}, f32[128,256]{1,0:T(8,128)S(1)}, u32[]{:S(2)}, u32[]{:S(2)}) collective-permute-start(f32[128,256]{1,0:T(8,128)S(1)} %get-tuple-element.113), channel_id=1, source_target_pairs={{0,2},{1,3},{2,4},{3,5},{4,6},{5,7},{6,0},{7,1},{8,10},{9,11},{10,... | collective-permute-start | bytes 393224 | tf_op jit(solution)/shard_map/ppermute | solution.py:441
  86.7 10.4 %collective-permute-start.20 = (f32[128,256]{1,0:T(8,128)S(1)}, f32[128,256]{1,0:T(8,128)S(1)}, u32[]{:S(2)}, u32[]{:S(2)}) collective-permute-start(f32[128,256]{1,0:T(8,128)S(1)} %get-tuple-element.114), channel_id=1, source_target_pairs={{0,4},{1,5},{2,6},{3,7},{4,0},{5,1},{6,2},{7,3},{8,12},{9,13},{10,... | collective-permute-start | bytes 393224 | tf_op jit(solution)/shard_map/ppermute | solution.py:441
  87.6 9.5 %collective-permute-start.21 = (f32[128,256]{1,0:T(8,128)S(1)}, f32[128,256]{1,0:T(8,128)S(1)}, u32[]{:S(2)}, u32[]{:S(2)}) collective-permute-start(f32[128,256]{1,0:T(8,128)S(1)} %get-tuple-element.115), channel_id=1, source_target_pairs={{0,6},{1,7},{2,0},{3,1},{4,2},{5,3},{6,4},{7,5},{8,14},{9,15},{10,... | collective-permute-start | bytes 393224 | tf_op jit(solution)/shard_map/ppermute | solution.py:441
  (3 other events, 10.0 us)

commit v12 on v11

--- a/solution.py
+++ b/solution.py
@@ -396,7 +396,7 @@
                 (sent[c],) = call(
                     functools.partial(relay_body, q, t), [out(came.shape)], name="relay"
                 )(came, held[c][4], held[c][6])
-        if t == max(planes - 3, 0):
+        if t == 0:
             ready = behind(tuple(token_parts), sent[0])
             handed = call(
                 functools.partial(hand_body, q, part), [out((n_dp, length, part))] * (q - 1), name="hand"

time: 98.7 us -> 95.2 us (0.965)
  starting transfers between devices: 32.9 us -> 30.2 us
    ppermute x3, starting transfers between devices: 6.29 us -> 3.87 us  [on_device(): grad_weight = grad_weight + lax.ppermute(pieces[r], 'seq', pairs)]
    ppermute x7, waiting for transfers between devices: 30.4 us -> 29.3 us  [swap(): return lax.ppermute(value, 'seq', pairs)]
    ppermute x6, waiting for transfers between devices: 13.6 us -> 14.6 us  [on_device(): came = lax.ppermute(sent[c], 'seq', pairs)]
where the time goes in v12:
time: 95.2 us; the launch traced here: 95 us
  waiting for transfers between devices  49.3 us (52%)
  starting transfers between devices  30.2 us (32%)
  Pallas kernels  12.2 us (13%)
  local copies, waits for them, and re-layouts  1.61 us (2%)
    ppermute x7, waiting for transfers between devices, swap(): return lax.ppermute(value, 'seq', pairs)  29.3 us
    ppermute x6, waiting for transfers between devices, on_device(): came = lax.ppermute(sent[c], 'seq', pairs)  14.6 us
    ppermute x6, starting transfers between devices, on_device(): came = lax.ppermute(sent[c], 'seq', pairs)  14.5 us
    pallas_call x17, Pallas kernels, run(): pl.pallas_call(body, out_shape=tuple((o[0] if isinstance(o, list) else pl...  12.2 us
    ppermute x7, starting transfers between devices, swap(): return lax.ppermute(value, 'seq', pairs)  8.19 us
    ppermute x6, waiting for transfers between devices, across(): return lax.ppermute(value, 'dp', [(i, i ^ r) for i in range(n_dp)])  4.89 us
    ppermute x3, starting transfers between devices, on_device(): grad_weight = grad_weight + lax.ppermute(pieces[r], 'seq', pairs)  3.87 us
    ppermute x6, starting transfers between devices, across(): return lax.ppermute(value, 'dp', [(i, i ^ r) for i in range(n_dp)])  3.61 us
  transfers between devices with their start and end apart: 22, of which 10 were waited for; matrix products, arithmetic and copies ran while one was open for 0% of the time, Pallas kernels for 11%

profile of v12, /device:TPU:0, one launch (start us, length us, event | category | flops | bytes accessed | tf_op | source)
XLA Modules:
  0.0 95.0 jit_solution(6107679291919262215)
XLA Ops:
  1.8 3.0 %collective-permute-start = (f32[2,128,640]{2,1,0:T(8,128)S(1)}, f32[2,128,640]{2,1,0:T(8,128)S(1)}, u32[]{:S(2)}, u32[]{:S(2)}) collective-permute-start(f32[2,128,640]{2,1,0:T(8,128)S(1)} %pack.3), channel_id=1, source_target_pairs={{0,1},{1,0},{2,3},{3,2},{4,5},{5,4},{6,7},{7,6},{8,9},{9,8},{10,11... | collective-permute-start | bytes 1966088 | tf_op jit(solution)/shard_map/ppermute | solution.py:324
  4.9 1.6 %copy-done.1 = bf16[4096,256]{1,0:T(8,128)(2,1)S(1)} copy-done((bf16[4096,256]{1,0:T(8,128)(2,1)S(1)}, bf16[4096,256]{1,0:T(8,128)(2,1)}, u32[]{:S(2)}) %copy-start.1) | copy-done | bytes 2097176
  7.1 1.2 %pack.2 = (f32[2,128,384]{2,1,0:T(8,128)S(1)}, bf16[2,128,1024]{2,1,0:T(8,128)(2,1)S(1)}) custom-call(bf16[128,2048]{1,0:T(8,128)(2,1)} %bitcast.11, bf16[128,2048]{1,0:T(8,128)(2,1)} %bitcast.13), custom_call_target="tpu_custom_call" | custom-call | tf_op jit(solution)/shard_map/pack/pallas_call | solution.py:63
  8.6 1.9 %collective-permute-start.5 = (f32[128,1024]{1,0:T(8,128)S(1)}, f32[128,1024]{1,0:T(8,128)S(1)}, u32[]{:S(2)}, u32[]{:S(2)}) collective-permute-start(f32[128,1024]{1,0:T(8,128)S(1)} %get-tuple-element.69), channel_id=1, source_target_pairs={{0,16},{8,24},{16,0},{24,8},{1,17},{9,25},{17,1},{25,9},{2,18},{10... | collective-permute-start | bytes 1572872 | tf_op jit(solution)/shard_map/ppermute | solution.py:327
  10.6 12.1 %collective-permute-done.1.refs_3_ = f32[144,256]{1,0:T(8,128)S(1)} collective-permute-done((f32[144,256]{1,0:T(8,128)S(1)}, f32[144,256]{1,0:T(8,128)S(1)}, u32[]{:S(2)}, u32[]{:S(2)}) %collective-permute-start.1) | collective-permute-done | bytes 147488 | tf_op jit(solution)/shard_map/ppermute | solution.py:324
  22.7 1.7 %collective-permute-start.3 = (f32[2,128,384]{2,1,0:T(8,128)S(1)}, f32[2,128,384]{2,1,0:T(8,128)S(1)}, u32[]{:S(2)}, u32[]{:S(2)}) collective-permute-start(f32[2,128,384]{2,1,0:T(8,128)S(1)} %get-tuple-element.64), channel_id=1, source_target_pairs={{0,1},{1,0},{2,3},{3,2},{4,5},{5,4},{6,7},{7,6},{8,9},{9,8},{10,11... | collective-permute-start | bytes 1179656 | tf_op jit(solution)/shard_map/ppermute | solution.py:324
  24.5 1.4 %states.2 = (bf16[4,2,128,640]{3,2,1,0:T(8,128)(2,1)S(1)}, f32[2,2,128,640]{3,2,1,0:T(8,128)S(1)}, f32[2,128,640]{2,1,0:T(8,128)S(1)}, f32[2,1,640]{2,1,0:T(1,12...) custom-call(bf16[2,128,1024]{2,1,0:T(8,128)(2,1)S(1)} %get-tuple-ele, ...), custom_call_target="tpu_custom_call" | custom-call | tf_op jit(solution)/shard_map/states/pallas_call | solution.py:63
  25.9 3.5 %collective-permute-start.2 = (f32[128,640]{1,0:T(8,128)S(1)}, f32[128,640]{1,0:T(8,128)S(1)}, u32[]{:S(2)}, u32[]{:S(2)}) collective-permute-start(f32[128,640]{1,0:T(8,128)S(1)} %get-tuple-element.62), channel_id=1, source_target_pairs={{0,2},{1,3},{6,4},{7,5},{8,10},{9,11},{14,12},{15,13},{16,18},{17,... | collective-permute-start | bytes 983048 | tf_op jit(solution)/shard_map/ppermute | solution.py:385
  29.4 3.6 %collective-permute-done.3.refs_1_ = f32[2,128,384]{2,1,0:T(8,128)S(1)} collective-permute-done((f32[2,128,384]{2,1,0:T(8,128)S(1)}, f32[2,128,384]{2,1,0:T(8,128)S(1)}, u32[]{:S(2)}, u32[]{:S(2)}) %collective-permute-start.3) | collective-permute-done | bytes 393248 | tf_op jit(solution)/shard_map/ppermute | solution.py:324
  33.0 1.3 %states.3 = (bf16[4,2,128,384]{3,2,1,0:T(8,128)(2,1)S(1)}, f32[2,2,128,384]{3,2,1,0:T(8,128)S(1)}, f32[2,128,384]{2,1,0:T(8,128)S(1)}, f32[2,1,384]{2,1,0:T(1,12...) custom-call(bf16[2,128,1024]{2,1,0:T(8,128)(2,1)S(1)} %get-tuple-ele, ...), custom_call_target="tpu_custom_call" | custom-call | tf_op jit(solution)/shard_map/states/pallas_call | solution.py:63
  36.7 7.1 %collective-permute-start.8 = (f32[128,384]{1,0:T(8,128)S(1)}, f32[128,384]{1,0:T(8,128)S(1)}, u32[]{:S(2)}, u32[]{:S(2)}) collective-permute-start(f32[128,384]{1,0:T(8,128)S(1)} %get-tuple-element.66), channel_id=1, source_target_pairs={{0,2},{1,3},{6,4},{7,5},{8,10},{9,11},{14,12},{15,13},{16,18},{17,... | collective-permute-start | bytes 589832 | tf_op jit(solution)/shard_map/ppermute | solution.py:385
  43.8 3.3 %collective-permute-done.8.came.refs_0_ = f32[128,384]{1,0:T(8,128)S(1)} collective-permute-done((f32[128,384]{1,0:T(8,128)S(1)}, f32[128,384]{1,0:T(8,128)S(1)}, u32[]{:S(2)}, u32[]{:S(2)}) %collective-permute-start.8) | collective-permute-done | bytes 196640 | tf_op jit(solution)/shard_map/ppermute | solution.py:385
  47.9 1.8 %local.2 = (f32[2,128,640]{2,1,0:T(8,128)S(1)}, f32[2,128,256]{2,1,0:T(8,128)S(1)}) custom-call(f32[32]{0:T(128)S(1)} %copy-done.4, bf16[4,2,128,640]{3,2,1,0:T(8,128)(2,1)S(1)} %get-tuple-element.74.rows16.refs_3_, bf16[2,128,256]{2,1,0:T(8,128)(2,1)S(1)} %get-tuple-element.75.bcs.refs_7_, f32[2,10,128]{2,1,0:T(8,128)S(1)} %get-tuple-element.76.cums, ...), custom_call_target="tpu_custom_call" | custom-call | tf_op jit(solution)/shard_map/local/pallas_call | solution.py:63
  49.8 1.3 %collective-permute-start.9 = (f32[128,640]{1,0:T(8,128)S(1)}, f32[128,640]{1,0:T(8,128)S(1)}, u32[]{:S(2)}, u32[]{:S(2)}) collective-permute-start(f32[128,640]{1,0:T(8,128)S(1)} %relay.6), channel_id=1, source_target_pairs={{4,6},{5,7},{2,0},{3,1},{12,14},{13,15},{10,8},{11,9},{20,22},{21,... | collective-permute-start | bytes 983048 | tf_op jit(solution)/shard_map/ppermute | solution.py:385
  51.1 1.6 %local.3 = (f32[2,128,384]{2,1,0:T(8,128)S(1)}, f32[2,128,256]{2,1,0:T(8,128)S(1)}) custom-call(f32[32]{0:T(128)S(1)} %copy-done.4, bf16[4,2,128,384]{3,2,1,0:T(8,128)(2,1)S(1)} %get-tuple-element.85.rows16.refs_3_, bf16[2,128,256]{2,1,0:T(8,128)(2,1)S(1)} %get-tuple-element.86.bcs.refs_7_, f32[2,6,128]{2,1,0:T(8,128)S(1)} %get-tuple-element.87.cums, ...), custom_call_target="tpu_custom_call" | custom-call | tf_op jit(solution)/shard_map/local/pallas_call | solution.py:63
  52.7 1.3 %collective-permute-start.11 = (f32[128,384]{1,0:T(8,128)S(1)}, f32[128,384]{1,0:T(8,128)S(1)}, u32[]{:S(2)}, u32[]{:S(2)}) collective-permute-start(f32[128,384]{1,0:T(8,128)S(1)} %relay.7), channel_id=1, source_target_pairs={{4,6},{5,7},{2,0},{3,1},{12,14},{13,15},{10,8},{11,9},{20,22},{21,... | collective-permute-start | bytes 589832 | tf_op jit(solution)/shard_map/ppermute | solution.py:385
  54.0 9.0 %collective-permute-done.9.refs_2_ = f32[128,640]{1,0:T(8,128)S(1)} collective-permute-done((f32[128,640]{1,0:T(8,128)S(1)}, f32[128,640]{1,0:T(8,128)S(1)}, u32[]{:S(2)}, u32[]{:S(2)}) %collective-permute-start.9) | collective-permute-done | bytes 327712 | tf_op jit(solution)/shard_map/ppermute | solution.py:385
  63.6 1.5 %collective-permute-done.11.refs_2_ = f32[128,384]{1,0:T(8,128)S(1)} collective-permute-done((f32[128,384]{1,0:T(8,128)S(1)}, f32[128,384]{1,0:T(8,128)S(1)}, u32[]{:S(2)}, u32[]{:S(2)}) %collective-permute-start.11) | collective-permute-done | bytes 196640 | tf_op jit(solution)/shard_map/ppermute | solution.py:385
  66.0 5.9 %collective-permute-done.15 = f32[2,128,256]{2,1,0:T(8,128)S(1)} collective-permute-done((f32[2,128,256]{2,1,0:T(8,128)S(1)}, f32[2,128,256]{2,1,0:T(8,128)S(1)}, u32[]{:S(2)}, u32[]{:S(2)}) %collective-permute-start.15) | collective-permute-done | bytes 262176 | tf_op jit(solution)/shard_map/ppermute | solution.py:324
  72.0 1.6 %collective-permute-start.17 = (f32[2,128,256]{2,1,0:T(8,128)S(1)}, f32[2,128,256]{2,1,0:T(8,128)S(1)}, u32[]{:S(2)}, u32[]{:S(2)}) collective-permute-start(f32[2,128,256]{2,1,0:T(8,128)S(1)} %add.12.refs_5_), channel_id=1, source_target_pairs={{0,16},{8,24},{16,0},{24,8},{1,17},{9,25},{17,1},{25,9},{2,18},{10... | collective-permute-start | bytes 786440 | tf_op jit(solution)/shard_map/ppermute | solution.py:327
  73.6 4.9 %collective-permute-done.17.refs_7_ = f32[2,128,256]{2,1,0:T(8,128)S(1)} collective-permute-done((f32[2,128,256]{2,1,0:T(8,128)S(1)}, f32[2,128,256]{2,1,0:T(8,128)S(1)}, u32[]{:S(2)}, u32[]{:S(2)}) %collective-permute-start.17) | collective-permute-done | bytes 262176 | tf_op jit(solution)/shard_map/ppermute | solution.py:327
  78.9 1.6 %collective-permute-start.13 = (f32[128,384]{1,0:T(8,128)S(1)}, f32[128,384]{1,0:T(8,128)S(1)}, u32[]{:S(2)}, u32[]{:S(2)}) collective-permute-start(f32[128,384]{1,0:T(8,128)S(1)} %get-tuple-element.104), channel_id=1, source_target_pairs={{0,1},{1,0},{2,3},{3,2},{4,5},{5,4},{6,7},{7,6},{8,9},{9,8},{10,11... | collective-permute-start | bytes 589832 | tf_op jit(solution)/shard_map/ppermute | solution.py:324
  81.4 3.0 %collective-permute-start.20 = (f32[128,256]{1,0:T(8,128)S(1)}, f32[128,256]{1,0:T(8,128)S(1)}, u32[]{:S(2)}, u32[]{:S(2)}) collective-permute-start(f32[128,256]{1,0:T(8,128)S(1)} %get-tuple-element.114), channel_id=1, source_target_pairs={{0,4},{1,5},{2,6},{3,7},{4,0},{5,1},{6,2},{7,3},{8,12},{9,13},{10,... | collective-permute-start | bytes 393224 | tf_op jit(solution)/shard_map/ppermute | solution.py:441
  85.2 7.6 %collective-permute-done.13.refs_3_ = f32[128,384]{1,0:T(8,128)S(1)} collective-permute-done((f32[128,384]{1,0:T(8,128)S(1)}, f32[128,384]{1,0:T(8,128)S(1)}, u32[]{:S(2)}, u32[]{:S(2)}) %collective-permute-start.13) | collective-permute-done | bytes 196640 | tf_op jit(solution)/shard_map/ppermute | solution.py:324
  (49 shorter events, 11.3 us)
Async XLA Ops:
  0.6 4.2 %copy-start.2 = (f32[1,32,128]{2,1,0:T(8,128)S(1)}, f32[1,32,128]{2,1,0:T(8,128)}, u32[]{:S(2)}) copy-start(f32[1,32,128]{2,1,0:T(8,128)} %param.11) | copy-start | bytes 49156
  1.8 22.7 %collective-permute-start = (f32[2,128,640]{2,1,0:T(8,128)S(1)}, f32[2,128,640]{2,1,0:T(8,128)S(1)}, u32[]{:S(2)}, u32[]{:S(2)}) collective-permute-start(f32[2,128,640]{2,1,0:T(8,128)S(1)} %pack.3), channel_id=1, source_target_pairs={{0,1},{1,0},{2,3},{3,2},{4,5},{5,4},{6,7},{7,6},{8,9},{9,8},{10,11... | collective-permute-start | bytes 1966088 | tf_op jit(solution)/shard_map/ppermute | solution.py:324
  6.9 15.8 %collective-permute-start.1 = (f32[144,256]{1,0:T(8,128)S(1)}, f32[144,256]{1,0:T(8,128)S(1)}, u32[]{:S(2)}, u32[]{:S(2)}) collective-permute-start(f32[144,256]{1,0:T(8,128)S(1)} %get-tuple-element.61), channel_id=1, source_target_pairs={{0,1},{1,0},{2,3},{3,2},{4,5},{5,4},{6,7},{7,6},{8,9},{9,8},{10,11... | collective-permute-start | bytes 442376 | tf_op jit(solution)/shard_map/ppermute | solution.py:324
  8.5 25.8 %collective-permute-start.4 = (f32[128,1024]{1,0:T(8,128)S(1)}, f32[128,1024]{1,0:T(8,128)S(1)}, u32[]{:S(2)}, u32[]{:S(2)}) collective-permute-start(f32[128,1024]{1,0:T(8,128)S(1)} %get-tuple-element.68), channel_id=1, source_target_pairs={{0,8},{8,0},{16,24},{24,16},{1,9},{9,1},{17,25},{25,17},{2,10},{10... | collective-permute-start | bytes 1572872 | tf_op jit(solution)/shard_map/ppermute | solution.py:327
  8.6 25.7 %collective-permute-start.5 = (f32[128,1024]{1,0:T(8,128)S(1)}, f32[128,1024]{1,0:T(8,128)S(1)}, u32[]{:S(2)}, u32[]{:S(2)}) collective-permute-start(f32[128,1024]{1,0:T(8,128)S(1)} %get-tuple-element.69), channel_id=1, source_target_pairs={{0,16},{8,24},{16,0},{24,8},{1,17},{9,25},{17,1},{25,9},{2,18},{10... | collective-permute-start | bytes 1572872 | tf_op jit(solution)/shard_map/ppermute | solution.py:327
  10.5 23.8 %collective-permute-start.6 = (f32[128,1024]{1,0:T(8,128)S(1)}, f32[128,1024]{1,0:T(8,128)S(1)}, u32[]{:S(2)}, u32[]{:S(2)}) collective-permute-start(f32[128,1024]{1,0:T(8,128)S(1)} %get-tuple-element.70), channel_id=1, source_target_pairs={{0,24},{8,16},{16,8},{24,0},{1,25},{9,17},{17,9},{25,1},{2,26},{10... | collective-permute-start | bytes 1572872 | tf_op jit(solution)/shard_map/ppermute | solution.py:327
  22.7 10.3 %collective-permute-start.3 = (f32[2,128,384]{2,1,0:T(8,128)S(1)}, f32[2,128,384]{2,1,0:T(8,128)S(1)}, u32[]{:S(2)}, u32[]{:S(2)}) collective-permute-start(f32[2,128,384]{2,1,0:T(8,128)S(1)} %get-tuple-element.64), channel_id=1, source_target_pairs={{0,1},{1,0},{2,3},{3,2},{4,5},{5,4},{6,7},{7,6},{8,9},{9,8},{10,11... | collective-permute-start | bytes 1179656 | tf_op jit(solution)/shard_map/ppermute | solution.py:324
  25.9 9.3 %collective-permute-start.2 = (f32[128,640]{1,0:T(8,128)S(1)}, f32[128,640]{1,0:T(8,128)S(1)}, u32[]{:S(2)}, u32[]{:S(2)}) collective-permute-start(f32[128,640]{1,0:T(8,128)S(1)} %get-tuple-element.62), channel_id=1, source_target_pairs={{0,2},{1,3},{6,4},{7,5},{8,10},{9,11},{14,12},{15,13},{16,18},{17,... | collective-permute-start | bytes 983048 | tf_op jit(solution)/shard_map/ppermute | solution.py:385
  35.3 12.6 %copy-start.4 = (f32[32]{0:T(128)S(1)}, f32[32]{0:T(128)}, u32[]{:S(2)}) copy-start(f32[32]{0:T(128)} %skip.3) | copy-start | bytes 388
  35.4 36.6 %collective-permute-start.14 = (f32[4,128,512]{2,1,0:T(8,128)S(1)}, f32[4,128,512]{2,1,0:T(8,128)S(1)}, u32[]{:S(2)}, u32[]{:S(2)}) collective-permute-start(f32[4,128,512]{2,1,0:T(8,128)S(1)} %hand.1), channel_id=1, source_target_pairs={{0,1},{1,0},{2,3},{3,2},{4,5},{5,4},{6,7},{7,6},{8,9},{9,8},{10,11... | collective-permute-start | bytes 3145736 | tf_op jit(solution)/shard_map/ppermute | solution.py:324
  36.0 13.6 %collective-permute-start.7 = (f32[128,640]{1,0:T(8,128)S(1)}, f32[128,640]{1,0:T(8,128)S(1)}, u32[]{:S(2)}, u32[]{:S(2)}) collective-permute-start(f32[128,640]{1,0:T(8,128)S(1)} %relay.4), channel_id=1, source_target_pairs={{2,4},{3,5},{4,2},{5,3},{10,12},{11,13},{12,10},{13,11},{18,20},{1... | collective-permute-start | bytes 983048 | tf_op jit(solution)/shard_map/ppermute | solution.py:385
  36.7 10.4 %collective-permute-start.8 = (f32[128,384]{1,0:T(8,128)S(1)}, f32[128,384]{1,0:T(8,128)S(1)}, u32[]{:S(2)}, u32[]{:S(2)}) collective-permute-start(f32[128,384]{1,0:T(8,128)S(1)} %get-tuple-element.66), channel_id=1, source_target_pairs={{0,2},{1,3},{6,4},{7,5},{8,10},{9,11},{14,12},{15,13},{16,18},{17,... | collective-permute-start | bytes 589832 | tf_op jit(solution)/shard_map/ppermute | solution.py:385
  47.2 5.4 %collective-permute-start.10 = (f32[128,384]{1,0:T(8,128)S(1)}, f32[128,384]{1,0:T(8,128)S(1)}, u32[]{:S(2)}, u32[]{:S(2)}) collective-permute-start(f32[128,384]{1,0:T(8,128)S(1)} %relay.5), channel_id=1, source_target_pairs={{2,4},{3,5},{4,2},{5,3},{10,12},{11,13},{12,10},{13,11},{18,20},{1... | collective-permute-start | bytes 589832 | tf_op jit(solution)/shard_map/ppermute | solution.py:385
  49.8 13.2 %collective-permute-start.9 = (f32[128,640]{1,0:T(8,128)S(1)}, f32[128,640]{1,0:T(8,128)S(1)}, u32[]{:S(2)}, u32[]{:S(2)}) collective-permute-start(f32[128,640]{1,0:T(8,128)S(1)} %relay.6), channel_id=1, source_target_pairs={{4,6},{5,7},{2,0},{3,1},{12,14},{13,15},{10,8},{11,9},{20,22},{21,... | collective-permute-start | bytes 983048 | tf_op jit(solution)/shard_map/ppermute | solution.py:385
  52.7 12.4 %collective-permute-start.11 = (f32[128,384]{1,0:T(8,128)S(1)}, f32[128,384]{1,0:T(8,128)S(1)}, u32[]{:S(2)}, u32[]{:S(2)}) collective-permute-start(f32[128,384]{1,0:T(8,128)S(1)} %relay.7), channel_id=1, source_target_pairs={{4,6},{5,7},{2,0},{3,1},{12,14},{13,15},{10,8},{11,9},{20,22},{21,... | collective-permute-start | bytes 589832 | tf_op jit(solution)/shard_map/ppermute | solution.py:385
  65.5 6.4 %collective-permute-start.15 = (f32[2,128,256]{2,1,0:T(8,128)S(1)}, f32[2,128,256]{2,1,0:T(8,128)S(1)}, u32[]{:S(2)}, u32[]{:S(2)}) collective-permute-start(f32[2,128,256]{2,1,0:T(8,128)S(1)} %get-tuple-element.110), channel_id=1, source_target_pairs={{0,1},{1,0},{2,3},{3,2},{4,5},{5,4},{6,7},{7,6},{8,9},{9,8},{10,11... | collective-permute-start | bytes 786440 | tf_op jit(solution)/shard_map/ppermute | solution.py:324
  72.0 6.4 %collective-permute-start.17 = (f32[2,128,256]{2,1,0:T(8,128)S(1)}, f32[2,128,256]{2,1,0:T(8,128)S(1)}, u32[]{:S(2)}, u32[]{:S(2)}) collective-permute-start(f32[2,128,256]{2,1,0:T(8,128)S(1)} %add.12.refs_5_), channel_id=1, source_target_pairs={{0,16},{8,24},{16,0},{24,8},{1,17},{9,25},{17,1},{25,9},{2,18},{10... | collective-permute-start | bytes 786440 | tf_op jit(solution)/shard_map/ppermute | solution.py:327
  73.6 6.9 %collective-permute-start.16 = (f32[2,128,256]{2,1,0:T(8,128)S(1)}, f32[2,128,256]{2,1,0:T(8,128)S(1)}, u32[]{:S(2)}, u32[]{:S(2)}) collective-permute-start(f32[2,128,256]{2,1,0:T(8,128)S(1)} %add.12.refs_5_), channel_id=1, source_target_pairs={{0,8},{8,0},{16,24},{24,16},{1,9},{9,1},{17,25},{25,17},{2,10},{10... | collective-permute-start | bytes 786440 | tf_op jit(solution)/shard_map/ppermute | solution.py:327
  78.5 2.0 %collective-permute-start.18 = (f32[2,128,256]{2,1,0:T(8,128)S(1)}, f32[2,128,256]{2,1,0:T(8,128)S(1)}, u32[]{:S(2)}, u32[]{:S(2)}) collective-permute-start(f32[2,128,256]{2,1,0:T(8,128)S(1)} %collective-permute-done.17.refs_7_), channel_id=1, source_target_pairs={{0,8},{8,0},{16,24},{24,16},{1,9},{9,1},{17,25},{25,17},{2,10},{10... | collective-permute-start | bytes 786440 | tf_op jit(solution)/shard_map/ppermute | solution.py:327
  78.5 14.3 %collective-permute-start.12 = (f32[128,640]{1,0:T(8,128)S(1)}, f32[128,640]{1,0:T(8,128)S(1)}, u32[]{:S(2)}, u32[]{:S(2)}) collective-permute-start(f32[128,640]{1,0:T(8,128)S(1)} %get-tuple-element.103), channel_id=1, source_target_pairs={{0,1},{1,0},{2,3},{3,2},{4,5},{5,4},{6,7},{7,6},{8,9},{9,8},{10,11... | collective-permute-start | bytes 983048 | tf_op jit(solution)/shard_map/ppermute | solution.py:324
  78.9 13.9 %collective-permute-start.13 = (f32[128,384]{1,0:T(8,128)S(1)}, f32[128,384]{1,0:T(8,128)S(1)}, u32[]{:S(2)}, u32[]{:S(2)}) collective-permute-start(f32[128,384]{1,0:T(8,128)S(1)} %get-tuple-element.104), channel_id=1, source_target_pairs={{0,1},{1,0},{2,3},{3,2},{4,5},{5,4},{6,7},{7,6},{8,9},{9,8},{10,11... | collective-permute-start | bytes 589832 | tf_op jit(solution)/shard_map/ppermute | solution.py:324
  81.4 12.3 %collective-permute-start.19 = (f32[128,256]{1,0:T(8,128)S(1)}, f32[128,256]{1,0:T(8,128)S(1)}, u32[]{:S(2)}, u32[]{:S(2)}) collective-permute-start(f32[128,256]{1,0:T(8,128)S(1)} %get-tuple-element.113), channel_id=1, source_target_pairs={{0,2},{1,3},{2,4},{3,5},{4,6},{5,7},{6,0},{7,1},{8,10},{9,11},{10,... | collective-permute-start | bytes 393224 | tf_op jit(solution)/shard_map/ppermute | solution.py:441
  81.4 12.8 %collective-permute-start.20 = (f32[128,256]{1,0:T(8,128)S(1)}, f32[128,256]{1,0:T(8,128)S(1)}, u32[]{:S(2)}, u32[]{:S(2)}) collective-permute-start(f32[128,256]{1,0:T(8,128)S(1)} %get-tuple-element.114), channel_id=1, source_target_pairs={{0,4},{1,5},{2,6},{3,7},{4,0},{5,1},{6,2},{7,3},{8,12},{9,13},{10,... | collective-permute-start | bytes 393224 | tf_op jit(solution)/shard_map/ppermute | solution.py:441
  84.4 9.8 %collective-permute-start.21 = (f32[128,256]{1,0:T(8,128)S(1)}, f32[128,256]{1,0:T(8,128)S(1)}, u32[]{:S(2)}, u32[]{:S(2)}) collective-permute-start(f32[128,256]{1,0:T(8,128)S(1)} %get-tuple-element.115), channel_id=1, source_target_pairs={{0,6},{1,7},{2,0},{3,1},{4,2},{5,3},{6,4},{7,5},{8,14},{9,15},{10,... | collective-permute-start | bytes 393224 | tf_op jit(solution)/shard_map/ppermute | solution.py:441
  (3 other events, 10.0 us)

commit v13 on v12

--- a/solution.py
+++ b/solution.py
@@ -383,7 +383,7 @@
         pairs += [(top * q + i, (top - 1) * q + i) for i in range(q)]
         for c in range(PARTS):
             came = lax.ppermute(sent[c], "seq", pairs)
-            if t == max(planes - 3, 0):
+            if t == planes - 2:
                 came = behind(came, local[c])
             if c > 0 and t < planes - 2:
                 came = behind(came, sent[c - 1])

time: 95.2 us -> 94 us (0.987)
  waiting for transfers between devices: 49.3 us -> 47.8 us
    ppermute x6, waiting for transfers between devices: 14.6 us -> 13.4 us  [on_device(): came = lax.ppermute(sent[c], 'seq', pairs)]
  transfers between devices with their start and end apart: 22 -> 22, of which waited for: 10 -> 9; matrix products, arithmetic and copies ran while one was open for 0% -> 0% of each run, Pallas kernels for 11% -> 12%
where the time goes in v13:
time: 94 us; the launch traced here: 93.8 us
  waiting for transfers between devices  47.8 us (51%)
  starting transfers between devices  30.5 us (32%)
  Pallas kernels  12.2 us (13%)
  local copies, waits for them, and re-layouts  1.6 us (2%)
    ppermute x7, waiting for transfers between devices, swap(): return lax.ppermute(value, 'seq', pairs)  28.9 us
    ppermute x6, starting transfers between devices, on_device(): came = lax.ppermute(sent[c], 'seq', pairs)  14.5 us
    ppermute x6, waiting for transfers between devices, on_device(): came = lax.ppermute(sent[c], 'seq', pairs)  13.4 us
    pallas_call x17, Pallas kernels, run(): pl.pallas_call(body, out_shape=tuple((o[0] if isinstance(o, list) else pl...  12.2 us
    ppermute x7, starting transfers between devices, swap(): return lax.ppermute(value, 'seq', pairs)  8.52 us
    ppermute x6, waiting for transfers between devices, across(): return lax.ppermute(value, 'dp', [(i, i ^ r) for i in range(n_dp)])  4.9 us
    ppermute x3, starting transfers between devices, on_device(): grad_weight = grad_weight + lax.ppermute(pieces[r], 'seq', pairs)  3.87 us
    ppermute x6, starting transfers between devices, across(): return lax.ppermute(value, 'dp', [(i, i ^ r) for i in range(n_dp)])  3.61 us
  transfers between devices with their start and end apart: 22, of which 9 were waited for; matrix products, arithmetic and copies ran while one was open for 0% of the time, Pallas kernels for 12%

profile of v13, /device:TPU:0, one launch (start us, length us, event | category | flops | bytes accessed | tf_op | source)
XLA Modules:
  0.0 93.8 jit_solution(13825250911517128632)
XLA Ops:
  0.7 1.2 %pack.3 = f32[2,128,640]{2,1,0:T(8,128)S(1)} custom-call(bf16[128,2048]{1,0:T(8,128)(2,1)} %bitcast.10, bf16[128,2048]{1,0:T(8,128)(2,1)} %bitcast.12), custom_call_target="tpu_custom_call" | custom-call | tf_op jit(solution)/shard_map/pack/pallas_call | solution.py:63
  1.8 3.0 %collective-permute-start = (f32[2,128,640]{2,1,0:T(8,128)S(1)}, f32[2,128,640]{2,1,0:T(8,128)S(1)}, u32[]{:S(2)}, u32[]{:S(2)}) collective-permute-start(f32[2,128,640]{2,1,0:T(8,128)S(1)} %pack.3), channel_id=1, source_target_pairs={{0,1},{1,0},{2,3},{3,2},{4,5},{5,4},{6,7},{7,6},{8,9},{9,8},{10,11... | collective-permute-start | bytes 1966088 | tf_op jit(solution)/shard_map/ppermute | solution.py:324
  4.9 1.6 %copy-done.1 = bf16[4096,256]{1,0:T(8,128)(2,1)S(1)} copy-done((bf16[4096,256]{1,0:T(8,128)(2,1)S(1)}, bf16[4096,256]{1,0:T(8,128)(2,1)}, u32[]{:S(2)}) %copy-start.1) | copy-done | bytes 2097176
  7.1 1.2 %pack.2 = (f32[2,128,384]{2,1,0:T(8,128)S(1)}, bf16[2,128,1024]{2,1,0:T(8,128)(2,1)S(1)}) custom-call(bf16[128,2048]{1,0:T(8,128)(2,1)} %bitcast.11, bf16[128,2048]{1,0:T(8,128)(2,1)} %bitcast.13), custom_call_target="tpu_custom_call" | custom-call | tf_op jit(solution)/shard_map/pack/pallas_call | solution.py:63
  8.6 1.9 %collective-permute-start.5 = (f32[128,1024]{1,0:T(8,128)S(1)}, f32[128,1024]{1,0:T(8,128)S(1)}, u32[]{:S(2)}, u32[]{:S(2)}) collective-permute-start(f32[128,1024]{1,0:T(8,128)S(1)} %get-tuple-element.69), channel_id=1, source_target_pairs={{0,16},{8,24},{16,0},{24,8},{1,17},{9,25},{17,1},{25,9},{2,18},{10... | collective-permute-start | bytes 1572872 | tf_op jit(solution)/shard_map/ppermute | solution.py:327
  10.6 12.1 %collective-permute-done.1.refs_3_ = f32[144,256]{1,0:T(8,128)S(1)} collective-permute-done((f32[144,256]{1,0:T(8,128)S(1)}, f32[144,256]{1,0:T(8,128)S(1)}, u32[]{:S(2)}, u32[]{:S(2)}) %collective-permute-start.1) | collective-permute-done | bytes 147488 | tf_op jit(solution)/shard_map/ppermute | solution.py:324
  22.7 1.7 %collective-permute-start.3 = (f32[2,128,384]{2,1,0:T(8,128)S(1)}, f32[2,128,384]{2,1,0:T(8,128)S(1)}, u32[]{:S(2)}, u32[]{:S(2)}) collective-permute-start(f32[2,128,384]{2,1,0:T(8,128)S(1)} %get-tuple-element.64), channel_id=1, source_target_pairs={{0,1},{1,0},{2,3},{3,2},{4,5},{5,4},{6,7},{7,6},{8,9},{9,8},{10,11... | collective-permute-start | bytes 1179656 | tf_op jit(solution)/shard_map/ppermute | solution.py:324
  24.5 1.4 %states.2 = (bf16[4,2,128,640]{3,2,1,0:T(8,128)(2,1)S(1)}, f32[2,2,128,640]{3,2,1,0:T(8,128)S(1)}, f32[2,128,640]{2,1,0:T(8,128)S(1)}, f32[2,1,640]{2,1,0:T(1,12...) custom-call(bf16[2,128,1024]{2,1,0:T(8,128)(2,1)S(1)} %get-tuple-ele, ...), custom_call_target="tpu_custom_call" | custom-call | tf_op jit(solution)/shard_map/states/pallas_call | solution.py:63
  25.9 3.5 %collective-permute-start.2 = (f32[128,640]{1,0:T(8,128)S(1)}, f32[128,640]{1,0:T(8,128)S(1)}, u32[]{:S(2)}, u32[]{:S(2)}) collective-permute-start(f32[128,640]{1,0:T(8,128)S(1)} %get-tuple-element.62), channel_id=1, source_target_pairs={{0,2},{1,3},{6,4},{7,5},{8,10},{9,11},{14,12},{15,13},{16,18},{17,... | collective-permute-start | bytes 983048 | tf_op jit(solution)/shard_map/ppermute | solution.py:385
  29.4 3.6 %collective-permute-done.3.refs_1_ = f32[2,128,384]{2,1,0:T(8,128)S(1)} collective-permute-done((f32[2,128,384]{2,1,0:T(8,128)S(1)}, f32[2,128,384]{2,1,0:T(8,128)S(1)}, u32[]{:S(2)}, u32[]{:S(2)}) %collective-permute-start.3) | collective-permute-done | bytes 393248 | tf_op jit(solution)/shard_map/ppermute | solution.py:324
  33.0 1.3 %states.3 = (bf16[4,2,128,384]{3,2,1,0:T(8,128)(2,1)S(1)}, f32[2,2,128,384]{3,2,1,0:T(8,128)S(1)}, f32[2,128,384]{2,1,0:T(8,128)S(1)}, f32[2,1,384]{2,1,0:T(1,12...) custom-call(bf16[2,128,1024]{2,1,0:T(8,128)(2,1)S(1)} %get-tuple-ele, ...), custom_call_target="tpu_custom_call" | custom-call | tf_op jit(solution)/shard_map/states/pallas_call | solution.py:63
  36.7 7.1 %collective-permute-start.8 = (f32[128,384]{1,0:T(8,128)S(1)}, f32[128,384]{1,0:T(8,128)S(1)}, u32[]{:S(2)}, u32[]{:S(2)}) collective-permute-start(f32[128,384]{1,0:T(8,128)S(1)} %get-tuple-element.66), channel_id=1, source_target_pairs={{0,2},{1,3},{6,4},{7,5},{8,10},{9,11},{14,12},{15,13},{16,18},{17,... | collective-permute-start | bytes 589832 | tf_op jit(solution)/shard_map/ppermute | solution.py:385
  43.8 3.3 %collective-permute-done.8.came.refs_0_ = f32[128,384]{1,0:T(8,128)S(1)} collective-permute-done((f32[128,384]{1,0:T(8,128)S(1)}, f32[128,384]{1,0:T(8,128)S(1)}, u32[]{:S(2)}, u32[]{:S(2)}) %collective-permute-start.8) | collective-permute-done | bytes 196640 | tf_op jit(solution)/shard_map/ppermute | solution.py:385
  47.9 1.3 %collective-permute-start.9 = (f32[128,640]{1,0:T(8,128)S(1)}, f32[128,640]{1,0:T(8,128)S(1)}, u32[]{:S(2)}, u32[]{:S(2)}) collective-permute-start(f32[128,640]{1,0:T(8,128)S(1)} %relay.6), channel_id=1, source_target_pairs={{4,6},{5,7},{2,0},{3,1},{12,14},{13,15},{10,8},{11,9},{20,22},{21,... | collective-permute-start | bytes 983048 | tf_op jit(solution)/shard_map/ppermute | solution.py:385
  49.3 1.3 %collective-permute-start.11 = (f32[128,384]{1,0:T(8,128)S(1)}, f32[128,384]{1,0:T(8,128)S(1)}, u32[]{:S(2)}, u32[]{:S(2)}) collective-permute-start(f32[128,384]{1,0:T(8,128)S(1)} %relay.7), channel_id=1, source_target_pairs={{4,6},{5,7},{2,0},{3,1},{12,14},{13,15},{10,8},{11,9},{20,22},{21,... | collective-permute-start | bytes 589832 | tf_op jit(solution)/shard_map/ppermute | solution.py:385
  50.6 1.8 %local.2 = (f32[2,128,640]{2,1,0:T(8,128)S(1)}, f32[2,128,256]{2,1,0:T(8,128)S(1)}) custom-call(f32[32]{0:T(128)S(1)} %copy-done.4, bf16[4,2,128,640]{3,2,1,0:T(8,128)(2,1)S(1)} %get-tuple-element.78.rows16.refs_3_, bf16[2,128,256]{2,1,0:T(8,128)(2,1)S(1)} %get-tuple-element.79.bcs.refs_7_, f32[2,10,128]{2,1,0:T(8,128)S(1)} %get-tuple-element.80.cums, ...), custom_call_target="tpu_custom_call" | custom-call | tf_op jit(solution)/shard_map/local/pallas_call | solution.py:63
  52.4 1.6 %local.3 = (f32[2,128,384]{2,1,0:T(8,128)S(1)}, f32[2,128,256]{2,1,0:T(8,128)S(1)}) custom-call(f32[32]{0:T(128)S(1)} %copy-done.4, bf16[4,2,128,384]{3,2,1,0:T(8,128)(2,1)S(1)} %get-tuple-element.91.rows16.refs_3_, bf16[2,128,256]{2,1,0:T(8,128)(2,1)S(1)} %get-tuple-element.92.bcs.refs_7_, f32[2,6,128]{2,1,0:T(8,128)S(1)} %get-tuple-element.93.cums, ...), custom_call_target="tpu_custom_call" | custom-call | tf_op jit(solution)/shard_map/local/pallas_call | solution.py:63
  54.0 9.3 %collective-permute-done.11.refs_2_ = f32[128,384]{1,0:T(8,128)S(1)} collective-permute-done((f32[128,384]{1,0:T(8,128)S(1)}, f32[128,384]{1,0:T(8,128)S(1)}, u32[]{:S(2)}, u32[]{:S(2)}) %collective-permute-start.11) | collective-permute-done | bytes 196640 | tf_op jit(solution)/shard_map/ppermute | solution.py:385
  65.2 5.6 %collective-permute-done.15 = f32[2,128,256]{2,1,0:T(8,128)S(1)} collective-permute-done((f32[2,128,256]{2,1,0:T(8,128)S(1)}, f32[2,128,256]{2,1,0:T(8,128)S(1)}, u32[]{:S(2)}, u32[]{:S(2)}) %collective-permute-start.15) | collective-permute-done | bytes 262176 | tf_op jit(solution)/shard_map/ppermute | solution.py:324
  70.8 1.5 %collective-permute-start.17 = (f32[2,128,256]{2,1,0:T(8,128)S(1)}, f32[2,128,256]{2,1,0:T(8,128)S(1)}, u32[]{:S(2)}, u32[]{:S(2)}) collective-permute-start(f32[2,128,256]{2,1,0:T(8,128)S(1)} %add.12.refs_5_), channel_id=1, source_target_pairs={{0,16},{8,24},{16,0},{24,8},{1,17},{9,25},{17,1},{25,9},{2,18},{10... | collective-permute-start | bytes 786440 | tf_op jit(solution)/shard_map/ppermute | solution.py:327
  72.4 4.9 %collective-permute-done.17.refs_7_ = f32[2,128,256]{2,1,0:T(8,128)S(1)} collective-permute-done((f32[2,128,256]{2,1,0:T(8,128)S(1)}, f32[2,128,256]{2,1,0:T(8,128)S(1)}, u32[]{:S(2)}, u32[]{:S(2)}) %collective-permute-start.17) | collective-permute-done | bytes 262176 | tf_op jit(solution)/shard_map/ppermute | solution.py:327
  78.0 1.2 %collective-permute-start.13 = (f32[128,384]{1,0:T(8,128)S(1)}, f32[128,384]{1,0:T(8,128)S(1)}, u32[]{:S(2)}, u32[]{:S(2)}) collective-permute-start(f32[128,384]{1,0:T(8,128)S(1)} %get-tuple-element.104), channel_id=1, source_target_pairs={{0,1},{1,0},{2,3},{3,2},{4,5},{5,4},{6,7},{7,6},{8,9},{9,8},{10,11... | collective-permute-start | bytes 589832 | tf_op jit(solution)/shard_map/ppermute | solution.py:324
  80.2 3.0 %collective-permute-start.20 = (f32[128,256]{1,0:T(8,128)S(1)}, f32[128,256]{1,0:T(8,128)S(1)}, u32[]{:S(2)}, u32[]{:S(2)}) collective-permute-start(f32[128,256]{1,0:T(8,128)S(1)} %get-tuple-element.114), channel_id=1, source_target_pairs={{0,4},{1,5},{2,6},{3,7},{4,0},{5,1},{6,2},{7,3},{8,12},{9,13},{10,... | collective-permute-start | bytes 393224 | tf_op jit(solution)/shard_map/ppermute | solution.py:441
  84.0 7.6 %collective-permute-done.13.refs_3_ = f32[128,384]{1,0:T(8,128)S(1)} collective-permute-done((f32[128,384]{1,0:T(8,128)S(1)}, f32[128,384]{1,0:T(8,128)S(1)}, u32[]{:S(2)}, u32[]{:S(2)}) %collective-permute-start.13) | collective-permute-done | bytes 196640 | tf_op jit(solution)/shard_map/ppermute | solution.py:324
  (49 shorter events, 10.8 us)
Async XLA Ops:
  0.6 4.2 %copy-start.2 = (f32[1,32,128]{2,1,0:T(8,128)S(1)}, f32[1,32,128]{2,1,0:T(8,128)}, u32[]{:S(2)}) copy-start(f32[1,32,128]{2,1,0:T(8,128)} %param.11) | copy-start | bytes 49156
  0.6 4.2 %copy-start.3 = (f32[1,32,128]{2,1,0:T(8,128)S(1)}, f32[1,32,128]{2,1,0:T(8,128)}, u32[]{:S(2)}) copy-start(f32[1,32,128]{2,1,0:T(8,128)} %param.10) | copy-start | bytes 49156
  1.8 22.7 %collective-permute-start = (f32[2,128,640]{2,1,0:T(8,128)S(1)}, f32[2,128,640]{2,1,0:T(8,128)S(1)}, u32[]{:S(2)}, u32[]{:S(2)}) collective-permute-start(f32[2,128,640]{2,1,0:T(8,128)S(1)} %pack.3), channel_id=1, source_target_pairs={{0,1},{1,0},{2,3},{3,2},{4,5},{5,4},{6,7},{7,6},{8,9},{9,8},{10,11... | collective-permute-start | bytes 1966088 | tf_op jit(solution)/shard_map/ppermute | solution.py:324
  6.9 15.8 %collective-permute-start.1 = (f32[144,256]{1,0:T(8,128)S(1)}, f32[144,256]{1,0:T(8,128)S(1)}, u32[]{:S(2)}, u32[]{:S(2)}) collective-permute-start(f32[144,256]{1,0:T(8,128)S(1)} %get-tuple-element.61), channel_id=1, source_target_pairs={{0,1},{1,0},{2,3},{3,2},{4,5},{5,4},{6,7},{7,6},{8,9},{9,8},{10,11... | collective-permute-start | bytes 442376 | tf_op jit(solution)/shard_map/ppermute | solution.py:324
  8.5 25.8 %collective-permute-start.4 = (f32[128,1024]{1,0:T(8,128)S(1)}, f32[128,1024]{1,0:T(8,128)S(1)}, u32[]{:S(2)}, u32[]{:S(2)}) collective-permute-start(f32[128,1024]{1,0:T(8,128)S(1)} %get-tuple-element.68), channel_id=1, source_target_pairs={{0,8},{8,0},{16,24},{24,16},{1,9},{9,1},{17,25},{25,17},{2,10},{10... | collective-permute-start | bytes 1572872 | tf_op jit(solution)/shard_map/ppermute | solution.py:327
  8.6 25.8 %collective-permute-start.5 = (f32[128,1024]{1,0:T(8,128)S(1)}, f32[128,1024]{1,0:T(8,128)S(1)}, u32[]{:S(2)}, u32[]{:S(2)}) collective-permute-start(f32[128,1024]{1,0:T(8,128)S(1)} %get-tuple-element.69), channel_id=1, source_target_pairs={{0,16},{8,24},{16,0},{24,8},{1,17},{9,25},{17,1},{25,9},{2,18},{10... | collective-permute-start | bytes 1572872 | tf_op jit(solution)/shard_map/ppermute | solution.py:327
  10.5 23.8 %collective-permute-start.6 = (f32[128,1024]{1,0:T(8,128)S(1)}, f32[128,1024]{1,0:T(8,128)S(1)}, u32[]{:S(2)}, u32[]{:S(2)}) collective-permute-start(f32[128,1024]{1,0:T(8,128)S(1)} %get-tuple-element.70), channel_id=1, source_target_pairs={{0,24},{8,16},{16,8},{24,0},{1,25},{9,17},{17,9},{25,1},{2,26},{10... | collective-permute-start | bytes 1572872 | tf_op jit(solution)/shard_map/ppermute | solution.py:327
  22.7 10.3 %collective-permute-start.3 = (f32[2,128,384]{2,1,0:T(8,128)S(1)}, f32[2,128,384]{2,1,0:T(8,128)S(1)}, u32[]{:S(2)}, u32[]{:S(2)}) collective-permute-start(f32[2,128,384]{2,1,0:T(8,128)S(1)} %get-tuple-element.64), channel_id=1, source_target_pairs={{0,1},{1,0},{2,3},{3,2},{4,5},{5,4},{6,7},{7,6},{8,9},{9,8},{10,11... | collective-permute-start | bytes 1179656 | tf_op jit(solution)/shard_map/ppermute | solution.py:324
  25.9 9.3 %collective-permute-start.2 = (f32[128,640]{1,0:T(8,128)S(1)}, f32[128,640]{1,0:T(8,128)S(1)}, u32[]{:S(2)}, u32[]{:S(2)}) collective-permute-start(f32[128,640]{1,0:T(8,128)S(1)} %get-tuple-element.62), channel_id=1, source_target_pairs={{0,2},{1,3},{6,4},{7,5},{8,10},{9,11},{14,12},{15,13},{16,18},{17,... | collective-permute-start | bytes 983048 | tf_op jit(solution)/shard_map/ppermute | solution.py:385
  35.4 35.4 %collective-permute-start.14 = (f32[4,128,512]{2,1,0:T(8,128)S(1)}, f32[4,128,512]{2,1,0:T(8,128)S(1)}, u32[]{:S(2)}, u32[]{:S(2)}) collective-permute-start(f32[4,128,512]{2,1,0:T(8,128)S(1)} %hand.1), channel_id=1, source_target_pairs={{0,1},{1,0},{2,3},{3,2},{4,5},{5,4},{6,7},{7,6},{8,9},{9,8},{10,11... | collective-permute-start | bytes 3145736 | tf_op jit(solution)/shard_map/ppermute | solution.py:324
  36.0 11.8 %collective-permute-start.7 = (f32[128,640]{1,0:T(8,128)S(1)}, f32[128,640]{1,0:T(8,128)S(1)}, u32[]{:S(2)}, u32[]{:S(2)}) collective-permute-start(f32[128,640]{1,0:T(8,128)S(1)} %relay.4), channel_id=1, source_target_pairs={{2,4},{3,5},{4,2},{5,3},{10,12},{11,13},{12,10},{13,11},{18,20},{1... | collective-permute-start | bytes 983048 | tf_op jit(solution)/shard_map/ppermute | solution.py:385
  36.7 10.4 %collective-permute-start.8 = (f32[128,384]{1,0:T(8,128)S(1)}, f32[128,384]{1,0:T(8,128)S(1)}, u32[]{:S(2)}, u32[]{:S(2)}) collective-permute-start(f32[128,384]{1,0:T(8,128)S(1)} %get-tuple-element.66), channel_id=1, source_target_pairs={{0,2},{1,3},{6,4},{7,5},{8,10},{9,11},{14,12},{15,13},{16,18},{17,... | collective-permute-start | bytes 589832 | tf_op jit(solution)/shard_map/ppermute | solution.py:385
  47.2 2.1 %collective-permute-start.10 = (f32[128,384]{1,0:T(8,128)S(1)}, f32[128,384]{1,0:T(8,128)S(1)}, u32[]{:S(2)}, u32[]{:S(2)}) collective-permute-start(f32[128,384]{1,0:T(8,128)S(1)} %relay.5), channel_id=1, source_target_pairs={{2,4},{3,5},{4,2},{5,3},{10,12},{11,13},{12,10},{13,11},{18,20},{1... | collective-permute-start | bytes 589832 | tf_op jit(solution)/shard_map/ppermute | solution.py:385
  47.9 15.3 %collective-permute-start.9 = (f32[128,640]{1,0:T(8,128)S(1)}, f32[128,640]{1,0:T(8,128)S(1)}, u32[]{:S(2)}, u32[]{:S(2)}) collective-permute-start(f32[128,640]{1,0:T(8,128)S(1)} %relay.6), channel_id=1, source_target_pairs={{4,6},{5,7},{2,0},{3,1},{12,14},{13,15},{10,8},{11,9},{20,22},{21,... | collective-permute-start | bytes 983048 | tf_op jit(solution)/shard_map/ppermute | solution.py:385
  49.3 14.0 %collective-permute-start.11 = (f32[128,384]{1,0:T(8,128)S(1)}, f32[128,384]{1,0:T(8,128)S(1)}, u32[]{:S(2)}, u32[]{:S(2)}) collective-permute-start(f32[128,384]{1,0:T(8,128)S(1)} %relay.7), channel_id=1, source_target_pairs={{4,6},{5,7},{2,0},{3,1},{12,14},{13,15},{10,8},{11,9},{20,22},{21,... | collective-permute-start | bytes 589832 | tf_op jit(solution)/shard_map/ppermute | solution.py:385
  64.3 6.4 %collective-permute-start.15 = (f32[2,128,256]{2,1,0:T(8,128)S(1)}, f32[2,128,256]{2,1,0:T(8,128)S(1)}, u32[]{:S(2)}, u32[]{:S(2)}) collective-permute-start(f32[2,128,256]{2,1,0:T(8,128)S(1)} %get-tuple-element.110), channel_id=1, source_target_pairs={{0,1},{1,0},{2,3},{3,2},{4,5},{5,4},{6,7},{7,6},{8,9},{9,8},{10,11... | collective-permute-start | bytes 786440 | tf_op jit(solution)/shard_map/ppermute | solution.py:324
  70.8 6.4 %collective-permute-start.17 = (f32[2,128,256]{2,1,0:T(8,128)S(1)}, f32[2,128,256]{2,1,0:T(8,128)S(1)}, u32[]{:S(2)}, u32[]{:S(2)}) collective-permute-start(f32[2,128,256]{2,1,0:T(8,128)S(1)} %add.12.refs_5_), channel_id=1, source_target_pairs={{0,16},{8,24},{16,0},{24,8},{1,17},{9,25},{17,1},{25,9},{2,18},{10... | collective-permute-start | bytes 786440 | tf_op jit(solution)/shard_map/ppermute | solution.py:327
  72.4 6.9 %collective-permute-start.16 = (f32[2,128,256]{2,1,0:T(8,128)S(1)}, f32[2,128,256]{2,1,0:T(8,128)S(1)}, u32[]{:S(2)}, u32[]{:S(2)}) collective-permute-start(f32[2,128,256]{2,1,0:T(8,128)S(1)} %add.12.refs_5_), channel_id=1, source_target_pairs={{0,8},{8,0},{16,24},{24,16},{1,9},{9,1},{17,25},{25,17},{2,10},{10... | collective-permute-start | bytes 786440 | tf_op jit(solution)/shard_map/ppermute | solution.py:327
  77.3 2.0 %collective-permute-start.18 = (f32[2,128,256]{2,1,0:T(8,128)S(1)}, f32[2,128,256]{2,1,0:T(8,128)S(1)}, u32[]{:S(2)}, u32[]{:S(2)}) collective-permute-start(f32[2,128,256]{2,1,0:T(8,128)S(1)} %collective-permute-done.17.refs_7_), channel_id=1, source_target_pairs={{0,8},{8,0},{16,24},{24,16},{1,9},{9,1},{17,25},{25,17},{2,10},{10... | collective-permute-start | bytes 786440 | tf_op jit(solution)/shard_map/ppermute | solution.py:327
  77.3 14.3 %collective-permute-start.12 = (f32[128,640]{1,0:T(8,128)S(1)}, f32[128,640]{1,0:T(8,128)S(1)}, u32[]{:S(2)}, u32[]{:S(2)}) collective-permute-start(f32[128,640]{1,0:T(8,128)S(1)} %get-tuple-element.103), channel_id=1, source_target_pairs={{0,1},{1,0},{2,3},{3,2},{4,5},{5,4},{6,7},{7,6},{8,9},{9,8},{10,11... | collective-permute-start | bytes 983048 | tf_op jit(solution)/shard_map/ppermute | solution.py:324
  78.0 13.6 %collective-permute-start.13 = (f32[128,384]{1,0:T(8,128)S(1)}, f32[128,384]{1,0:T(8,128)S(1)}, u32[]{:S(2)}, u32[]{:S(2)}) collective-permute-start(f32[128,384]{1,0:T(8,128)S(1)} %get-tuple-element.104), channel_id=1, source_target_pairs={{0,1},{1,0},{2,3},{3,2},{4,5},{5,4},{6,7},{7,6},{8,9},{9,8},{10,11... | collective-permute-start | bytes 589832 | tf_op jit(solution)/shard_map/ppermute | solution.py:324
  80.2 12.3 %collective-permute-start.19 = (f32[128,256]{1,0:T(8,128)S(1)}, f32[128,256]{1,0:T(8,128)S(1)}, u32[]{:S(2)}, u32[]{:S(2)}) collective-permute-start(f32[128,256]{1,0:T(8,128)S(1)} %get-tuple-element.113), channel_id=1, source_target_pairs={{0,2},{1,3},{2,4},{3,5},{4,6},{5,7},{6,0},{7,1},{8,10},{9,11},{10,... | collective-permute-start | bytes 393224 | tf_op jit(solution)/shard_map/ppermute | solution.py:441
  80.2 12.8 %collective-permute-start.20 = (f32[128,256]{1,0:T(8,128)S(1)}, f32[128,256]{1,0:T(8,128)S(1)}, u32[]{:S(2)}, u32[]{:S(2)}) collective-permute-start(f32[128,256]{1,0:T(8,128)S(1)} %get-tuple-element.114), channel_id=1, source_target_pairs={{0,4},{1,5},{2,6},{3,7},{4,0},{5,1},{6,2},{7,3},{8,12},{9,13},{10,... | collective-permute-start | bytes 393224 | tf_op jit(solution)/shard_map/ppermute | solution.py:441
  83.2 9.8 %collective-permute-start.21 = (f32[128,256]{1,0:T(8,128)S(1)}, f32[128,256]{1,0:T(8,128)S(1)}, u32[]{:S(2)}, u32[]{:S(2)}) collective-permute-start(f32[128,256]{1,0:T(8,128)S(1)} %get-tuple-element.115), channel_id=1, source_target_pairs={{0,6},{1,7},{2,0},{3,1},{4,2},{5,3},{6,4},{7,5},{8,14},{9,15},{10,... | collective-permute-start | bytes 393224 | tf_op jit(solution)/shard_map/ppermute | solution.py:441
  (3 other events, 9.3 us)
